TPU v7x, 32 devices: a whole 2x2x4 slice. The times are simulated.
32 devices in a mesh: wide: 8 (over y, x, core), narrow: 4 (over z).
Axes of the slice: x: 2, y: 2, z: 4, core: 2. Of those that a mesh axis runs over, the one named last changes fastest.
Arguments:
- tokens: bfloat16 [8192, 768], P(('wide', 'narrow')), may hold values from -6 to 6
- norm_gain: bfloat16 [768], P(('wide', 'narrow')), may hold values from 0.25 to 1.75
- w_in: bfloat16 [768, 3, 3072], P(('wide', 'narrow')), may hold values from -0.21875 to 0.21875
- conv_w: bfloat16 [4, 1536], P(None, ('wide', 'narrow')), may hold values from -0.5 to 0.5
- conv_b: bfloat16 [1536], P(('wide', 'narrow')), may hold values from -0.5 to 0.5
- w_x: bfloat16 [1536, 3, 80], P(('wide', 'narrow')), may hold values from -0.15625 to 0.15625
- w_dt: bfloat16 [48, 3, 1536], P(None, None, ('wide', 'narrow')), may hold values from -0.875 to 0.875
- dt_bias: bfloat16 [3, 1536], P(None, ('wide', 'narrow')), may hold values from -6.875 to -2.25
- a_log: bfloat16 [1536, 16], P(('wide', 'narrow')), may hold values from 0 to 2.765625
- d_skip: bfloat16 [1536], P(('wide', 'narrow')), may hold values from 0.5 to 1.5
- w_out: bfloat16 [1536, 3, 768], P(('wide', 'narrow')), may hold values from -0.4375 to 0.4375
- mod_ids: int32 [8192], P(('wide', 'narrow')), may hold values from 0 to 2, as said below
- split_at: int32 [8], P('wide'), may hold values from 128 to 896, as said below
- cotangent: bfloat16 [8192, 768], P(('wide', 'narrow')), may hold values from -6 to 6
Outputs:
- mixed: bfloat16 [8192, 768], P(('wide', 'narrow'))
- grad_tokens: bfloat16 [8192, 768], P(('wide', 'narrow'))
- grad_norm_gain: float32 [768], P(('wide', 'narrow'))
- grad_w_in: float32 [768, 3, 3072], P(('wide', 'narrow'))
- grad_conv_w: float32 [4, 1536], P(None, ('wide', 'narrow'))
- grad_conv_b: float32 [1536], P(('wide', 'narrow'))
- grad_w_x: float32 [1536, 3, 80], P(('wide', 'narrow'))
- grad_w_dt: float32 [48, 3, 1536], P(None, None, ('wide', 'narrow'))
- grad_dt_bias: float32 [3, 1536], P(None, ('wide', 'narrow'))
- grad_a_log: float32 [1536, 16], P(('wide', 'narrow'))
- grad_d_skip: float32 [1536], P(('wide', 'narrow'))
- grad_w_out: float32 [1536, 3, 768], P(('wide', 'narrow'))
Inputs may be any that keep to these rules, and one draw needn't show every extreme that they name: `mod_ids`: each aligned run of 128 tokens holds one modality. Tokens [0, split_at[g]) of group g form one sequence and [split_at[g], 1024) another; the shorter one has fewer than 256 tokens.
All inputs are finite; a program needn't handle non-finite values.
Results may differ from a plain program's by a relative error of at most 0.014.
Values may be sent and summed in bfloat16 or wider, within the bound.
No kernel may reach another device: no remote copies, remote signals or barrier semaphores. Data moves between devices by JAX's collectives and lax.ppermute only.
A program may use at most 384 MiB of HBM per device.

v0:
```python
import jax
import jax.numpy as jnp
from jax import lax
from jax.sharding import PartitionSpec as P

MODS = 3
RUN = 128
SCAN_BLOCK = 64


epsilon = 1e-05


def shifted(block, axis, distance):
    devices = range(lax.axis_size(axis))
    route = [(i - distance, i) for i in devices if i - distance in devices]
    return lax.ppermute(block, axis, route)


def entering(value, axis, combine, identity):
    peers, mine = (lax.axis_size(axis), lax.axis_index(axis))
    everything = jax.tree.map(
        lambda part, kind: lax.all_gather(part.astype(kind), axis),
        value,
        (jnp.bfloat16, jnp.bfloat16),
    )
    start = jax.tree.map(
        lambda part, zero: jnp.broadcast_to(jnp.asarray(zero, part.dtype), part.shape),
        value,
        identity,
    )

    def turn(k, before):
        reached = k < mine
        new = combine(
            before, jax.tree.map(lambda part, own: part[k].astype(own.dtype), everything, value)
        )
        return jax.tree.map(lambda a, b: jnp.where(reached, a, b), new, before)

    return lax.fori_loop(0, peers, turn, start)


def carried_in(part, axis, combine, identity):
    count = lax.axis_size(axis)
    place = lax.axis_index(axis)
    ahead = count - 1 - place
    gathered = jax.tree.map(lambda a: lax.all_gather(a, axis), part)
    state = jax.tree.map(lambda a, e: jnp.zeros_like(a) + jnp.asarray(e, a.dtype), part, identity)

    def one(turn, state):
        source = count - 1 - turn
        return combine(
            state, jax.tree.map(lambda a: lax.dynamic_index_in_dim(a, source, 0, False), gathered)
        )

    return lax.fori_loop(0, ahead, one, state)


def chain_pairs(earlier, later):
    return (earlier[0] * later[0], later[0] * earlier[1] + later[1])


def by_tile(left_rows, weights, tile_kinds, flipped):
    blocks = left_rows.reshape(tile_kinds.shape[0], -1, left_rows.shape[1])

    def one_tile(member):
        block_rows, modality = member
        chosen = lax.dynamic_index_in_dim(weights, modality, 1, keepdims=False)
        if flipped:
            return lax.dot_general(
                block_rows, chosen, (((1,), (1,)), ((), ())), preferred_element_type=jnp.float32
            )
        return jnp.dot(block_rows, chosen, preferred_element_type=jnp.float32)

    produced = lax.map(one_tile, (blocks, tile_kinds))
    return produced.reshape(left_rows.shape[0], -1)


def tile_grads(left_rows, right_rows, tile_kinds):
    tile_count = tile_kinds.shape[0]
    left_blocks = left_rows.reshape(tile_count, -1, left_rows.shape[1])
    right_blocks = right_rows.reshape(tile_count, -1, right_rows.shape[1])

    def accumulate(running, member):
        left_block, right_block, modality = member
        product = lax.dot_general(
            left_block, right_block, (((0,), (0,)), ((), ())), preferred_element_type=jnp.float32
        )
        slot_now = lax.dynamic_index_in_dim(running, modality, 1, keepdims=False)
        return (lax.dynamic_update_index_in_dim(running, slot_now + product, modality, 1), None)

    empty_grad = jnp.zeros((left_rows.shape[1], MODS, right_rows.shape[1]), jnp.float32)
    return lax.scan(accumulate, empty_grad, (left_blocks, right_blocks, tile_kinds))[0]


def fetch_rest(pieces):
    return (
        lax.all_gather(pieces[0], "wide", axis=0, tiled=True),
        lax.all_gather(pieces[1], "wide", axis=2, tiled=True),
        lax.all_gather(pieces[2], "wide", axis=1, tiled=True),
        lax.all_gather(pieces[3], "wide", axis=0, tiled=True),
        lax.all_gather(pieces[4], "wide", axis=1, tiled=True),
        lax.all_gather(pieces[5], "wide", axis=0, tiled=True),
        lax.all_gather(pieces[6], "wide", axis=0, tiled=True),
        lax.all_gather(pieces[7], "wide", axis=0, tiled=True),
    )


def fold_in_rows(weights, gains, folder, initial):
    return folder(
        initial,
        (
            lax.all_gather(weights, "wide", axis=0, tiled=True),
            lax.all_gather(gains, "wide", axis=0, tiled=True),
        ),
        jnp.int32(0),
    )


def sum_grads(in_term, own_rows, grads):
    grad_in_w = lax.psum_scatter(
        in_term(jnp.int32(0), lax.axis_size(("wide", "narrow")) * own_rows),
        ("wide", "narrow"),
        scatter_dimension=0,
        tiled=True,
    )
    summed = (
        lax.psum_scatter(grads[0], ("wide", "narrow"), scatter_dimension=0, tiled=True),
        lax.psum_scatter(grads[1], ("wide", "narrow"), scatter_dimension=2, tiled=True),
        lax.psum_scatter(grads[2], ("wide", "narrow"), scatter_dimension=1, tiled=True),
        lax.psum_scatter(grads[3], ("wide", "narrow"), scatter_dimension=0, tiled=True),
        lax.psum_scatter(grads[4], ("wide", "narrow"), scatter_dimension=1, tiled=True),
        lax.psum_scatter(grads[5], ("wide", "narrow"), scatter_dimension=0, tiled=True),
        lax.psum_scatter(grads[6], ("wide", "narrow"), scatter_dimension=0, tiled=True),
        lax.psum_scatter(grads[7], ("wide", "narrow"), scatter_dimension=0, tiled=True),
        lax.psum_scatter(grads[8], ("wide", "narrow"), scatter_dimension=0, tiled=True),
    )
    return (grad_in_w, summed)


def body(
    tokens,
    norm_gain,
    w_in,
    conv_w,
    conv_b,
    w_x,
    w_dt,
    dt_bias,
    a_log,
    d_skip,
    w_out,
    mod_ids,
    split_at,
    cotangent,
):
    row_count = tokens.shape[0]
    model_width = tokens.shape[1]
    inner = w_in.shape[2] // 2
    dt_rank = w_dt.shape[0]
    state_size = a_log.shape[1]
    conv_taps = conv_w.shape[0]
    shared = (
        lax.all_gather(w_in, "narrow", axis=0, tiled=True),
        lax.all_gather(norm_gain, "narrow", axis=0, tiled=True),
        lax.all_gather(w_x, "narrow", axis=0, tiled=True),
        lax.all_gather(w_dt, "narrow", axis=2, tiled=True),
        lax.all_gather(dt_bias, "narrow", axis=1, tiled=True),
        lax.all_gather(w_out, "narrow", axis=0, tiled=True),
        lax.all_gather(conv_w, "narrow", axis=1, tiled=True),
        lax.all_gather(conv_b, "narrow", axis=0, tiled=True),
        lax.all_gather(a_log, "narrow", axis=0, tiled=True),
        lax.all_gather(d_skip, "narrow", axis=0, tiled=True),
    )
    in_pair = (shared[0], shared[1])
    rest_pieces = shared[2:]
    places = lax.axis_index("narrow") * row_count + jnp.arange(row_count, dtype=jnp.int32)
    split_point = split_at[0]
    offsets = places - jnp.where(places >= split_point, split_point, 0)
    keeps = jnp.where((places == 0) | (places == split_point), 0.0, 1.0).astype(jnp.float32)
    tile_kinds = mod_ids.reshape(-1, RUN)[:, 0]
    onehot_low = (mod_ids[:, None] == jnp.arange(MODS, dtype=jnp.int32)[None, :]).astype(
        jnp.bfloat16
    )
    token_values = tokens.astype(jnp.float32)
    row_scale = lax.rsqrt(jnp.mean(token_values * token_values, axis=1, keepdims=True) + epsilon)
    scaled = token_values * row_scale

    def forward_fold(carried, pieces, first_row):
        weights, gains = pieces
        piece_in = (scaled * gains.astype(jnp.float32)).astype(jnp.bfloat16)
        return (by_tile(piece_in, weights, tile_kinds, False), piece_in)

    initial_in = (
        jnp.zeros((row_count, 2 * inner), jnp.float32),
        jnp.zeros((row_count, model_width), jnp.bfloat16),
    )
    projected_in, normed = fold_in_rows(in_pair[0], in_pair[1], forward_fold, initial_in)
    weights_x, weights_dt, bias_dt, weights_out, taps_w, taps_b, log_rates, skip_gain = fetch_rest(
        rest_pieces
    )
    front_half = projected_in[:, :inner]
    gate_half = projected_in[:, inner:]
    edge_rows = shifted(front_half[row_count - (conv_taps - 1) :], "narrow", 1)
    extended = jnp.concatenate([edge_rows, front_half], axis=0)
    taps_float = taps_w.astype(jnp.float32)
    valid_masks = [
        (offsets >= lag_steps).astype(jnp.float32)[:, None] for lag_steps in range(conv_taps)
    ]
    summed = jnp.zeros_like(front_half) + taps_b.astype(jnp.float32)
    for lag_steps in range(conv_taps):
        tap_index = conv_taps - 1 - lag_steps
        summed = (
            summed
            + taps_float[tap_index]
            * extended[tap_index : tap_index + row_count]
            * valid_masks[lag_steps]
        )
    mixed_low = jax.nn.silu(summed).astype(jnp.bfloat16)
    mixed_values = mixed_low.astype(jnp.float32)
    projected_x = by_tile(mixed_low, weights_x, tile_kinds, False)
    dt_low = projected_x[:, :dt_rank].astype(jnp.bfloat16)
    b_rows = projected_x[:, dt_rank : dt_rank + state_size]
    c_rows = projected_x[:, dt_rank + state_size :]
    bias_rows = jnp.dot(onehot_low, bias_dt, preferred_element_type=jnp.float32)
    dt_pre = by_tile(dt_low, weights_dt, tile_kinds, False) + bias_rows
    steps_dt = jax.nn.softplus(dt_pre)
    decay_rates = -jnp.exp(log_rates.astype(jnp.float32))
    block_count = row_count // SCAN_BLOCK

    def blocked(member):
        return member.reshape((block_count, SCAN_BLOCK) + member.shape[1:])

    dt_blocks = blocked(steps_dt)
    b_blocks = blocked(b_rows)
    c_blocks = blocked(c_rows)
    u_blocks = blocked(mixed_values)
    keep_blocks = blocked(keeps)

    def local_block(carried, member):
        state_now, product = carried
        block_dt, block_b, block_c, block_u, block_keep = member
        decay_now = jnp.exp(block_dt[:, :, None] * decay_rates[None]) * block_keep[:, None, None]
        pushed = (block_dt * block_u)[:, :, None] * block_b[:, None, :]
        pushed = pushed.at[0].add(decay_now[0] * state_now)
        cumulative, states_in = lax.associative_scan(chain_pairs, (decay_now, pushed), axis=0)
        outputs = jnp.einsum("ten,tn->te", states_in, block_c)
        return ((states_in[-1], product * cumulative[-1]), (outputs, state_now))

    zero_state = jnp.zeros((inner, state_size), jnp.float32)
    local_carry, local_blocks = lax.scan(
        local_block,
        (zero_state, jnp.ones_like(zero_state)),
        (dt_blocks, b_blocks, c_blocks, u_blocks, keep_blocks),
    )
    local_final, local_product = local_carry
    local_out, local_starts = local_blocks
    incoming = entering(
        (local_product, local_final),
        "narrow",
        chain_pairs,
        (jnp.ones_like(local_product), jnp.zeros_like(local_final)),
    )[1]

    def from_start(carried, block_dt, block_keep):
        total_dt, alive = carried
        running_dt = total_dt[None] + jnp.cumsum(block_dt, axis=0)
        alive_rows = alive * jnp.cumprod(block_keep)
        factors = jnp.exp(running_dt[:, :, None] * decay_rates[None]) * alive_rows[:, None, None]
        entry = jnp.exp(total_dt[:, None] * decay_rates) * alive
        return ((running_dt[-1], alive_rows[-1]), factors, entry)

    start_carry = (jnp.zeros((inner,), jnp.float32), jnp.ones((), jnp.float32))

    def correct_block(carried, member):
        block_dt, block_c, block_keep = member
        carried, factors, entry = from_start(carried, block_dt, block_keep)
        extra = jnp.einsum("ten,tn->te", factors * incoming[None], block_c)
        return (carried, (extra, entry * incoming))

    extra_out, start_shift = lax.scan(
        correct_block, start_carry, (dt_blocks, c_blocks, keep_blocks)
    )[1]
    true_starts = local_starts + start_shift
    ssm_out = (local_out + extra_out).reshape(row_count, inner) + skip_gain.astype(
        jnp.float32
    ) * mixed_values
    gate_act = jax.nn.silu(gate_half)
    gated = (ssm_out * gate_act).astype(jnp.bfloat16)
    branch_out = by_tile(gated, weights_out, tile_kinds, False)
    mixed = (token_values + branch_out).astype(jnp.bfloat16)
    rest_again = lax.optimization_barrier((rest_pieces, mixed))[0]
    back_x, back_dt, back_bias, back_out, back_taps, back_tapb, back_log, back_skip = fetch_rest(
        rest_again
    )
    d_gated = by_tile(cotangent, back_out, tile_kinds, True)
    grad_out = tile_grads(gated, cotangent, tile_kinds)
    d_ssm = d_gated * gate_act
    sig_gate = jax.nn.sigmoid(gate_half)
    d_gate = d_gated * ssm_out * sig_gate * (1.0 + gate_half * (1.0 - sig_gate))
    grad_skip = jnp.sum(d_ssm * mixed_values, axis=0)
    d_mixed = d_ssm * back_skip.astype(jnp.float32)
    dssm_blocks = blocked(d_ssm)

    def adjoint_seed(carried, member):
        block_dt, block_c, block_keep, block_dy = member
        carried, factors, entry = from_start(carried, block_dt, block_keep)
        return (carried, jnp.einsum("ten,te,tn->en", factors, block_dy, block_c))

    left_seed = jnp.sum(
        lax.scan(adjoint_seed, start_carry, (dt_blocks, c_blocks, keep_blocks, dssm_blocks))[1],
        axis=0,
    )
    arriving = carried_in(
        (local_product, left_seed),
        "narrow",
        chain_pairs,
        (jnp.ones_like(local_product), jnp.zeros_like(left_seed)),
    )[1]

    def backward_block(message, member):
        block_dt, block_b, block_c, block_u, block_keep, block_start, block_dy = member
        decay_now = jnp.exp(block_dt[:, :, None] * decay_rates[None]) * block_keep[:, None, None]
        pushed = (block_dt * block_u)[:, :, None] * block_b[:, None, :]
        pushed = pushed.at[0].add(decay_now[0] * block_start)
        states_in = lax.associative_scan(chain_pairs, (decay_now, pushed), axis=0)[1]
        before = jnp.concatenate([block_start[None], states_in[:-1]], axis=0)
        seeded = block_dy[:, :, None] * block_c[:, None, :]
        seeded = seeded.at[-1].add(message)
        following = jnp.concatenate([decay_now[1:], jnp.ones_like(decay_now[:1])], axis=0)
        adjoint = lax.associative_scan(chain_pairs, (following, seeded), reverse=True, axis=0)[1]
        weighted = adjoint * before * decay_now
        adjoint_b = jnp.einsum("ten,tn->te", adjoint, block_b)
        grad_rates = jnp.einsum("ten,te->en", weighted, block_dt)
        grad_steps = jnp.einsum("ten,en->te", weighted, decay_rates) + adjoint_b * block_u
        grad_b_rows = jnp.einsum("ten,te->tn", adjoint, block_dt * block_u)
        grad_c_rows = jnp.einsum("ten,te->tn", states_in, block_dy)
        return (
            decay_now[0] * adjoint[0],
            (grad_rates, grad_steps, grad_b_rows, grad_c_rows, adjoint_b * block_dt),
        )

    block_grads = lax.scan(
        backward_block,
        arriving,
        (dt_blocks, b_blocks, c_blocks, u_blocks, keep_blocks, true_starts, dssm_blocks),
        reverse=True,
    )[1]
    grad_rates = jnp.sum(block_grads[0], axis=0)
    grad_steps = block_grads[1].reshape(row_count, inner)
    grad_b_rows = block_grads[2].reshape(row_count, state_size)
    grad_c_rows = block_grads[3].reshape(row_count, state_size)
    d_mixed = d_mixed + block_grads[4].reshape(row_count, inner)
    grad_log = grad_rates * decay_rates
    d_pre = (grad_steps * jax.nn.sigmoid(dt_pre)).astype(jnp.bfloat16)
    grad_bias = lax.dot_general(
        onehot_low, d_pre, (((0,), (0,)), ((), ())), preferred_element_type=jnp.float32
    )
    grad_dt_w = tile_grads(dt_low, d_pre, tile_kinds)
    grad_dt_low = by_tile(d_pre, back_dt, tile_kinds, True)
    d_projected = jnp.concatenate([grad_dt_low, grad_b_rows, grad_c_rows], axis=1).astype(
        jnp.bfloat16
    )
    grad_x_w = tile_grads(mixed_low, d_projected, tile_kinds)
    d_mixed = d_mixed + by_tile(d_projected, back_x, tile_kinds, True)
    sig_pre = jax.nn.sigmoid(summed)
    d_summed = d_mixed * sig_pre * (1.0 + summed * (1.0 - sig_pre))
    taps_back = back_taps.astype(jnp.float32)
    d_extended = jnp.zeros((row_count + conv_taps - 1, inner), jnp.float32)
    taps_grad = []
    for tap_index in range(conv_taps):
        masked = d_summed * valid_masks[conv_taps - 1 - tap_index]
        d_extended = d_extended.at[tap_index : tap_index + row_count].add(
            taps_back[tap_index] * masked
        )
        taps_grad.append(jnp.sum(masked * extended[tap_index : tap_index + row_count], axis=0))
    grad_taps_w = jnp.stack(taps_grad, axis=0)
    grad_conv_b = jnp.sum(d_summed, axis=0)
    returned = shifted(d_extended[: conv_taps - 1], "narrow", -1)
    d_front = d_extended[conv_taps - 1 :]
    d_front = d_front.at[row_count - (conv_taps - 1) :].add(returned)
    d_projected_in = jnp.concatenate([d_front, d_gate], axis=1).astype(jnp.bfloat16)
    in_again = lax.optimization_barrier((in_pair, d_projected_in))[0]

    def backward_fold(carried, pieces, first_row):
        weights, gains = pieces
        part_grad = by_tile(d_projected_in, weights, tile_kinds, True)
        gains_seen = gains.astype(jnp.float32)
        return (part_grad, gains_seen)

    initial_back = (
        jnp.zeros((row_count, model_width), jnp.float32),
        jnp.zeros((model_width,), jnp.float32),
    )
    grad_normed, gain_full = fold_in_rows(in_again[0], in_again[1], backward_fold, initial_back)

    def in_term(first_row, row_span):
        return tile_grads(normed, d_projected_in, tile_kinds)

    grad_gain = jnp.sum(grad_normed * scaled, axis=0)
    d_scaled = grad_normed * gain_full[None]
    inner_prod = jnp.mean(d_scaled * token_values, axis=1, keepdims=True)
    grad_tokens = (
        cotangent.astype(jnp.float32)
        + row_scale * d_scaled
        - token_values * (row_scale * row_scale * row_scale) * inner_prod
    )
    grad_in_w, summed_grads = sum_grads(
        in_term,
        w_in.shape[0],
        (
            grad_x_w,
            grad_dt_w,
            grad_bias,
            grad_out,
            grad_taps_w,
            grad_conv_b,
            grad_log,
            grad_skip,
            grad_gain,
        ),
    )
    return (
        mixed,
        grad_tokens.astype(jnp.bfloat16),
        summed_grads[8],
        grad_in_w,
        summed_grads[4],
        summed_grads[5],
        summed_grads[0],
        summed_grads[1],
        summed_grads[2],
        summed_grads[6],
        summed_grads[7],
        summed_grads[3],
    )


def solution(mesh):
    return jax.shard_map(
        body,
        mesh=mesh,
        in_specs=(
            P(("wide", "narrow"), None),
            P(("wide", "narrow")),
            P(("wide", "narrow"), None, None),
            P(None, ("wide", "narrow")),
            P(("wide", "narrow")),
            P(("wide", "narrow"), None, None),
            P(None, None, ("wide", "narrow")),
            P(None, ("wide", "narrow")),
            P(("wide", "narrow"), None),
            P(("wide", "narrow")),
            P(("wide", "narrow"), None, None),
            P(("wide", "narrow")),
            P("wide"),
            P(("wide", "narrow"), None),
        ),
        out_specs=(
            P(("wide", "narrow"), None),
            P(("wide", "narrow"), None),
            P(("wide", "narrow")),
            P(("wide", "narrow"), None, None),
            P(None, ("wide", "narrow")),
            P(("wide", "narrow")),
            P(("wide", "narrow"), None, None),
            P(None, None, ("wide", "narrow")),
            P(None, ("wide", "narrow")),
            P(("wide", "narrow"), None),
            P(("wide", "narrow")),
            P(("wide", "narrow"), None, None),
        ),
        check_vma=False,
    )
```

profile of v0, /device:TPU:0, one launch (start us, length us, event | category | flops | bytes accessed | tf_op | source)
XLA Modules:
  0.0 3656.1 jit_solution(8427539930646420615)
XLA Ops:
  8.0 44.7 %all-gather.17.cloned.1.call-done = bf16[96,3,3072]{2,0,1:T(8,128)(2,1)} async-done(((bf16[24,3,3072]{2,0,1:T(8,128)(2,1)}), bf16[96,3,3072]{2,0,1:T(8,128)(2,1)}) %all-gather.17.cloned.1.call-update) | async-done | bytes 1769488 | tf_op jit(solution)/shard_map/all_gather | solution.py:164
  91.0 23.2 all-reduce.63
  295.9 891.7 %while.245 = (s32[]{:T(128)}, f32[1536,16]{0,1:T(8,128)}, f32[1536,16]{0,1:T(8,128)}, f32[4,64,1536]{2,1,0:T(8,128)}, f32[4,1536,16]{1,2,0:T(8,128)}, /*index=5*...) while((s32[]{:T(128)}, f32[1536,16]{0,1:T(8,128)}, ...), condition=%wide.region_8.9_spmd.clone, body=%wide.region_7.8_spmd.clone.sunk | while | flops 25116672 | bytes 360117824 | solution.py:251
  419.2 20.0 pad.791
  642.1 20.0 pad.791
  713.8 19.9 pad.795
  865.0 20.0 pad.791
  936.7 19.9 pad.795
  1087.8 20.0 pad.791
  1159.6 19.9 pad.795
  1352.5 27.1 while.235
  1381.8 53.5 %all-gather.3 = f32[6144,16]{1,0:T(8,128)} all-gather(f32[1536,16]{1,0:T(8,128)S(1)} %reduce_sum.100), channel_id=5, replica_groups=mesh['wide'=8,'narrow'=4] {'narrow'}, dimensions={0}, use_global_device_ids=true | all-gather | bytes 491520 | tf_op jit(solution)/shard_map/all_gather | solution.py:47
  1445.8 1239.9 %while.237 = (s32[]{:T(128)}, f32[1536,16]{0,1:T(8,128)S(1)}, f32[4,1536,16]{1,2,0:T(8,128)}, f32[4,64,1536]{2,1,0:T(8,128)}, bf16[4,64,16]{1,2,0:T(8,128)(2,1)}...) while((s32[]{:T(128)}, f32[1536,16]{0,1:T(8,128)S(1)}, ...), condition=%wide.region_27.28_spmd, body=%wide.region_26.27_spmd.sunk | while | flops 66527232 | bytes 662337856 | solution.py:343
  1557.6 20.1 pad.743
  1694.3 20.1 pad.753
  1721.3 20.2 pad.754
  1861.4 20.1 pad.743
  1998.0 20.1 pad.753
  2025.1 20.2 pad.754
  2165.1 20.1 pad.743
  2301.8 20.1 pad.753
  2328.8 20.2 pad.754
  2469.0 20.1 pad.743
  2605.6 20.1 pad.753
  2632.6 20.2 pad.754
  2813.5 23.8 while.241
  2851.6 39.4 %all-reduce.61 = (f32[768]{0:T(1024)S(1)}, f32[1536]{0:T(1024)S(1)}, f32[1536]{0:T(1024)S(1)}) all-reduce(f32[768]{0:T(1024)S(1)} %get-tuple-element.1889, f32[1536]{0:T(1024)S(1)} %get-tuple-element.1887, f32[1536]{0:T(1024)S(1)} %copy-done.92), channel_id=6, replica_groups=mesh['wide'=8,'narrow'=4] {'wide','narrow'}, use_global_device_ids=true, to_apply=%region_36.37.clone | all-reduce | flops 3840 | bytes 30720
  2907.3 98.3 %reduce-scatter.28.cloned.1.call-done = f32[48,16]{1,0:T(8,128)} async-done(((f32[1536,16]{1,0:T(8,128)}), f32[48,16]{1,0:T(8,128)}) %reduce-scatter.28.cloned.1.call-update) | async-done | bytes 3088
  3007.1 100.0 %reduce-scatter.24.cloned.1.call-done = f32[48,144]{1,0:T(8,128)} async-done(((f32[1536,144]{1,0:T(8,128)}), f32[48,144]{1,0:T(8,128)}) %reduce-scatter.24.cloned.1.call-update) | async-done | bytes 27664
  3108.7 102.2 %reduce-scatter.18.cloned.1.call-done = f32[48,3,80]{2,0,1:T(8,128)} async-done(((f32[1536,3,80]{2,0,1:T(8,128)}), f32[48,3,80]{2,0,1:T(8,128)}) %reduce-scatter.18.cloned.1.call-update) | async-done | bytes 46096 | tf_op jit(solution)/shard_map/reduce_scatter | solution.py:128
  3210.9 169.5 %reduce-scatter.20.cloned.1.call-done = f32[48,3,768]{2,0,1:T(8,128)} async-done(((f32[1536,3,768]{2,0,1:T(8,128)}), f32[48,3,768]{2,0,1:T(8,128)}) %reduce-scatter.20.cloned.1.call-update) | async-done | bytes 442384 | tf_op jit(solution)/shard_map/reduce_scatter | solution.py:131
  3380.4 268.7 %reduce-scatter.16.cloned.1.call-done = f32[24,3,3072]{2,0,1:T(8,128)} async-done(((f32[768,3,3072]{2,0,1:T(8,128)}), f32[24,3,3072]{2,0,1:T(8,128)}) %reduce-scatter.16.cloned.1.call-update) | async-done | bytes 884752 | tf_op jit(solution)/shard_map/reduce_scatter | solution.py:121
  (1643 shorter events, 2412.8 us)
Async XLA Ops:
  7.2 45.6 %copy-start.84 = (bf16[48,3,768]{2,0,1:T(8,128)(2,1)S(1)}, bf16[48,3,768]{2,0,1:T(8,128)(2,1)}, u32[]{:S(2)}) copy-start(bf16[48,3,768]{2,0,1:T(8,128)(2,1)} %param.76) | copy-start | bytes 663556
  7.2 45.5 %all-gather.17.cloned.1.call-start = ((), (), s32[]{:S(2)}) async-start(), calls=%async_computation.7 | async-start | bytes 2211840 | tf_op jit(solution)/shard_map/all_gather | solution.py:164
  7.9 195.0 %all-gather.19.cloned.1.call-start = ((), (), s32[]{:S(2)}) async-start(), calls=%async_computation.8 | async-start | bytes 15925248 | tf_op jit(solution)/shard_map/all_gather | solution.py:113
  52.6 26.0 copy-start.116
  52.7 62.1 %copy-start.63 = (bf16[256,768]{1,0:T(8,128)(2,1)S(1)}, bf16[256,768]{1,0:T(8,128)(2,1)}, u32[]{:S(2)}) copy-start(bf16[256,768]{1,0:T(8,128)(2,1)} %param.66) | copy-start | bytes 1179652
  52.7 1190.9 %all-gather.21.cloned.1.call-start = ((), (), s32[]{:S(2)}) async-start(), calls=%async_computation.9 | async-start | bytes 7962624 | tf_op jit(solution)/shard_map/all_gather | solution.py:101
  72.5 1261.5 %all-gather.23.cloned.1.call-start = ((), (), s32[]{:S(2)}) async-start(), calls=%async_computation.10 | async-start | bytes 7962624 | tf_op jit(solution)/shard_map/all_gather | solution.py:101
  114.9 50.2 %copy-start.87 = (bf16[48,3,48]{2,0,1:T(8,128)(2,1)S(1)}, bf16[48,3,48]{2,0,1:T(8,128)(2,1)}, u32[]{:S(2)}) copy-start(bf16[48,3,48]{2,0,1:T(8,128)(2,1)} %param.72) | copy-start | bytes 41476
  114.9 64.6 %copy-start.107 = (bf16[48,16]{0,1:T(8,128)(2,1)S(1)}, bf16[48,16]{0,1:T(8,128)(2,1)}, u32[]{:S(2)}) copy-start(bf16[48,16]{0,1:T(8,128)(2,1)} %param.74) | copy-start | bytes 4612
  115.5 86.3 %copy-start.95 = (f32[256]{0:T(256)}, f32[256]{0:T(256)S(1)}, u32[]{:S(2)}) copy-start(f32[256]{0:T(256)S(1)} %get-tuple-element.2229) | copy-start | bytes 3076
  215.5 25.8 copy-start.53
  215.6 25.8 copy-start.59
  216.2 49.5 %collective-permute-start = (f32[3,1536]{1,0:T(4,128)}, f32[3,1536]{1,0:T(4,128)}, u32[]{:S(2)}, u32[]{:S(2)}) collective-permute-start(f32[3,1536]{1,0:T(4,128)} %slice.1593), channel_id=1, source_target_pairs={{0,1},{1,2},{2,3},{4,5},{5,6},{6,7},{8,9},{9,10},{10,11},{12,13},{... | collective-permute-start | bytes 55304 | tf_op jit(solution)/shard_map/ppermute | solution.py:17
  304.9 81.0 %copy-start.6 = (f32[32,1536,16]{1,2,0:T(8,128)}, f32[32,1536,16]{1,2,0:T(8,128)S(1)}, u32[]{:S(2)}) copy-start(f32[32,1536,16]{1,2,0:T(8,128)S(1)} %get-tuple-element.3074) | copy-start | bytes 9437188 | tf_op jit(solution)/shard_map/while
  527.8 81.0 %copy-start.6 = (f32[32,1536,16]{1,2,0:T(8,128)}, f32[32,1536,16]{1,2,0:T(8,128)S(1)}, u32[]{:S(2)}) copy-start(f32[32,1536,16]{1,2,0:T(8,128)S(1)} %get-tuple-element.3074) | copy-start | bytes 9437188 | tf_op jit(solution)/shard_map/while
  750.7 81.0 %copy-start.6 = (f32[32,1536,16]{1,2,0:T(8,128)}, f32[32,1536,16]{1,2,0:T(8,128)S(1)}, u32[]{:S(2)}) copy-start(f32[32,1536,16]{1,2,0:T(8,128)S(1)} %get-tuple-element.3074) | copy-start | bytes 9437188 | tf_op jit(solution)/shard_map/while
  973.6 81.0 %copy-start.6 = (f32[32,1536,16]{1,2,0:T(8,128)}, f32[32,1536,16]{1,2,0:T(8,128)S(1)}, u32[]{:S(2)}) copy-start(f32[32,1536,16]{1,2,0:T(8,128)S(1)} %get-tuple-element.3074) | copy-start | bytes 9437188 | tf_op jit(solution)/shard_map/while
  1187.5 29.5 copy-start.65
  1257.7 1580.3 %all-gather.25.cloned.1.call-start = ((), (), s32[]{:S(2)}) async-start(), calls=%async_computation.11 | async-start | bytes 15925248 | tf_op jit(solution)/shard_map/all_gather | solution.py:113
  1258.7 1635.1 %reduce-scatter.26.cloned.1.call-start = ((), (), s32[]{:S(2)}) async-start(), calls=%async_computation.17 | async-start | bytes 811008
  1721.3 26.3 slice-start
  2025.1 26.3 slice-start
  2328.8 26.3 slice-start
  2632.6 26.3 slice-start
  2714.0 191.9 %reduce-scatter.22.cloned.1.call-start = ((), (), s32[]{:S(2)}) async-start(), calls=%async_computation.15 | async-start | bytes 811008
  2715.3 290.3 %reduce-scatter.28.cloned.1.call-start = ((), (), s32[]{:S(2)}) async-start(), calls=%async_computation.18 | async-start | bytes 811008
  2716.6 390.4 %reduce-scatter.24.cloned.1.call-start = ((), (), s32[]{:S(2)}) async-start(), calls=%async_computation.16 | async-start | bytes 1622016
  2729.6 481.3 %reduce-scatter.18.cloned.1.call-start = ((), (), s32[]{:S(2)}) async-start(), calls=%async_computation.13 | async-start | bytes 2433024 | tf_op jit(solution)/shard_map/reduce_scatter | solution.py:128
  2743.4 637.0 %reduce-scatter.20.cloned.1.call-start = ((), (), s32[]{:S(2)}) async-start(), calls=%async_computation.14 | async-start | bytes 14598144 | tf_op jit(solution)/shard_map/reduce_scatter | solution.py:131
  2765.9 883.1 %reduce-scatter.16.cloned.1.call-start = ((), (), s32[]{:S(2)}) async-start(), calls=%async_computation.12 | async-start | bytes 29196288 | tf_op jit(solution)/shard_map/reduce_scatter | solution.py:121
  2791.4 5.7 collective-permute-start.1
  2838.1 54.7 %copy-start.106 = (f32[256]{0:T(256)S(1)}, f32[256]{0:T(256)}, u32[]{:S(2)}) copy-start(f32[256]{0:T(256)} %get-tuple-element.2228) | copy-start | bytes 3076
  (283 other events, 1190.5 us)
Sparse Core Ops, SparseCore 0:
  9.6 43.0 all-gather.16
  54.5 78.0 all-gather.18
  134.5 50.7 all-gather.20
  1257.9 53.0 all-gather.22
  1312.7 79.2 all-gather.24
  2714.1 92.0 reduce-scatter.25
  2811.3 94.5 reduce-scatter.21
  2911.0 94.5 reduce-scatter.27
  3010.9 96.0 reduce-scatter.23
  3112.7 98.1 reduce-scatter.17
  3218.5 161.8 reduce-scatter.19
  3388.3 260.6 reduce-scatter.15
where the time goes:
time: 3710 us; the launch traced here: 3660 us
  local copies, waits for them, and re-layouts  1580 us (43%)
  waiting for transfers between devices  798 us (22%)
  other arithmetic  695 us (19%)
  blocking collectives  360 us (10%)
  matrix products  119 us (3%)
  loops' own time  81.1 us (2%)
    pad x72, local copies, waits for them, and re-layouts, local_block(): lax.associative_scan(chain_pairs, (decay_now, pushed), axis=0)  493 us
    pad x40, local copies, waits for them, and re-layouts, backward_block(): lax.associative_scan(chain_pairs, (decay_now, pushed), axis=0)[1]  336 us
    pad x40, local copies, waits for them, and re-layouts, backward_block(): lax.associative_scan(chain_pairs, (following, seeded), reverse=True, axis=0)  307 us
    reduce_scatter x1, waiting for transfers between devices, sum_grads(): lax.psum_scatter(in_term(jnp.int32(0), lax.axis_size(('wide', 'narrow'))...  269 us
    unnamed x16, waiting for transfers between devices  210 us
    reduce_scatter x1, waiting for transfers between devices, sum_grads(): lax.psum_scatter(grads[3], ('wide', 'narrow'), scatter_dimension=0, tiled...  169 us
    while x464, local copies, waits for them, and re-layouts  169 us
    reduce_scatter x1, waiting for transfers between devices, sum_grads(): lax.psum_scatter(grads[0], ('wide', 'narrow'), scatter_dimension=0, tiled...  102 us
  transfers between devices with their start and end apart: 14, of which 8 were waited for; matrix products, arithmetic and copies ran while one was open for 63% of the time, Pallas kernels for 0%

commit v1 on v0

v1 whole, which is shorter than its diff:
```python
import functools

import jax
import jax.numpy as jnp
from jax import lax
from jax.experimental import pallas as pl
from jax.experimental.pallas import tpu as pltpu
from jax.sharding import PartitionSpec as P

MODS = 3
RUN = 128
LANES = 128
EPSILON = 1e-05
LOG2E = 1.4426950408889634
FAR = 1e30
VMEM_LIMIT = 60 * 1024 * 1024

f32 = jnp.float32
bf16 = jnp.bfloat16


def swap(block, axis, flip):
    count = lax.axis_size(axis)
    return lax.ppermute(block, axis, [(i, i ^ flip) for i in range(count)])


def gather_narrow(block):
    return [block] + [swap(block, "narrow", s) for s in range(1, lax.axis_size("narrow"))]


def gather_wide(block):
    chips = lax.axis_size("wide") // 2
    near = [block] + [swap(block, "wide", 2 * s) for s in range(1, chips)]
    far = [swap(piece, "wide", 1) for piece in near]
    return [piece for pair in zip(near, far) for piece in pair]


def dot(a, b, ca, cb):
    return lax.dot_general(a, b, (((ca,), (cb,)), ((), ())), preferred_element_type=f32)


def call(kernel, outs, ins, scratch=(), cost=None):
    spaces = {"v": pltpu.VMEM, "s": pltpu.SMEM, "a": pl.ANY}
    return pl.pallas_call(
        kernel,
        out_shape=[jax.ShapeDtypeStruct(shape, dtype) for shape, dtype, _ in outs],
        in_specs=[pl.BlockSpec(memory_space=spaces[space]) for _, space in ins],
        out_specs=[pl.BlockSpec(memory_space=spaces[space]) for _, _, space in outs],
        scratch_shapes=list(scratch),
        compiler_params=pltpu.CompilerParams(vmem_limit_bytes=VMEM_LIMIT),
        cost_estimate=cost,
    )(*[array for array, _ in ins])


def place_pieces(pieces, target, sem, me, rows):
    copies = []
    for s, piece in enumerate(pieces):
        at = pl.multiple_of((me ^ s) * rows, 16)
        copy = pltpu.make_async_copy(piece, target.at[pl.ds(at, rows), :], sem.at[s])
        copy.start()
        copies.append(copy)
    return copies


def run_kind(kinds, n, run, per):
    return kinds[((run // per) ^ n) * per + run % per]


def spread_kernel(wid, ep, out_cols, x_cols, meta, *refs):
    pieces = refs[:wid]
    w_out, w_x, w_dt, table = refs[wid : wid + 4]
    rest, sems = refs[wid + 4 :]
    w = meta[1]
    copies = []
    for s, piece in enumerate(pieces):
        at = pl.multiple_of((w ^ s) * ep, 16)
        rows = pl.ds(at, ep)
        for k, (target, first, width) in enumerate(
            ((rest, out_cols + x_cols, rest.shape[1]), (w_x, out_cols, x_cols), (w_out, 0, out_cols))
        ):
            copy = pltpu.make_async_copy(
                piece.at[:, pl.ds(first, width)], target.at[rows, :], sems.at[k, s]
            )
            copy.start()
            copies.append(copy)
    for copy in copies:
        copy.wait()
    turned = rest[...].astype(f32).T
    dt_rows = w_dt.shape[0]
    w_dt[...] = turned[:dt_rows].astype(bf16)
    table[...] = turned[dt_rows:]


T_BIAS, T_CONV_B, T_CONV, T_SKIP, T_LOG = 0, 3, 4, 8, 16


def in_kernel(nar, wid, rpd, taps, meta, kinds, *refs):
    toks, w_pieces = refs[:nar], refs[nar : nar + wid]
    table, w_x = refs[nar + wid : nar + wid + 2]
    normed_o, front_o, gate_o, csum_o, mixed_o, px_o = refs[nar + wid + 2 : nar + wid + 8]
    xs, wf, tok_sem, w_sem = refs[nar + wid + 8 :]
    n, w, split = meta[0], meta[1], meta[2]
    es = gate_o.shape[1]
    tok_copies = place_pieces(toks, xs, tok_sem, n, toks[0].shape[0])
    w_copies = place_pieces(w_pieces, wf, w_sem, w, w_pieces[0].shape[0])
    for copy in tok_copies + w_copies:
        copy.wait()
    gain_at = MODS * 2 * es
    gain = wf[:, gain_at : gain_at + LANES].astype(f32).T[0:1, :]
    front_o[0:8, :] = jnp.zeros((8, es), f32)

    def one_run(r, carry):
        rows = pl.ds(pl.multiple_of(r * RUN, RUN), RUN)
        kind = run_kind(kinds, n, r, rpd)
        x = xs[rows, :].astype(f32)
        scale = lax.rsqrt(jnp.mean(x * x, axis=1, keepdims=True) + EPSILON)
        normed = (x * scale * gain).astype(bf16)
        normed_o[rows, :] = normed
        both = dot(normed, wf[:, pl.ds(pl.multiple_of(kind * (2 * es), LANES), 2 * es)], 1, 0)
        front_o[pl.ds(pl.multiple_of(r * RUN + 8, 8), RUN), :] = both[:, :es]
        gate_o[rows, :] = both[:, es:]
        ext = front_o[pl.ds(pl.multiple_of(r * RUN, 8), RUN + 8), :]
        place = r * RUN + lax.broadcasted_iota(jnp.int32, (RUN, 1), 0)
        offset = place - jnp.where(place >= split, split, 0)
        csum = jnp.broadcast_to(table[T_CONV_B : T_CONV_B + 1, :], (RUN, es))
        for lag in range(taps):
            tap = table[T_CONV + taps - 1 - lag : T_CONV + taps - lag, :]
            valid = (offset >= lag).astype(f32)
            csum = csum + tap * ext[8 - lag : 8 - lag + RUN, :] * valid
        csum_o[rows, :] = csum
        mixed = (csum * jax.nn.sigmoid(csum)).astype(bf16)
        mixed_o[rows, :] = mixed
        px = dot(mixed, w_x[:, pl.ds(pl.multiple_of(kind * LANES, LANES), LANES)], 1, 0)
        px_o[:, pl.ds(pl.multiple_of(r * RUN, LANES), RUN)] = px.T[: px_o.shape[0]].astype(bf16)
        return carry

    lax.fori_loop(0, xs.shape[0] // RUN, one_run, 0)


def cot_kernel(nar, rpd, meta, kinds, *refs):
    pieces = refs[:nar]
    w_out, gate_r = refs[nar : nar + 2]
    cot_o, dssm_o, dgate_o, act_o = refs[nar + 2 : nar + 6]
    (sem,) = refs[nar + 6 :]
    n = meta[0]
    d = cot_o.shape[1]
    for copy in place_pieces(pieces, cot_o, sem, n, pieces[0].shape[0]):
        copy.wait()

    def one_run(r, carry):
        rows = pl.ds(pl.multiple_of(r * RUN, RUN), RUN)
        kind = run_kind(kinds, n, r, rpd)
        d_gated = dot(cot_o[rows, :], w_out[:, pl.ds(pl.multiple_of(kind * d, LANES), d)], 1, 1)
        gate = gate_r[rows, :]
        sig = jax.nn.sigmoid(gate)
        act = gate * sig
        act_o[rows, :] = act
        dssm_o[rows, :] = d_gated * act
        dgate_o[rows, :] = d_gated * sig * (1.0 + gate * (1.0 - sig))
        return carry

    lax.fori_loop(0, cot_o.shape[0] // RUN, one_run, 0)


def softplus(v):
    return jnp.maximum(v, 0.0) + jnp.log1p(jnp.exp(-jnp.abs(v)))


def scan_kernel(nar, rpd, rank, meta, kinds, *refs):
    px_pieces = refs[:nar]
    w_dt, table, mixed_r, dssm_r = refs[nar : nar + 4]
    ssm_o, dpx_o, gmix_o, dpre_o, dlow_o, glog_o, gskip_o = refs[nar + 4 : nar + 11]
    pxs, pre_s, step_s, states, bb, cb, ps, qs, gb, gc, dtk, dtu = refs[nar + 11 :]
    n, split = meta[0], meta[2]
    total, es = mixed_r.shape
    ns = states.shape[1]
    groups = es // LANES
    runs = total // RUN
    lane = [slice(g * LANES, (g + 1) * LANES) for g in range(groups)]
    rates = -jnp.exp(table[T_LOG : T_LOG + ns, :])
    rates2 = rates * LOG2E
    half = ns // 2
    pxs[...] = sum(piece[...].astype(f32) for piece in px_pieces)
    skip = table[T_SKIP : T_SKIP + 1, :]

    def rows_of(r):
        return pl.ds(pl.multiple_of(r * RUN, RUN), RUN)

    def spread(r, at, target):
        block = pxs[at : at + ns, pl.ds(pl.multiple_of(r * RUN, LANES), RUN)]
        for t in range(RUN):
            target[t] = jnp.broadcast_to(block[:, t : t + 1], (ns, LANES))

    def prepare(r):
        rows = rows_of(r)
        steps = step_s[rows, :]
        place = r * RUN + lax.broadcasted_iota(jnp.int32, (RUN, 1), 0)
        reset = (place == 0) | (place == split)
        dtk[...] = jnp.where(reset, FAR, steps)
        dtu[...] = steps * mixed_r[rows, :].astype(f32)
        spread(r, rank, bb)
        spread(r, rank + ns, cb)

    def row(tile, j, g):
        return jnp.broadcast_to(tile[j : j + 1, lane[g]], (ns, LANES))

    def folded(ref):
        outs = []
        for g in range(groups):
            out = ref[g, pl.ds(0, RUN, stride=half), :]
            for s in range(1, half):
                out = out + ref[g, pl.ds(s, RUN, stride=half), :]
            outs.append(out)
        return jnp.concatenate(outs, axis=1)

    states[0] = jnp.zeros((ns, es), f32)

    def forward(r, hs):
        rows = rows_of(r)
        kind = run_kind(kinds, n, r, rpd)
        low = pxs[:rank, pl.ds(pl.multiple_of(r * RUN, LANES), RUN)].astype(bf16)
        dlow_o[:, pl.ds(pl.multiple_of(r * RUN, LANES), RUN)] = low
        weights = w_dt[pl.ds(pl.multiple_of(kind * rank, 16), rank), :]
        pre = dot(low, weights, 0, 0) + table[pl.ds(T_BIAS + kind, 1), :]
        pre_s[rows, :] = pre
        step_s[rows, :] = softplus(pre)
        prepare(r)

        def eight(i, hs):
            hs = list(hs)
            at = pl.ds(pl.multiple_of(i * 8, 8), 8)
            k8, u8 = dtk[at, :], dtu[at, :]
            for j in range(8):
                t = i * 8 + j
                bt, ct = bb[t], cb[t]
                for g in range(groups):
                    decay = jnp.exp2(row(k8, j, g) * rates2[:, lane[g]])
                    hs[g] = decay * hs[g] + row(u8, j, g) * bt
                    states[r * RUN + t + 1, :, lane[g]] = hs[g]
                    part = hs[g] * ct
                    ps[g, pl.ds(pl.multiple_of(t * half, half), half), :] = part[:half] + part[half:]
            return tuple(hs)

        hs = lax.fori_loop(0, RUN // 8, eight, hs)
        ssm_o[rows, :] = folded(ps) + skip * mixed_r[rows, :].astype(f32)
        return hs

    zero = jnp.zeros((ns, LANES), f32)
    lax.fori_loop(0, runs, forward, (zero,) * groups)
    gskip_o[...] = jnp.zeros_like(gskip_o)
    picks = lax.broadcasted_iota(jnp.int32, (2 * ns, LANES), 0)

    def backward(back, carry):
        r = runs - 1 - back
        rows = rows_of(r)
        kind = run_kind(kinds, n, r, rpd)
        prepare(r)

        def eight(back_i, carry):
            ms, hs, gr = [list(part) for part in carry]
            i = RUN // 8 - 1 - back_i
            at = pl.ds(pl.multiple_of(i * 8, 8), 8)
            k8, u8 = dtk[at, :], dtu[at, :]
            y8 = dssm_r[pl.ds(pl.multiple_of(r * RUN + i * 8, 8), 8), :]
            for j in reversed(range(8)):
                t = i * 8 + j
                bt, ct = bb[t], cb[t]
                gb_sum, gc_sum = None, None
                for g in range(groups):
                    dt = row(k8, j, g)
                    dy = row(y8, j, g)
                    adjoint = dy * ct + ms[g]
                    before = states[r * RUN + t, :, lane[g]]
                    c_part = dy * hs[g]
                    b_part = adjoint * row(u8, j, g)
                    gb_sum = b_part if gb_sum is None else gb_sum + b_part
                    gc_sum = c_part if gc_sum is None else gc_sum + c_part
                    lb = adjoint * bt
                    fold_at = pl.ds(pl.multiple_of(t * half, half), half)
                    ps[g, fold_at, :] = lb[:half] + lb[half:]
                    ms[g] = jnp.exp2(dt * rates2[:, lane[g]]) * adjoint
                    weighted = ms[g] * before
                    by_rate = weighted * rates[:, lane[g]]
                    qs[g, fold_at, :] = by_rate[:half] + by_rate[half:]
                    gr[g] = gr[g] + weighted * dt
                    hs[g] = before
                gb[pl.ds(pl.multiple_of(t * ns, ns), ns), :] = gb_sum
                gc[pl.ds(pl.multiple_of(t * ns, ns), ns), :] = gc_sum
            return tuple(ms), tuple(hs), tuple(gr)

        carry = lax.fori_loop(0, RUN // 8, eight, carry)
        mixed = mixed_r[rows, :].astype(f32)
        lb, by_rate = folded(ps), folded(qs)
        dssm = dssm_r[rows, :]
        grad_steps = by_rate + lb * mixed
        gmix_o[rows, :] = dssm * skip + lb * step_s[rows, :]
        gskip_o[...] += jnp.sum(dssm * mixed, axis=0, keepdims=True)
        dpre = (grad_steps * jax.nn.sigmoid(pre_s[rows, :])).astype(bf16)
        dpre_o[rows, :] = dpre
        weights = w_dt[pl.ds(pl.multiple_of(kind * rank, 16), rank), :]
        dlow = dot(weights, dpre, 1, 1)
        dbc = jnp.zeros((2 * ns, RUN), f32)
        for k in range(ns):
            for shift, ref in ((0, gb), (ns, gc)):
                pick = (picks == k + shift).astype(bf16)
                dbc = dbc + dot(pick, ref[pl.ds(k, RUN, stride=ns), :].astype(bf16), 1, 1)
        at = pl.ds(pl.multiple_of(r * RUN, LANES), RUN)
        dpx_o[:rank, at] = dlow.astype(bf16)
        dpx_o[rank:, at] = dbc.astype(bf16)
        return carry

    last = tuple(states[total, :, lane[g]] for g in range(groups))
    done = lax.fori_loop(0, runs, backward, ((zero,) * groups, last, (zero,) * groups))
    for g in range(groups):
        glog_o[:, lane[g]] = done[2][g] * rates[:, lane[g]]


def out_kernel(nar, wid, rpd, ep, rank, meta, kinds, *refs):
    ssm_r, act_r, dgate_r, w_out, cot_r, normed_r, dpre_r, dlow_r, glog_r, gskip_r = refs[:10]
    mixed_os = refs[10 : 10 + nar]
    dgate_o, table_o, same_o, peer_o = refs[10 + nar : 14 + nar]
    acc_out, acc_in, branch = refs[14 + nar :]
    n, w = meta[0], meta[1]
    total, es = ssm_r.shape
    d = cot_r.shape[1]
    acc_out[...] = jnp.zeros_like(acc_out)
    acc_in[...] = jnp.zeros_like(acc_in)
    table_o[...] = jnp.zeros_like(table_o)

    def one_run(r, carry):
        rows = pl.ds(pl.multiple_of(r * RUN, RUN), RUN)
        kind = run_kind(kinds, n, r, rpd)
        ssm = ssm_r[rows, :]
        gated = (ssm * act_r[rows, :]).astype(bf16)
        wide_at = pl.ds(pl.multiple_of(kind * d, LANES), d)
        es_at = pl.ds(pl.multiple_of(kind * es, LANES), es)
        branch[rows, :] = dot(gated, w_out[:, wide_at], 1, 0).astype(bf16)
        acc_out[:, wide_at] += dot(gated, cot_r[rows, :], 0, 0)
        dgate = (dgate_r[rows, :] * ssm).astype(bf16)
        dgate_o[rows, :] = dgate
        acc_in[:, es_at] += dot(normed_r[rows, :], dgate, 0, 0)
        dpre = dpre_r[rows, :]
        low = dlow_r[:, pl.ds(pl.multiple_of(r * RUN, LANES), RUN)]
        table_o[pl.ds(pl.multiple_of(kind * rank, 8), rank), :] += dot(low, dpre, 1, 0)
        table_o[pl.ds(MODS * rank + T_BIAS + kind, 1), :] += jnp.sum(
            dpre.astype(f32), axis=0, keepdims=True
        )
        return carry

    lax.fori_loop(0, total // RUN, one_run, 0)
    base = MODS * rank
    table_o[base + T_SKIP : base + T_SKIP + 1, :] = gskip_r[...]
    table_o[base + T_LOG : base + T_LOG + glog_r.shape[0], :] = glog_r[...]
    size = mixed_os[0].shape[0]
    for s in range(nar):
        mixed_os[s][...] = branch[pl.ds(pl.multiple_of((n ^ s) * size, RUN), size), :]
    core = w & 1
    in_rows = acc_in.shape[0] // wid
    width = acc_in.shape[1]
    for ref, parity in ((same_o, core), (peer_o, 1 - core)):
        for c in range(wid // 2):
            place = 2 * c + parity
            ref[c, :in_rows, :] = acc_in[
                pl.ds(pl.multiple_of(place * in_rows, 16), in_rows), :
            ].astype(bf16)
            block = acc_out[pl.ds(pl.multiple_of(place * ep, 16), ep), :].astype(bf16)
            for k in range(block.shape[1] // width):
                first = in_rows + k * ep
                ref[c, first : first + ep, :] = block[:, k * width : (k + 1) * width]


def pair_kernel(chips, meta, same, peer, *outs):
    chip = meta[1] // 2
    for s in range(chips):
        outs[s][...] = (same[chip ^ s].astype(f32) + peer[chip ^ s].astype(f32)).astype(bf16)


def total_kernel(count, *refs):
    refs[count][...] = sum(piece[...].astype(f32) for piece in refs[:count])


def back_kernel(nar, wid, rpd, taps, ep, meta, kinds, *refs):
    dpx_pieces = refs[:nar]
    w_pieces = refs[nar : nar + wid]
    toks = refs[nar + wid : nar + wid + nar]
    at = 2 * nar + wid
    table, w_x, gmix_r, csum_r, front_r, mixed_r, normed_r, dgate_r, table_r = refs[at : at + 9]
    dn_os = refs[at + 9 : at + 9 + nar]
    same_o, peer_o = refs[at + 9 + nar : at + 11 + nar]
    wf, xs, dconv, dn_s, acc_in, acc_x, small, gain_s, w_sem, tok_sem = refs[at + 11 + nar :]
    n, w, split = meta[0], meta[1], meta[2]
    total, es = gmix_r.shape
    d = normed_r.shape[1]
    runs = total // RUN
    w_copies = place_pieces(w_pieces, wf, w_sem, w, w_pieces[0].shape[0])
    tok_copies = place_pieces(toks, xs, tok_sem, n, toks[0].shape[0])
    acc_in[...] = jnp.zeros_like(acc_in)
    acc_x[...] = jnp.zeros_like(acc_x)
    small[...] = jnp.zeros_like(small)
    gain_s[...] = jnp.zeros_like(gain_s)
    dconv[total : total + 8, :] = jnp.zeros((8, es), f32)
    for copy in w_copies + tok_copies:
        copy.wait()
    xw = dpx_pieces[0].shape[0]

    def one_run(back, carry):
        r = runs - 1 - back
        rows = pl.ds(pl.multiple_of(r * RUN, RUN), RUN)
        kind = run_kind(kinds, n, r, rpd)
        lanes_at = pl.ds(pl.multiple_of(r * RUN, LANES), RUN)
        dpx = sum(piece[:, lanes_at].astype(f32) for piece in dpx_pieces)
        dpx = jnp.concatenate([dpx, jnp.zeros((LANES - xw, RUN), f32)], axis=0).T.astype(bf16)
        x_at = pl.ds(pl.multiple_of(kind * LANES, LANES), LANES)
        acc_x[:, x_at] += dot(mixed_r[rows, :], dpx, 0, 0)
        gmix = gmix_r[rows, :] + dot(dpx, w_x[:, x_at], 1, 1)
        csum = csum_r[rows, :]
        sig = jax.nn.sigmoid(csum)
        dc = gmix * sig * (1.0 + csum * (1.0 - sig))
        dconv[rows, :] = dc
        place = r * RUN + lax.broadcasted_iota(jnp.int32, (RUN + 8, 1), 0)
        offset = place - jnp.where(place >= split, split, 0)
        ext = dconv[pl.ds(pl.multiple_of(r * RUN, 8), RUN + 8), :]
        lagged = front_r[pl.ds(pl.multiple_of(r * RUN, 8), RUN + 8), :]
        d_front = jnp.zeros((RUN, es), f32)
        for lag in range(taps):
            tap = taps - 1 - lag
            valid = (offset >= lag).astype(f32)
            masked = ext * valid
            d_front = d_front + table[T_CONV + tap : T_CONV + tap + 1, :] * masked[lag : lag + RUN, :]
            small[T_CONV + tap : T_CONV + tap + 1, :] += jnp.sum(
                masked[:RUN] * lagged[8 - lag : 8 - lag + RUN, :], axis=0, keepdims=True
            )
        small[T_CONV_B : T_CONV_B + 1, :] += jnp.sum(dc, axis=0, keepdims=True)
        d_both = jnp.concatenate([d_front.astype(bf16), dgate_r[rows, :]], axis=1)
        acc_in[:, pl.ds(pl.multiple_of(kind * es, LANES), es)] += dot(
            normed_r[rows, :], d_both[:, :es], 0, 0
        )
        weights = wf[:, pl.ds(pl.multiple_of(kind * (2 * es), LANES), 2 * es)]
        dn = dot(d_both, weights, 1, 1)
        dn_s[rows, :] = dn.astype(bf16)
        x = xs[rows, :].astype(f32)
        scale = lax.rsqrt(jnp.mean(x * x, axis=1, keepdims=True) + EPSILON)
        gain_s[...] += jnp.sum(dn * (x * scale), axis=0, keepdims=True)
        return carry

    lax.fori_loop(0, runs, one_run, 0)
    size = dn_os[0].shape[0]
    for s in range(nar):
        dn_os[s][...] = dn_s[pl.ds(pl.multiple_of((n ^ s) * size, RUN), size), :]
    width = acc_in.shape[1]
    acc_in_rows = acc_in.shape[0] // wid
    gain = jnp.broadcast_to(gain_s[...], (LANES, d)).T
    xs_gain = dconv
    xs_gain[0:d, 0:LANES] = gain
    base = table_r.shape[0] - 2 * 16 if False else table_r.shape[0] - small.shape[0]
    rest = jnp.concatenate([table_r[:base, :], table_r[base:, :] + small[...]], axis=0)
    pad = 256 - rest.shape[0]
    rest = jnp.concatenate([rest, jnp.zeros((pad, es), f32)], axis=0).T
    xcols = acc_x.shape[1]
    acc_x_all = jnp.concatenate([acc_x[...], rest], axis=1)
    fill = width + LANES - acc_x_all.shape[1]
    if fill:
        acc_x_all = jnp.concatenate([acc_x_all, jnp.zeros((es, fill), f32)], axis=1)
    wf_rows = acc_x_all.astype(bf16)
    wf[0:es, 0 : width + LANES] = wf_rows
    core = w & 1
    for ref, parity in ((same_o, core), (peer_o, 1 - core)):
        for c in range(wid // 2):
            place = 2 * c + parity
            in_at = pl.ds(pl.multiple_of(place * acc_in_rows, 16), acc_in_rows)
            ref[c, :acc_in_rows, :width] = acc_in[in_at, :].astype(bf16)
            ref[c, :acc_in_rows, width:] = xs_gain[in_at, 0:LANES].astype(bf16)
            ref[c, acc_in_rows:, :] = wf[pl.ds(pl.multiple_of(place * ep, 16), ep), 0 : width + LANES]


def tokens_kernel(nar, x_r, cot_r, gain_r, *refs):
    dn = sum(piece[...].astype(f32) for piece in refs[:nar])
    out = refs[nar]
    x = x_r[...].astype(f32)
    scale = lax.rsqrt(jnp.mean(x * x, axis=1, keepdims=True) + EPSILON)
    q = dn * gain_r[...]
    dotted = jnp.mean(q * x, axis=1, keepdims=True)
    out[...] = (cot_r[...].astype(f32) + scale * q - x * (scale * scale * scale) * dotted).astype(bf16)


def body(
    tokens,
    norm_gain,
    w_in,
    conv_w,
    conv_b,
    w_x,
    w_dt,
    dt_bias,
    a_log,
    d_skip,
    w_out,
    mod_ids,
    split_at,
    cotangent,
):
    nar, wid = lax.axis_size("narrow"), lax.axis_size("wide")
    chips = wid // 2
    n, w = lax.axis_index("narrow"), lax.axis_index("wide")
    own, d = tokens.shape
    total = nar * own
    rpd = own // RUN
    rank, xw, ns, taps = w_dt.shape[0], w_x.shape[2], a_log.shape[1], conv_w.shape[0]
    er = w_out.shape[0]
    inner = er * nar * wid
    ep = -(-er // 16) * 16
    es = ep * wid
    dr = w_in.shape[0]
    width = MODS * es
    meta = jnp.stack([n, w, split_at[0]]).astype(jnp.int32)

    kinds = mod_ids.reshape(rpd, RUN)[:, 0]
    kinds = jnp.concatenate(gather_narrow(kinds))
    out_cols, x_cols = MODS * d, MODS * LANES
    lane_rows = jnp.concatenate(
        [
            w_dt.reshape(rank * MODS, er).reshape(rank, MODS, er).transpose(1, 0, 2).reshape(-1, er),
            dt_bias,
            conv_b[None],
            conv_w,
            d_skip[None],
            jnp.zeros((T_LOG - T_SKIP - 1, er), bf16),
            a_log.T,
        ],
        axis=0,
    )
    table_rows = T_LOG + ns
    lane_rows = jnp.pad(lane_rows, ((0, 256 - lane_rows.shape[0]), (0, 0)))
    pack = jnp.concatenate(
        [
            w_out.reshape(er, out_cols),
            jnp.pad(w_x, ((0, 0), (0, 0), (0, LANES - xw))).reshape(er, x_cols),
            lane_rows.T,
        ],
        axis=1,
    )
    pack = jnp.pad(pack, ((0, ep - er), (0, 0)))
    pack_pieces = gather_wide(pack)
    wi = w_in.reshape(dr, MODS, 2, wid, nar, er)
    wi = jnp.pad(wi, ((0, 0),) * 5 + ((0, ep - er),))
    wi = wi.transpose(4, 0, 1, 2, 3, 5).reshape(nar, dr, 2 * width)
    wi = jnp.concatenate(
        [wi, jnp.broadcast_to(norm_gain[None, :, None], (nar, dr, LANES))], axis=2
    )
    wi = lax.all_to_all(wi, "narrow", 0, 0)
    wi = wi.reshape(nar * dr, 2 * width + LANES)
    wi_pieces = gather_wide(wi)
    tok_pieces = gather_narrow(tokens)
    cot_pieces = gather_narrow(cotangent)

    w_out_l, w_x_l, w_dt_l, table = call(
        functools.partial(spread_kernel, wid, ep, out_cols, x_cols),
        [
            ((es, out_cols), bf16, "v"),
            ((es, x_cols), bf16, "v"),
            ((MODS * rank, es), bf16, "v"),
            ((256 - MODS * rank, es), f32, "v"),
        ],
        [(meta, "s")] + [(p, "a") for p in pack_pieces],
        [pltpu.VMEM((es, 256), bf16), pltpu.SemaphoreType.DMA((3, wid))],
    )
    wf_shape = (nar * dr * wid, 2 * width + LANES)
    normed, front, gate, csum, mixed, px = call(
        functools.partial(in_kernel, nar, wid, rpd, taps),
        [
            ((total, d), bf16, "v"),
            ((total + 8, es), f32, "v"),
            ((total, es), f32, "v"),
            ((total, es), f32, "v"),
            ((total, es), bf16, "v"),
            ((xw, total), bf16, "v"),
        ],
        [(meta, "s"), (kinds, "s")]
        + [(p, "a") for p in tok_pieces]
        + [(p, "a") for p in wi_pieces]
        + [(table, "v"), (w_x_l, "v")],
        [
            pltpu.VMEM((total, d), bf16),
            pltpu.VMEM(wf_shape, bf16),
            pltpu.SemaphoreType.DMA((nar,)),
            pltpu.SemaphoreType.DMA((wid,)),
        ],
    )
    px_pieces = gather_narrow(px)
    cot, dssm, dgate_f, act = call(
        functools.partial(cot_kernel, nar, rpd),
        [((total, d), bf16, "v")] + [((total, es), f32, "v")] * 3,
        [(meta, "s"), (kinds, "s")]
        + [(p, "a") for p in cot_pieces]
        + [(w_out_l, "v"), (gate, "v")],
        [pltpu.SemaphoreType.DMA((nar,))],
    )
    ssm, dpx, gmix, dpre, dlow, glog, gskip = call(
        functools.partial(scan_kernel, nar, rpd, rank),
        [
            ((total, es), f32, "v"),
            ((xw, total), bf16, "v"),
            ((total, es), f32, "v"),
            ((total, es), bf16, "v"),
            ((rank, total), bf16, "v"),
            ((ns, es), f32, "v"),
            ((1, es), f32, "v"),
        ],
        [(meta, "s"), (kinds, "s")]
        + [(p, "v") for p in px_pieces]
        + [(w_dt_l, "v"), (table, "v"), (mixed, "v"), (dssm, "v")],
        [
            pltpu.VMEM((xw, total), f32),
            pltpu.VMEM((total, es), f32),
            pltpu.VMEM((total, es), f32),
            pltpu.VMEM((total + 1, ns, es), f32),
            pltpu.VMEM((RUN, ns, LANES), f32),
            pltpu.VMEM((RUN, ns, LANES), f32),
            pltpu.VMEM((es // LANES, RUN * ns // 2, LANES), f32),
            pltpu.VMEM((es // LANES, RUN * ns // 2, LANES), f32),
            pltpu.VMEM((RUN * ns, LANES), f32),
            pltpu.VMEM((RUN * ns, LANES), f32),
            pltpu.VMEM((RUN, es), f32),
            pltpu.VMEM((RUN, es), f32),
        ],
    )
    dpx_pieces = gather_narrow(dpx)
    in_rows = d // wid
    rows_a = in_rows + ep * (out_cols // width)
    res = call(
        functools.partial(out_kernel, nar, wid, rpd, ep, rank),
        [((own, d), bf16, "v")] * nar
        + [((total, es), bf16, "v"), ((MODS * rank + table_rows, es), f32, "v")]
        + [((chips, rows_a, width), bf16, "v")] * 2,
        [(meta, "s"), (kinds, "s")]
        + [(a, "v") for a in (ssm, act, dgate_f, w_out_l, cot, normed, dpre, dlow, glog, gskip)],
        [
            pltpu.VMEM((es, out_cols), f32),
            pltpu.VMEM((d, width), f32),
            pltpu.VMEM((total, d), bf16),
        ],
    )
    branch_parts, (dgate, table_g, same_a, peer_a) = res[:nar], res[nar:]
    branch_pieces = [branch_parts[0]] + [
        swap(branch_parts[s], "narrow", s) for s in range(1, nar)
    ]

    def over_wide(same, peer):
        peer = swap(peer, "wide", 1)
        shape = same.shape[1:]
        parts = call(
            functools.partial(pair_kernel, chips),
            [(shape, bf16, "v")] * chips,
            [(meta, "s"), (same, "v"), (peer, "v")],
        )
        parts = [parts[0]] + [swap(parts[s], "wide", 2 * s) for s in range(1, chips)]
        return call(
            functools.partial(total_kernel, chips), [(shape, f32, "v")], [(p, "v") for p in parts]
        )[0]

    sum_a = over_wide(same_a, peer_a)
    rows_b = in_rows + ep
    res = call(
        functools.partial(back_kernel, nar, wid, rpd, taps, ep),
        [((own, d), bf16, "v")] * nar + [((chips, rows_b, width + LANES), bf16, "v")] * 2,
        [(meta, "s"), (kinds, "s")]
        + [(p, "v") for p in dpx_pieces]
        + [(p, "a") for p in wi_pieces]
        + [(p, "a") for p in tok_pieces]
        + [(a, "v") for a in (table, w_x_l, gmix, csum, front, mixed, normed, dgate, table_g)],
        [
            pltpu.VMEM(wf_shape, bf16),
            pltpu.VMEM((total, d), bf16),
            pltpu.VMEM((total + 8, es), f32),
            pltpu.VMEM((total, d), bf16),
            pltpu.VMEM((d, width), f32),
            pltpu.VMEM((es, x_cols), f32),
            pltpu.VMEM((table_rows, es), f32),
            pltpu.VMEM((1, d), f32),
            pltpu.SemaphoreType.DMA((wid,)),
            pltpu.SemaphoreType.DMA((nar,)),
        ],
    )
    dn_parts, (same_b, peer_b) = res[:nar], res[nar:]
    dn_pieces = [dn_parts[0]] + [swap(dn_parts[s], "narrow", s) for s in range(1, nar)]
    sum_b = over_wide(same_b, peer_b)

    mixed_out = (
        tokens.astype(f32) + sum(p.astype(f32) for p in branch_pieces)
    ).astype(bf16)
    gain_row = jnp.concatenate(
        [wi_pieces[0][:, 2 * width]], axis=0
    )
    gain_full = jnp.zeros((wid, nar * dr), bf16)
    for s in range(wid):
        gain_full = lax.dynamic_update_slice(
            gain_full, wi_pieces[s][:, 2 * width][None], (w ^ s, 0)
        )
    del gain_row
    grad_tokens = call(
        functools.partial(tokens_kernel, nar),
        [((own, d), bf16, "v")],
        [(tokens, "v"), (cotangent, "v"), (gain_full.reshape(1, d).astype(f32), "v")]
        + [(p, "v") for p in dn_pieces],
    )[0]

    back = jnp.concatenate(
        [sum_a[:in_rows].astype(bf16), sum_b[:in_rows].astype(bf16)], axis=1
    ).reshape(nar, dr, -1)
    back = lax.all_to_all(back, "narrow", 0, 0).astype(f32)

    def channels(part):
        part = part.reshape(nar, dr, MODS, wid, ep)[..., :er]
        return part.transpose(1, 2, 3, 0, 4).reshape(dr, MODS, inner)

    grad_w_in = jnp.concatenate(
        [channels(back[:, :, width : 2 * width]), channels(back[:, :, :width])], axis=2
    )
    grad_gain = jnp.sum(back[:, :, 2 * width], axis=0)
    grad_w_out = sum_a[in_rows:].reshape(out_cols // width, ep, width)
    grad_w_out = grad_w_out.transpose(1, 0, 2).reshape(ep, MODS, d)[:er]
    small = sum_b[in_rows:][:er]
    grad_w_x = small[:, :x_cols].reshape(er, MODS, LANES)[:, :, :xw]
    lane_g = small[:, x_cols : x_cols + 256].T
    base = MODS * rank
    grad_w_dt = lane_g[:base].reshape(MODS, rank, er).transpose(1, 0, 2)
    grad_dt_bias = lane_g[base + T_BIAS : base + T_BIAS + MODS]
    grad_conv_w = lane_g[base + T_CONV : base + T_CONV + taps]
    grad_conv_b = lane_g[base + T_CONV_B]
    grad_skip = lane_g[base + T_SKIP]
    grad_log = lane_g[base + T_LOG : base + T_LOG + ns].T
    return (
        mixed_out,
        grad_tokens,
        grad_gain,
        grad_w_in,
        grad_conv_w,
        grad_conv_b,
        grad_w_x,
        grad_w_dt,
        grad_dt_bias,
        grad_log,
        grad_skip,
        grad_w_out,
    )


def solution(mesh):
    both = ("wide", "narrow")
    return jax.shard_map(
        body,
        mesh=mesh,
        in_specs=(
            P(both, None),
            P(both),
            P(both, None, None),
            P(None, both),
            P(both),
            P(both, None, None),
            P(None, None, both),
            P(None, both),
            P(both, None),
            P(both),
            P(both, None, None),
            P(both),
            P("wide"),
            P(both, None),
        ),
        out_specs=(
            P(both, None),
            P(both, None),
            P(both),
            P(both, None, None),
            P(None, both),
            P(both),
            P(both, None, None),
            P(None, None, both),
            P(None, both),
            P(both, None),
            P(both),
            P(both, None, None),
        ),
        check_vma=False,
    )
```

time: 3710 us -> 355 us (0.10); the launches traced: 3660 us -> 350 us
  local copies, waits for them, and re-layouts: 1580 us -> 38.1 us
  other arithmetic: 695 us -> 5.5 us
  waiting for transfers between devices: 798 us -> 120 us
  blocking collectives: 360 us -> 0 us
  Pallas kernels: 0 us -> 120 us
  matrix products: 119 us -> 0 us
  loops' own time: 81.1 us -> 0 us
  starting transfers between devices: 5.9 us -> 63.8 us
    pad x152 -> x1, local copies, waits for them, and re-layouts: 1140 us -> 0.03 us  [body(): jnp.pad(w_x, ((0, 0), (0, 0), (0, LANES - xw))).reshape(er, x_cols)]
    reduce_scatter x3 -> x0, waiting for transfers between devices: 540 us -> none  [the longest x1 269 us: sum_grads(): lax.psum_scatter(in_term(jnp.int32(0), lax.axis_size(('wide', 'narrow'))...]
    add x149 -> x0, other arithmetic: 357 us -> none  [the longest x47 95.4 us: chain_pairs(): return (earlier[0] * later[0], later[0] * earlier[1] + later[1])]
    all_gather x18 -> x0, blocking collectives: 273 us -> none  [the longest x2 68.6 us: carried_in(): gathered = jax.tree.map(lambda a: lax.all_gather(a, axis), part)]
    unnamed x16 -> x0, waiting for transfers between devices: 210 us -> none
    while x473 -> x0, local copies, waits for them, and re-layouts: 189 us -> none
    mul x107 -> x0, other arithmetic: 131 us -> none  [the longest x68 89.3 us: chain_pairs(): return (earlier[0] * later[0], later[0] * earlier[1] + later[1])]
    pallas_call x0 -> x11, Pallas kernels: none -> 120 us  [call(): pl.pallas_call(kernel, out_shape=[jax.ShapeDtypeStruct(shape, dtype) for...]
  transfers between devices with their start and end apart: 14 -> 45, of which waited for: 8 -> 16; matrix products, arithmetic and copies ran while one was open for 63% -> 6% of each run, Pallas kernels for 0% -> 15%
where the time goes in v1:
time: 355 us; the launch traced here: 350 us
  waiting for transfers between devices  120 us (34%)
  Pallas kernels  120 us (34%)
  starting transfers between devices  63.8 us (18%)
  local copies, waits for them, and re-layouts  38.1 us (11%)
  other arithmetic  5.5 us (2%)
    pallas_call x11, Pallas kernels, call(): pl.pallas_call(kernel, out_shape=[jax.ShapeDtypeStruct(shape, dtype) for...  120 us
    ppermute x43, waiting for transfers between devices, swap(): return lax.ppermute(block, axis, [(i, i ^ flip) for i in range(count)])  119 us
    ppermute x43, starting transfers between devices, swap(): return lax.ppermute(block, axis, [(i, i ^ flip) for i in range(count)])  54 us
    unnamed x100, local copies, waits for them, and re-layouts  11.4 us
  transfers between devices with their start and end apart: 45, of which 16 were waited for; matrix products, arithmetic and copies ran while one was open for 6% of the time, Pallas kernels for 15%

profile of v1, /device:TPU:0, one launch (start us, length us, event | category | flops | bytes accessed | tf_op | source)
XLA Modules:
  0.0 349.8 jit_solution(12793639555862502947)
XLA Ops:
  0.6 3.4 reshape.89
  6.6 6.3 %all-to-all-start = ((bf16[4,24,2432]{2,1,0:T(8,128)(2,1)}), bf16[4,24,2432]{2,1,0:T(8,128)(2,1)S(1)}, u32[]{:S(2)}, u32[]{:S(2)}) async-start(bf16[4,24,2432]{2,1,0:T(8,128)(2,1)} %pad_maximum_fusion.1), calls=%async_computation | async-start | bytes 933888 | tf_op jit(solution)/shard_map/all_to_all | solution.py:550
  19.6 11.8 %collective-permute-done = s32[2]{0:T(128)S(1)} collective-permute-done((s32[2]{0:T(128)S(1)}, s32[2]{0:T(128)S(1)}, u32[]{:S(2)}, u32[]{:S(2)}) %collective-permute-start) | collective-permute-done | bytes 40 | tf_op jit(solution)/shard_map/ppermute | solution.py:24
  38.1 3.1 collective-permute-done.2
  46.7 19.2 %collective-permute-done.4.refs_2_.refs_14_ = bf16[256,768]{1,0:T(8,128)(2,1)S(1)} collective-permute-done((bf16[256,768]{1,0:T(8,128)(2,1)S(1)}, bf16[256,768]{1,0:T(8,128)(2,1)S(1)}, u32[]{:S(2)}, u32[]{:S(2)}) %collective-permute-start.4) | collective-permute-done | bytes 393248 | tf_op jit(solution)/shard_map/ppermute | solution.py:24
  66.0 2.4 collective-permute-start.11
  69.7 10.7 %collective-permute-done.11.refs_10_ = bf16[96,2432]{1,0:T(8,128)(2,1)S(1)} collective-permute-done((bf16[96,2432]{1,0:T(8,128)(2,1)S(1)}, bf16[96,2432]{1,0:T(8,128)(2,1)S(1)}, u32[]{:S(2)}, u32[]{:S(2)}) %collective-permute-start.11) | collective-permute-done | bytes 466976 | tf_op jit(solution)/shard_map/ppermute | solution.py:24
  80.5 9.1 %collective-permute-done.7.refs_6_ = bf16[96,2432]{1,0:T(8,128)(2,1)} collective-permute-done((bf16[96,2432]{1,0:T(8,128)(2,1)S(1)}, bf16[96,2432]{1,0:T(8,128)(2,1)}, u32[]{:S(2)}, u32[]{:S(2)}) %collective-permute-start.7) | collective-permute-done | bytes 466976 | tf_op jit(solution)/shard_map/ppermute | solution.py:24
  89.6 3.1 collective-permute-start.24
  95.9 4.0 %shard_map.229 = (bf16[384,2304]{1,0:T(8,128)(2,1)}, bf16[384,384]{1,0:T(8,128)(2,1)}, bf16[144,384]{1,0:T(8,128)(2,1)}, f32[112,384]{1,0:T(8,128)}) custom-call(s32[3]{0:T(128)} %pad_add_fusion.meta, bf16[48,2944]{1,0:T(8,128)(2,1)} %copy-done.14, bf16[48,2944]{1,0:T(8,128)(2,1)} %collective-permute-done.13.refs_1_, bf16[48,2944]{1,0:T(8,128)(2,1)} %copy-done.25, ...), custom_call_target="tpu_custom_call" | custom-call | tf_op jit(solution)/shard_map/pallas_call | solution.py:44
  100.8 11.9 %shard_map.230 = (bf16[1024,768]{1,0:T(8,128)(2,1)}, f32[1032,384]{1,0:T(8,128)}, f32[1024,384]{1,0:T(8,128)}, f32[1024,384]{1,0:T(8,128)}, bf16[1024,384]{1,0:T(8,128)(2,1)}, /*index=5*/bf16[80,1024]{1,0:T(8,128)(2,1)}) custom-call(s32[3]{0:T(128)} %pad_add_fusion.meta, s32[8]{0:T(128)} %pad_add_fusion.1.kinds, bf16[256,768]{1,0:T(8,128)(2,1)} %x_r.1, ...), custom_call_target="tpu_custom_call" | custom-call | tf_op jit(solution)/shard_map/pallas_call | solution.py:44
  112.8 3.1 collective-permute-start.21
  117.2 2.7 collective-permute-done.24.refs_2_
  119.9 8.3 %shard_map.231 = (bf16[1024,768]{1,0:T(8,128)(2,1)}, f32[1024,384]{1,0:T(8,128)}, f32[1024,384]{1,0:T(8,128)}, f32[1024,384]{1,0:T(8,128)}) custom-call(s32[3]{0:T(128)} %pad_add_fusion.meta, s32[8]{0:T(128)} %pad_add_fusion.1.kinds, bf16[256,768]{1,0:T(8,128)(2,1)} %cot_r.1, bf16[256,768]{1,0:T(8,128)(2,1)} %copy-done.21, ...), custom_call_target="tpu_custom_call" | custom-call | tf_op jit(solution)/shard_map/pallas_call | solution.py:44
  128.2 10.5 %collective-permute-done.21.refs_2_ = bf16[80,1024]{1,0:T(8,128)(2,1)S(1)} collective-permute-done((bf16[80,1024]{1,0:T(8,128)(2,1)}, bf16[80,1024]{1,0:T(8,128)(2,1)S(1)}, u32[]{:S(2)}, u32[]{:S(2)}) %collective-permute-start.21) | collective-permute-done | bytes 163872 | tf_op jit(solution)/shard_map/ppermute | solution.py:24
  139.5 51.6 %shard_map.232 = (f32[1024,384]{1,0:T(8,128)}, bf16[80,1024]{1,0:T(8,128)(2,1)}, f32[1024,384]{1,0:T(8,128)}, bf16[1024,384]{1,0:T(8,128)(2,1)}, bf16[48,1024]{1...) custom-call(s32[3]{0:T(128)} %pad_add_fusion.meta, s32[8]{0:T(128)} %pad_add_fusion.1.kinds, ...), custom_call_target="tpu_custom_call" | custom-call | tf_op jit(solution)/shard_map/pallas_call | solution.py:44
  191.1 5.5 %collective-permute-start.29 = (bf16[80,1024]{1,0:T(8,128)(2,1)}, bf16[80,1024]{1,0:T(8,128)(2,1)S(1)}, u32[]{:S(2)}, u32[]{:S(2)}) collective-permute-start(bf16[80,1024]{1,0:T(8,128)(2,1)} %get-tuple-element.76.refs_0_), channel_id=1, source_target_pairs={{0,1},{1,0},{2,3},{3,2},{4,5},{5,4},{6,7},{7,6},{8,9},{9,8},{10,11... | collective-permute-start | bytes 491528 | tf_op jit(solution)/shard_map/ppermute | solution.py:24
  199.1 12.4 %shard_map.233 = (bf16[256,768]{1,0:T(8,128)(2,1)}, bf16[256,768]{1,0:T(8,128)(2,1)}, bf16[256,768]{1,0:T(8,128)(2,1)}, bf16[256,768]{1,0:T(8,128)(2,1)}, bf16[1...) custom-call(s32[3]{0:T(128)} %pad_add_fusion.meta, ...), custom_call_target="tpu_custom_call" | custom-call | tf_op jit(solution)/shard_map/pallas_call | solution.py:44
  212.4 17.6 %shard_map.234 = (bf16[256,768]{1,0:T(8,128)(2,1)}, bf16[256,768]{1,0:T(8,128)(2,1)}, bf16[256,768]{1,0:T(8,128)(2,1)}, bf16[256,768]{1,0:T(8,128)(2,1)}, bf16[4...) custom-call(s32[3]{0:T(128)} %pad_add_fusion.meta, s32[8]{0:T(128)} %pad_add_fusion.1.kinds, ...), custom_call_target="tpu_custom_call" | custom-call | tf_op jit(solution)/shard_map/pallas_call | solution.py:44
  230.6 3.0 collective-permute-done.39.peer
  234.7 3.2 shard_map.238
  245.5 3.3 shard_map.236
  251.1 2.3 collective-permute-start.26
  254.0 5.0 %collective-permute-done.41.refs_2_ = bf16[144,1280]{1,0:T(8,128)(2,1)S(1)} collective-permute-done((bf16[144,1280]{1,0:T(8,128)(2,1)}, bf16[144,1280]{1,0:T(8,128)(2,1)S(1)}, u32[]{:S(2)}, u32[]{:S(2)}) %collective-permute-start.41) | collective-permute-done | bytes 368672 | tf_op jit(solution)/shard_map/ppermute | solution.py:24
  262.3 3.2 collective-permute-start.27
  270.9 2.4 shard_map.239
  274.3 2.5 collective-permute-done.37.refs_2_
  280.0 2.5 shard_map.237
  286.7 3.5 all-to-all-start.1
  290.2 16.5 %collective-permute-done.27 = bf16[256,768]{1,0:T(8,128)(2,1)S(1)} collective-permute-done((bf16[256,768]{1,0:T(8,128)(2,1)}, bf16[256,768]{1,0:T(8,128)(2,1)S(1)}, u32[]{:S(2)}, u32[]{:S(2)}) %collective-permute-start.27) | collective-permute-done | bytes 393248 | tf_op jit(solution)/shard_map/ppermute | solution.py:24
  307.7 21.4 %collective-permute-done.33.refs_2_ = bf16[256,768]{1,0:T(8,128)(2,1)S(1)} collective-permute-done((bf16[256,768]{1,0:T(8,128)(2,1)}, bf16[256,768]{1,0:T(8,128)(2,1)S(1)}, u32[]{:S(2)}, u32[]{:S(2)}) %collective-permute-start.33) | collective-permute-done | bytes 393248 | tf_op jit(solution)/shard_map/ppermute | solution.py:24
  329.8 2.9 shard_map.235
  (230 shorter events, 79.3 us)
Async XLA Ops:
  6.6 36.9 %all-to-all-start = ((bf16[4,24,2432]{2,1,0:T(8,128)(2,1)}), bf16[4,24,2432]{2,1,0:T(8,128)(2,1)S(1)}, u32[]{:S(2)}, u32[]{:S(2)}) async-start(bf16[4,24,2432]{2,1,0:T(8,128)(2,1)} %pad_maximum_fusion.1), calls=%async_computation | async-start | bytes 933888 | tf_op jit(solution)/shard_map/all_to_all | solution.py:550
  13.9 27.8 %collective-permute-start.14 = (bf16[48,2944]{1,0:T(8,128)(2,1)S(1)}, bf16[48,2944]{1,0:T(8,128)(2,1)S(1)}, u32[]{:S(2)}, u32[]{:S(2)}) collective-permute-start(bf16[48,2944]{1,0:T(8,128)(2,1)S(1)} %pad_maximum_fusion.3.refs_0_), channel_id=1, source_target_pairs={{0,8},{4,12},{8,0},{12,4},{16,24},{20,28},{24,16},{28,20},{1,9},{5... | collective-permute-start | bytes 847880 | tf_op jit(solution)/shard_map/ppermute | solution.py:24
  15.4 28.1 %collective-permute-start.16 = (bf16[48,2944]{1,0:T(8,128)(2,1)S(1)}, bf16[48,2944]{1,0:T(8,128)(2,1)S(1)}, u32[]{:S(2)}, u32[]{:S(2)}) collective-permute-start(bf16[48,2944]{1,0:T(8,128)(2,1)S(1)} %pad_maximum_fusion.3.refs_0_), channel_id=1, source_target_pairs={{0,16},{4,20},{8,24},{12,28},{16,0},{20,4},{24,8},{28,12},{1,17},{... | collective-permute-start | bytes 847880 | tf_op jit(solution)/shard_map/ppermute | solution.py:24
  16.9 26.6 %collective-permute-start.18 = (bf16[48,2944]{1,0:T(8,128)(2,1)S(1)}, bf16[48,2944]{1,0:T(8,128)(2,1)S(1)}, u32[]{:S(2)}, u32[]{:S(2)}) collective-permute-start(bf16[48,2944]{1,0:T(8,128)(2,1)S(1)} %pad_maximum_fusion.3.refs_0_), channel_id=1, source_target_pairs={{0,24},{4,28},{8,16},{12,20},{16,8},{20,12},{24,0},{28,4},{1,25},{... | collective-permute-start | bytes 847880 | tf_op jit(solution)/shard_map/ppermute | solution.py:24
  17.4 28.6 %collective-permute-start.3 = (bf16[256,768]{1,0:T(8,128)(2,1)S(1)}, bf16[256,768]{1,0:T(8,128)(2,1)S(1)}, u32[]{:S(2)}, u32[]{:S(2)}) collective-permute-start(bf16[256,768]{1,0:T(8,128)(2,1)S(1)} %copy-done), channel_id=1, source_target_pairs={{0,1},{1,0},{2,3},{3,2},{4,5},{5,4},{6,7},{7,6},{8,9},{9,8},{10,11... | collective-permute-start | bytes 1179656 | tf_op jit(solution)/shard_map/ppermute | solution.py:24
  41.2 24.7 %collective-permute-start.4 = (bf16[256,768]{1,0:T(8,128)(2,1)S(1)}, bf16[256,768]{1,0:T(8,128)(2,1)S(1)}, u32[]{:S(2)}, u32[]{:S(2)}) collective-permute-start(bf16[256,768]{1,0:T(8,128)(2,1)S(1)} %copy-done), channel_id=1, source_target_pairs={{0,2},{1,3},{2,0},{3,1},{4,6},{5,7},{6,4},{7,5},{8,10},{9,11},{10,... | collective-permute-start | bytes 1179656 | tf_op jit(solution)/shard_map/ppermute | solution.py:24
  41.7 26.7 %collective-permute-start.5 = (bf16[256,768]{1,0:T(8,128)(2,1)S(1)}, bf16[256,768]{1,0:T(8,128)(2,1)S(1)}, u32[]{:S(2)}, u32[]{:S(2)}) collective-permute-start(bf16[256,768]{1,0:T(8,128)(2,1)S(1)} %copy-done), channel_id=1, source_target_pairs={{0,3},{1,2},{2,1},{3,0},{4,7},{5,6},{6,5},{7,4},{8,11},{9,10},{10,... | collective-permute-start | bytes 1179656 | tf_op jit(solution)/shard_map/ppermute | solution.py:24
  44.3 24.9 %collective-permute-start.9 = (bf16[96,2432]{1,0:T(8,128)(2,1)S(1)}, bf16[96,2432]{1,0:T(8,128)(2,1)S(1)}, u32[]{:S(2)}, u32[]{:S(2)}) collective-permute-start(bf16[96,2432]{1,0:T(8,128)(2,1)S(1)} %bitcast.58), channel_id=1, source_target_pairs={{0,16},{4,20},{8,24},{12,28},{16,0},{20,4},{24,8},{28,12},{1,17},{... | collective-permute-start | bytes 1400840 | tf_op jit(solution)/shard_map/ppermute | solution.py:24
  45.8 23.1 %collective-permute-start.15 = (bf16[48,2944]{1,0:T(8,128)(2,1)S(1)}, bf16[48,2944]{1,0:T(8,128)(2,1)}, u32[]{:S(2)}, u32[]{:S(2)}) collective-permute-start(bf16[48,2944]{1,0:T(8,128)(2,1)S(1)} %collective-permute-done.14.refs_2_), channel_id=1, source_target_pairs={{0,4},{4,0},{8,12},{12,8},{16,20},{20,16},{24,28},{28,24},{1,5},{5... | collective-permute-start | bytes 847880 | tf_op jit(solution)/shard_map/ppermute | solution.py:24
  46.0 23.6 %collective-permute-start.17 = (bf16[48,2944]{1,0:T(8,128)(2,1)S(1)}, bf16[48,2944]{1,0:T(8,128)(2,1)S(1)}, u32[]{:S(2)}, u32[]{:S(2)}) collective-permute-start(bf16[48,2944]{1,0:T(8,128)(2,1)S(1)} %collective-permute-done.16.refs_4_), channel_id=1, source_target_pairs={{0,4},{4,0},{8,12},{12,8},{16,20},{20,16},{24,28},{28,24},{1,5},{5... | collective-permute-start | bytes 847880 | tf_op jit(solution)/shard_map/ppermute | solution.py:24
  68.4 21.1 %collective-permute-start.7 = (bf16[96,2432]{1,0:T(8,128)(2,1)S(1)}, bf16[96,2432]{1,0:T(8,128)(2,1)}, u32[]{:S(2)}, u32[]{:S(2)}) collective-permute-start(bf16[96,2432]{1,0:T(8,128)(2,1)S(1)} %bitcast.60), channel_id=1, source_target_pairs={{0,8},{4,12},{8,0},{12,4},{16,24},{20,28},{24,16},{28,20},{1,9},{5... | collective-permute-start | bytes 1400840 | tf_op jit(solution)/shard_map/ppermute | solution.py:24
  69.0 20.6 %collective-permute-start.6 = (bf16[96,2432]{1,0:T(8,128)(2,1)S(1)}, bf16[96,2432]{1,0:T(8,128)(2,1)S(1)}, u32[]{:S(2)}, u32[]{:S(2)}) collective-permute-start(bf16[96,2432]{1,0:T(8,128)(2,1)S(1)} %bitcast.61), channel_id=1, source_target_pairs={{0,4},{4,0},{8,12},{12,8},{16,20},{20,16},{24,28},{28,24},{1,5},{5... | collective-permute-start | bytes 1400840 | tf_op jit(solution)/shard_map/ppermute | solution.py:24
  69.2 23.5 %collective-permute-start.10 = (bf16[96,2432]{1,0:T(8,128)(2,1)S(1)}, bf16[96,2432]{1,0:T(8,128)(2,1)S(1)}, u32[]{:S(2)}, u32[]{:S(2)}) collective-permute-start(bf16[96,2432]{1,0:T(8,128)(2,1)S(1)} %collective-permute-done.9.refs_8_), channel_id=1, source_target_pairs={{0,4},{4,0},{8,12},{12,8},{16,20},{20,16},{24,28},{28,24},{1,5},{5... | collective-permute-start | bytes 1400840 | tf_op jit(solution)/shard_map/ppermute | solution.py:24
  69.6 20.0 %collective-permute-start.19 = (bf16[48,2944]{1,0:T(8,128)(2,1)}, bf16[48,2944]{1,0:T(8,128)(2,1)}, u32[]{:S(2)}, u32[]{:S(2)}) collective-permute-start(bf16[48,2944]{1,0:T(8,128)(2,1)} %copy-done.27), channel_id=1, source_target_pairs={{0,4},{4,0},{8,12},{12,8},{16,20},{20,16},{24,28},{28,24},{1,5},{5... | collective-permute-start | bytes 847880 | tf_op jit(solution)/shard_map/ppermute | solution.py:24
  80.4 19.4 %collective-permute-start.12 = (bf16[96,2432]{1,0:T(8,128)(2,1)S(1)}, bf16[96,2432]{1,0:T(8,128)(2,1)S(1)}, u32[]{:S(2)}, u32[]{:S(2)}) collective-permute-start(bf16[96,2432]{1,0:T(8,128)(2,1)S(1)} %collective-permute-done.11.refs_10_), channel_id=1, source_target_pairs={{0,4},{4,0},{8,12},{12,8},{16,20},{20,16},{24,28},{28,24},{1,5},{5... | collective-permute-start | bytes 1400840 | tf_op jit(solution)/shard_map/ppermute | solution.py:24
  89.6 26.4 %collective-permute-start.23 = (bf16[256,768]{1,0:T(8,128)(2,1)}, bf16[256,768]{1,0:T(8,128)(2,1)S(1)}, u32[]{:S(2)}, u32[]{:S(2)}) collective-permute-start(bf16[256,768]{1,0:T(8,128)(2,1)} %cot_r.1), channel_id=1, source_target_pairs={{0,1},{1,0},{2,3},{3,2},{4,5},{5,4},{6,7},{7,6},{8,9},{9,8},{10,11... | collective-permute-start | bytes 1179656 | tf_op jit(solution)/shard_map/ppermute | solution.py:24
  89.6 30.3 %collective-permute-start.24 = (bf16[256,768]{1,0:T(8,128)(2,1)}, bf16[256,768]{1,0:T(8,128)(2,1)}, u32[]{:S(2)}, u32[]{:S(2)}) collective-permute-start(bf16[256,768]{1,0:T(8,128)(2,1)} %cot_r.1), channel_id=1, source_target_pairs={{0,2},{1,3},{2,0},{3,1},{4,6},{5,7},{6,4},{7,5},{8,10},{9,11},{10,... | collective-permute-start | bytes 1179656 | tf_op jit(solution)/shard_map/ppermute | solution.py:24
  92.7 27.2 %collective-permute-start.25 = (bf16[256,768]{1,0:T(8,128)(2,1)}, bf16[256,768]{1,0:T(8,128)(2,1)}, u32[]{:S(2)}, u32[]{:S(2)}) collective-permute-start(bf16[256,768]{1,0:T(8,128)(2,1)} %cot_r.1), channel_id=1, source_target_pairs={{0,3},{1,2},{2,1},{3,0},{4,7},{5,6},{6,5},{7,4},{8,11},{9,10},{10,... | collective-permute-start | bytes 1179656 | tf_op jit(solution)/shard_map/ppermute | solution.py:24
  112.8 25.9 %collective-permute-start.21 = (bf16[80,1024]{1,0:T(8,128)(2,1)}, bf16[80,1024]{1,0:T(8,128)(2,1)S(1)}, u32[]{:S(2)}, u32[]{:S(2)}) collective-permute-start(bf16[80,1024]{1,0:T(8,128)(2,1)} %get-tuple-element.57.refs_0_), channel_id=1, source_target_pairs={{0,2},{1,3},{2,0},{3,1},{4,6},{5,7},{6,4},{7,5},{8,10},{9,11},{10,... | collective-permute-start | bytes 491528 | tf_op jit(solution)/shard_map/ppermute | solution.py:24
  115.9 22.8 %collective-permute-start.22 = (bf16[80,1024]{1,0:T(8,128)(2,1)}, bf16[80,1024]{1,0:T(8,128)(2,1)S(1)}, u32[]{:S(2)}, u32[]{:S(2)}) collective-permute-start(bf16[80,1024]{1,0:T(8,128)(2,1)} %get-tuple-element.57.refs_0_), channel_id=1, source_target_pairs={{0,3},{1,2},{2,1},{3,0},{4,7},{5,6},{6,5},{7,4},{8,11},{9,10},{10,... | collective-permute-start | bytes 491528 | tf_op jit(solution)/shard_map/ppermute | solution.py:24
  191.1 20.4 %collective-permute-start.29 = (bf16[80,1024]{1,0:T(8,128)(2,1)}, bf16[80,1024]{1,0:T(8,128)(2,1)S(1)}, u32[]{:S(2)}, u32[]{:S(2)}) collective-permute-start(bf16[80,1024]{1,0:T(8,128)(2,1)} %get-tuple-element.76.refs_0_), channel_id=1, source_target_pairs={{0,1},{1,0},{2,3},{3,2},{4,5},{5,4},{6,7},{7,6},{8,9},{9,8},{10,11... | collective-permute-start | bytes 491528 | tf_op jit(solution)/shard_map/ppermute | solution.py:24
  239.3 19.6 %collective-permute-start.41 = (bf16[144,1280]{1,0:T(8,128)(2,1)}, bf16[144,1280]{1,0:T(8,128)(2,1)S(1)}, u32[]{:S(2)}, u32[]{:S(2)}) collective-permute-start(bf16[144,1280]{1,0:T(8,128)(2,1)} %get-tuple-element.96), channel_id=1, source_target_pairs={{0,16},{4,20},{8,24},{12,28},{16,0},{20,4},{24,8},{28,12},{1,17},{... | collective-permute-start | bytes 1105928 | tf_op jit(solution)/shard_map/ppermute | solution.py:24
  242.7 18.9 %collective-permute-start.42 = (bf16[144,1280]{1,0:T(8,128)(2,1)}, bf16[144,1280]{1,0:T(8,128)(2,1)S(1)}, u32[]{:S(2)}, u32[]{:S(2)}) collective-permute-start(bf16[144,1280]{1,0:T(8,128)(2,1)} %get-tuple-element.97), channel_id=1, source_target_pairs={{0,24},{4,28},{8,16},{12,20},{16,8},{20,12},{24,0},{28,4},{1,25},{... | collective-permute-start | bytes 1105928 | tf_op jit(solution)/shard_map/ppermute | solution.py:24
  251.1 32.5 %collective-permute-start.26 = (bf16[256,768]{1,0:T(8,128)(2,1)}, bf16[256,768]{1,0:T(8,128)(2,1)S(1)}, u32[]{:S(2)}, u32[]{:S(2)}) collective-permute-start(bf16[256,768]{1,0:T(8,128)(2,1)} %get-tuple-element.73), channel_id=1, source_target_pairs={{0,1},{1,0},{2,3},{3,2},{4,5},{5,4},{6,7},{7,6},{8,9},{9,8},{10,11... | collective-permute-start | bytes 1179656 | tf_op jit(solution)/shard_map/ppermute | solution.py:24
  253.5 23.3 %collective-permute-start.37 = (bf16[192,1152]{1,0:T(8,128)(2,1)}, bf16[192,1152]{1,0:T(8,128)(2,1)S(1)}, u32[]{:S(2)}, u32[]{:S(2)}) collective-permute-start(bf16[192,1152]{1,0:T(8,128)(2,1)} %get-tuple-element.90), channel_id=1, source_target_pairs={{0,16},{4,20},{8,24},{12,28},{16,0},{20,4},{24,8},{28,12},{1,17},{... | collective-permute-start | bytes 1327112 | tf_op jit(solution)/shard_map/ppermute | solution.py:24
  258.9 20.1 %collective-permute-start.38 = (bf16[192,1152]{1,0:T(8,128)(2,1)}, bf16[192,1152]{1,0:T(8,128)(2,1)S(1)}, u32[]{:S(2)}, u32[]{:S(2)}) collective-permute-start(bf16[192,1152]{1,0:T(8,128)(2,1)} %get-tuple-element.91), channel_id=1, source_target_pairs={{0,24},{4,28},{8,16},{12,20},{16,8},{20,12},{24,0},{28,4},{1,25},{... | collective-permute-start | bytes 1327112 | tf_op jit(solution)/shard_map/ppermute | solution.py:24
  262.3 44.3 %collective-permute-start.27 = (bf16[256,768]{1,0:T(8,128)(2,1)}, bf16[256,768]{1,0:T(8,128)(2,1)S(1)}, u32[]{:S(2)}, u32[]{:S(2)}) collective-permute-start(bf16[256,768]{1,0:T(8,128)(2,1)} %get-tuple-element.74), channel_id=1, source_target_pairs={{0,2},{1,3},{2,0},{3,1},{4,6},{5,7},{6,4},{7,5},{8,10},{9,11},{10,... | collective-permute-start | bytes 1179656 | tf_op jit(solution)/shard_map/ppermute | solution.py:24
  267.0 39.7 %collective-permute-start.28 = (bf16[256,768]{1,0:T(8,128)(2,1)}, bf16[256,768]{1,0:T(8,128)(2,1)S(1)}, u32[]{:S(2)}, u32[]{:S(2)}) collective-permute-start(bf16[256,768]{1,0:T(8,128)(2,1)} %get-tuple-element.75), channel_id=1, source_target_pairs={{0,3},{1,2},{2,1},{3,0},{4,7},{5,6},{6,5},{7,4},{8,11},{9,10},{10,... | collective-permute-start | bytes 1179656 | tf_op jit(solution)/shard_map/ppermute | solution.py:24
  276.8 30.9 %collective-permute-start.32 = (bf16[256,768]{1,0:T(8,128)(2,1)}, bf16[256,768]{1,0:T(8,128)(2,1)S(1)}, u32[]{:S(2)}, u32[]{:S(2)}) collective-permute-start(bf16[256,768]{1,0:T(8,128)(2,1)} %get-tuple-element.83), channel_id=1, source_target_pairs={{0,1},{1,0},{2,3},{3,2},{4,5},{5,4},{6,7},{7,6},{8,9},{9,8},{10,11... | collective-permute-start | bytes 1179656 | tf_op jit(solution)/shard_map/ppermute | solution.py:24
  279.0 50.1 %collective-permute-start.33 = (bf16[256,768]{1,0:T(8,128)(2,1)}, bf16[256,768]{1,0:T(8,128)(2,1)S(1)}, u32[]{:S(2)}, u32[]{:S(2)}) collective-permute-start(bf16[256,768]{1,0:T(8,128)(2,1)} %get-tuple-element.84), channel_id=1, source_target_pairs={{0,2},{1,3},{2,0},{3,1},{4,6},{5,7},{6,4},{7,5},{8,10},{9,11},{10,... | collective-permute-start | bytes 1179656 | tf_op jit(solution)/shard_map/ppermute | solution.py:24
  283.7 45.4 %collective-permute-start.34 = (bf16[256,768]{1,0:T(8,128)(2,1)}, bf16[256,768]{1,0:T(8,128)(2,1)}, u32[]{:S(2)}, u32[]{:S(2)}) collective-permute-start(bf16[256,768]{1,0:T(8,128)(2,1)} %get-tuple-element.85), channel_id=1, source_target_pairs={{0,3},{1,2},{2,1},{3,0},{4,7},{5,6},{6,5},{7,4},{8,11},{9,10},{10,... | collective-permute-start | bytes 1179656 | tf_op jit(solution)/shard_map/ppermute | solution.py:24
  286.7 54.5 %all-to-all-start.1 = ((bf16[4,24,2432]{2,1,0:T(8,128)(2,1)}), bf16[4,24,2432]{2,1,0:T(8,128)(2,1)S(1)}, u32[]{:S(2)}, u32[]{:S(2)}) async-start(bf16[4,24,2432]{2,1,0:T(8,128)(2,1)} %bitcast.11), calls=%async_computation.1 | async-start | bytes 933888 | tf_op jit(solution)/shard_map/all_to_all | solution.py:710
  (59 other events, 672.1 us)

commit v2 on v1

v2 whole, which is shorter than its diff:
```python
import functools
import math

import jax
import jax.numpy as jnp
from jax import lax
from jax.experimental import pallas as pl
from jax.experimental.pallas import tpu as pltpu
from jax.sharding import PartitionSpec as P

MODS = 3
RUN = 128
LANES = 128
EPSILON = 1e-05
LOG2E = 1.4426950408889634
FAR = 1e30
VMEM_LIMIT = 60 * 1024 * 1024
VMEM_SPARE = 6 * 1024 * 1024

f32 = jnp.float32
bf16 = jnp.bfloat16


def swap(block, axis, flip):
    count = lax.axis_size(axis)
    return lax.ppermute(block, axis, [(i, i ^ flip) for i in range(count)])


def gather_narrow(block):
    return [block] + [swap(block, "narrow", s) for s in range(1, lax.axis_size("narrow"))]


def relay_narrow(block, *earlier):
    count = lax.axis_size("narrow")
    pieces = {0: block}
    for s in sorted(range(1, count), key=lambda s: (s.bit_count(), -s)):
        low_bit = s & -s
        if s == low_bit:
            pieces[s] = swap(block, "narrow", s)
        else:
            pieces[s] = swap(after(pieces[s ^ low_bit], *earlier), "narrow", low_bit)
    return [pieces[s] for s in range(count)]


def add_narrow(block, *beside):
    flip = lax.axis_size("narrow") // 2
    while flip:
        got = swap(block, "narrow", flip)
        block = (after(block, *beside).astype(f32) + got.astype(f32)).astype(bf16)
        flip //= 2
        beside = ()
    return block


def scatter_narrow(parts):
    return [parts[0]] + [swap(parts[s], "narrow", s) for s in range(1, len(parts))]


def sum_narrow(parts, *earlier):
    parts = list(parts)
    arrived = [parts[0]]
    for s in range(len(parts) - 1, 0, -1):
        low_bit = s & -s
        got = swap(parts[s], "narrow", low_bit)
        if s == low_bit:
            arrived.append(got)
        else:
            rest = s ^ low_bit
            parts[rest] = (after(parts[rest], *earlier).astype(f32) + got.astype(f32)).astype(bf16)
    return arrived, parts[-2]


def near_wide(block):
    return [block] + [swap(block, "wide", 2 * s) for s in range(1, lax.axis_size("wide") // 2)]


def far_wide(near):
    return [piece for block in near for piece in (block, swap(block, "wide", 1))]


def after(value, *earlier):
    return lax.optimization_barrier((value,) + earlier)[0] if earlier else value


def dot(a, b, ca, cb):
    return lax.dot_general(a, b, (((ca,), (cb,)), ((), ())), preferred_element_type=f32)


def call(kernel, outs, ins, scratch=(), us=1.0):
    spaces = {"v": pltpu.VMEM, "s": pltpu.SMEM, "a": pl.ANY}
    held = [(array.shape, array.dtype) for array, space in ins if space == "v"]
    held += [(shape, dtype) for shape, dtype, space in outs if space == "v"]
    held += [(part.shape, part.dtype) for part in scratch if part.memory_space == pltpu.VMEM]
    need = sum(math.prod(shape) * jnp.dtype(dtype).itemsize for shape, dtype in held)
    need = VMEM_LIMIT
    return pl.pallas_call(
        kernel,
        out_shape=[jax.ShapeDtypeStruct(shape, dtype) for shape, dtype, _ in outs],
        in_specs=[pl.BlockSpec(memory_space=spaces[space]) for _, space in ins],
        out_specs=[pl.BlockSpec(memory_space=spaces[space]) for _, _, space in outs],
        scratch_shapes=list(scratch),
        compiler_params=pltpu.CompilerParams(vmem_limit_bytes=need),
        cost_estimate=pl.CostEstimate(flops=int(us * 1.1e9), bytes_accessed=1, transcendentals=0),
    )(*[array for array, _ in ins])


def place_pieces(pieces, target, sem, me, rows):
    copies = []
    for s, piece in enumerate(pieces):
        at = pl.multiple_of((me ^ s) * rows, 16)
        copy = pltpu.make_async_copy(piece, target.at[pl.ds(at, rows), :], sem.at[s])
        copy.start()
        copies.append(copy)
    return copies


def split_kernel(
    er, ep, wid, below, meta, w_r, gain_r, out_r, x_r, dt_r, bias_r, conv_r, conv_b_r, skip_r, log_r, *refs
):
    nar = len(refs) - 4
    outs, (small_o, out_o, rows_s, lanes) = refs[:nar], refs[nar:]
    inner = wid * nar * er
    es = wid * ep
    dr = w_r.shape[1]
    gain = jnp.broadcast_to(gain_r[...], (dr, LANES)).astype(bf16)
    for half in range(2):
        first = half * (MODS * es + LANES)
        for m in range(MODS):
            row = w_r[m, :, half * inner : (half + 1) * inner].astype(f32)
            for k in range(nar):
                parts = []
                for v in range(wid):
                    parts.append(row[:, (v * nar + k) * er : (v * nar + k + 1) * er])
                    if ep > er:
                        parts.append(jnp.zeros((dr, ep - er), f32))
                rows_s[k, :, first + m * es : first + (m + 1) * es] = jnp.concatenate(parts, axis=1).astype(bf16)
    for s in range(nar):
        rows_s[s, :, MODS * es : MODS * es + LANES] = gain
    for s in range(nar):
        outs[s][...] = rows_s[meta[0] ^ s]
    out_whole = jnp.concatenate([out_r[m].astype(f32) for m in range(MODS)], axis=1)
    if ep > er:
        out_whole = jnp.concatenate([out_whole, jnp.zeros((ep - er, out_whole.shape[1]), f32)], axis=0)
    out_w = out_o.shape[1]
    for k in range(out_whole.shape[1] // out_w):
        out_o[k * ep : (k + 1) * ep, :] = out_whole[:, k * out_w : (k + 1) * out_w].astype(bf16)
    rank = dt_r.shape[1]
    lanes[...] = jnp.zeros_like(lanes)
    for m in range(MODS):
        lanes[m * rank : (m + 1) * rank, :er] = dt_r[m].astype(f32)
    base = MODS * rank
    for at, ref in ((T_BIAS, bias_r), (T_CONV_B, conv_b_r), (T_CONV, conv_r), (T_SKIP, skip_r), (T_LOG, log_r)):
        lanes[base + at : base + at + ref.shape[0], :er] = ref[...].astype(f32)
    turned = lanes[...].T[:ep]
    xw = x_r.shape[2]
    columns = []
    for m in range(MODS):
        part = x_r[m].astype(f32)
        if ep > er:
            part = jnp.concatenate([part, jnp.zeros((ep - er, xw), f32)], axis=0)
        columns += [part, jnp.zeros((ep, LANES - xw), f32)]
    small = jnp.concatenate(columns + [turned], axis=1)
    cols = small.shape[1]
    small_o[...] = jnp.zeros_like(small_o)
    for c in range(-(-ep // below)):
        part = small[c * below : min(ep, (c + 1) * below)]
        small_o[: part.shape[0], c * cols : (c + 1) * cols] = part.astype(bf16)


def join_kernel(meta, *refs):
    pieces, (small, out_rows, front_o, gate_o) = refs[:-4], refs[-4:]
    nar, dr = len(pieces), pieces[0].shape[0]
    row = lax.broadcasted_iota(jnp.int32, (nar * dr, dr), 0)
    col = lax.broadcasted_iota(jnp.int32, (nar * dr, dr), 1)
    joined = sum(
        dot((row == (meta[0] ^ s) * dr + col).astype(bf16), piece[...], 1, 0)
        for s, piece in enumerate(pieces)
    ).astype(bf16)
    front_o[: nar * dr, :] = joined[:, : front_o.shape[1]]
    front_o[nar * dr :, :] = small[...]
    gate_o[: nar * dr, :] = joined[:, front_o.shape[1] :]
    gate_o[nar * dr :, :] = out_rows[...]


T_BIAS, T_CONV_B, T_CONV, T_SKIP, T_LOG = 0, 3, 4, 8, 16


def in_kernel(nar, wid, rpd, taps, ep, rank, meta, *refs):
    toks, w_pieces = refs[:nar], refs[nar : nar + wid]
    normed_o, front_o, csum_o, mixed_o, px_o, kinds_o, w_x, w_dt_o, table_o, gain_o = refs[nar + wid : nar + wid + 10]
    xs, wf, rest, tok_sem, w_sem, rest_sem = refs[nar + wid + 10 :]
    n, w, split = meta[0], meta[1], meta[2]
    total, es = csum_o.shape
    width = MODS * es
    rows_w = wf.shape[0] // wid
    piece_rows = toks[0].shape[0]
    copies = []
    cols = rest.shape[1]
    below = w_pieces[0].shape[0] - rows_w
    x_cols = w_x.shape[1]
    for s, piece in enumerate(w_pieces):
        for c in range(-(-ep // below)):
            count = min(below, ep - c * below)
            at = pl.multiple_of((w ^ s) * ep + c * below, 16)
            copies.append(
                pltpu.make_async_copy(
                    piece.at[pl.ds(rows_w, count), pl.ds(c * cols, cols)],
                    rest.at[pl.ds(at, count), :],
                    rest_sem.at[c, s],
                )
            )
    tok_copies, w_copies = [], []
    for s, piece in enumerate(toks):
        at = pl.multiple_of((n ^ s) * piece_rows, 16)
        tok_copies.append(
            pltpu.make_async_copy(piece, xs.at[pl.ds(at, piece_rows), :], tok_sem.at[s])
        )
    for s, piece in enumerate(w_pieces):
        at = pl.multiple_of((w ^ s) * rows_w, 16)
        w_copies.append(
            pltpu.make_async_copy(
                piece.at[pl.ds(0, rows_w), pl.ds(0, wf.shape[1])], wf.at[pl.ds(at, rows_w), :], w_sem.at[s]
            )
        )
    for copy in copies + tok_copies + w_copies:
        copy.start()
    for copy in copies:
        copy.wait()
    w_x[...] = rest[:, :x_cols]
    turned = rest[:, x_cols:].astype(f32).T
    w_dt_o[...] = turned[: MODS * rank].astype(bf16)
    table_o[...] = turned[MODS * rank :]
    for copy in tok_copies:
        copy.wait()
    for p in range(nar):
        tail = xs[(p + 1) * piece_rows - 16 : (p + 1) * piece_rows, :LANES].astype(f32)
        row = lax.broadcasted_iota(jnp.int32, tail.shape, 0)
        for j in range(rpd):
            kinds_o[p * rpd + j] = jnp.max(jnp.where(row == j, tail, 0.0)).astype(jnp.int32)
    for copy in w_copies:
        copy.wait()
    gain = wf[:, width : width + LANES].astype(f32).T[0:1, :]
    gain_o[...] = gain
    front_o[0:8, :] = jnp.zeros((8, es), f32)

    def one_run(r, before):
        rows = pl.ds(pl.multiple_of(r * RUN, RUN), RUN)
        kind = kinds_o[r]
        x_at = pl.multiple_of((r // rpd) * piece_rows + (r % rpd) * RUN, 16)
        x = xs[pl.ds(x_at, RUN), :].astype(f32)
        scale = lax.rsqrt(jnp.mean(x * x, axis=1, keepdims=True) + EPSILON)
        normed = (x * scale * gain).astype(bf16)
        normed_o[rows, :] = normed
        front = dot(normed, wf[:, pl.ds(pl.multiple_of(kind * es, LANES), es)], 1, 0)
        front_o[pl.ds(pl.multiple_of(r * RUN + 8, 8), RUN), :] = front
        ext = jnp.concatenate([before, front], axis=0)
        place = r * RUN + lax.broadcasted_iota(jnp.int32, (RUN, 1), 0)
        offset = place - jnp.where(place >= split, split, 0)
        csum = jnp.broadcast_to(table_o[T_CONV_B : T_CONV_B + 1, :], (RUN, es))
        for lag in range(taps):
            tap = table_o[T_CONV + taps - 1 - lag : T_CONV + taps - lag, :]
            valid = (offset >= lag).astype(f32)
            csum = csum + tap * ext[8 - lag : 8 - lag + RUN, :] * valid
        csum_o[rows, :] = csum
        mixed = (csum * jax.nn.sigmoid(csum)).astype(bf16)
        mixed_o[rows, :] = mixed
        px = dot(mixed, w_x[:, pl.ds(pl.multiple_of(kind * LANES, LANES), LANES)], 1, 0)
        px_o[:, pl.ds(pl.multiple_of(r * RUN, LANES), RUN)] = px.T[: px_o.shape[0]].astype(bf16)
        return front[RUN - 8 :]

    lax.fori_loop(0, total // RUN, one_run, jnp.zeros((8, es), f32))


def gate_kernel(wid, meta, kinds, *refs):
    pieces, (normed_r, act_o, slope_o, wg, w_sem) = refs[:wid], refs[wid:]
    es = act_o.shape[1]
    width = wg.shape[1]
    rows_w = wg.shape[0] // wid
    copies = []
    for s, piece in enumerate(pieces):
        at = pl.multiple_of((meta[1] ^ s) * rows_w, 16)
        source = piece.at[pl.ds(0, rows_w), :]
        copies.append(pltpu.make_async_copy(source, wg.at[pl.ds(at, rows_w), :], w_sem.at[s]))
        copies[-1].start()
    for copy in copies:
        copy.wait()

    def one_run(r, carry):
        rows = pl.ds(pl.multiple_of(r * RUN, RUN), RUN)
        gate = dot(normed_r[rows, :], wg[:, pl.ds(pl.multiple_of(kinds[r] * es, LANES), es)], 1, 0)
        sig = jax.nn.sigmoid(gate)
        act_o[rows, :] = gate * sig
        slope_o[rows, :] = sig * (1.0 + gate * (1.0 - sig))
        return carry

    lax.fori_loop(0, normed_r.shape[0] // RUN, one_run, 0)


def cot_kernel(nar, wid, meta, kinds, *refs):
    cots, pieces = refs[:nar], refs[nar : nar + wid]
    act_r, slope_r, cot_o, w_out_o, dssm_o, dgate_o, cot_sem, out_sem = refs[nar + wid :]
    total, d = cot_o.shape
    copies = place_pieces(cots, cot_o, cot_sem, meta[0], cots[0].shape[0])
    width = pieces[0].shape[1]
    ep = w_out_o.shape[0] // wid
    blocks = w_out_o.shape[1] // width
    first = pieces[0].shape[0] - blocks * ep
    for s, piece in enumerate(pieces):
        at = pl.multiple_of((meta[1] ^ s) * ep, 16)
        for k in range(blocks):
            copies.append(
                pltpu.make_async_copy(
                    piece.at[pl.ds(first + k * ep, ep), :],
                    w_out_o.at[pl.ds(at, ep), pl.ds(k * width, width)],
                    out_sem.at[k, s],
                )
            )
            copies[-1].start()
    for copy in copies:
        copy.wait()

    def one_run(r, carry):
        rows = pl.ds(pl.multiple_of(r * RUN, RUN), RUN)
        d_gated = dot(cot_o[rows, :], w_out_o[:, pl.ds(pl.multiple_of(kinds[r] * d, LANES), d)], 1, 1)
        dssm_o[rows, :] = d_gated * act_r[rows, :]
        dgate_o[rows, :] = d_gated * slope_r[rows, :]
        return carry

    lax.fori_loop(0, total // RUN, one_run, 0)


def softplus(v):
    return jnp.maximum(v, 0.0) + jnp.log1p(jnp.exp(-jnp.abs(v)))


def scan_kernel(rank, meta, kinds, *refs):
    px_r, w_dt, table, mixed_r, dssm_r = refs[:5]
    ssm_o, dpx_o, gmix_o, dpre_o, dlow_o, glog_o, gskip_o = refs[5:12]
    pxs, pre_s, step_s, states, bc, ps, qs, gs, fs, dtk, dtu, r1s, r2s = refs[12:]
    split = meta[2]
    total, es = mixed_r.shape
    ns = states.shape[1]
    groups = es // LANES
    runs = total // RUN
    lane = [slice(g * LANES, (g + 1) * LANES) for g in range(groups)]
    rates = -jnp.exp(table[T_LOG : T_LOG + ns, :])
    r1s[...] = rates
    r2s[...] = rates * LOG2E
    half = ns // 2
    pxs[...] = px_r[...].astype(f32)
    skip = table[T_SKIP : T_SKIP + 1, :]

    def rows_of(r):
        return pl.ds(pl.multiple_of(r * RUN, RUN), RUN)

    k_row = lax.broadcasted_iota(jnp.int32, (ns, LANES), 1)
    own_row = (k_row % ns == lax.broadcasted_iota(jnp.int32, (ns, LANES), 0)) & (k_row < 4 * ns)
    own_row = own_row.astype(f32)
    k_col = lax.broadcasted_iota(jnp.int32, (LANES, 2 * LANES), 0)
    b_or_c = lax.broadcasted_iota(jnp.int32, (LANES, 2 * LANES), 1) // LANES
    ones = ((k_col % (2 * ns)) // ns == b_or_c).astype(bf16)

    def spread(r):
        block = pxs[rank : rank + 2 * ns, pl.ds(pl.multiple_of(r * RUN, LANES), RUN)]
        high = block.astype(bf16).astype(f32)
        parts = jnp.concatenate([high, block - high, jnp.zeros((LANES - 4 * ns, RUN), f32)], axis=0)
        picked = parts.T[:, None, :] * own_row[None]
        bc[bc_rows(r), :] = dot(picked.reshape(RUN * ns, LANES).astype(bf16), ones, 1, 0)

    def bc_rows(r):
        if bc.shape[0] == RUN * ns:
            return pl.ds(0, RUN * ns)
        return pl.ds(pl.multiple_of(r * (RUN * ns), RUN * ns), RUN * ns)

    def prepare(r, again):
        rows = rows_of(r)
        steps = step_s[rows, :]
        place = r * RUN + lax.broadcasted_iota(jnp.int32, (RUN, 1), 0)
        reset = (place == 0) | (place == split)
        dtk[...] = jnp.where(reset, FAR, steps)
        dtu[...] = steps * mixed_r[rows, :].astype(f32)
        if not again or bc.shape[0] == RUN * ns:
            spread(r)

    def row(tile, j, g):
        return jnp.broadcast_to(tile[j : j + 1, lane[g]], (ns, LANES))

    def folded(ref):
        outs = []
        for g in range(groups):
            out = ref[g, pl.ds(0, RUN, stride=half), :]
            for s in range(1, half):
                out = out + ref[g, pl.ds(s, RUN, stride=half), :]
            outs.append(out)
        return jnp.concatenate(outs, axis=1)

    states[0] = jnp.zeros((ns, es), bf16)

    def forward(r, hs):
        rows = rows_of(r)
        kind = kinds[r]
        low = pxs[:rank, pl.ds(pl.multiple_of(r * RUN, LANES), RUN)].astype(bf16)
        dlow_o[:, pl.ds(pl.multiple_of(r * RUN, LANES), RUN)] = low
        weights = w_dt[pl.ds(pl.multiple_of(kind * rank, 16), rank), :]
        pre = dot(low, weights, 0, 0) + table[pl.ds(T_BIAS + kind, 1), :]
        pre_s[rows, :] = pre
        step_s[rows, :] = softplus(pre)
        prepare(r, False)

        def eight(i, hs):
            hs = list(hs)
            at = pl.ds(pl.multiple_of(i * 16, 16), 16)
            k8, u8 = dtk[at, :], dtu[at, :]
            bcv = bc.at[bc_rows(r), :].at[pl.ds(pl.multiple_of(i * (16 * ns), 16 * ns), 16 * ns), :]
            psv = ps.at[:, pl.ds(pl.multiple_of(i * (16 * half), 16 * half), 16 * half), :]
            stv = states.at[pl.ds(r * RUN + i * 16 + 1, 16)]
            for j in range(16):
                bt = bcv[j * ns : (j + 1) * ns, :LANES]
                ct = bcv[j * ns : (j + 1) * ns, LANES:]
                for g in range(groups):
                    decay = jnp.exp2(row(k8, j, g) * r2s[:, lane[g]])
                    hs[g] = decay * hs[g] + row(u8, j, g) * bt
                    stv[j, :, lane[g]] = hs[g].astype(bf16)
                    part = hs[g] * ct
                    psv[g, j * half : (j + 1) * half, :] = part[:half] + part[half:]
            return tuple(hs)

        hs = lax.fori_loop(0, RUN // 16, eight, hs)
        ssm_o[rows, :] = folded(ps) + skip * mixed_r[rows, :].astype(f32)
        return hs

    zero = jnp.zeros((ns, LANES), f32)
    lax.fori_loop(0, runs, forward, (zero,) * groups)
    gskip_o[...] = jnp.zeros_like(gskip_o)
    gather_k = lax.broadcasted_iota(jnp.int32, (2 * LANES, LANES), 0) // LANES
    gather_l = lax.broadcasted_iota(jnp.int32, (2 * LANES, LANES), 1) // ns
    gather = (gather_k == gather_l).astype(bf16)
    keep_n = lax.broadcasted_iota(jnp.int32, (ns, LANES), 0)
    keep = (lax.broadcasted_iota(jnp.int32, (ns, LANES), 1) % ns == keep_n).astype(f32)

    def backward(back, carry):
        r = runs - 1 - back
        rows = rows_of(r)
        kind = kinds[r]
        prepare(r, True)

        def eight(back_i, carry):
            ms, hs, gr = [list(part) for part in carry]
            i = RUN // 16 - 1 - back_i
            at = pl.ds(pl.multiple_of(i * 16, 16), 16)
            k8, u8 = dtk[at, :], dtu[at, :]
            y8 = dssm_r[pl.ds(pl.multiple_of(r * RUN + i * 16, 16), 16), :]
            bcv = bc.at[bc_rows(r), :].at[pl.ds(pl.multiple_of(i * (16 * ns), 16 * ns), 16 * ns), :]
            psv = ps.at[:, pl.ds(pl.multiple_of(i * (16 * half), 16 * half), 16 * half), :]
            qsv = qs.at[:, pl.ds(pl.multiple_of(i * (16 * half), 16 * half), 16 * half), :]
            stv = states.at[pl.ds(r * RUN + i * 16, 16)]
            gsv = gs.at[pl.ds(pl.multiple_of(i * (16 * ns), 16 * ns), 16 * ns), :]
            for j in reversed(range(16)):
                bt = bcv[j * ns : (j + 1) * ns, :LANES]
                ct = bcv[j * ns : (j + 1) * ns, LANES:]
                gb_sum, gc_sum = None, None
                for g in range(groups):
                    dt = row(k8, j, g)
                    dy = row(y8, j, g)
                    adjoint = dy * ct + ms[g]
                    before = stv[j, :, lane[g]].astype(f32)
                    c_part = dy * hs[g]
                    b_part = adjoint * row(u8, j, g)
                    gb_sum = b_part if gb_sum is None else gb_sum + b_part
                    gc_sum = c_part if gc_sum is None else gc_sum + c_part
                    lb = adjoint * bt
                    fold_at = slice(j * half, (j + 1) * half)
                    psv[g, fold_at, :] = lb[:half] + lb[half:]
                    ms[g] = jnp.exp2(dt * r2s[:, lane[g]]) * adjoint
                    weighted = ms[g] * before
                    by_rate = weighted * r1s[:, lane[g]]
                    qsv[g, fold_at, :] = by_rate[:half] + by_rate[half:]
                    gr[g] = gr[g] + weighted * dt
                    hs[g] = before
                gsv[j * ns : (j + 1) * ns, :LANES] = gb_sum.astype(bf16)
                gsv[j * ns : (j + 1) * ns, LANES:] = gc_sum.astype(bf16)
            return tuple(ms), tuple(hs), tuple(gr)

        carry = lax.fori_loop(0, RUN // 16, eight, carry)
        mixed = mixed_r[rows, :].astype(f32)
        lb, by_rate = folded(ps), folded(qs)
        dssm = dssm_r[rows, :]
        grad_steps = by_rate + lb * mixed
        gmix_o[rows, :] = dssm * skip + lb * step_s[rows, :]
        gskip_o[...] += jnp.sum(dssm * mixed, axis=0, keepdims=True)
        dpre = (grad_steps * jax.nn.sigmoid(pre_s[rows, :])).astype(bf16)
        dpre_o[rows, :] = dpre
        weights = w_dt[pl.ds(pl.multiple_of(kind * rank, 16), rank), :]
        dlow = dot(weights, dpre, 1, 1)
        sums = dot(gs[...], gather, 1, 0).reshape(RUN, ns, LANES) * keep[None]
        fs[...] = (sums[:, :half] + sums[:, half:]).reshape(RUN * half, LANES)
        dbc = fs[pl.ds(0, RUN, stride=half), :]
        for s in range(1, half):
            dbc = dbc + fs[pl.ds(s, RUN, stride=half), :]
        dbc = dbc.T[: 2 * ns]
        at = pl.ds(pl.multiple_of(r * RUN, LANES), RUN)
        dpx_o[:rank, at] = dlow.astype(bf16)
        dpx_o[rank:, at] = dbc.astype(bf16)
        return carry

    last = tuple(states[total, :, lane[g]].astype(f32) for g in range(groups))
    done = lax.fori_loop(0, runs, backward, ((zero,) * groups, last, (zero,) * groups))
    for g in range(groups):
        glog_o[:, lane[g]] = done[2][g] * rates[:, lane[g]]


def scan_call(rank, xw, ns, meta, kinds, px, w_dt_l, table, mixed, dssm):
    total, es = mixed.shape
    bc_runs = total // RUN if total * ns * 2 * LANES * 4 <= 20 * 1024 * 1024 else 1
    return call(
        functools.partial(scan_kernel, rank),
        [
            ((total, es), f32, "v"),
            ((xw, total), bf16, "v"),
            ((total, es), f32, "v"),
            ((total, es), bf16, "v"),
            ((rank, total), bf16, "v"),
            ((ns, es), f32, "v"),
            ((1, es), f32, "v"),
        ],
        [(meta, "s"), (kinds, "s")]
        + [(px, "v"), (w_dt_l, "v"), (table, "v"), (mixed, "v"), (dssm, "v")],
        [
            pltpu.VMEM((xw, total), f32),
            pltpu.VMEM((total, es), f32),
            pltpu.VMEM((total, es), f32),
            pltpu.VMEM((total + 1, ns, es), bf16),
            pltpu.VMEM((bc_runs * RUN * ns, 2 * LANES), f32),
            pltpu.VMEM((es // LANES, RUN * ns // 2, LANES), f32),
            pltpu.VMEM((es // LANES, RUN * ns // 2, LANES), f32),
            pltpu.VMEM((RUN * ns, 2 * LANES), bf16),
            pltpu.VMEM((RUN * ns // 2, LANES), f32),
            pltpu.VMEM((RUN, es), f32),
            pltpu.VMEM((RUN, es), f32),
            pltpu.VMEM((ns, es), f32),
            pltpu.VMEM((ns, es), f32),
        ],
        us=40.0,
    )


def split_rows(acc, place, rows):
    return acc[pl.ds(pl.multiple_of(place * rows, 16), rows), :]


def grads_kernel(wid, ep, rank, meta, kinds, *refs):
    ssm_r, gated_r, dgate_r, cot_r, normed_r, dpre_r, dlow_r, glog_r, gskip_r = refs[:9]
    dgate_o, table_o, blocks_o, acc_out, acc_in = refs[9:]
    total, es = ssm_r.shape
    d = cot_r.shape[1]
    acc_out[...] = jnp.zeros_like(acc_out)
    acc_in[...] = jnp.zeros_like(acc_in)
    table_o[...] = jnp.zeros_like(table_o)
    base = MODS * rank

    def one_run(r, carry):
        rows = pl.ds(pl.multiple_of(r * RUN, RUN), RUN)
        kind = kinds[r]
        ssm = ssm_r[rows, :]
        gated = gated_r[rows, :]
        wide_at = pl.ds(pl.multiple_of(kind * d, LANES), d)
        es_at = pl.ds(pl.multiple_of(kind * es, LANES), es)
        acc_out[:, wide_at] += dot(gated, cot_r[rows, :], 0, 0)
        dgate = (dgate_r[rows, :] * ssm).astype(bf16)
        dgate_o[rows, :] = dgate
        acc_in[:, es_at] += dot(normed_r[rows, :], dgate, 0, 0)
        dpre = dpre_r[rows, :]
        low = dlow_r[:, pl.ds(pl.multiple_of(r * RUN, LANES), RUN)]
        table_o[pl.ds(pl.multiple_of(kind * rank, 8), rank), :] += dot(low, dpre, 1, 0)
        table_o[pl.ds(base + T_BIAS + kind, 1), :] += jnp.sum(dpre.astype(f32), axis=0, keepdims=True)
        return carry

    lax.fori_loop(0, total // RUN, one_run, 0)
    table_o[base + T_SKIP : base + T_SKIP + 1, :] = gskip_r[...]
    table_o[base + T_LOG : base + T_LOG + glog_r.shape[0], :] = glog_r[...]
    in_rows, width = acc_in.shape[0] // wid, acc_in.shape[1]
    for v in range(wid):
        blocks_o[v, :in_rows, :] = acc_in[v * in_rows : (v + 1) * in_rows, :].astype(bf16)
        block = acc_out[v * ep : (v + 1) * ep, :].astype(bf16)
        for k in range(block.shape[1] // width):
            first = in_rows + k * ep
            blocks_o[v, first : first + ep, :] = block[:, k * width : (k + 1) * width]


def branch_kernel(nar, meta, kinds, ssm_r, act_r, w_out, *refs):
    outs, gated_o, branch = refs[:nar], refs[nar], refs[nar + 1]
    d = branch.shape[1]

    def one_run(r, carry):
        rows = pl.ds(pl.multiple_of(r * RUN, RUN), RUN)
        wide_at = pl.ds(pl.multiple_of(kinds[r] * d, LANES), d)
        gated = (ssm_r[rows, :] * act_r[rows, :]).astype(bf16)
        gated_o[rows, :] = gated
        branch[rows, :] = dot(gated, w_out[:, wide_at], 1, 0).astype(bf16)
        return carry

    lax.fori_loop(0, branch.shape[0] // RUN, one_run, 0)
    size = outs[0].shape[0]
    for s in range(nar):
        outs[s][...] = branch[pl.ds(pl.multiple_of((meta[0] ^ s) * size, RUN), size), :]


def pair_kernel(chips, meta, same, peer, *outs):
    chip = meta[1] // 2
    for s in range(chips):
        outs[s][...] = (same[chip ^ s].astype(f32) + peer[chip ^ s].astype(f32)).astype(bf16)


def conv_kernel(nar, wid, taps, ep, meta, kinds, *refs):
    dpx_pieces = refs[:nar]
    table, w_x, gmix_r, csum_r, front_r, mixed_r, normed_r, table_r = refs[nar : nar + 8]
    dfront_o, same_o, peer_o, acc_in, acc_x, small, turned = refs[nar + 8 :]
    split = meta[2]
    total, es = gmix_r.shape
    runs = total // RUN
    acc_in[...] = jnp.zeros_like(acc_in)
    acc_x[...] = jnp.zeros_like(acc_x)
    small[...] = jnp.zeros_like(small)
    xw = dpx_pieces[0].shape[0]

    def one_run(back, later):
        r = runs - 1 - back
        rows = pl.ds(pl.multiple_of(r * RUN, RUN), RUN)
        kind = kinds[r]
        lanes_at = pl.ds(pl.multiple_of(r * RUN, LANES), RUN)
        dpx = sum(piece[:, lanes_at].astype(f32) for piece in dpx_pieces)
        dpx = jnp.concatenate([dpx, jnp.zeros((LANES - xw, RUN), f32)], axis=0).T.astype(bf16)
        x_at = pl.ds(pl.multiple_of(kind * LANES, LANES), LANES)
        acc_x[:, x_at] += dot(mixed_r[rows, :], dpx, 0, 0)
        gmix = gmix_r[rows, :] + dot(dpx, w_x[:, x_at], 1, 1)
        csum = csum_r[rows, :]
        sig = jax.nn.sigmoid(csum)
        dc = gmix * sig * (1.0 + csum * (1.0 - sig))
        place = r * RUN + lax.broadcasted_iota(jnp.int32, (RUN + 8, 1), 0)
        offset = place - jnp.where(place >= split, split, 0)
        ext = jnp.concatenate([dc, later], axis=0)
        lagged = front_r[pl.ds(pl.multiple_of(r * RUN, 8), RUN + 8), :]
        d_front = jnp.zeros((RUN, es), f32)
        for lag in range(taps):
            tap = taps - 1 - lag
            masked = ext * (offset >= lag).astype(f32)
            d_front = d_front + table[T_CONV + tap : T_CONV + tap + 1, :] * masked[lag : lag + RUN, :]
            small[T_CONV + tap : T_CONV + tap + 1, :] += jnp.sum(
                masked[:RUN] * lagged[8 - lag : 8 - lag + RUN, :], axis=0, keepdims=True
            )
        small[T_CONV_B : T_CONV_B + 1, :] += jnp.sum(dc, axis=0, keepdims=True)
        d_front = d_front.astype(bf16)
        dfront_o[rows, :] = d_front
        acc_in[:, pl.ds(pl.multiple_of(kind * es, LANES), es)] += dot(normed_r[rows, :], d_front, 0, 0)
        return dc[:8]

    lax.fori_loop(0, runs, one_run, jnp.zeros((8, es), f32))
    in_rows, width = acc_in.shape[0] // wid, acc_in.shape[1]
    base = table_r.shape[0] - small.shape[0]
    rest = jnp.concatenate([table_r[:base, :], table_r[base:, :] + small[...]], axis=0)
    rest = jnp.concatenate([rest, jnp.zeros((256 - rest.shape[0], es), f32)], axis=0).T
    x_cols = acc_x.shape[1]
    turned[:, :x_cols] = acc_x[...].astype(bf16)
    turned[:, x_cols : x_cols + 256] = rest.astype(bf16)
    turned[:, x_cols + 256 :] = jnp.zeros((es, width - x_cols - 256), bf16)
    core = meta[1] & 1
    for ref, parity in ((same_o, core), (peer_o, 1 - core)):
        for c in range(wid // 2):
            place = 2 * c + parity
            ref[c, :in_rows, :] = split_rows(acc_in, place, in_rows).astype(bf16)
            ref[c, in_rows:, :] = split_rows(turned, place, ep)


def normed_kernel(nar, wid, meta, kinds, *refs):
    fronts, gates = refs[:wid], refs[wid : 2 * wid]
    dfront_r, dgate_r = refs[2 * wid : 2 * wid + 2]
    outs = refs[2 * wid + 2 : 2 * wid + 2 + nar]
    wf, wg, dn, f_sem, g_sem = refs[2 * wid + 2 + nar :]
    w = meta[1]
    total, es = dfront_r.shape
    rows_w = wf.shape[0] // wid
    copies = []
    width = MODS * es
    for pieces, target, sem in ((fronts, wf, f_sem), (gates, wg, g_sem)):
        for s, piece in enumerate(pieces):
            at = pl.multiple_of((w ^ s) * rows_w, 16)
            copies.append(
                pltpu.make_async_copy(
                    piece.at[pl.ds(0, rows_w), pl.ds(0, width)], target.at[pl.ds(at, rows_w), :], sem.at[s]
                )
            )
            copies[-1].start()
    for copy in copies:
        copy.wait()

    def one_run(r, carry):
        rows = pl.ds(pl.multiple_of(r * RUN, RUN), RUN)
        at = pl.ds(pl.multiple_of(kinds[r] * es, LANES), es)
        dn[rows, :] = (dot(dfront_r[rows, :], wf[:, at], 1, 1) + dot(dgate_r[rows, :], wg[:, at], 1, 1)).astype(bf16)
        return carry

    lax.fori_loop(0, total // RUN, one_run, 0)
    size = outs[0].shape[0]
    for s in range(nar):
        outs[s][...] = dn[pl.ds(pl.multiple_of((meta[0] ^ s) * size, RUN), size), :]


def total_a_kernel(er, ep, blocks, in_o, out_o):
    d = out_o.shape[2]
    in_rows = in_o.shape[0]
    summed = sum(blocks[v].astype(f32) for v in range(blocks.shape[0]))
    in_o[...] = summed[:in_rows].astype(bf16)
    wide = jnp.concatenate([summed[at : at + ep] for at in range(in_rows, summed.shape[0], ep)], axis=1)
    for m in range(MODS):
        out_o[m] = wide[:er, m * d : (m + 1) * d]


def total_b_kernel(nar, chips, er, rank, taps, ns, meta, *refs):
    pieces, gate_r, outs = refs[:chips], refs[chips], refs[chips + 1 : chips + 1 + nar]
    x_o, dt_o, bias_o, conv_o, conv_b_o, log_o, skip_o, rows_s = refs[chips + 1 + nar :]
    in_rows, width = gate_r.shape
    dr = outs[0].shape[0]
    summed = sum(piece[...].astype(f32) for piece in pieces)
    gate = gate_r[...].astype(f32)
    for k in range(nar):
        rows_s[k, :, :width] = summed[k * dr : (k + 1) * dr].astype(bf16)
        rows_s[k, :, width:] = gate[k * dr : (k + 1) * dr].astype(bf16)
    for s in range(nar):
        outs[s][...] = rows_s[meta[0] ^ s]
    rest = summed[in_rows:]
    x_cols = MODS * LANES
    for m in range(MODS):
        x_o[m] = rest[:er, m * LANES : m * LANES + x_o.shape[2]]
    lanes = rest[:, x_cols : x_cols + 256]
    pad = LANES - lanes.shape[0]
    turned = jnp.concatenate([lanes, jnp.zeros((pad, 256), f32)], axis=0).T[:, :er]
    base = MODS * rank
    for m in range(MODS):
        dt_o[m] = turned[m * rank : (m + 1) * rank]
    bias_o[...] = turned[base + T_BIAS : base + T_BIAS + MODS]
    conv_o[...] = turned[base + T_CONV : base + T_CONV + taps]
    conv_b_o[...] = turned[base + T_CONV_B : base + T_CONV_B + 1]
    skip_o[...] = turned[base + T_SKIP : base + T_SKIP + 1]
    log_o[...] = turned[base + T_LOG : base + T_LOG + ns]


def tokens_kernel(x_r, cot_r, gain_r, *refs):
    pieces, out = refs[:-1], refs[-1]
    x = x_r[...].astype(f32)
    scale = lax.rsqrt(jnp.mean(x * x, axis=1, keepdims=True) + EPSILON)
    q = sum(piece[...].astype(f32) for piece in pieces) * gain_r[...]
    dotted = jnp.mean(q * x, axis=1, keepdims=True)
    out[...] = (cot_r[...].astype(f32) + scale * q - x * (scale * scale * scale) * dotted).astype(bf16)


def mixed_kernel(x_r, *refs):
    pieces, out = refs[:-1], refs[-1]
    out[...] = (x_r[...].astype(f32) + sum(piece[...].astype(f32) for piece in pieces)).astype(bf16)


def w_in_kernel(nar, wid, er, ep, meta, *refs):
    pieces, (w_r, gain_r, grad_o, gain_o, rows_s) = refs[:nar], refs[nar:]
    es = wid * ep
    inner = wid * nar * er
    for s in range(nar):
        rows_s[meta[0] ^ s] = pieces[s][...].astype(f32)
    sums = 0.0
    for half in range(2):
        for m in range(MODS):
            first = (half * MODS + m) * es
            parts = [rows_s[k, :, first : first + es] for k in range(nar)]
            row = jnp.concatenate(
                [parts[k][:, v * ep : v * ep + er] for v in range(wid) for k in range(nar)], axis=1
            )
            at = slice(half * inner, (half + 1) * inner)
            grad_o[m, :, at] = row
            sums = sums + jnp.sum(row * w_r[m, :, at].astype(f32), axis=1, keepdims=True)
    gain_o[...] = sums / gain_r[...]


def body(
    tokens,
    norm_gain,
    w_in,
    conv_w,
    conv_b,
    w_x,
    w_dt,
    dt_bias,
    a_log,
    d_skip,
    w_out,
    mod_ids,
    split_at,
    cotangent,
):
    nar, wid = lax.axis_size("narrow"), lax.axis_size("wide")
    chips = wid // 2
    n, w = lax.axis_index("narrow"), lax.axis_index("wide")
    own, d = tokens.shape
    total = nar * own
    rpd = own // RUN
    rank, xw, ns, taps = w_dt.shape[0], w_x.shape[2], a_log.shape[1], conv_w.shape[0]
    er = w_out.shape[0]
    inner = er * nar * wid
    ep = -(-er // 16) * 16
    es = ep * wid
    dr = w_in.shape[0]
    width = MODS * es
    meta = jnp.stack([n, w, split_at[0]]).astype(jnp.int32)

    front_w = width + LANES
    gain_col = norm_gain.astype(f32)[:, None]
    w_in_m = w_in.transpose(1, 0, 2)
    out_cols, x_cols = MODS * d, MODS * LANES
    table_rows = T_LOG + ns
    small_cols = x_cols + 256
    blocks = front_w // small_cols
    below = -(-(-(-ep // blocks)) // 16) * 16
    res = call(
        functools.partial(split_kernel, er, ep, wid, below),
        [((dr, front_w + width), bf16, "v")] * nar
        + [((below, front_w), bf16, "v"), ((ep * (out_cols // width), width), bf16, "v")],
        [(meta, "s")]
        + [
            (a, "v")
            for a in (
                w_in_m,
                gain_col,
                w_out.transpose(1, 0, 2),
                w_x.transpose(1, 0, 2),
                w_dt.transpose(1, 0, 2),
                dt_bias,
                conv_w,
                conv_b[None],
                d_skip[None],
                a_log.T,
            )
        ],
        [
            pltpu.VMEM((nar, dr, front_w + width), bf16),
            pltpu.VMEM((256, LANES), f32),
        ],
        us=3.0,
    )
    parts, (small, out_rows) = res[:nar], res[nar:]

    parts = scatter_narrow(parts)
    front_rows, gate_rows = call(
        join_kernel,
        [
            ((nar * dr + below, front_w), bf16, "v"),
            ((nar * dr + out_rows.shape[0], width), bf16, "v"),
        ],
        [(meta, "s")] + [(p, "v") for p in parts] + [(small, "v"), (out_rows, "v")],
        us=2.0,
    )
    front_near = near_wide(front_rows)
    front_pieces = far_wide(front_near)
    run_kinds = mod_ids.reshape(rpd, RUN)[:, :1].astype(bf16)
    tail = jnp.pad(jnp.broadcast_to(run_kinds, (rpd, d)), ((0, 16 - rpd), (0, 0)))
    tok_pieces = relay_narrow(jnp.concatenate([tokens, tail], axis=0))
    gate_near = near_wide(after(gate_rows, *front_near[1:]))
    normed, front, csum, mixed, px, kinds, w_x_l, w_dt_l, table, gain_full = call(
        functools.partial(in_kernel, nar, wid, rpd, taps, ep, rank),
        [
            ((total, d), bf16, "v"),
            ((total + 8, es), f32, "v"),
            ((total, es), f32, "v"),
            ((total, es), bf16, "v"),
            ((xw, total), bf16, "v"),
            ((nar * rpd,), jnp.int32, "s"),
            ((es, x_cols), bf16, "v"),
            ((MODS * rank, es), bf16, "v"),
            ((256 - MODS * rank, es), f32, "v"),
            ((1, d), f32, "v"),
        ],
        [(meta, "s")] + [(p, "a") for p in tok_pieces] + [(p, "a") for p in front_pieces],
        [
            pltpu.VMEM((nar * (own + 16), d), bf16),
            pltpu.VMEM((d, front_w), bf16),
            pltpu.VMEM((es, small_cols), bf16),
            pltpu.SemaphoreType.DMA((nar,)),
            pltpu.SemaphoreType.DMA((wid,)),
            pltpu.SemaphoreType.DMA((-(-ep // below), wid)),
        ],
        us=9.0,
    )
    cot_pieces = relay_narrow(after(cotangent, *tok_pieces[1:]), px)
    gate_pieces = far_wide([after(piece, px) for piece in gate_near])
    act, slope = call(
        functools.partial(gate_kernel, wid),
        [((total, es), f32, "v")] * 2,
        [(meta, "s"), (kinds, "s")] + [(p, "a") for p in gate_pieces] + [(after(normed, *cot_pieces[1:3]), "v")],
        [pltpu.VMEM((d, width), bf16), pltpu.SemaphoreType.DMA((wid,))],
        us=0.1,
    )
    px_total = add_narrow(px, act)
    cot, w_out_l, dssm, dgate_f = call(
        functools.partial(cot_kernel, nar, wid),
        [((total, d), bf16, "v"), ((es, out_cols), bf16, "v")] + [((total, es), f32, "v")] * 2,
        [(meta, "s"), (kinds, "s")]
        + [(p, "a") for p in cot_pieces]
        + [(p, "a") for p in gate_pieces]
        + [(act, "v"), (slope, "v")],
        [pltpu.SemaphoreType.DMA((nar,)), pltpu.SemaphoreType.DMA((out_cols // width, wid))],
        us=7.0,
    )
    ssm, dpx, gmix, dpre, dlow, glog, gskip = scan_call(
        rank, xw, ns, meta, kinds, px_total, w_dt_l, table, mixed, dssm
    )
    dpx_pieces = gather_narrow(dpx)
    res = call(
        functools.partial(branch_kernel, nar),
        [((own, d), bf16, "v")] * nar + [((total, es), bf16, "v")],
        [(meta, "s"), (kinds, "s"), (ssm, "v"), (act, "v"), (w_out_l, "v")],
        [pltpu.VMEM((total, d), bf16)],
        us=5.0,
    )

    branch_parts, gated = res[:nar], res[nar]
    branch_pieces, branch_kept = sum_narrow(branch_parts)
    branch_d1 = branch_pieces[-1]
    in_rows = d // wid
    rows_a = in_rows + ep * (out_cols // width)
    dgate, table_g, blocks_a = call(
        functools.partial(grads_kernel, wid, ep, rank),
        [((total, es), bf16, "v")]
        + [((MODS * rank + table_rows, es), f32, "v")]
        + [((wid, rows_a, width), bf16, "v")],
        [(meta, "s"), (kinds, "s")]
        + [(a, "v") for a in (ssm, gated, dgate_f, cot, normed, dpre, dlow, glog, gskip)],
        [pltpu.VMEM((es, out_cols), f32), pltpu.VMEM((d, width), f32)],
        us=9.0,
    )
    def over_wide(same, peer, *earlier):
        peer = swap(peer, "wide", 1)
        same = after(same, *earlier) if earlier else same
        parts = call(
            functools.partial(pair_kernel, chips),
            [(same.shape[1:], bf16, "v")] * chips,
            [(meta, "s"), (same, "v"), (peer, "v")],
            us=3.0,
        )
        return [parts[0]] + [swap(parts[s], "wide", 2 * s) for s in range(1, chips)]

    blocks_a = lax.all_to_all(blocks_a, "wide", 0, 0)
    rows_b = in_rows + ep
    dpx_pieces = after(tuple(dpx_pieces), branch_kept, branch_d1)
    dfront, same_b, peer_b = call(
        functools.partial(conv_kernel, nar, wid, taps, ep),
        [((total, es), bf16, "v")] + [((chips, rows_b, width), bf16, "v")] * 2,
        [(meta, "s"), (kinds, "s")]
        + [(p, "v") for p in dpx_pieces]
        + [(a, "v") for a in (table, w_x_l, gmix, csum, front, mixed, normed, table_g)],
        [
            pltpu.VMEM((d, width), f32),
            pltpu.VMEM((es, x_cols), f32),
            pltpu.VMEM((table_rows, es), f32),
            pltpu.VMEM((es, width), bf16),
        ],
        us=12.0,
    )
    dn_parts = call(
        functools.partial(normed_kernel, nar, wid),
        [((own, d), bf16, "v")] * nar,
        [(meta, "s"), (kinds, "s")]
        + [(p, "a") for p in front_pieces]
        + [(p, "a") for p in gate_pieces]
        + [(after(dfront, *branch_pieces[1:]), "v"), (dgate, "v")],
        [
            pltpu.VMEM((d, width), bf16),
            pltpu.VMEM((d, width), bf16),
            pltpu.VMEM((total, d), bf16),
            pltpu.SemaphoreType.DMA((wid,)),
            pltpu.SemaphoreType.DMA((wid,)),
        ],
        us=30.0,
    )
    pieces_b = over_wide(same_b, peer_b, dn_parts[0])
    dn_pieces, _ = sum_narrow(dn_parts, pieces_b[0])

    mixed_out = call(
        mixed_kernel,
        [((own, d), bf16, "v")],
        [(tokens, "v")] + [(p, "v") for p in after(tuple(branch_pieces), pieces_b[0])],
        us=2.0,
    )[0]
    gate_sum, grad_w_out = call(
        functools.partial(total_a_kernel, er, ep),
        [((in_rows, width), bf16, "v"), ((MODS, er, d), f32, "v")],
        [(after(blocks_a, mixed_out), "v")],
        us=3.0,
    )
    res = call(
        functools.partial(total_b_kernel, nar, chips, er, rank, taps, ns),
        [((dr, 2 * width), bf16, "v")] * nar
        + [
            ((MODS, er, xw), f32, "v"),
            ((MODS, rank, er), f32, "v"),
            ((MODS, er), f32, "v"),
            ((taps, er), f32, "v"),
            ((1, er), f32, "v"),
            ((ns, er), f32, "v"),
            ((1, er), f32, "v"),
        ],
        [(meta, "s")] + [(p, "v") for p in pieces_b] + [(gate_sum, "v")],
        [pltpu.VMEM((nar, dr, 2 * width), bf16)],
        us=3.0,
    )
    back_parts = res[:nar]
    grad_w_x, grad_w_dt, grad_dt_bias, grad_conv_w, grad_conv_b, grad_log, grad_skip = res[nar:]
    back_pieces = scatter_narrow(back_parts)
    grad_tokens = call(
        tokens_kernel,
        [((own, d), bf16, "v")],
        [(tokens, "v"), (cotangent, "v"), (gain_full, "v")]
        + [(p, "v") for p in after(tuple(dn_pieces), back_parts[0])],
        us=3.0,
    )[0]
    grad_w_in, grad_gain = call(
        functools.partial(w_in_kernel, nar, wid, er, ep),
        [((MODS, dr, 2 * inner), f32, "v"), ((dr, 1), f32, "v")],
        [(meta, "s")]
        + [(p, "v") for p in back_pieces]
        + [(w_in_m, "v"), (gain_col, "v")],
        [pltpu.VMEM((nar, dr, 2 * width), f32)],
        us=4.0,
    )
    grad_w_in, grad_w_out = grad_w_in.transpose(1, 0, 2), grad_w_out.transpose(1, 0, 2)
    grad_w_x, grad_w_dt = grad_w_x.transpose(1, 0, 2), grad_w_dt.transpose(1, 0, 2)
    grad_log = grad_log.T
    return (
        mixed_out,
        grad_tokens,
        grad_gain[:, 0],
        grad_w_in,
        grad_conv_w,
        grad_conv_b[0],
        grad_w_x,
        grad_w_dt,
        grad_dt_bias,
        grad_log,
        grad_skip[0],
        grad_w_out,
    )


def solution(mesh):
    both = ("wide", "narrow")
    return jax.shard_map(
        body,
        mesh=mesh,
        in_specs=(
            P(both, None),
            P(both),
            P(both, None, None),
            P(None, both),
            P(both),
            P(both, None, None),
            P(None, None, both),
            P(None, both),
            P(both, None),
            P(both),
            P(both, None, None),
            P(both),
            P("wide"),
            P(both, None),
        ),
        out_specs=(
            P(both, None),
            P(both, None),
            P(both),
            P(both, None, None),
            P(None, both),
            P(both),
            P(both, None, None),
            P(None, None, both),
            P(None, both),
            P(both, None),
            P(both),
            P(both, None, None),
        ),
        check_vma=False,
    )
```

time: 355 us -> 254 us (0.72); the launches traced: 350 us -> 254 us
  waiting for transfers between devices: 120 us -> 64.9 us
  local copies, waits for them, and re-layouts: 38.1 us -> 7.28 us
  starting transfers between devices: 63.8 us -> 47.2 us
  Pallas kernels: 120 us -> 126 us
    ppermute x43 -> x41, waiting for transfers between devices: 119 us -> 64.9 us  [swap(): return lax.ppermute(block, axis, [(i, i ^ flip) for i in range(count)])]
    slice x19 -> x1, local copies, waits for them, and re-layouts: 12.4 us -> 0.12 us  [body(): run_kinds = mod_ids.reshape(rpd, RUN)[:, :1].astype(bf16)]
    reshape x13 -> x0, local copies, waits for them, and re-layouts: 11.7 us -> none  [the longest x4 3.54 us: channels(): part = part.reshape(nar, dr, MODS, wid, ep)[..., :er]]
    ppermute x43 -> x41, starting transfers between devices: 54 us -> 43.4 us  [swap(): return lax.ppermute(block, axis, [(i, i ^ flip) for i in range(count)])]
    all_to_all x2 -> x1, starting transfers between devices: 9.78 us -> 3.85 us  [body(): blocks_a = lax.all_to_all(blocks_a, 'wide', 0, 0)]
    pallas_call x11 -> x16, Pallas kernels: 120 us -> 126 us  [call(): pl.pallas_call(kernel, out_shape=[jax.ShapeDtypeStruct(shape, dtype) for...]
    unnamed x100 -> x60, local copies, waits for them, and re-layouts: 11.4 us -> 6.47 us
  transfers between devices with their start and end apart: 45 -> 42, of which waited for: 16 -> 16; matrix products, arithmetic and copies ran while one was open for 6% -> 2% of each run, Pallas kernels for 15% -> 28%
where the time goes in v2:
time: 254 us
  Pallas kernels  126 us (50%)
  waiting for transfers between devices  64.9 us (26%)
  starting transfers between devices  47.2 us (19%)
  local copies, waits for them, and re-layouts  7.28 us (3%)
  other arithmetic  6.59 us (3%)
    pallas_call x16, Pallas kernels, call(): pl.pallas_call(kernel, out_shape=[jax.ShapeDtypeStruct(shape, dtype) for...  126 us
    ppermute x41, waiting for transfers between devices, swap(): return lax.ppermute(block, axis, [(i, i ^ flip) for i in range(count)])  64.9 us
    ppermute x41, starting transfers between devices, swap(): return lax.ppermute(block, axis, [(i, i ^ flip) for i in range(count)])  43.4 us
    unnamed x60, local copies, waits for them, and re-layouts  6.47 us
  transfers between devices with their start and end apart: 42, of which 16 were waited for; matrix products, arithmetic and copies ran while one was open for 2% of the time, Pallas kernels for 28%

profile of v2, /device:TPU:0, one launch (start us, length us, event | category | flops | bytes accessed | tf_op | source)
XLA Modules:
  0.0 253.6 jit_solution(10699965541186545464)
XLA Ops:
  3.3 2.4 shard_map.229
  5.7 3.1 %collective-permute-start.3 = (bf16[24,2432]{1,0:T(8,128)(2,1)}, bf16[24,2432]{1,0:T(8,128)(2,1)S(1)}, u32[]{:S(2)}, u32[]{:S(2)}) collective-permute-start(bf16[24,2432]{1,0:T(8,128)(2,1)} %get-tuple-element.101), channel_id=1, source_target_pairs={{0,1},{1,0},{2,3},{3,2},{4,5},{5,4},{6,7},{7,6},{8,9},{9,8},{10,11... | collective-permute-start | bytes 350216 | tf_op jit(solution)/shard_map/ppermute | solution.py:26
  8.8 2.6 %collective-permute-start.4 = (bf16[24,2432]{1,0:T(8,128)(2,1)}, bf16[24,2432]{1,0:T(8,128)(2,1)S(1)}, u32[]{:S(2)}, u32[]{:S(2)}) collective-permute-start(bf16[24,2432]{1,0:T(8,128)(2,1)} %get-tuple-element.102), channel_id=1, source_target_pairs={{0,2},{1,3},{2,0},{3,1},{4,6},{5,7},{6,4},{7,5},{8,10},{9,11},{10,... | collective-permute-start | bytes 350216 | tf_op jit(solution)/shard_map/ppermute | solution.py:26
  13.6 2.5 collective-permute-start
  16.1 13.7 %collective-permute-done.4.refs_2_ = bf16[24,2432]{1,0:T(8,128)(2,1)S(1)} collective-permute-done((bf16[24,2432]{1,0:T(8,128)(2,1)}, bf16[24,2432]{1,0:T(8,128)(2,1)S(1)}, u32[]{:S(2)}, u32[]{:S(2)}) %collective-permute-start.4) | collective-permute-done | bytes 116768 | tf_op jit(solution)/shard_map/ppermute | solution.py:26
  30.5 2.7 %shard_map.230 = (bf16[128,1280]{1,0:T(8,128)(2,1)}, bf16[192,1152]{1,0:T(8,128)(2,1)}) custom-call(s32[3]{0:T(128)} %pad_add_fusion.meta, bf16[24,2432]{1,0:T(8,128)(2,1)} %get-tuple-element.100.refs_0_, bf16[24,2432]{1,0:T(8,128)(2,1)} %copy-done.23, bf16[24,2432]{1,0:T(8,128)(2,1)} %copy-done.24, bf16[24,2432]{1,0:T(8,128)(2,1)} %copy-done.25, ...), custom_call_target="tpu_custom_call" | custom-call | flops 2200000000 | bytes 1 | tf_op jit(solution)/shard_map/pallas_call | solution.py:96
  36.7 3.3 %collective-permute-done.1.refs_2_ = bf16[272,768]{1,0:T(8,128)(2,1)S(1)} collective-permute-done((bf16[272,768]{1,0:T(8,128)(2,1)S(1)}, bf16[272,768]{1,0:T(8,128)(2,1)S(1)}, u32[]{:S(2)}, u32[]{:S(2)}) %collective-permute-start.1) | collective-permute-done | bytes 417824 | tf_op jit(solution)/shard_map/ppermute | solution.py:26
  40.1 3.9 %collective-permute-done.9.refs_8_.refs_4_ = bf16[128,1280]{1,0:T(8,128)(2,1)S(1)} collective-permute-done((bf16[128,1280]{1,0:T(8,128)(2,1)}, bf16[128,1280]{1,0:T(8,128)(2,1)S(1)}, u32[]{:S(2)}, u32[]{:S(2)}) %collective-permute-start.9) | collective-permute-done | bytes 327712 | tf_op jit(solution)/shard_map/ppermute | solution.py:26
  45.6 4.8 %collective-permute-done.2.refs_3_ = bf16[272,768]{1,0:T(8,128)(2,1)S(1)} collective-permute-done((bf16[272,768]{1,0:T(8,128)(2,1)S(1)}, bf16[272,768]{1,0:T(8,128)(2,1)S(1)}, u32[]{:S(2)}, u32[]{:S(2)}) %collective-permute-start.2) | collective-permute-done | bytes 417824 | tf_op jit(solution)/shard_map/ppermute | solution.py:26
  50.4 2.4 collective-permute-start.18
  53.9 2.7 %collective-permute-start.21 = (bf16[256,768]{1,0:T(8,128)(2,1)S(1)}, bf16[256,768]{1,0:T(8,128)(2,1)}, u32[]{:S(2)}, u32[]{:S(2)}) collective-permute-start(bf16[256,768]{1,0:T(8,128)(2,1)S(1)} %copy-done.16), channel_id=1, source_target_pairs={{0,2},{1,3},{2,0},{3,1},{4,6},{5,7},{6,4},{7,5},{8,10},{9,11},{10,... | collective-permute-start | bytes 1179656 | tf_op jit(solution)/shard_map/ppermute | solution.py:26
  57.8 11.2 %shard_map.231 = (bf16[1024,768]{1,0:T(8,128)(2,1)}, f32[1032,384]{1,0:T(8,128)}, f32[1024,384]{1,0:T(8,128)}, bf16[1024,384]{1,0:T(8,128)(2,1)}, bf16[80,1024]{...) custom-call(s32[3]{0:T(128)} %pad_add_fusion.meta, ...), custom_call_target="tpu_custom_call" | custom-call | flops 9900000256 | bytes 1 | tf_op jit(solution)/shard_map/pallas_call | solution.py:96
  71.4 2.7 %collective-permute-done.21.refs_2_ = bf16[256,768]{1,0:T(8,128)(2,1)} collective-permute-done((bf16[256,768]{1,0:T(8,128)(2,1)S(1)}, bf16[256,768]{1,0:T(8,128)(2,1)}, u32[]{:S(2)}, u32[]{:S(2)}) %collective-permute-start.21) | collective-permute-done | bytes 393248 | tf_op jit(solution)/shard_map/ppermute | solution.py:26
  78.0 7.1 %shard_map.232 = (f32[1024,384]{1,0:T(8,128)}, f32[1024,384]{1,0:T(8,128)}) custom-call(s32[3]{0:T(128)} %pad_add_fusion.meta, s32[8]{0:T(128)} %get-tuple-element.107.kinds, bf16[192,1152]{1,0:T(8,128)(2,1)} %get-tuple-element.111.refs_0_.refs_4_.refs_8_, bf16[192,1152]{1,0:T(8,128)(2,1)} %copy-done.5, bf16[192,1152]{1,0:T(8,128)(2,1)} %copy-done.4, ...), custom_call_target="tpu_custom_call" | custom-call | flops 110000000 | bytes 1 | tf_op jit(solution)/shard_map/pallas_call | solution.py:96
  87.5 5.1 %collective-permute-done.23 = bf16[80,1024]{1,0:T(8,128)(2,1)S(1)} collective-permute-done((bf16[80,1024]{1,0:T(8,128)(2,1)S(1)}, bf16[80,1024]{1,0:T(8,128)(2,1)S(1)}, u32[]{:S(2)}, u32[]{:S(2)}) %collective-permute-start.23) | collective-permute-done | bytes 163872 | tf_op jit(solution)/shard_map/ppermute | solution.py:26
  93.3 6.6 %collective-permute-done.24.refs_3_ = bf16[256,768]{1,0:T(8,128)(2,1)S(1)} collective-permute-done((bf16[256,768]{1,0:T(8,128)(2,1)}, bf16[256,768]{1,0:T(8,128)(2,1)S(1)}, u32[]{:S(2)}, u32[]{:S(2)}) %collective-permute-start.24) | collective-permute-done | bytes 393248 | tf_op jit(solution)/shard_map/ppermute | solution.py:26
  100.6 9.0 %shard_map.233 = (bf16[1024,768]{1,0:T(8,128)(2,1)}, bf16[384,2304]{1,0:T(8,128)(2,1)}, f32[1024,384]{1,0:T(8,128)}, f32[1024,384]{1,0:T(8,128)}) custom-call(s32[3]{0:T(128)} %pad_add_fusion.meta, s32[8]{0:T(128)} %get-tuple-element.107.kinds, bf16[256,768]{1,0:T(8,128)(2,1)} %cot_r.1, bf16[256,768]{1,0:T(8,128)(2,1)} %collective-permute-done.20.refs_1_, ...), custom_call_target="tpu_custom_call" | custom-call | flops 7699999744 | bytes 1 | tf_op jit(solution)/shard_map/pallas_call | solution.py:96
  109.7 39.2 %shard_map.234 = (f32[1024,384]{1,0:T(8,128)}, bf16[80,1024]{1,0:T(8,128)(2,1)}, f32[1024,384]{1,0:T(8,128)}, bf16[1024,384]{1,0:T(8,128)(2,1)}, bf16[48,1024]{1...) custom-call(s32[3]{0:T(128)} %pad_add_fusion.meta, s32[8]{0:T(128)} %get-tuple-element.107.kinds, ...), custom_call_target="tpu_custom_call" | custom-call | flops 44000002048 | bytes 1 | tf_op jit(solution)/shard_map/pallas_call | solution.py:96
  153.2 6.1 %shard_map.235 = (bf16[256,768]{1,0:T(8,128)(2,1)}, bf16[256,768]{1,0:T(8,128)(2,1)}, bf16[256,768]{1,0:T(8,128)(2,1)}, bf16[256,768]{1,0:T(8,128)(2,1)}, bf16[1024,384]{1,0:T(8,128)(2,1)}) custom-call(s32[3]{0:T(128)} %pad_add_fusion.meta, s32[8]{0:T(128)} %get-tuple-element.107.kinds, f32[1024,384]{1,0:T(8,128)} %get-tuple-element.126.ssm_r.refs_0_, ...), custom_call_target="tpu_custom_call" | custom-call | flops 5500000256 | bytes 1 | tf_op jit(solution)/shard_map/pallas_call | solution.py:96
  161.4 10.0 %shard_map.236 = (bf16[1024,384]{1,0:T(8,128)(2,1)}, f32[176,384]{1,0:T(8,128)}, bf16[8,192,1152]{2,1,0:T(8,128)(2,1)}) custom-call(s32[3]{0:T(128)} %pad_add_fusion.meta, s32[8]{0:T(128)} %get-tuple-element.107.kinds, f32[1024,384]{1,0:T(8,128)} %get-tuple-element.126.ssm_r.refs_0_, bf16[1024,384]{1,0:T(8,128)(2,1)} %get-tuple-element.141.refs_1_, ...), custom_call_target="tpu_custom_call" | custom-call | flops 9900000256 | bytes 1 | tf_op jit(solution)/shard_map/pallas_call | solution.py:96
  171.4 3.8 %all-to-all-start = ((bf16[8,192,1152]{2,1,0:T(8,128)(2,1)}), bf16[8,192,1152]{2,1,0:T(8,128)(2,1)S(1)}, u32[]{:S(2)}, u32[]{:S(2)}) async-start(bf16[8,192,1152]{2,1,0:T(8,128)(2,1)} %get-tuple-element.168), calls=%async_computation | async-start | bytes 7077888 | tf_op jit(solution)/shard_map/all_to_all | solution.py:947
  177.7 2.8 %collective-permute-done.27.refs_2_ = bf16[256,768]{1,0:T(8,128)(2,1)} collective-permute-done((bf16[256,768]{1,0:T(8,128)(2,1)}, bf16[256,768]{1,0:T(8,128)(2,1)}, u32[]{:S(2)}, u32[]{:S(2)}) %collective-permute-start.27) | collective-permute-done | bytes 393248 | tf_op jit(solution)/shard_map/ppermute | solution.py:26
  180.4 12.7 %shard_map.237 = (bf16[1024,384]{1,0:T(8,128)(2,1)}, bf16[4,144,1152]{2,1,0:T(8,128)(2,1)}, bf16[4,144,1152]{2,1,0:T(8,128)(2,1)}) custom-call(s32[3]{0:T(128)} %pad_add_fusion.meta, s32[8]{0:T(128)} %get-tuple-element.107.kinds, bf16[80,1024]{1,0:T(8,128)(2,1)} %get-tuple-element.133.refs_0_, bf16[80,1024]{1,0:T(8,128)(2,1)} %collective-permute-done.28.refs_1_, ...), custom_call_target="tpu_custom_call" | custom-call | flops 13200000000 | bytes 1 | tf_op jit(solution)/shard_map/pallas_call | solution.py:96
  193.1 3.6 %collective-permute-done.26.refs_1_ = bf16[256,768]{1,0:T(8,128)(2,1)} collective-permute-done((bf16[256,768]{1,0:T(8,128)(2,1)S(1)}, bf16[256,768]{1,0:T(8,128)(2,1)}, u32[]{:S(2)}, u32[]{:S(2)}) %collective-permute-start.26) | collective-permute-done | bytes 393248 | tf_op jit(solution)/shard_map/ppermute | solution.py:26
  196.8 8.9 %shard_map.238 = (bf16[256,768]{1,0:T(8,128)(2,1)}, bf16[256,768]{1,0:T(8,128)(2,1)}, bf16[256,768]{1,0:T(8,128)(2,1)}, bf16[256,768]{1,0:T(8,128)(2,1)}) custom-call(s32[3]{0:T(128)} %pad_add_fusion.meta, s32[8]{0:T(128)} %get-tuple-element.107.kinds, bf16[128,1280]{1,0:T(8,128)(2,1)} %get-tuple-element.106.refs_4_.refs_0_, ...), custom_call_target="tpu_custom_call" | custom-call | flops 32999999488 | bytes 1 | tf_op jit(solution)/shard_map/pallas_call | solution.py:96
  207.7 2.9 %shard_map.239 = (bf16[144,1152]{1,0:T(8,128)(2,1)}, bf16[144,1152]{1,0:T(8,128)(2,1)}, bf16[144,1152]{1,0:T(8,128)(2,1)}, bf16[144,1152]{1,0:T(8,128)(2,1)}) custom-call(s32[3]{0:T(128)} %pad_add_fusion.meta, bf16[4,144,1152]{2,1,0:T(8,128)(2,1)} %get-tuple-element.154.same, bf16[4,144,1152]{2,1,0:T(8,128)(2,1)} %collective-permute-done.31.peer), custom_call_target="tpu_custom_call" | custom-call | flops 3300000000 | bytes 1 | tf_op jit(solution)/shard_map/pallas_call | solution.py:96
  214.1 3.9 %collective-permute-done.32 = bf16[256,768]{1,0:T(8,128)(2,1)} collective-permute-done((bf16[256,768]{1,0:T(8,128)(2,1)}, bf16[256,768]{1,0:T(8,128)(2,1)}, u32[]{:S(2)}, u32[]{:S(2)}) %collective-permute-start.32) | collective-permute-done | bytes 393248 | tf_op jit(solution)/shard_map/ppermute | solution.py:26
  224.6 3.2 %shard_map.241 = (bf16[96,1152]{1,0:T(8,128)(2,1)}, f32[3,48,768]{2,1,0:T(8,128)}) custom-call(bf16[8,192,1152]{2,1,0:T(8,128)(2,1)} %copy-done), custom_call_target="tpu_custom_call" | custom-call | flops 3300000000 | bytes 1 | tf_op jit(solution)/shard_map/pallas_call | solution.py:96
  227.8 3.7 %collective-permute-done.37.refs_3_ = bf16[144,1152]{1,0:T(8,128)(2,1)} collective-permute-done((bf16[144,1152]{1,0:T(8,128)(2,1)}, bf16[144,1152]{1,0:T(8,128)(2,1)}, u32[]{:S(2)}, u32[]{:S(2)}) %collective-permute-start.37) | collective-permute-done | bytes 331808 | tf_op jit(solution)/shard_map/ppermute | solution.py:26
  238.3 6.6 %collective-permute-done.33.refs_1_ = bf16[256,768]{1,0:T(8,128)(2,1)} collective-permute-done((bf16[256,768]{1,0:T(8,128)(2,1)}, bf16[256,768]{1,0:T(8,128)(2,1)}, u32[]{:S(2)}, u32[]{:S(2)}) %collective-permute-start.33) | collective-permute-done | bytes 393248 | tf_op jit(solution)/shard_map/ppermute | solution.py:26
  244.9 2.7 %shard_map.243 = bf16[256,768]{1,0:T(8,128)(2,1)} custom-call(bf16[256,768]{1,0:T(8,128)(2,1)} %x_r.3, bf16[256,768]{1,0:T(8,128)(2,1)} %cot_r.1, f32[1,768]{1,0:T(1,128)} %get-tuple-element.160.gain_r, bf16[256,768]{1,0:T(8,128)(2,1)} %get-tuple-element.172.refs_0_, bf16[256,768]{1,0:T(8,128)(2,1)} %collective-permute-done.33.refs_1_, ...), custom_call_target="tpu_custom_call" | custom-call | flops 3300000000 | bytes 1 | tf_op jit(solution)/shard_map/pallas_call | solution.py:96
  249.0 3.3 %shard_map.244 = (f32[3,24,3072]{2,1,0:T(8,128)}, f32[24,1]{1,0:T(8,128)}) custom-call(s32[3]{0:T(128)} %pad_add_fusion.meta, bf16[24,2304]{1,0:T(8,128)(2,1)} %get-tuple-element.171.refs_0_, bf16[24,2304]{1,0:T(8,128)(2,1)} %copy-done.26, bf16[24,2304]{1,0:T(8,128)(2,1)} %copy-done.27, bf16[24,2304]{1,0:T(8,128)(2,1)} %copy-done.28, ...), custom_call_target="tpu_custom_call" | custom-call | flops 4400000000 | bytes 1 | tf_op jit(solution)/shard_map/pallas_call | solution.py:96
  (140 shorter events, 52.7 us)
Async XLA Ops:
  5.7 10.4 %collective-permute-start.3 = (bf16[24,2432]{1,0:T(8,128)(2,1)}, bf16[24,2432]{1,0:T(8,128)(2,1)S(1)}, u32[]{:S(2)}, u32[]{:S(2)}) collective-permute-start(bf16[24,2432]{1,0:T(8,128)(2,1)} %get-tuple-element.101), channel_id=1, source_target_pairs={{0,1},{1,0},{2,3},{3,2},{4,5},{5,4},{6,7},{7,6},{8,9},{9,8},{10,11... | collective-permute-start | bytes 350216 | tf_op jit(solution)/shard_map/ppermute | solution.py:26
  8.8 21.1 %collective-permute-start.4 = (bf16[24,2432]{1,0:T(8,128)(2,1)}, bf16[24,2432]{1,0:T(8,128)(2,1)S(1)}, u32[]{:S(2)}, u32[]{:S(2)}) collective-permute-start(bf16[24,2432]{1,0:T(8,128)(2,1)} %get-tuple-element.102), channel_id=1, source_target_pairs={{0,2},{1,3},{2,0},{3,1},{4,6},{5,7},{6,4},{7,5},{8,10},{9,11},{10,... | collective-permute-start | bytes 350216 | tf_op jit(solution)/shard_map/ppermute | solution.py:26
  11.4 18.5 %collective-permute-start.5 = (bf16[24,2432]{1,0:T(8,128)(2,1)}, bf16[24,2432]{1,0:T(8,128)(2,1)S(1)}, u32[]{:S(2)}, u32[]{:S(2)}) collective-permute-start(bf16[24,2432]{1,0:T(8,128)(2,1)} %get-tuple-element.103), channel_id=1, source_target_pairs={{0,3},{1,2},{2,1},{3,0},{4,7},{5,6},{6,5},{7,4},{8,11},{9,10},{10,... | collective-permute-start | bytes 350216 | tf_op jit(solution)/shard_map/ppermute | solution.py:26
  11.7 28.3 %collective-permute-start.1 = (bf16[272,768]{1,0:T(8,128)(2,1)S(1)}, bf16[272,768]{1,0:T(8,128)(2,1)S(1)}, u32[]{:S(2)}, u32[]{:S(2)}) collective-permute-start(bf16[272,768]{1,0:T(8,128)(2,1)S(1)} %pad_maximum_fusion.refs_0_), channel_id=1, source_target_pairs={{0,2},{1,3},{2,0},{3,1},{4,6},{5,7},{6,4},{7,5},{8,10},{9,11},{10,... | collective-permute-start | bytes 1253384 | tf_op jit(solution)/shard_map/ppermute | solution.py:26
  13.6 26.4 %collective-permute-start = (bf16[272,768]{1,0:T(8,128)(2,1)S(1)}, bf16[272,768]{1,0:T(8,128)(2,1)S(1)}, u32[]{:S(2)}, u32[]{:S(2)}) collective-permute-start(bf16[272,768]{1,0:T(8,128)(2,1)S(1)} %pad_maximum_fusion.refs_0_), channel_id=1, source_target_pairs={{0,1},{1,0},{2,3},{3,2},{4,5},{5,4},{6,7},{7,6},{8,9},{9,8},{10,11... | collective-permute-start | bytes 1253384 | tf_op jit(solution)/shard_map/ppermute | solution.py:26
  33.2 10.8 %collective-permute-start.9 = (bf16[128,1280]{1,0:T(8,128)(2,1)}, bf16[128,1280]{1,0:T(8,128)(2,1)S(1)}, u32[]{:S(2)}, u32[]{:S(2)}) collective-permute-start(bf16[128,1280]{1,0:T(8,128)(2,1)} %get-tuple-element.106.refs_4_.refs_0_), channel_id=1, source_target_pairs={{0,16},{4,20},{8,24},{12,28},{16,0},{20,4},{24,8},{28,12},{1,17},{... | collective-permute-start | bytes 983048 | tf_op jit(solution)/shard_map/ppermute | solution.py:26
  40.0 10.4 %collective-permute-start.2 = (bf16[272,768]{1,0:T(8,128)(2,1)S(1)}, bf16[272,768]{1,0:T(8,128)(2,1)S(1)}, u32[]{:S(2)}, u32[]{:S(2)}) collective-permute-start(bf16[272,768]{1,0:T(8,128)(2,1)S(1)} %collective-permute-done.1.refs_2_), channel_id=1, source_target_pairs={{0,1},{1,0},{2,3},{3,2},{4,5},{5,4},{6,7},{7,6},{8,9},{9,8},{10,11... | collective-permute-start | bytes 1253384 | tf_op jit(solution)/shard_map/ppermute | solution.py:26
  40.0 12.8 %collective-permute-start.6 = (bf16[128,1280]{1,0:T(8,128)(2,1)}, bf16[128,1280]{1,0:T(8,128)(2,1)}, u32[]{:S(2)}, u32[]{:S(2)}) collective-permute-start(bf16[128,1280]{1,0:T(8,128)(2,1)} %get-tuple-element.106.refs_4_.refs_0_), channel_id=1, source_target_pairs={{0,4},{4,0},{8,12},{12,8},{16,20},{20,16},{24,28},{28,24},{1,5},{5... | collective-permute-start | bytes 983048 | tf_op jit(solution)/shard_map/ppermute | solution.py:26
  45.6 11.0 %collective-permute-start.8 = (bf16[128,1280]{1,0:T(8,128)(2,1)S(1)}, bf16[128,1280]{1,0:T(8,128)(2,1)S(1)}, u32[]{:S(2)}, u32[]{:S(2)}) collective-permute-start(bf16[128,1280]{1,0:T(8,128)(2,1)S(1)} %collective-permute-done.7.refs_6_.refs_2_), channel_id=1, source_target_pairs={{0,4},{4,0},{8,12},{12,8},{16,20},{20,16},{24,28},{28,24},{1,5},{5... | collective-permute-start | bytes 983048 | tf_op jit(solution)/shard_map/ppermute | solution.py:26
  50.4 18.7 %collective-permute-start.18 = (bf16[192,1152]{1,0:T(8,128)(2,1)}, bf16[192,1152]{1,0:T(8,128)(2,1)S(1)}, u32[]{:S(2)}, u32[]{:S(2)}) collective-permute-start(bf16[192,1152]{1,0:T(8,128)(2,1)} %get-tuple-element.111.refs_0_.refs_4_.refs_8_), channel_id=1, source_target_pairs={{0,24},{4,28},{8,16},{12,20},{16,8},{20,12},{24,0},{28,4},{1,25},{... | collective-permute-start | bytes 1327112 | tf_op jit(solution)/shard_map/ppermute | solution.py:26
  52.8 18.1 %collective-permute-start.16 = (bf16[192,1152]{1,0:T(8,128)(2,1)}, bf16[192,1152]{1,0:T(8,128)(2,1)S(1)}, u32[]{:S(2)}, u32[]{:S(2)}) collective-permute-start(bf16[192,1152]{1,0:T(8,128)(2,1)} %get-tuple-element.111.refs_0_.refs_4_.refs_8_), channel_id=1, source_target_pairs={{0,16},{4,20},{8,24},{12,28},{16,0},{20,4},{24,8},{28,12},{1,17},{... | collective-permute-start | bytes 1327112 | tf_op jit(solution)/shard_map/ppermute | solution.py:26
  53.3 17.7 %collective-permute-start.14 = (bf16[192,1152]{1,0:T(8,128)(2,1)}, bf16[192,1152]{1,0:T(8,128)(2,1)S(1)}, u32[]{:S(2)}, u32[]{:S(2)}) collective-permute-start(bf16[192,1152]{1,0:T(8,128)(2,1)} %get-tuple-element.111.refs_0_.refs_4_.refs_8_), channel_id=1, source_target_pairs={{0,8},{4,12},{8,0},{12,4},{16,24},{20,28},{24,16},{28,20},{1,9},{5... | collective-permute-start | bytes 1327112 | tf_op jit(solution)/shard_map/ppermute | solution.py:26
  53.9 20.2 %collective-permute-start.21 = (bf16[256,768]{1,0:T(8,128)(2,1)S(1)}, bf16[256,768]{1,0:T(8,128)(2,1)}, u32[]{:S(2)}, u32[]{:S(2)}) collective-permute-start(bf16[256,768]{1,0:T(8,128)(2,1)S(1)} %copy-done.16), channel_id=1, source_target_pairs={{0,2},{1,3},{2,0},{3,1},{4,6},{5,7},{6,4},{7,5},{8,10},{9,11},{10,... | collective-permute-start | bytes 1179656 | tf_op jit(solution)/shard_map/ppermute | solution.py:26
  57.4 17.8 %collective-permute-start.20 = (bf16[256,768]{1,0:T(8,128)(2,1)S(1)}, bf16[256,768]{1,0:T(8,128)(2,1)}, u32[]{:S(2)}, u32[]{:S(2)}) collective-permute-start(bf16[256,768]{1,0:T(8,128)(2,1)S(1)} %copy-done.16), channel_id=1, source_target_pairs={{0,1},{1,0},{2,3},{3,2},{4,5},{5,4},{6,7},{7,6},{8,9},{9,8},{10,11... | collective-permute-start | bytes 1179656 | tf_op jit(solution)/shard_map/ppermute | solution.py:26
  86.1 13.8 %collective-permute-start.24 = (bf16[256,768]{1,0:T(8,128)(2,1)}, bf16[256,768]{1,0:T(8,128)(2,1)S(1)}, u32[]{:S(2)}, u32[]{:S(2)}) collective-permute-start(bf16[256,768]{1,0:T(8,128)(2,1)} %collective-permute-done.21.refs_2_), channel_id=1, source_target_pairs={{0,1},{1,0},{2,3},{3,2},{4,5},{5,4},{6,7},{7,6},{8,9},{9,8},{10,11... | collective-permute-start | bytes 1179656 | tf_op jit(solution)/shard_map/ppermute | solution.py:26
  148.9 28.8 %collective-permute-start.28 = (bf16[80,1024]{1,0:T(8,128)(2,1)}, bf16[80,1024]{1,0:T(8,128)(2,1)}, u32[]{:S(2)}, u32[]{:S(2)}) collective-permute-start(bf16[80,1024]{1,0:T(8,128)(2,1)} %get-tuple-element.133.refs_0_), channel_id=1, source_target_pairs={{0,1},{1,0},{2,3},{3,2},{4,5},{5,4},{6,7},{7,6},{8,9},{9,8},{10,11... | collective-permute-start | bytes 491528 | tf_op jit(solution)/shard_map/ppermute | solution.py:26
  149.7 27.9 %collective-permute-start.29 = (bf16[80,1024]{1,0:T(8,128)(2,1)}, bf16[80,1024]{1,0:T(8,128)(2,1)}, u32[]{:S(2)}, u32[]{:S(2)}) collective-permute-start(bf16[80,1024]{1,0:T(8,128)(2,1)} %get-tuple-element.133.refs_0_), channel_id=1, source_target_pairs={{0,2},{1,3},{2,0},{3,1},{4,6},{5,7},{6,4},{7,5},{8,10},{9,11},{10,... | collective-permute-start | bytes 491528 | tf_op jit(solution)/shard_map/ppermute | solution.py:26
  151.1 26.6 %collective-permute-start.30 = (bf16[80,1024]{1,0:T(8,128)(2,1)}, bf16[80,1024]{1,0:T(8,128)(2,1)}, u32[]{:S(2)}, u32[]{:S(2)}) collective-permute-start(bf16[80,1024]{1,0:T(8,128)(2,1)} %get-tuple-element.133.refs_0_), channel_id=1, source_target_pairs={{0,3},{1,2},{2,1},{3,0},{4,7},{5,6},{6,5},{7,4},{8,11},{9,10},{10,... | collective-permute-start | bytes 491528 | tf_op jit(solution)/shard_map/ppermute | solution.py:26
  159.4 15.9 %collective-permute-start.25 = (bf16[256,768]{1,0:T(8,128)(2,1)}, bf16[256,768]{1,0:T(8,128)(2,1)}, u32[]{:S(2)}, u32[]{:S(2)}) collective-permute-start(bf16[256,768]{1,0:T(8,128)(2,1)} %get-tuple-element.130), channel_id=1, source_target_pairs={{0,1},{1,0},{2,3},{3,2},{4,5},{5,4},{6,7},{7,6},{8,9},{9,8},{10,11... | collective-permute-start | bytes 1179656 | tf_op jit(solution)/shard_map/ppermute | solution.py:26
  159.4 21.1 %collective-permute-start.27 = (bf16[256,768]{1,0:T(8,128)(2,1)}, bf16[256,768]{1,0:T(8,128)(2,1)}, u32[]{:S(2)}, u32[]{:S(2)}) collective-permute-start(bf16[256,768]{1,0:T(8,128)(2,1)} %get-tuple-element.131), channel_id=1, source_target_pairs={{0,1},{1,0},{2,3},{3,2},{4,5},{5,4},{6,7},{7,6},{8,9},{9,8},{10,11... | collective-permute-start | bytes 1179656 | tf_op jit(solution)/shard_map/ppermute | solution.py:26
  171.4 51.4 %all-to-all-start = ((bf16[8,192,1152]{2,1,0:T(8,128)(2,1)}), bf16[8,192,1152]{2,1,0:T(8,128)(2,1)S(1)}, u32[]{:S(2)}, u32[]{:S(2)}) async-start(bf16[8,192,1152]{2,1,0:T(8,128)(2,1)} %get-tuple-element.168), calls=%async_computation | async-start | bytes 7077888 | tf_op jit(solution)/shard_map/all_to_all | solution.py:947
  176.5 20.2 %collective-permute-start.26 = (bf16[256,768]{1,0:T(8,128)(2,1)S(1)}, bf16[256,768]{1,0:T(8,128)(2,1)}, u32[]{:S(2)}, u32[]{:S(2)}) collective-permute-start(bf16[256,768]{1,0:T(8,128)(2,1)S(1)} %add_convert_fusion.1), channel_id=1, source_target_pairs={{0,2},{1,3},{2,0},{3,1},{4,6},{5,7},{6,4},{7,5},{8,10},{9,11},{10,... | collective-permute-start | bytes 1179656 | tf_op jit(solution)/shard_map/ppermute | solution.py:26
  193.1 14.6 %collective-permute-start.31 = (bf16[4,144,1152]{2,1,0:T(8,128)(2,1)}, bf16[4,144,1152]{2,1,0:T(8,128)(2,1)}, u32[]{:S(2)}, u32[]{:S(2)}) collective-permute-start(bf16[4,144,1152]{2,1,0:T(8,128)(2,1)} %get-tuple-element.155), channel_id=1, source_target_pairs={{0,4},{4,0},{8,12},{12,8},{16,20},{20,16},{24,28},{28,24},{1,5},{5... | collective-permute-start | bytes 3981320 | tf_op jit(solution)/shard_map/ppermute | solution.py:26
  205.6 12.4 %collective-permute-start.32 = (bf16[256,768]{1,0:T(8,128)(2,1)}, bf16[256,768]{1,0:T(8,128)(2,1)}, u32[]{:S(2)}, u32[]{:S(2)}) collective-permute-start(bf16[256,768]{1,0:T(8,128)(2,1)} %get-tuple-element.163), channel_id=1, source_target_pairs={{0,1},{1,0},{2,3},{3,2},{4,5},{5,4},{6,7},{7,6},{8,9},{9,8},{10,11... | collective-permute-start | bytes 1179656 | tf_op jit(solution)/shard_map/ppermute | solution.py:26
  205.7 32.6 %collective-permute-start.34 = (bf16[256,768]{1,0:T(8,128)(2,1)}, bf16[256,768]{1,0:T(8,128)(2,1)}, u32[]{:S(2)}, u32[]{:S(2)}) collective-permute-start(bf16[256,768]{1,0:T(8,128)(2,1)} %get-tuple-element.164), channel_id=1, source_target_pairs={{0,1},{1,0},{2,3},{3,2},{4,5},{5,4},{6,7},{7,6},{8,9},{9,8},{10,11... | collective-permute-start | bytes 1179656 | tf_op jit(solution)/shard_map/ppermute | solution.py:26
  210.6 17.2 %collective-permute-start.35 = (bf16[144,1152]{1,0:T(8,128)(2,1)}, bf16[144,1152]{1,0:T(8,128)(2,1)}, u32[]{:S(2)}, u32[]{:S(2)}) collective-permute-start(bf16[144,1152]{1,0:T(8,128)(2,1)} %get-tuple-element.165), channel_id=1, source_target_pairs={{0,8},{4,12},{8,0},{12,4},{16,24},{20,28},{24,16},{28,20},{1,9},{5... | collective-permute-start | bytes 995336 | tf_op jit(solution)/shard_map/ppermute | solution.py:26
  212.3 15.5 %collective-permute-start.36 = (bf16[144,1152]{1,0:T(8,128)(2,1)}, bf16[144,1152]{1,0:T(8,128)(2,1)}, u32[]{:S(2)}, u32[]{:S(2)}) collective-permute-start(bf16[144,1152]{1,0:T(8,128)(2,1)} %get-tuple-element.166), channel_id=1, source_target_pairs={{0,16},{4,20},{8,24},{12,28},{16,0},{20,4},{24,8},{28,12},{1,17},{... | collective-permute-start | bytes 995336 | tf_op jit(solution)/shard_map/ppermute | solution.py:26
  213.8 17.7 %collective-permute-start.37 = (bf16[144,1152]{1,0:T(8,128)(2,1)}, bf16[144,1152]{1,0:T(8,128)(2,1)}, u32[]{:S(2)}, u32[]{:S(2)}) collective-permute-start(bf16[144,1152]{1,0:T(8,128)(2,1)} %get-tuple-element.167), channel_id=1, source_target_pairs={{0,24},{4,28},{8,16},{12,20},{16,8},{20,12},{24,0},{28,4},{1,25},{... | collective-permute-start | bytes 995336 | tf_op jit(solution)/shard_map/ppermute | solution.py:26
  219.8 25.1 %collective-permute-start.33 = (bf16[256,768]{1,0:T(8,128)(2,1)}, bf16[256,768]{1,0:T(8,128)(2,1)}, u32[]{:S(2)}, u32[]{:S(2)}) collective-permute-start(bf16[256,768]{1,0:T(8,128)(2,1)} %add_convert_fusion), channel_id=1, source_target_pairs={{0,2},{1,3},{2,0},{3,1},{4,6},{5,7},{6,4},{7,5},{8,10},{9,11},{10,... | collective-permute-start | bytes 1179656 | tf_op jit(solution)/shard_map/ppermute | solution.py:26
  233.8 13.8 %collective-permute-start.38 = (bf16[24,2304]{1,0:T(8,128)(2,1)}, bf16[24,2304]{1,0:T(8,128)(2,1)S(1)}, u32[]{:S(2)}, u32[]{:S(2)}) collective-permute-start(bf16[24,2304]{1,0:T(8,128)(2,1)} %get-tuple-element.175), channel_id=1, source_target_pairs={{0,1},{1,0},{2,3},{3,2},{4,5},{5,4},{6,7},{7,6},{8,9},{9,8},{10,11... | collective-permute-start | bytes 331784 | tf_op jit(solution)/shard_map/ppermute | solution.py:26
  233.9 13.7 %collective-permute-start.39 = (bf16[24,2304]{1,0:T(8,128)(2,1)}, bf16[24,2304]{1,0:T(8,128)(2,1)S(1)}, u32[]{:S(2)}, u32[]{:S(2)}) collective-permute-start(bf16[24,2304]{1,0:T(8,128)(2,1)} %get-tuple-element.176), channel_id=1, source_target_pairs={{0,2},{1,3},{2,0},{3,1},{4,6},{5,7},{6,4},{7,5},{8,10},{9,11},{10,... | collective-permute-start | bytes 331784 | tf_op jit(solution)/shard_map/ppermute | solution.py:26
  236.1 11.5 %collective-permute-start.40 = (bf16[24,2304]{1,0:T(8,128)(2,1)}, bf16[24,2304]{1,0:T(8,128)(2,1)S(1)}, u32[]{:S(2)}, u32[]{:S(2)}) collective-permute-start(bf16[24,2304]{1,0:T(8,128)(2,1)} %get-tuple-element.177), channel_id=1, source_target_pairs={{0,3},{1,2},{2,1},{3,0},{4,7},{5,6},{6,5},{7,4},{8,11},{9,10},{10,... | collective-permute-start | bytes 331784 | tf_op jit(solution)/shard_map/ppermute | solution.py:26
  (40 other events, 309.4 us)

commit v3 on v2

--- a/solution.py
+++ b/solution.py
@@ -10,6 +10,7 @@
 
 MODS = 3
 RUN = 128
+CHUNKS = 4
 LANES = 128
 EPSILON = 1e-05
 LOG2E = 1.4426950408889634
@@ -86,7 +87,7 @@
     return lax.dot_general(a, b, (((ca,), (cb,)), ((), ())), preferred_element_type=f32)
 
 
-def call(kernel, outs, ins, scratch=(), us=1.0):
+def call(kernel, outs, ins, scratch=(), us=1.0, aliases=None):
     spaces = {"v": pltpu.VMEM, "s": pltpu.SMEM, "a": pl.ANY}
     held = [(array.shape, array.dtype) for array, space in ins if space == "v"]
     held += [(shape, dtype) for shape, dtype, space in outs if space == "v"]
@@ -99,19 +100,64 @@
         in_specs=[pl.BlockSpec(memory_space=spaces[space]) for _, space in ins],
         out_specs=[pl.BlockSpec(memory_space=spaces[space]) for _, _, space in outs],
         scratch_shapes=list(scratch),
+        input_output_aliases=aliases or {},
         compiler_params=pltpu.CompilerParams(vmem_limit_bytes=need),
         cost_estimate=pl.CostEstimate(flops=int(us * 1.1e9), bytes_accessed=1, transcendentals=0),
     )(*[array for array, _ in ins])
 
 
 def place_pieces(pieces, target, sem, me, rows):
-    copies = []
-    for s, piece in enumerate(pieces):
-        at = pl.multiple_of((me ^ s) * rows, 16)
-        copy = pltpu.make_async_copy(piece, target.at[pl.ds(at, rows), :], sem.at[s])
+    return [
+        pltpu.make_async_copy(
+            piece.at[pl.ds(0, rows), pl.ds(0, target.shape[1])],
+            target.at[pl.ds(pl.multiple_of((me ^ s) * rows, 16), rows), :],
+            sem.at[s],
+        )
+        for s, piece in enumerate(pieces)
+    ]
+
+
+def place_w_out(pieces, target, sem, me):
+    wid, width = len(pieces), pieces[0].shape[1]
+    ep, blocks = target.shape[0] // len(pieces), target.shape[1] // pieces[0].shape[1]
+    first = pieces[0].shape[0] - blocks * ep
+    return [
+        pltpu.make_async_copy(
+            pieces[s].at[pl.ds(first + k * ep, ep), :],
+            target.at[pl.ds(pl.multiple_of((me ^ s) * ep, 16), ep), pl.ds(k * width, width)],
+            sem.at[k, s],
+        )
+        for s in range(wid)
+        for k in range(blocks)
+    ]
+
+
+def move_rows(pairs, sem, slot, first, rows):
+    at = pl.multiple_of(first, 16)
+    return [
+        pltpu.make_async_copy(
+            pair[0].at[pl.ds(at, rows), :],
+            pair[1].at[pl.ds(pl.multiple_of(first + (pair[2] if len(pair) > 2 else 0), 16), rows), :],
+            sem.at[k, slot],
+        )
+        for k, pair in enumerate(pairs)
+    ]
+
+
+def each(first, count, step, carry=0):
+    for k in range(count):
+        carry = step(first + k, carry)
+    return carry
+
+
+def begin(copies):
+    for copy in copies:
         copy.start()
-        copies.append(copy)
-    return copies
+
+
+def finish(copies):
+    for copy in copies:
+        copy.wait()
 
 
 def split_kernel(
@@ -122,7 +168,9 @@
     inner = wid * nar * er
     es = wid * ep
     dr = w_r.shape[1]
-    gain = jnp.broadcast_to(gain_r[...], (dr, LANES)).astype(bf16)
+    gain = gain_r[...].astype(f32)
+    gain = jnp.concatenate([gain, jnp.zeros((1, LANES - dr), f32)], axis=1)
+    gain = jnp.broadcast_to(gain, (LANES, LANES)).T[:dr].astype(bf16)
     for half in range(2):
         first = half * (MODS * es + LANES)
         for m in range(MODS):
@@ -187,8 +235,10 @@
 
 def in_kernel(nar, wid, rpd, taps, ep, rank, meta, *refs):
     toks, w_pieces = refs[:nar], refs[nar : nar + wid]
-    normed_o, front_o, csum_o, mixed_o, px_o, kinds_o, w_x, w_dt_o, table_o, gain_o = refs[nar + wid : nar + wid + 10]
-    xs, wf, rest, tok_sem, w_sem, rest_sem = refs[nar + wid + 10 :]
+    hbm_os = refs[nar + wid : nar + wid + 4]
+    px_o, kinds_o, w_x, w_dt_o, table_o, gain_o = refs[nar + wid + 4 : nar + wid + 10]
+    normed_o, front_o, csum_o, mixed_o, xs, wf, rest, tok_sem, w_sem, rest_sem, out_sem = refs[nar + wid + 10 :]
+    outs = list(zip((normed_o, front_o, csum_o, mixed_o), hbm_os))
     n, w, split = meta[0], meta[1], meta[2]
     total, es = csum_o.shape
     width = MODS * es
@@ -241,7 +291,6 @@
         copy.wait()
     gain = wf[:, width : width + LANES].astype(f32).T[0:1, :]
     gain_o[...] = gain
-    front_o[0:8, :] = jnp.zeros((8, es), f32)
 
     def one_run(r, before):
         rows = pl.ds(pl.multiple_of(r * RUN, RUN), RUN)
@@ -252,7 +301,7 @@
         normed = (x * scale * gain).astype(bf16)
         normed_o[rows, :] = normed
         front = dot(normed, wf[:, pl.ds(pl.multiple_of(kind * es, LANES), es)], 1, 0)
-        front_o[pl.ds(pl.multiple_of(r * RUN + 8, 8), RUN), :] = front
+        front_o[rows, :] = front
         ext = jnp.concatenate([before, front], axis=0)
         place = r * RUN + lax.broadcasted_iota(jnp.int32, (RUN, 1), 0)
         offset = place - jnp.where(place >= split, split, 0)
@@ -268,22 +317,28 @@
         px_o[:, pl.ds(pl.multiple_of(r * RUN, LANES), RUN)] = px.T[: px_o.shape[0]].astype(bf16)
         return front[RUN - 8 :]
 
-    lax.fori_loop(0, total // RUN, one_run, jnp.zeros((8, es), f32))
+    before = jnp.zeros((8, es), f32)
+    size = total // CHUNKS
+    for c in range(CHUNKS):
+        before = each(c * size // RUN, size // RUN, one_run, before)
+        begin(move_rows(outs, out_sem, c, c * size, size))
+    for c in range(CHUNKS):
+        finish(move_rows(outs, out_sem, c, c * size, size))
 
 
 def gate_kernel(wid, meta, kinds, *refs):
-    pieces, (normed_r, act_o, slope_o, wg, w_sem) = refs[:wid], refs[wid:]
-    es = act_o.shape[1]
-    width = wg.shape[1]
-    rows_w = wg.shape[0] // wid
-    copies = []
-    for s, piece in enumerate(pieces):
-        at = pl.multiple_of((meta[1] ^ s) * rows_w, 16)
-        source = piece.at[pl.ds(0, rows_w), :]
-        copies.append(pltpu.make_async_copy(source, wg.at[pl.ds(at, rows_w), :], w_sem.at[s]))
-        copies[-1].start()
-    for copy in copies:
-        copy.wait()
+    pieces, (normed_h, act_h, slope_h, normed_r, act_o, slope_o, wg, w_sem, in_sem, out_sem) = refs[:wid], refs[wid:]
+    total, es = act_o.shape
+    size = total // CHUNKS
+    weights = place_pieces(pieces, wg, w_sem, meta[1], wg.shape[0] // wid)
+    arriving = [move_rows([(normed_h, normed_r)], in_sem, c, c * size, size) for c in range(CHUNKS)]
+    leaving = [
+        move_rows([(act_o, act_h), (slope_o, slope_h)], out_sem, c, c * size, size) for c in range(CHUNKS)
+    ]
+    begin(weights)
+    for copies in arriving:
+        begin(copies)
+    finish(weights)
 
     def one_run(r, carry):
         rows = pl.ds(pl.multiple_of(r * RUN, RUN), RUN)
@@ -293,40 +348,51 @@
         slope_o[rows, :] = sig * (1.0 + gate * (1.0 - sig))
         return carry
 
-    lax.fori_loop(0, normed_r.shape[0] // RUN, one_run, 0)
+    for c in range(CHUNKS):
+        finish(arriving[c])
+        each(c * size // RUN, size // RUN, one_run)
+        begin(leaving[c])
+    for copies in leaving:
+        finish(copies)
 
 
 def cot_kernel(nar, wid, meta, kinds, *refs):
     cots, pieces = refs[:nar], refs[nar : nar + wid]
-    act_r, slope_r, cot_o, w_out_o, dssm_o, dgate_o, cot_sem, out_sem = refs[nar + wid :]
-    total, d = cot_o.shape
-    copies = place_pieces(cots, cot_o, cot_sem, meta[0], cots[0].shape[0])
-    width = pieces[0].shape[1]
-    ep = w_out_o.shape[0] // wid
-    blocks = w_out_o.shape[1] // width
-    first = pieces[0].shape[0] - blocks * ep
-    for s, piece in enumerate(pieces):
-        at = pl.multiple_of((meta[1] ^ s) * ep, 16)
-        for k in range(blocks):
-            copies.append(
-                pltpu.make_async_copy(
-                    piece.at[pl.ds(first + k * ep, ep), :],
-                    w_out_o.at[pl.ds(at, ep), pl.ds(k * width, width)],
-                    out_sem.at[k, s],
-                )
-            )
-            copies[-1].start()
-    for copy in copies:
-        copy.wait()
+    act_h, slope_h, cot_h, w_out_h, dssm_h, dgate_h = refs[nar + wid : nar + wid + 6]
+    act_r, slope_r, cot_r, w_out, dssm_o, dgate_o = refs[nar + wid + 6 : nar + wid + 12]
+    cot_sem, w_sem, in_sem, out_sem, w_out_sem = refs[nar + wid + 12 :]
+    total, d = cot_r.shape
+    size = total // nar
+    weights = place_w_out(pieces, w_out, w_sem, meta[1])
+    cot_copies = place_pieces(cots, cot_r, cot_sem, meta[0], size)
+    firsts = [(meta[0] ^ s) * size for s in range(nar)]
+    arriving = [move_rows([(act_h, act_r), (slope_h, slope_r)], in_sem, s, firsts[s], size) for s in range(nar)]
+    leaving = [
+        move_rows([(dssm_o, dssm_h), (dgate_o, dgate_h), (cot_r, cot_h)], out_sem, s, firsts[s], size)
+        for s in range(nar)
+    ]
+    w_out_leaving = pltpu.make_async_copy(w_out, w_out_h, w_out_sem)
+    begin(weights)
+    for s in range(nar):
+        begin([cot_copies[s]] + arriving[s])
+    finish(weights)
+    w_out_leaving.start()
 
     def one_run(r, carry):
         rows = pl.ds(pl.multiple_of(r * RUN, RUN), RUN)
-        d_gated = dot(cot_o[rows, :], w_out_o[:, pl.ds(pl.multiple_of(kinds[r] * d, LANES), d)], 1, 1)
+        d_gated = dot(cot_r[rows, :], w_out[:, pl.ds(pl.multiple_of(kinds[r] * d, LANES), d)], 1, 1)
         dssm_o[rows, :] = d_gated * act_r[rows, :]
         dgate_o[rows, :] = d_gated * slope_r[rows, :]
         return carry
 
-    lax.fori_loop(0, total // RUN, one_run, 0)
+    for s in range(nar):
+        finish([cot_copies[s]] + arriving[s])
+        first = (meta[0] ^ s) * (size // RUN)
+        each(first, size // RUN, one_run)
+        begin(leaving[s])
+    for copies in leaving:
+        finish(copies)
+    w_out_leaving.wait()
 
 
 def softplus(v):
@@ -334,14 +400,20 @@
 
 
 def scan_kernel(rank, meta, kinds, *refs):
-    px_r, w_dt, table, mixed_r, dssm_r = refs[:5]
-    ssm_o, dpx_o, gmix_o, dpre_o, dlow_o, glog_o, gskip_o = refs[5:12]
-    pxs, pre_s, step_s, states, bc, ps, qs, gs, fs, dtk, dtu, r1s, r2s = refs[12:]
+    px_r, w_dt, table, mixed_h, dssm_h = refs[:5]
+    ssm_h, gmix_h, dpre_h, dpx_o, dlow_o, glog_o, gskip_o = refs[5:12]
+    mixed_r, dssm_r, ssm_o, gmix_o, dpre_o, in_sem, ssm_sem, out_sem = refs[12:20]
+    pxs, pre_s, step_s, states, bc, qs, gs, fs, dtk, dtu, r1s, r2s, cblk, bblk, adjs = refs[20:]
     split = meta[2]
     total, es = mixed_r.shape
     ns = states.shape[1]
     groups = es // LANES
     runs = total // RUN
+    arriving = [
+        pltpu.make_async_copy(mixed_h, mixed_r, in_sem.at[0]),
+        pltpu.make_async_copy(dssm_h, dssm_r, in_sem.at[1]),
+    ]
+    begin(arriving)
     lane = [slice(g * LANES, (g + 1) * LANES) for g in range(groups)]
     rates = -jnp.exp(table[T_LOG : T_LOG + ns, :])
     r1s[...] = rates
@@ -354,32 +426,46 @@
         return pl.ds(pl.multiple_of(r * RUN, RUN), RUN)
 
     k_row = lax.broadcasted_iota(jnp.int32, (ns, LANES), 1)
-    own_row = (k_row % ns == lax.broadcasted_iota(jnp.int32, (ns, LANES), 0)) & (k_row < 4 * ns)
+    own_row = (k_row % ns == lax.broadcasted_iota(jnp.int32, (ns, LANES), 0)) & (k_row < 2 * ns)
     own_row = own_row.astype(f32)
     k_col = lax.broadcasted_iota(jnp.int32, (LANES, 2 * LANES), 0)
     b_or_c = lax.broadcasted_iota(jnp.int32, (LANES, 2 * LANES), 1) // LANES
-    ones = ((k_col % (2 * ns)) // ns == b_or_c).astype(bf16)
+    ones = (k_col // ns == b_or_c).astype(bf16)
+
+    tile_k = lax.broadcasted_iota(jnp.int32, (LANES, 16 * ns), 0)
+    tile_l = lax.broadcasted_iota(jnp.int32, (LANES, 16 * ns), 1)
+    tile_b = (tile_k == tile_l % ns).astype(bf16)
+    tile_c = (tile_k == tile_l % ns + ns).astype(bf16)
+    tile_t = lax.broadcasted_iota(jnp.int32, (RUN, 16 * ns), 0) % 16
+    own_t = (tile_t == lax.broadcasted_iota(jnp.int32, (RUN, 16 * ns), 1) // ns).astype(f32)
 
     def spread(r):
         block = pxs[rank : rank + 2 * ns, pl.ds(pl.multiple_of(r * RUN, LANES), RUN)]
-        high = block.astype(bf16).astype(f32)
-        parts = jnp.concatenate([high, block - high, jnp.zeros((LANES - 4 * ns, RUN), f32)], axis=0)
+        parts = jnp.concatenate([block, jnp.zeros((LANES - 2 * ns, RUN), f32)], axis=0)
         picked = parts.T[:, None, :] * own_row[None]
         bc[bc_rows(r), :] = dot(picked.reshape(RUN * ns, LANES).astype(bf16), ones, 1, 0)
+        cblk[rows_of(r), :] = (dot(parts.T.astype(bf16), tile_c, 1, 0) * own_t).astype(bf16)
+        bblk[rows_of(r), :] = (dot(parts.T.astype(bf16), tile_b, 1, 0) * own_t).astype(bf16)
 
     def bc_rows(r):
         if bc.shape[0] == RUN * ns:
             return pl.ds(0, RUN * ns)
         return pl.ds(pl.multiple_of(r * (RUN * ns), RUN * ns), RUN * ns)
 
-    def prepare(r, again):
-        rows = rows_of(r)
-        steps = step_s[rows, :]
+    arriving[0].wait()
+    for r in range(runs):
+        rows, lanes_at = slice(r * RUN, (r + 1) * RUN), slice(r * RUN, (r + 1) * RUN)
+        low = px_r[:rank, lanes_at]
+        dlow_o[:, lanes_at] = low
+        weights = w_dt[pl.ds(pl.multiple_of(kinds[r] * rank, 16), rank), :]
+        pre = dot(low, weights, 0, 0) + table[pl.ds(T_BIAS + kinds[r], 1), :]
+        pre_s[rows, :] = pre
+        steps = softplus(pre)
+        step_s[rows, :] = steps
         place = r * RUN + lax.broadcasted_iota(jnp.int32, (RUN, 1), 0)
-        reset = (place == 0) | (place == split)
-        dtk[...] = jnp.where(reset, FAR, steps)
-        dtu[...] = steps * mixed_r[rows, :].astype(f32)
-        if not again or bc.shape[0] == RUN * ns:
+        dtk[rows, :] = jnp.where((place == 0) | (place == split), FAR, steps)
+        dtu[rows, :] = steps * mixed_r[rows, :].astype(f32)
+        if bc.shape[0] > RUN * ns:
             spread(r)
 
     def row(tile, j, g):
@@ -398,40 +484,35 @@
 
     def forward(r, hs):
         rows = rows_of(r)
-        kind = kinds[r]
-        low = pxs[:rank, pl.ds(pl.multiple_of(r * RUN, LANES), RUN)].astype(bf16)
-        dlow_o[:, pl.ds(pl.multiple_of(r * RUN, LANES), RUN)] = low
-        weights = w_dt[pl.ds(pl.multiple_of(kind * rank, 16), rank), :]
-        pre = dot(low, weights, 0, 0) + table[pl.ds(T_BIAS + kind, 1), :]
-        pre_s[rows, :] = pre
-        step_s[rows, :] = softplus(pre)
-        prepare(r, False)
+        if bc.shape[0] == RUN * ns:
+            spread(r)
 
         def eight(i, hs):
             hs = list(hs)
-            at = pl.ds(pl.multiple_of(i * 16, 16), 16)
+            at = pl.ds(pl.multiple_of(r * RUN + i * 32, 32), 32)
             k8, u8 = dtk[at, :], dtu[at, :]
-            bcv = bc.at[bc_rows(r), :].at[pl.ds(pl.multiple_of(i * (16 * ns), 16 * ns), 16 * ns), :]
-            psv = ps.at[:, pl.ds(pl.multiple_of(i * (16 * half), 16 * half), 16 * half), :]
-            stv = states.at[pl.ds(r * RUN + i * 16 + 1, 16)]
-            for j in range(16):
+            bcv = bc.at[bc_rows(r), :].at[pl.ds(pl.multiple_of(i * (32 * ns), 32 * ns), 32 * ns), :]
+            stv = states.at[pl.ds(r * RUN + i * 32 + 1, 32)]
+            for j in range(32):
                 bt = bcv[j * ns : (j + 1) * ns, :LANES]
-                ct = bcv[j * ns : (j + 1) * ns, LANES:]
                 for g in range(groups):
                     decay = jnp.exp2(row(k8, j, g) * r2s[:, lane[g]])
                     hs[g] = decay * hs[g] + row(u8, j, g) * bt
                     stv[j, :, lane[g]] = hs[g].astype(bf16)
-                    part = hs[g] * ct
-                    psv[g, j * half : (j + 1) * half, :] = part[:half] + part[half:]
             return tuple(hs)
 
-        hs = lax.fori_loop(0, RUN // 16, eight, hs)
-        ssm_o[rows, :] = folded(ps) + skip * mixed_r[rows, :].astype(f32)
+        hs = lax.fori_loop(0, RUN // 32, eight, hs)
+        for q in range(RUN // 16):
+            at = pl.ds(pl.multiple_of(r * RUN + q * 16, 16), 16)
+            block = states[pl.ds(r * RUN + q * 16 + 1, 16)].reshape(16 * ns, es)
+            ssm_o[at, :] = dot(cblk[at, :], block, 1, 0) + skip * mixed_r[at, :].astype(f32)
+        begin(move_rows([(ssm_o, ssm_h)], ssm_sem, r, r * RUN, RUN))
         return hs
 
     zero = jnp.zeros((ns, LANES), f32)
     lax.fori_loop(0, runs, forward, (zero,) * groups)
     gskip_o[...] = jnp.zeros_like(gskip_o)
+    arriving[1].wait()
     gather_k = lax.broadcasted_iota(jnp.int32, (2 * LANES, LANES), 0) // LANES
     gather_l = lax.broadcasted_iota(jnp.int32, (2 * LANES, LANES), 1) // ns
     gather = (gather_k == gather_l).astype(bf16)
@@ -442,21 +523,21 @@
         r = runs - 1 - back
         rows = rows_of(r)
         kind = kinds[r]
-        prepare(r, True)
+        if bc.shape[0] == RUN * ns:
+            spread(r)
 
         def eight(back_i, carry):
             ms, hs, gr = [list(part) for part in carry]
-            i = RUN // 16 - 1 - back_i
-            at = pl.ds(pl.multiple_of(i * 16, 16), 16)
+            i = RUN // 32 - 1 - back_i
+            at = pl.ds(pl.multiple_of(r * RUN + i * 32, 32), 32)
             k8, u8 = dtk[at, :], dtu[at, :]
-            y8 = dssm_r[pl.ds(pl.multiple_of(r * RUN + i * 16, 16), 16), :]
-            bcv = bc.at[bc_rows(r), :].at[pl.ds(pl.multiple_of(i * (16 * ns), 16 * ns), 16 * ns), :]
-            psv = ps.at[:, pl.ds(pl.multiple_of(i * (16 * half), 16 * half), 16 * half), :]
-            qsv = qs.at[:, pl.ds(pl.multiple_of(i * (16 * half), 16 * half), 16 * half), :]
-            stv = states.at[pl.ds(r * RUN + i * 16, 16)]
-            gsv = gs.at[pl.ds(pl.multiple_of(i * (16 * ns), 16 * ns), 16 * ns), :]
-            for j in reversed(range(16)):
-                bt = bcv[j * ns : (j + 1) * ns, :LANES]
+            y8 = dssm_r[pl.ds(pl.multiple_of(r * RUN + i * 32, 32), 32), :]
+            bcv = bc.at[bc_rows(r), :].at[pl.ds(pl.multiple_of(i * (32 * ns), 32 * ns), 32 * ns), :]
+            adv = adjs.at[pl.ds(i * 32, 32)]
+            qsv = qs.at[:, pl.ds(pl.multiple_of(i * (32 * half), 32 * half), 32 * half), :]
+            stv = states.at[pl.ds(r * RUN + i * 32, 32)]
+            gsv = gs.at[pl.ds(pl.multiple_of(i * (32 * ns), 32 * ns), 32 * ns), :]
+            for j in reversed(range(32)):
                 ct = bcv[j * ns : (j + 1) * ns, LANES:]
                 gb_sum, gc_sum = None, None
                 for g in range(groups):
@@ -468,9 +549,8 @@
                     b_part = adjoint * row(u8, j, g)
                     gb_sum = b_part if gb_sum is None else gb_sum + b_part
                     gc_sum = c_part if gc_sum is None else gc_sum + c_part
-                    lb = adjoint * bt
                     fold_at = slice(j * half, (j + 1) * half)
-                    psv[g, fold_at, :] = lb[:half] + lb[half:]
+                    adv[j, :, lane[g]] = adjoint.astype(bf16)
                     ms[g] = jnp.exp2(dt * r2s[:, lane[g]]) * adjoint
                     weighted = ms[g] * before
                     by_rate = weighted * r1s[:, lane[g]]
@@ -481,9 +561,21 @@
                 gsv[j * ns : (j + 1) * ns, LANES:] = gc_sum.astype(bf16)
             return tuple(ms), tuple(hs), tuple(gr)
 
-        carry = lax.fori_loop(0, RUN // 16, eight, carry)
+        carry = lax.fori_loop(0, RUN // 32, eight, carry)
         mixed = mixed_r[rows, :].astype(f32)
-        lb, by_rate = folded(ps), folded(qs)
+        by_rate = folded(qs)
+        lb = jnp.concatenate(
+            [
+                dot(
+                    bblk[pl.ds(pl.multiple_of(r * RUN + q * 16, 16), 16), :],
+                    adjs[q * 16 : (q + 1) * 16].reshape(16 * ns, es),
+                    1,
+                    0,
+                )
+                for q in range(RUN // 16)
+            ],
+            axis=0,
+        )
         dssm = dssm_r[rows, :]
         grad_steps = by_rate + lb * mixed
         gmix_o[rows, :] = dssm * skip + lb * step_s[rows, :]
@@ -501,12 +593,20 @@
         at = pl.ds(pl.multiple_of(r * RUN, LANES), RUN)
         dpx_o[:rank, at] = dlow.astype(bf16)
         dpx_o[rank:, at] = dbc.astype(bf16)
+        begin(move_rows([(gmix_o, gmix_h), (dpre_o, dpre_h)], out_sem, r, r * RUN, RUN))
         return carry
 
     last = tuple(states[total, :, lane[g]].astype(f32) for g in range(groups))
     done = lax.fori_loop(0, runs, backward, ((zero,) * groups, last, (zero,) * groups))
     for g in range(groups):
         glog_o[:, lane[g]] = done[2][g] * rates[:, lane[g]]
+
+    def settle(r, carry):
+        finish(move_rows([(ssm_o, ssm_h)], ssm_sem, r, r * RUN, RUN))
+        finish(move_rows([(gmix_o, gmix_h), (dpre_o, dpre_h)], out_sem, r, r * RUN, RUN))
+        return carry
+
+    lax.fori_loop(0, runs, settle, 0)
 
 
 def scan_call(rank, xw, ns, meta, kinds, px, w_dt_l, table, mixed, dssm):
@@ -515,30 +615,40 @@
     return call(
         functools.partial(scan_kernel, rank),
         [
-            ((total, es), f32, "v"),
+            ((total, es), f32, "a"),
+            ((total, es), f32, "a"),
+            ((total, es), bf16, "a"),
             ((xw, total), bf16, "v"),
-            ((total, es), f32, "v"),
-            ((total, es), bf16, "v"),
             ((rank, total), bf16, "v"),
             ((ns, es), f32, "v"),
             ((1, es), f32, "v"),
         ],
         [(meta, "s"), (kinds, "s")]
-        + [(px, "v"), (w_dt_l, "v"), (table, "v"), (mixed, "v"), (dssm, "v")],
+        + [(px, "v"), (w_dt_l, "v"), (table, "v"), (mixed, "a"), (dssm, "a")],
         [
+            pltpu.VMEM((total, es), bf16),
+            pltpu.VMEM((total, es), f32),
+            pltpu.VMEM((total, es), f32),
+            pltpu.VMEM((total, es), f32),
+            pltpu.VMEM((total, es), bf16),
+            pltpu.SemaphoreType.DMA((2,)),
+            pltpu.SemaphoreType.DMA((1, total // RUN)),
+            pltpu.SemaphoreType.DMA((2, total // RUN)),
             pltpu.VMEM((xw, total), f32),
             pltpu.VMEM((total, es), f32),
             pltpu.VMEM((total, es), f32),
             pltpu.VMEM((total + 1, ns, es), bf16),
             pltpu.VMEM((bc_runs * RUN * ns, 2 * LANES), f32),
             pltpu.VMEM((es // LANES, RUN * ns // 2, LANES), f32),
-            pltpu.VMEM((es // LANES, RUN * ns // 2, LANES), f32),
             pltpu.VMEM((RUN * ns, 2 * LANES), bf16),
             pltpu.VMEM((RUN * ns // 2, LANES), f32),
-            pltpu.VMEM((RUN, es), f32),
-            pltpu.VMEM((RUN, es), f32),
+            pltpu.VMEM((total, es), f32),
+            pltpu.VMEM((total, es), f32),
             pltpu.VMEM((ns, es), f32),
             pltpu.VMEM((ns, es), f32),
+            pltpu.VMEM((total, 16 * ns), bf16),
+            pltpu.VMEM((total, 16 * ns), bf16),
+            pltpu.VMEM((RUN, ns, es), bf16),
         ],
         us=40.0,
     )
@@ -549,10 +659,17 @@
 
 
 def grads_kernel(wid, ep, rank, meta, kinds, *refs):
-    ssm_r, gated_r, dgate_r, cot_r, normed_r, dpre_r, dlow_r, glog_r, gskip_r = refs[:9]
-    dgate_o, table_o, blocks_o, acc_out, acc_in = refs[9:]
+    hbm, (dlow_r, glog_r, gskip_r) = refs[:6], refs[6:9]
+    dgate_h, blocks_h, table_o = refs[9:12]
+    rows_in, (dgate_o, blocks_o, acc_out, acc_in, in_sem, out_sem, block_sem) = refs[12:18], refs[18:]
+    ssm_r, gated_r, dgate_r, cot_r, normed_r, dpre_r = rows_in
     total, es = ssm_r.shape
     d = cot_r.shape[1]
+    size = total // CHUNKS
+    arriving = [move_rows(list(zip(hbm, rows_in)), in_sem, c, c * size, size) for c in range(CHUNKS)]
+    leaving = [move_rows([(dgate_o, dgate_h)], out_sem, c, c * size, size) for c in range(CHUNKS)]
+    for copies in arriving:
+        begin(copies)
     acc_out[...] = jnp.zeros_like(acc_out)
     acc_in[...] = jnp.zeros_like(acc_in)
     table_o[...] = jnp.zeros_like(table_o)
@@ -561,12 +678,10 @@
     def one_run(r, carry):
         rows = pl.ds(pl.multiple_of(r * RUN, RUN), RUN)
         kind = kinds[r]
-        ssm = ssm_r[rows, :]
-        gated = gated_r[rows, :]
         wide_at = pl.ds(pl.multiple_of(kind * d, LANES), d)
         es_at = pl.ds(pl.multiple_of(kind * es, LANES), es)
-        acc_out[:, wide_at] += dot(gated, cot_r[rows, :], 0, 0)
-        dgate = (dgate_r[rows, :] * ssm).astype(bf16)
+        acc_out[:, wide_at] += dot(gated_r[rows, :], cot_r[rows, :], 0, 0)
+        dgate = (dgate_r[rows, :] * ssm_r[rows, :]).astype(bf16)
         dgate_o[rows, :] = dgate
         acc_in[:, es_at] += dot(normed_r[rows, :], dgate, 0, 0)
         dpre = dpre_r[rows, :]
@@ -575,21 +690,46 @@
         table_o[pl.ds(base + T_BIAS + kind, 1), :] += jnp.sum(dpre.astype(f32), axis=0, keepdims=True)
         return carry
 
-    lax.fori_loop(0, total // RUN, one_run, 0)
-    table_o[base + T_SKIP : base + T_SKIP + 1, :] = gskip_r[...]
-    table_o[base + T_LOG : base + T_LOG + glog_r.shape[0], :] = glog_r[...]
+    for c in range(CHUNKS):
+        finish(arriving[c])
+        each(c * size // RUN, size // RUN, one_run)
+        begin(leaving[c])
     in_rows, width = acc_in.shape[0] // wid, acc_in.shape[1]
+    block_copies = [
+        pltpu.make_async_copy(blocks_o.at[v], blocks_h.at[v], block_sem.at[v]) for v in range(wid)
+    ]
     for v in range(wid):
         blocks_o[v, :in_rows, :] = acc_in[v * in_rows : (v + 1) * in_rows, :].astype(bf16)
         block = acc_out[v * ep : (v + 1) * ep, :].astype(bf16)
         for k in range(block.shape[1] // width):
             first = in_rows + k * ep
             blocks_o[v, first : first + ep, :] = block[:, k * width : (k + 1) * width]
-
-
-def branch_kernel(nar, meta, kinds, ssm_r, act_r, w_out, *refs):
-    outs, gated_o, branch = refs[:nar], refs[nar], refs[nar + 1]
-    d = branch.shape[1]
+        block_copies[v].start()
+    table_o[base + T_SKIP : base + T_SKIP + 1, :] = gskip_r[...]
+    table_o[base + T_LOG : base + T_LOG + glog_r.shape[0], :] = glog_r[...]
+    for copies in leaving + [block_copies]:
+        finish(copies)
+
+
+def branch_kernel(nar, meta, kinds, ssm_h, act_h, w_out_h, *refs):
+    outs, gated_h = refs[:nar], refs[nar]
+    ssm_r, act_r, w_out, gated_o, branch, w_sem, in_sem, out_sem, part_sem = refs[nar + 1 :]
+    total, d = branch.shape
+    size = total // nar
+    weights = pltpu.make_async_copy(w_out_h, w_out, w_sem)
+    firsts = [(meta[0] ^ s) * size for s in range(nar)]
+    arriving = [move_rows([(ssm_h, ssm_r), (act_h, act_r)], in_sem, s, firsts[s], size) for s in range(nar)]
+    leaving = [move_rows([(gated_o, gated_h)], out_sem, s, firsts[s], size) for s in range(nar)]
+    part_copies = [
+        pltpu.make_async_copy(
+            branch.at[pl.ds(pl.multiple_of(firsts[s], RUN), size), :], outs[s], part_sem.at[s]
+        )
+        for s in range(nar)
+    ]
+    weights.start()
+    for s in reversed(range(nar)):
+        begin(arriving[s])
+    weights.wait()
 
     def one_run(r, carry):
         rows = pl.ds(pl.multiple_of(r * RUN, RUN), RUN)
@@ -599,10 +739,13 @@
         branch[rows, :] = dot(gated, w_out[:, wide_at], 1, 0).astype(bf16)
         return carry
 
-    lax.fori_loop(0, branch.shape[0] // RUN, one_run, 0)
-    size = outs[0].shape[0]
-    for s in range(nar):
-        outs[s][...] = branch[pl.ds(pl.multiple_of((meta[0] ^ s) * size, RUN), size), :]
+    for s in reversed(range(nar)):
+        finish(arriving[s])
+        first = (meta[0] ^ s) * (size // RUN)
+        each(first, size // RUN, one_run)
+        begin(leaving[s] + [part_copies[s]])
+    for copies in leaving + [part_copies]:
+        finish(copies)
 
 
 def pair_kernel(chips, meta, same, peer, *outs):
@@ -613,11 +756,22 @@
 
 def conv_kernel(nar, wid, taps, ep, meta, kinds, *refs):
     dpx_pieces = refs[:nar]
-    table, w_x, gmix_r, csum_r, front_r, mixed_r, normed_r, table_r = refs[nar : nar + 8]
-    dfront_o, same_o, peer_o, acc_in, acc_x, small, turned = refs[nar + 8 :]
+    table, w_x, table_r = refs[nar : nar + 3]
+    hbm = refs[nar + 3 : nar + 8]
+    dfront_h, same_h, peer_h = refs[nar + 8 : nar + 11]
+    rows_in = refs[nar + 11 : nar + 16]
+    dfront_o, same_o, peer_o, acc_in, acc_x, small, turned, in_sem, out_sem, block_sem = refs[nar + 16 :]
+    gmix_r, csum_r, front_r, mixed_r, normed_r = rows_in
     split = meta[2]
     total, es = gmix_r.shape
     runs = total // RUN
+    size = total // CHUNKS
+    moves = [(a, b, 16) if b is front_r else (a, b) for a, b in zip(hbm, rows_in)]
+    arriving = [move_rows(moves, in_sem, c, c * size, size) for c in range(CHUNKS)]
+    leaving = [move_rows([(dfront_o, dfront_h)], out_sem, c, c * size, size) for c in range(CHUNKS)]
+    for c in reversed(range(CHUNKS)):
+        begin(arriving[c])
+    front_r[0:16, :] = jnp.zeros((16, es), f32)
     acc_in[...] = jnp.zeros_like(acc_in)
     acc_x[...] = jnp.zeros_like(acc_x)
     small[...] = jnp.zeros_like(small)
@@ -639,7 +793,7 @@
         place = r * RUN + lax.broadcasted_iota(jnp.int32, (RUN + 8, 1), 0)
         offset = place - jnp.where(place >= split, split, 0)
         ext = jnp.concatenate([dc, later], axis=0)
-        lagged = front_r[pl.ds(pl.multiple_of(r * RUN, 8), RUN + 8), :]
+        lagged = front_r[pl.ds(pl.multiple_of(r * RUN + 8, 8), RUN + 8), :]
         d_front = jnp.zeros((RUN, es), f32)
         for lag in range(taps):
             tap = taps - 1 - lag
@@ -654,7 +808,15 @@
         acc_in[:, pl.ds(pl.multiple_of(kind * es, LANES), es)] += dot(normed_r[rows, :], d_front, 0, 0)
         return dc[:8]
 
-    lax.fori_loop(0, runs, one_run, jnp.zeros((8, es), f32))
+    later = jnp.zeros((8, es), f32)
+    for c in reversed(range(CHUNKS)):
+        if c == CHUNKS - 1:
+            finish(arriving[c])
+        if c:
+            finish(arriving[c - 1])
+        back = (CHUNKS - 1 - c) * size // RUN
+        later = each(back, size // RUN, one_run, later)
+        begin(leaving[c])
     in_rows, width = acc_in.shape[0] // wid, acc_in.shape[1]
     base = table_r.shape[0] - small.shape[0]
     rest = jnp.concatenate([table_r[:base, :], table_r[base:, :] + small[...]], axis=0)
@@ -664,34 +826,39 @@
     turned[:, x_cols : x_cols + 256] = rest.astype(bf16)
     turned[:, x_cols + 256 :] = jnp.zeros((es, width - x_cols - 256), bf16)
     core = meta[1] & 1
-    for ref, parity in ((same_o, core), (peer_o, 1 - core)):
+    block_copies = []
+    for k, (ref, out, parity) in enumerate(((peer_o, peer_h, 1 - core), (same_o, same_h, core))):
         for c in range(wid // 2):
             place = 2 * c + parity
             ref[c, :in_rows, :] = split_rows(acc_in, place, in_rows).astype(bf16)
             ref[c, in_rows:, :] = split_rows(turned, place, ep)
+            block_copies.append(pltpu.make_async_copy(ref.at[c], out.at[c], block_sem.at[k, c]))
+            block_copies[-1].start()
+    for copies in leaving + [block_copies]:
+        finish(copies)
 
 
 def normed_kernel(nar, wid, meta, kinds, *refs):
     fronts, gates = refs[:wid], refs[wid : 2 * wid]
-    dfront_r, dgate_r = refs[2 * wid : 2 * wid + 2]
+    dfront_h, dgate_h = refs[2 * wid : 2 * wid + 2]
     outs = refs[2 * wid + 2 : 2 * wid + 2 + nar]
-    wf, wg, dn, f_sem, g_sem = refs[2 * wid + 2 + nar :]
-    w = meta[1]
+    dfront_r, dgate_r, wf, wg, dn, f_sem, g_sem, in_sem, part_sem = refs[2 * wid + 2 + nar :]
     total, es = dfront_r.shape
-    rows_w = wf.shape[0] // wid
-    copies = []
-    width = MODS * es
-    for pieces, target, sem in ((fronts, wf, f_sem), (gates, wg, g_sem)):
-        for s, piece in enumerate(pieces):
-            at = pl.multiple_of((w ^ s) * rows_w, 16)
-            copies.append(
-                pltpu.make_async_copy(
-                    piece.at[pl.ds(0, rows_w), pl.ds(0, width)], target.at[pl.ds(at, rows_w), :], sem.at[s]
-                )
-            )
-            copies[-1].start()
-    for copy in copies:
-        copy.wait()
+    size = total // nar
+    weights = place_pieces(fronts, wf, f_sem, meta[1], wf.shape[0] // wid)
+    weights += place_pieces(gates, wg, g_sem, meta[1], wg.shape[0] // wid)
+    firsts = [(meta[0] ^ s) * size for s in range(nar)]
+    arriving = [
+        move_rows([(dfront_h, dfront_r), (dgate_h, dgate_r)], in_sem, s, firsts[s], size) for s in range(nar)
+    ]
+    part_copies = [
+        pltpu.make_async_copy(dn.at[pl.ds(pl.multiple_of(firsts[s], RUN), size), :], outs[s], part_sem.at[s])
+        for s in range(nar)
+    ]
+    begin(weights)
+    for s in reversed(range(nar)):
+        begin(arriving[s])
+    finish(weights)
 
     def one_run(r, carry):
         rows = pl.ds(pl.multiple_of(r * RUN, RUN), RUN)
@@ -699,10 +866,12 @@
         dn[rows, :] = (dot(dfront_r[rows, :], wf[:, at], 1, 1) + dot(dgate_r[rows, :], wg[:, at], 1, 1)).astype(bf16)
         return carry
 
-    lax.fori_loop(0, total // RUN, one_run, 0)
-    size = outs[0].shape[0]
-    for s in range(nar):
-        outs[s][...] = dn[pl.ds(pl.multiple_of((meta[0] ^ s) * size, RUN), size), :]
+    for s in reversed(range(nar)):
+        finish(arriving[s])
+        first = (meta[0] ^ s) * (size // RUN)
+        each(first, size // RUN, one_run)
+        part_copies[s].start()
+    finish(part_copies)
 
 
 def total_a_kernel(er, ep, blocks, in_o, out_o):
@@ -716,15 +885,13 @@
 
 
 def total_b_kernel(nar, chips, er, rank, taps, ns, meta, *refs):
-    pieces, gate_r, outs = refs[:chips], refs[chips], refs[chips + 1 : chips + 1 + nar]
-    x_o, dt_o, bias_o, conv_o, conv_b_o, log_o, skip_o, rows_s = refs[chips + 1 + nar :]
-    in_rows, width = gate_r.shape
+    pieces, outs = refs[:chips], refs[chips : chips + nar]
+    x_o, dt_o, bias_o, conv_o, conv_b_o, log_o, skip_o, rows_s = refs[chips + nar :]
     dr = outs[0].shape[0]
+    in_rows = nar * dr
     summed = sum(piece[...].astype(f32) for piece in pieces)
-    gate = gate_r[...].astype(f32)
     for k in range(nar):
-        rows_s[k, :, :width] = summed[k * dr : (k + 1) * dr].astype(bf16)
-        rows_s[k, :, width:] = gate[k * dr : (k + 1) * dr].astype(bf16)
+        rows_s[k] = summed[k * dr : (k + 1) * dr].astype(bf16)
     for s in range(nar):
         outs[s][...] = rows_s[meta[0] ^ s]
     rest = summed[in_rows:]
@@ -758,24 +925,51 @@
     out[...] = (x_r[...].astype(f32) + sum(piece[...].astype(f32) for piece in pieces)).astype(bf16)
 
 
-def w_in_kernel(nar, wid, er, ep, meta, *refs):
-    pieces, (w_r, gain_r, grad_o, gain_o, rows_s) = refs[:nar], refs[nar:]
-    es = wid * ep
-    inner = wid * nar * er
+def in_order(parts, er, ep, wid):
+    return jnp.concatenate([part[:, v * ep : v * ep + er] for v in range(wid) for part in parts], axis=1)
+
+
+def gate_rows_kernel(wid, er, ep, rows_r, w_h, grad_h, sums_o, w_r, grad_s, w_sem, out_sem):
+    nar, dr, _ = rows_r.shape
+    es, inner = wid * ep, wid * nar * er
+    loading = pltpu.make_async_copy(w_h.at[:, :, pl.ds(inner, inner)], w_r, w_sem)
+    loading.start()
+    sums = 0.0
+    for m in range(MODS):
+        row = in_order([rows_r[k, :, m * es : (m + 1) * es].astype(f32) for k in range(nar)], er, ep, wid)
+        grad_s[m] = row
+        if m == 0:
+            loading.wait()
+        sums = sums + jnp.sum(row * w_r[m].astype(f32), axis=1, keepdims=True)
+    storing = pltpu.make_async_copy(grad_s, grad_h.at[:, :, pl.ds(inner, inner)], out_sem)
+    storing.start()
+    sums_o[...] = jnp.broadcast_to(sums, (dr, LANES))
+    storing.wait()
+
+
+def front_rows_kernel(nar, wid, er, ep, meta, *refs):
+    pieces, (w_h, gain_r, sums_r, _, grad_h, gain_o, rows_s, w_r, grad_s, w_sem, out_sem) = refs[:nar], refs[nar:]
+    dr = pieces[0].shape[0]
+    es, inner = wid * ep, wid * nar * er
+    loading = pltpu.make_async_copy(w_h.at[:, :, pl.ds(0, inner)], w_r, w_sem)
+    loading.start()
     for s in range(nar):
         rows_s[meta[0] ^ s] = pieces[s][...].astype(f32)
-    sums = 0.0
-    for half in range(2):
-        for m in range(MODS):
-            first = (half * MODS + m) * es
-            parts = [rows_s[k, :, first : first + es] for k in range(nar)]
-            row = jnp.concatenate(
-                [parts[k][:, v * ep : v * ep + er] for v in range(wid) for k in range(nar)], axis=1
-            )
-            at = slice(half * inner, (half + 1) * inner)
-            grad_o[m, :, at] = row
-            sums = sums + jnp.sum(row * w_r[m, :, at].astype(f32), axis=1, keepdims=True)
-    gain_o[...] = sums / gain_r[...]
+    sums = sums_r[...]
+    storing = []
+    for m in range(MODS):
+        row = in_order([rows_s[k, :, m * es : (m + 1) * es] for k in range(nar)], er, ep, wid)
+        grad_s[m] = row
+        storing.append(
+            pltpu.make_async_copy(grad_s.at[m], grad_h.at[m, :, pl.ds(0, inner)], out_sem.at[m])
+        )
+        storing[m].start()
+        if m == 0:
+            loading.wait()
+        sums = sums + jnp.sum(row * w_r[m].astype(f32), axis=1, keepdims=True)
+    sums = jnp.concatenate([sums, jnp.zeros((LANES - dr, LANES), f32)], axis=0).T[0:1, :dr]
+    gain_o[...] = sums / gain_r[...].astype(f32)
+    finish(storing)
 
 
 def body(
@@ -810,7 +1004,7 @@
     meta = jnp.stack([n, w, split_at[0]]).astype(jnp.int32)
 
     front_w = width + LANES
-    gain_col = norm_gain.astype(f32)[:, None]
+    gain_row = norm_gain[None]
     w_in_m = w_in.transpose(1, 0, 2)
     out_cols, x_cols = MODS * d, MODS * LANES
     table_rows = T_LOG + ns
@@ -826,7 +1020,7 @@
             (a, "v")
             for a in (
                 w_in_m,
-                gain_col,
+                gain_row,
                 w_out.transpose(1, 0, 2),
                 w_x.transpose(1, 0, 2),
                 w_dt.transpose(1, 0, 2),
@@ -864,10 +1058,10 @@
     normed, front, csum, mixed, px, kinds, w_x_l, w_dt_l, table, gain_full = call(
         functools.partial(in_kernel, nar, wid, rpd, taps, ep, rank),
         [
-            ((total, d), bf16, "v"),
-            ((total + 8, es), f32, "v"),
-            ((total, es), f32, "v"),
-            ((total, es), bf16, "v"),
+            ((total, d), bf16, "a"),
+            ((total, es), f32, "a"),
+            ((total, es), f32, "a"),
+            ((total, es), bf16, "a"),
             ((xw, total), bf16, "v"),
             ((nar * rpd,), jnp.int32, "s"),
             ((es, x_cols), bf16, "v"),
@@ -877,12 +1071,17 @@
         ],
         [(meta, "s")] + [(p, "a") for p in tok_pieces] + [(p, "a") for p in front_pieces],
         [
+            pltpu.VMEM((total, d), bf16),
+            pltpu.VMEM((total, es), f32),
+            pltpu.VMEM((total, es), f32),
+            pltpu.VMEM((total, es), bf16),
             pltpu.VMEM((nar * (own + 16), d), bf16),
             pltpu.VMEM((d, front_w), bf16),
             pltpu.VMEM((es, small_cols), bf16),
             pltpu.SemaphoreType.DMA((nar,)),
             pltpu.SemaphoreType.DMA((wid,)),
             pltpu.SemaphoreType.DMA((-(-ep // below), wid)),
+            pltpu.SemaphoreType.DMA((4, CHUNKS)),
         ],
         us=9.0,
     )
@@ -890,49 +1089,97 @@
     gate_pieces = far_wide([after(piece, px) for piece in gate_near])
     act, slope = call(
         functools.partial(gate_kernel, wid),
-        [((total, es), f32, "v")] * 2,
-        [(meta, "s"), (kinds, "s")] + [(p, "a") for p in gate_pieces] + [(after(normed, *cot_pieces[1:3]), "v")],
-        [pltpu.VMEM((d, width), bf16), pltpu.SemaphoreType.DMA((wid,))],
+        [((total, es), f32, "a")] * 2,
+        [(meta, "s"), (kinds, "s")]
+        + [(p, "a") for p in gate_pieces]
+        + [(after(normed, *cot_pieces[1:3]), "a")],
+        [
+            pltpu.VMEM((total, d), bf16),
+            pltpu.VMEM((total, es), f32),
+            pltpu.VMEM((total, es), f32),
+            pltpu.VMEM((d, width), bf16),
+            pltpu.SemaphoreType.DMA((wid,)),
+            pltpu.SemaphoreType.DMA((1, CHUNKS)),
+            pltpu.SemaphoreType.DMA((2, CHUNKS)),
+        ],
         us=0.1,
     )
-    px_total = add_narrow(px, act)
+    px_total = add_narrow(px, act, cot_pieces[-1])
     cot, w_out_l, dssm, dgate_f = call(
         functools.partial(cot_kernel, nar, wid),
-        [((total, d), bf16, "v"), ((es, out_cols), bf16, "v")] + [((total, es), f32, "v")] * 2,
+        [((total, d), bf16, "a"), ((es, out_cols), bf16, "a")] + [((total, es), f32, "a")] * 2,
         [(meta, "s"), (kinds, "s")]
         + [(p, "a") for p in cot_pieces]
         + [(p, "a") for p in gate_pieces]
-        + [(act, "v"), (slope, "v")],
-        [pltpu.SemaphoreType.DMA((nar,)), pltpu.SemaphoreType.DMA((out_cols // width, wid))],
+        + [(act, "a"), (slope, "a")],
+        [
+            pltpu.VMEM((total, es), f32),
+            pltpu.VMEM((total, es), f32),
+            pltpu.VMEM((total, d), bf16),
+            pltpu.VMEM((es, out_cols), bf16),
+            pltpu.VMEM((total, es), f32),
+            pltpu.VMEM((total, es), f32),
+            pltpu.SemaphoreType.DMA((nar,)),
+            pltpu.SemaphoreType.DMA((out_cols // width, wid)),
+            pltpu.SemaphoreType.DMA((2, nar)),
+            pltpu.SemaphoreType.DMA((3, nar)),
+            pltpu.SemaphoreType.DMA(()),
+        ],
         us=7.0,
     )
-    ssm, dpx, gmix, dpre, dlow, glog, gskip = scan_call(
+    ssm, gmix, dpre, dpx, dlow, glog, gskip = scan_call(
         rank, xw, ns, meta, kinds, px_total, w_dt_l, table, mixed, dssm
     )
     dpx_pieces = gather_narrow(dpx)
     res = call(
         functools.partial(branch_kernel, nar),
-        [((own, d), bf16, "v")] * nar + [((total, es), bf16, "v")],
-        [(meta, "s"), (kinds, "s"), (ssm, "v"), (act, "v"), (w_out_l, "v")],
-        [pltpu.VMEM((total, d), bf16)],
+        [((own, d), bf16, "a")] * nar + [((total, es), bf16, "a")],
+        [(meta, "s"), (kinds, "s"), (ssm, "a"), (act, "a"), (w_out_l, "a")],
+        [
+            pltpu.VMEM((total, es), f32),
+            pltpu.VMEM((total, es), f32),
+            pltpu.VMEM((es, out_cols), bf16),
+            pltpu.VMEM((total, es), bf16),
+            pltpu.VMEM((total, d), bf16),
+            pltpu.SemaphoreType.DMA(()),
+            pltpu.SemaphoreType.DMA((2, nar)),
+            pltpu.SemaphoreType.DMA((1, nar)),
+            pltpu.SemaphoreType.DMA((nar,)),
+        ],
         us=5.0,
     )
-
     branch_parts, gated = res[:nar], res[nar]
-    branch_pieces, branch_kept = sum_narrow(branch_parts)
-    branch_d1 = branch_pieces[-1]
+    branch_pieces = scatter_narrow(branch_parts)
     in_rows = d // wid
     rows_a = in_rows + ep * (out_cols // width)
-    dgate, table_g, blocks_a = call(
+    dgate, blocks_a, table_g = call(
         functools.partial(grads_kernel, wid, ep, rank),
-        [((total, es), bf16, "v")]
-        + [((MODS * rank + table_rows, es), f32, "v")]
-        + [((wid, rows_a, width), bf16, "v")],
+        [
+            ((total, es), bf16, "a"),
+            ((wid, rows_a, width), bf16, "a"),
+            ((MODS * rank + table_rows, es), f32, "v"),
+        ],
         [(meta, "s"), (kinds, "s")]
-        + [(a, "v") for a in (ssm, gated, dgate_f, cot, normed, dpre, dlow, glog, gskip)],
-        [pltpu.VMEM((es, out_cols), f32), pltpu.VMEM((d, width), f32)],
+        + [(a, "a") for a in (ssm, gated, dgate_f, cot, normed, dpre)]
+        + [(a, "v") for a in (dlow, glog, gskip)],
+        [
+            pltpu.VMEM((total, es), f32),
+            pltpu.VMEM((total, es), bf16),
+            pltpu.VMEM((total, es), f32),
+            pltpu.VMEM((total, d), bf16),
+            pltpu.VMEM((total, d), bf16),
+            pltpu.VMEM((total, es), bf16),
+            pltpu.VMEM((total, es), bf16),
+            pltpu.VMEM((wid, rows_a, width), bf16),
+            pltpu.VMEM((es, out_cols), f32),
+            pltpu.VMEM((d, width), f32),
+            pltpu.SemaphoreType.DMA((6, CHUNKS)),
+            pltpu.SemaphoreType.DMA((1, CHUNKS)),
+            pltpu.SemaphoreType.DMA((wid,)),
+        ],
         us=9.0,
     )
+
     def over_wide(same, peer, *earlier):
         peer = swap(peer, "wide", 1)
         same = after(same, *earlier) if earlier else same
@@ -946,34 +1193,49 @@
 
     blocks_a = lax.all_to_all(blocks_a, "wide", 0, 0)
     rows_b = in_rows + ep
-    dpx_pieces = after(tuple(dpx_pieces), branch_kept, branch_d1)
     dfront, same_b, peer_b = call(
         functools.partial(conv_kernel, nar, wid, taps, ep),
-        [((total, es), bf16, "v")] + [((chips, rows_b, width), bf16, "v")] * 2,
+        [((total, es), bf16, "a")] + [((chips, rows_b, width), bf16, "a")] * 2,
         [(meta, "s"), (kinds, "s")]
         + [(p, "v") for p in dpx_pieces]
-        + [(a, "v") for a in (table, w_x_l, gmix, csum, front, mixed, normed, table_g)],
+        + [(a, "v") for a in (table, w_x_l, table_g)]
+        + [(a, "a") for a in (gmix, csum, front, mixed, normed)],
         [
+            pltpu.VMEM((total, es), f32),
+            pltpu.VMEM((total, es), f32),
+            pltpu.VMEM((total + 16, es), f32),
+            pltpu.VMEM((total, es), bf16),
+            pltpu.VMEM((total, d), bf16),
+            pltpu.VMEM((total, es), bf16),
+            pltpu.VMEM((chips, rows_b, width), bf16),
+            pltpu.VMEM((chips, rows_b, width), bf16),
             pltpu.VMEM((d, width), f32),
             pltpu.VMEM((es, x_cols), f32),
             pltpu.VMEM((table_rows, es), f32),
             pltpu.VMEM((es, width), bf16),
+            pltpu.SemaphoreType.DMA((5, CHUNKS)),
+            pltpu.SemaphoreType.DMA((1, CHUNKS)),
+            pltpu.SemaphoreType.DMA((2, chips)),
         ],
         us=12.0,
     )
     dn_parts = call(
         functools.partial(normed_kernel, nar, wid),
-        [((own, d), bf16, "v")] * nar,
+        [((own, d), bf16, "a")] * nar,
         [(meta, "s"), (kinds, "s")]
         + [(p, "a") for p in front_pieces]
         + [(p, "a") for p in gate_pieces]
-        + [(after(dfront, *branch_pieces[1:]), "v"), (dgate, "v")],
+        + [(dfront, "a"), (dgate, "a")],
         [
+            pltpu.VMEM((total, es), bf16),
+            pltpu.VMEM((total, es), bf16),
             pltpu.VMEM((d, width), bf16),
             pltpu.VMEM((d, width), bf16),
             pltpu.VMEM((total, d), bf16),
             pltpu.SemaphoreType.DMA((wid,)),
             pltpu.SemaphoreType.DMA((wid,)),
+            pltpu.SemaphoreType.DMA((2, nar)),
+            pltpu.SemaphoreType.DMA((nar,)),
         ],
         us=30.0,
     )
@@ -992,9 +1254,10 @@
         [(after(blocks_a, mixed_out), "v")],
         us=3.0,
     )
+    gate_back = lax.all_to_all(gate_sum.reshape(nar, dr, width), "narrow", 0, 0)
     res = call(
         functools.partial(total_b_kernel, nar, chips, er, rank, taps, ns),
-        [((dr, 2 * width), bf16, "v")] * nar
+        [((dr, width), bf16, "v")] * nar
         + [
             ((MODS, er, xw), f32, "v"),
             ((MODS, rank, er), f32, "v"),
@@ -1004,8 +1267,8 @@
             ((ns, er), f32, "v"),
             ((1, er), f32, "v"),
         ],
-        [(meta, "s")] + [(p, "v") for p in pieces_b] + [(gate_sum, "v")],
-        [pltpu.VMEM((nar, dr, 2 * width), bf16)],
+        [(meta, "s")] + [(p, "v") for p in after(tuple(pieces_b), gate_sum)],
+        [pltpu.VMEM((nar, dr, width), bf16)],
         us=3.0,
     )
     back_parts = res[:nar]
@@ -1018,14 +1281,27 @@
         + [(p, "v") for p in after(tuple(dn_pieces), back_parts[0])],
         us=3.0,
     )[0]
+    half_scratch = [
+        pltpu.VMEM((MODS, dr, inner), bf16),
+        pltpu.VMEM((MODS, dr, inner), f32),
+        pltpu.SemaphoreType.DMA(()),
+    ]
+    grad_w_in, gate_sums = call(
+        functools.partial(gate_rows_kernel, wid, er, ep),
+        [((MODS, dr, 2 * inner), f32, "a"), ((dr, LANES), f32, "v")],
+        [(after(gate_back, grad_tokens), "v"), (w_in_m, "a")],
+        half_scratch + [pltpu.SemaphoreType.DMA(())],
+        us=3.0,
+    )
     grad_w_in, grad_gain = call(
-        functools.partial(w_in_kernel, nar, wid, er, ep),
-        [((MODS, dr, 2 * inner), f32, "v"), ((dr, 1), f32, "v")],
+        functools.partial(front_rows_kernel, nar, wid, er, ep),
+        [((MODS, dr, 2 * inner), f32, "a"), ((1, dr), f32, "v")],
         [(meta, "s")]
         + [(p, "v") for p in back_pieces]
-        + [(w_in_m, "v"), (gain_col, "v")],
-        [pltpu.VMEM((nar, dr, 2 * width), f32)],
-        us=4.0,
+        + [(w_in_m, "a"), (gain_row, "v"), (gate_sums, "v"), (grad_w_in, "a")],
+        [pltpu.VMEM((nar, dr, width), f32)] + half_scratch + [pltpu.SemaphoreType.DMA((MODS,))],
+        us=3.0,
+        aliases={nar + 4: 0},
     )
     grad_w_in, grad_w_out = grad_w_in.transpose(1, 0, 2), grad_w_out.transpose(1, 0, 2)
     grad_w_x, grad_w_dt = grad_w_x.transpose(1, 0, 2), grad_w_dt.transpose(1, 0, 2)
@@ -1033,7 +1309,7 @@
     return (
         mixed_out,
         grad_tokens,
-        grad_gain[:, 0],
+        grad_gain[0],
         grad_w_in,
         grad_conv_w,
         grad_conv_b[0],

time: 254 us -> 234 us (0.921)
  waiting for transfers between devices: 64.9 us -> 52.1 us
  Pallas kernels: 126 us -> 114 us
  starting transfers between devices: 47.2 us -> 56.4 us
  other arithmetic: 6.59 us -> 3.32 us
    ppermute x41, waiting for transfers between devices: 64.9 us -> 52.1 us  [swap(): return lax.ppermute(block, axis, [(i, i ^ flip) for i in range(count)])]
    pallas_call x16 -> x17, Pallas kernels: 126 us -> 114 us  [call(): pl.pallas_call(kernel, out_shape=[jax.ShapeDtypeStruct(shape, dtype) for...]
    ppermute x41, starting transfers between devices: 43.4 us -> 48.8 us  [swap(): return lax.ppermute(block, axis, [(i, i ^ flip) for i in range(count)])]
    all_to_all x0 -> x1, starting transfers between devices: none -> 3.63 us  [body(): gate_back = lax.all_to_all(gate_sum.reshape(nar, dr, width), 'narrow', 0, 0)]
    unnamed x60 -> x62, local copies, waits for them, and re-layouts: 6.47 us -> 5.53 us
  transfers between devices with their start and end apart: 42 -> 43, of which waited for: 16 -> 15; matrix products, arithmetic and copies ran while one was open for 2% -> 1% of each run, Pallas kernels for 28% -> 31%
where the time goes in v3:
time: 234 us
  Pallas kernels  114 us (49%)
  starting transfers between devices  56.4 us (24%)
  waiting for transfers between devices  52.1 us (22%)
  local copies, waits for them, and re-layouts  5.64 us (2%)
  other arithmetic  3.32 us (1%)
    pallas_call x17, Pallas kernels, call(): pl.pallas_call(kernel, out_shape=[jax.ShapeDtypeStruct(shape, dtype) for...  114 us
    ppermute x41, waiting for transfers between devices, swap(): return lax.ppermute(block, axis, [(i, i ^ flip) for i in range(count)])  52.1 us
    ppermute x41, starting transfers between devices, swap(): return lax.ppermute(block, axis, [(i, i ^ flip) for i in range(count)])  48.8 us
    unnamed x62, local copies, waits for them, and re-layouts  5.53 us
  transfers between devices with their start and end apart: 43, of which 15 were waited for; matrix products, arithmetic and copies ran while one was open for 1% of the time, Pallas kernels for 31%

profile of v3, /device:TPU:0, one launch (start us, length us, event | category | flops | bytes accessed | tf_op | source)
XLA Modules:
  0.0 233.5 jit_solution(17168116862333752565)
XLA Ops:
  4.3 3.1 %collective-permute-start.3 = (bf16[24,2432]{1,0:T(8,128)(2,1)}, bf16[24,2432]{1,0:T(8,128)(2,1)S(1)}, u32[]{:S(2)}, u32[]{:S(2)}) collective-permute-start(bf16[24,2432]{1,0:T(8,128)(2,1)} %get-tuple-element.104), channel_id=1, source_target_pairs={{0,1},{1,0},{2,3},{3,2},{4,5},{5,4},{6,7},{7,6},{8,9},{9,8},{10,11... | collective-permute-start | bytes 350216 | tf_op jit(solution)/shard_map/ppermute | solution.py:27
  7.4 2.6 %collective-permute-start.4 = (bf16[24,2432]{1,0:T(8,128)(2,1)}, bf16[24,2432]{1,0:T(8,128)(2,1)S(1)}, u32[]{:S(2)}, u32[]{:S(2)}) collective-permute-start(bf16[24,2432]{1,0:T(8,128)(2,1)} %get-tuple-element.105), channel_id=1, source_target_pairs={{0,2},{1,3},{2,0},{3,1},{4,6},{5,7},{6,4},{7,5},{8,10},{9,11},{10,... | collective-permute-start | bytes 350216 | tf_op jit(solution)/shard_map/ppermute | solution.py:27
  12.3 2.5 %collective-permute-start = (bf16[272,768]{1,0:T(8,128)(2,1)S(1)}, bf16[272,768]{1,0:T(8,128)(2,1)S(1)}, u32[]{:S(2)}, u32[]{:S(2)}) collective-permute-start(bf16[272,768]{1,0:T(8,128)(2,1)S(1)} %pad_maximum_fusion.refs_0_), channel_id=1, source_target_pairs={{0,1},{1,0},{2,3},{3,2},{4,5},{5,4},{6,7},{7,6},{8,9},{9,8},{10,11... | collective-permute-start | bytes 1253384 | tf_op jit(solution)/shard_map/ppermute | solution.py:27
  14.8 13.7 %collective-permute-done.4.refs_2_ = bf16[24,2432]{1,0:T(8,128)(2,1)S(1)} collective-permute-done((bf16[24,2432]{1,0:T(8,128)(2,1)}, bf16[24,2432]{1,0:T(8,128)(2,1)S(1)}, u32[]{:S(2)}, u32[]{:S(2)}) %collective-permute-start.4) | collective-permute-done | bytes 116768 | tf_op jit(solution)/shard_map/ppermute | solution.py:27
  29.2 2.7 %shard_map.230 = (bf16[128,1280]{1,0:T(8,128)(2,1)}, bf16[192,1152]{1,0:T(8,128)(2,1)}) custom-call(s32[3]{0:T(128)} %pad_add_fusion.meta, bf16[24,2432]{1,0:T(8,128)(2,1)} %get-tuple-element.103.refs_0_, bf16[24,2432]{1,0:T(8,128)(2,1)} %copy-done.24, bf16[24,2432]{1,0:T(8,128)(2,1)} %copy-done.25, bf16[24,2432]{1,0:T(8,128)(2,1)} %copy-done.26, ...), custom_call_target="tpu_custom_call" | custom-call | flops 2200000000 | bytes 1 | tf_op jit(solution)/shard_map/pallas_call | solution.py:97
  35.3 3.3 %collective-permute-done.1.refs_2_ = bf16[272,768]{1,0:T(8,128)(2,1)S(1)} collective-permute-done((bf16[272,768]{1,0:T(8,128)(2,1)S(1)}, bf16[272,768]{1,0:T(8,128)(2,1)S(1)}, u32[]{:S(2)}, u32[]{:S(2)}) %collective-permute-start.1) | collective-permute-done | bytes 417824 | tf_op jit(solution)/shard_map/ppermute | solution.py:27
  40.2 3.4 %collective-permute-done.9.refs_8_.refs_4_ = bf16[128,1280]{1,0:T(8,128)(2,1)S(1)} collective-permute-done((bf16[128,1280]{1,0:T(8,128)(2,1)}, bf16[128,1280]{1,0:T(8,128)(2,1)S(1)}, u32[]{:S(2)}, u32[]{:S(2)}) %collective-permute-start.9) | collective-permute-done | bytes 327712 | tf_op jit(solution)/shard_map/ppermute | solution.py:27
  44.1 4.9 %collective-permute-done.2.refs_3_ = bf16[272,768]{1,0:T(8,128)(2,1)S(1)} collective-permute-done((bf16[272,768]{1,0:T(8,128)(2,1)S(1)}, bf16[272,768]{1,0:T(8,128)(2,1)S(1)}, u32[]{:S(2)}, u32[]{:S(2)}) %collective-permute-start.2) | collective-permute-done | bytes 417824 | tf_op jit(solution)/shard_map/ppermute | solution.py:27
  52.5 2.8 %collective-permute-start.21 = (bf16[256,768]{1,0:T(8,128)(2,1)S(1)}, bf16[256,768]{1,0:T(8,128)(2,1)}, u32[]{:S(2)}, u32[]{:S(2)}) collective-permute-start(bf16[256,768]{1,0:T(8,128)(2,1)S(1)} %copy-done.17), channel_id=1, source_target_pairs={{0,2},{1,3},{2,0},{3,1},{4,6},{5,7},{6,4},{7,5},{8,10},{9,11},{10,... | collective-permute-start | bytes 1179656 | tf_op jit(solution)/shard_map/ppermute | solution.py:27
  56.4 8.8 %shard_map.231 = (bf16[1024,768]{1,0:T(8,128)(2,1)}, f32[1024,384]{1,0:T(8,128)}, f32[1024,384]{1,0:T(8,128)}, bf16[1024,384]{1,0:T(8,128)(2,1)}, bf16[80,1024]{...) custom-call(s32[3]{0:T(128)} %pad_add_fusion.meta, ...), custom_call_target="tpu_custom_call" | custom-call | flops 9900000256 | bytes 1 | tf_op jit(solution)/shard_map/pallas_call | solution.py:97
  65.3 4.2 %collective-permute-done.16.refs_4_.refs_8_.refs_12_ = bf16[192,1152]{1,0:T(8,128)(2,1)S(1)} collective-permute-done((bf16[192,1152]{1,0:T(8,128)(2,1)}, bf16[192,1152]{1,0:T(8,128)(2,1)S(1)}, u32[]{:S(2)}, u32[]{:S(2)}) %collective-permute-start.16) | collective-permute-done | bytes 442400 | tf_op jit(solution)/shard_map/ppermute | solution.py:27
  76.4 5.4 %shard_map.232 = (f32[1024,384]{1,0:T(8,128)}, f32[1024,384]{1,0:T(8,128)}) custom-call(s32[3]{0:T(128)} %pad_add_fusion.meta, s32[8]{0:T(128)} %get-tuple-element.110.kinds, bf16[192,1152]{1,0:T(8,128)(2,1)} %get-tuple-element.114.refs_0_.refs_4_.refs_8_, bf16[192,1152]{1,0:T(8,128)(2,1)} %copy-done.5, bf16[192,1152]{1,0:T(8,128)(2,1)} %copy-done.4, ...), custom_call_target="tpu_custom_call" | custom-call | flops 110000000 | bytes 1 | tf_op jit(solution)/shard_map/pallas_call | solution.py:97
  81.8 6.0 %collective-permute-done.22.refs_3_ = bf16[256,768]{1,0:T(8,128)(2,1)S(1)} collective-permute-done((bf16[256,768]{1,0:T(8,128)(2,1)}, bf16[256,768]{1,0:T(8,128)(2,1)S(1)}, u32[]{:S(2)}, u32[]{:S(2)}) %collective-permute-start.22) | collective-permute-done | bytes 393248 | tf_op jit(solution)/shard_map/ppermute | solution.py:27
  87.8 2.7 %collective-permute-start.24 = (bf16[80,1024]{1,0:T(8,128)(2,1)S(1)}, bf16[80,1024]{1,0:T(8,128)(2,1)S(1)}, u32[]{:S(2)}, u32[]{:S(2)}) collective-permute-start(bf16[80,1024]{1,0:T(8,128)(2,1)S(1)} %add_convert_fusion.2), channel_id=1, source_target_pairs={{0,1},{1,0},{2,3},{3,2},{4,5},{5,4},{6,7},{7,6},{8,9},{9,8},{10,11... | collective-permute-start | bytes 491528 | tf_op jit(solution)/shard_map/ppermute | solution.py:27
  90.5 6.7 %shard_map.233 = (bf16[1024,768]{1,0:T(8,128)(2,1)}, bf16[384,2304]{1,0:T(8,128)(2,1)}, f32[1024,384]{1,0:T(8,128)}, f32[1024,384]{1,0:T(8,128)}) custom-call(s32[3]{0:T(128)} %pad_add_fusion.meta, s32[8]{0:T(128)} %get-tuple-element.110.kinds, bf16[256,768]{1,0:T(8,128)(2,1)} %cot_r.1, bf16[256,768]{1,0:T(8,128)(2,1)} %collective-permute-done.20.refs_1_, ...), custom_call_target="tpu_custom_call" | custom-call | flops 7699999744 | bytes 1 | tf_op jit(solution)/shard_map/pallas_call | solution.py:97
  97.9 35.8 %shard_map.234 = (f32[1024,384]{1,0:T(8,128)}, f32[1024,384]{1,0:T(8,128)}, bf16[1024,384]{1,0:T(8,128)(2,1)}, bf16[80,1024]{1,0:T(8,128)(2,1)}, bf16[48,1024]{1...) custom-call(s32[3]{0:T(128)} %pad_add_fusion.meta, s32[8]{0:T(128)} %get-tuple-element.110.kinds, ...), custom_call_target="tpu_custom_call" | custom-call | flops 44000002048 | bytes 1 | tf_op jit(solution)/shard_map/pallas_call | solution.py:97
  135.3 2.9 %collective-permute-start.28 = (bf16[80,1024]{1,0:T(8,128)(2,1)}, bf16[80,1024]{1,0:T(8,128)(2,1)}, u32[]{:S(2)}, u32[]{:S(2)}) collective-permute-start(bf16[80,1024]{1,0:T(8,128)(2,1)} %get-tuple-element.135.refs_0_), channel_id=1, source_target_pairs={{0,1},{1,0},{2,3},{3,2},{4,5},{5,4},{6,7},{7,6},{8,9},{9,8},{10,11... | collective-permute-start | bytes 491528 | tf_op jit(solution)/shard_map/ppermute | solution.py:27
  138.2 4.8 %shard_map.235 = (bf16[256,768]{1,0:T(8,128)(2,1)}, bf16[256,768]{1,0:T(8,128)(2,1)}, bf16[256,768]{1,0:T(8,128)(2,1)}, bf16[256,768]{1,0:T(8,128)(2,1)}, bf16[1024,384]{1,0:T(8,128)(2,1)}) custom-call(s32[3]{0:T(128)} %pad_add_fusion.meta, s32[8]{0:T(128)} %get-tuple-element.110.kinds, f32[1024,384]{1,0:T(8,128)} %get-tuple-element.129.ssm_h.refs_0_, ...), custom_call_target="tpu_custom_call" | custom-call | flops 5500000256 | bytes 1 | tf_op jit(solution)/shard_map/pallas_call | solution.py:97
  143.0 8.8 %shard_map.236 = (bf16[1024,384]{1,0:T(8,128)(2,1)}, bf16[8,192,1152]{2,1,0:T(8,128)(2,1)}, f32[176,384]{1,0:T(8,128)}) custom-call(s32[3]{0:T(128)} %pad_add_fusion.meta, s32[8]{0:T(128)} %get-tuple-element.110.kinds, f32[1024,384]{1,0:T(8,128)} %get-tuple-element.129.ssm_h.refs_0_, bf16[1024,384]{1,0:T(8,128)(2,1)} %get-tuple-element.137.refs_1_, ...), custom_call_target="tpu_custom_call" | custom-call | flops 9900000256 | bytes 1 | tf_op jit(solution)/shard_map/pallas_call | solution.py:97
  151.8 3.9 %all-to-all-start = ((bf16[8,192,1152]{2,1,0:T(8,128)(2,1)}), bf16[8,192,1152]{2,1,0:T(8,128)(2,1)S(1)}, u32[]{:S(2)}, u32[]{:S(2)}) async-start(bf16[8,192,1152]{2,1,0:T(8,128)(2,1)} %get-tuple-element.167), calls=%async_computation | async-start | bytes 7077888 | tf_op jit(solution)/shard_map/all_to_all | solution.py:1194
  157.7 2.5 %collective-permute-start.27 = (bf16[256,768]{1,0:T(8,128)(2,1)}, bf16[256,768]{1,0:T(8,128)(2,1)}, u32[]{:S(2)}, u32[]{:S(2)}) collective-permute-start(bf16[256,768]{1,0:T(8,128)(2,1)} %get-tuple-element.134), channel_id=1, source_target_pairs={{0,3},{1,2},{2,1},{3,0},{4,7},{5,6},{6,5},{7,4},{8,11},{9,10},{10,... | collective-permute-start | bytes 1179656 | tf_op jit(solution)/shard_map/ppermute | solution.py:27
  160.2 10.6 %shard_map.237 = (bf16[1024,384]{1,0:T(8,128)(2,1)}, bf16[4,144,1152]{2,1,0:T(8,128)(2,1)}, bf16[4,144,1152]{2,1,0:T(8,128)(2,1)}) custom-call(s32[3]{0:T(128)} %pad_add_fusion.meta, s32[8]{0:T(128)} %get-tuple-element.110.kinds, bf16[80,1024]{1,0:T(8,128)(2,1)} %get-tuple-element.135.refs_0_, bf16[80,1024]{1,0:T(8,128)(2,1)} %collective-permute-done.28.refs_1_, ...), custom_call_target="tpu_custom_call" | custom-call | flops 13200000000 | bytes 1 | tf_op jit(solution)/shard_map/pallas_call | solution.py:97
  170.9 7.7 %shard_map.238 = (bf16[256,768]{1,0:T(8,128)(2,1)}, bf16[256,768]{1,0:T(8,128)(2,1)}, bf16[256,768]{1,0:T(8,128)(2,1)}, bf16[256,768]{1,0:T(8,128)(2,1)}) custom-call(s32[3]{0:T(128)} %pad_add_fusion.meta, s32[8]{0:T(128)} %get-tuple-element.110.kinds, bf16[128,1280]{1,0:T(8,128)(2,1)} %get-tuple-element.109.refs_4_.refs_0_, ...), custom_call_target="tpu_custom_call" | custom-call | flops 32999999488 | bytes 1 | tf_op jit(solution)/shard_map/pallas_call | solution.py:97
  180.7 3.0 %shard_map.239 = (bf16[144,1152]{1,0:T(8,128)(2,1)}, bf16[144,1152]{1,0:T(8,128)(2,1)}, bf16[144,1152]{1,0:T(8,128)(2,1)}, bf16[144,1152]{1,0:T(8,128)(2,1)}) custom-call(s32[3]{0:T(128)} %pad_add_fusion.meta, bf16[4,144,1152]{2,1,0:T(8,128)(2,1)} %get-tuple-element.152.same, bf16[4,144,1152]{2,1,0:T(8,128)(2,1)} %collective-permute-done.31.peer), custom_call_target="tpu_custom_call" | custom-call | flops 3300000000 | bytes 1 | tf_op jit(solution)/shard_map/pallas_call | solution.py:97
  189.5 4.0 %collective-permute-done.32 = bf16[256,768]{1,0:T(8,128)(2,1)} collective-permute-done((bf16[256,768]{1,0:T(8,128)(2,1)}, bf16[256,768]{1,0:T(8,128)(2,1)}, u32[]{:S(2)}, u32[]{:S(2)}) %collective-permute-start.32) | collective-permute-done | bytes 393248 | tf_op jit(solution)/shard_map/ppermute | solution.py:27
  195.4 4.0 %collective-permute-start.33 = (bf16[256,768]{1,0:T(8,128)(2,1)}, bf16[256,768]{1,0:T(8,128)(2,1)}, u32[]{:S(2)}, u32[]{:S(2)}) collective-permute-start(bf16[256,768]{1,0:T(8,128)(2,1)} %add_convert_fusion), channel_id=1, source_target_pairs={{0,2},{1,3},{2,0},{3,1},{4,6},{5,7},{6,4},{7,5},{8,10},{9,11},{10,... | collective-permute-start | bytes 1179656 | tf_op jit(solution)/shard_map/ppermute | solution.py:27
  203.6 3.2 %shard_map.241 = (bf16[96,1152]{1,0:T(8,128)(2,1)}, f32[3,48,768]{2,1,0:T(8,128)}) custom-call(bf16[8,192,1152]{2,1,0:T(8,128)(2,1)} %copy-done), custom_call_target="tpu_custom_call" | custom-call | flops 3300000000 | bytes 1 | tf_op jit(solution)/shard_map/pallas_call | solution.py:97
  206.8 3.6 %all-to-all-start.1 = ((bf16[4,24,1152]{2,1,0:T(8,128)(2,1)}), bf16[4,24,1152]{2,1,0:T(8,128)(2,1)S(1)}, u32[]{:S(2)}, u32[]{:S(2)}) async-start(bf16[4,24,1152]{2,1,0:T(8,128)(2,1)} %bitcast.21), calls=%async_computation.1 | async-start | bytes 442368 | tf_op jit(solution)/shard_map/all_to_all | solution.py:1257
  218.5 3.8 %collective-permute-done.33.refs_1_ = bf16[256,768]{1,0:T(8,128)(2,1)} collective-permute-done((bf16[256,768]{1,0:T(8,128)(2,1)}, bf16[256,768]{1,0:T(8,128)(2,1)}, u32[]{:S(2)}, u32[]{:S(2)}) %collective-permute-start.33) | collective-permute-done | bytes 393248 | tf_op jit(solution)/shard_map/ppermute | solution.py:27
  222.3 2.7 %shard_map.243 = bf16[256,768]{1,0:T(8,128)(2,1)} custom-call(bf16[256,768]{1,0:T(8,128)(2,1)} %x_r.3, bf16[256,768]{1,0:T(8,128)(2,1)} %cot_r.1, f32[1,768]{1,0:T(1,128)} %get-tuple-element.159.gain_r, bf16[256,768]{1,0:T(8,128)(2,1)} %get-tuple-element.175.refs_0_, bf16[256,768]{1,0:T(8,128)(2,1)} %collective-permute-done.33.refs_1_, ...), custom_call_target="tpu_custom_call" | custom-call | flops 3300000000 | bytes 1 | tf_op jit(solution)/shard_map/pallas_call | solution.py:97
  225.7 3.5 %shard_map.244 = (f32[3,24,3072]{2,1,0:T(8,128)}, f32[24,128]{1,0:T(8,128)}) custom-call(bf16[4,24,1152]{2,1,0:T(8,128)(2,1)} %copy-done.12, bf16[3,24,3072]{2,1,0:T(8,128)(2,1)} %bitcast.23), custom_call_target="tpu_custom_call" | custom-call | flops 3300000000 | bytes 1 | tf_op jit(solution)/shard_map/pallas_call | solution.py:97
  229.9 3.5 %shard_map.245 = (f32[3,24,3072]{2,1,0:T(8,128)}, f32[1,24]{1,0:T(1,128)}) custom-call(s32[3]{0:T(128)} %pad_add_fusion.meta, bf16[24,1152]{1,0:T(8,128)(2,1)} %get-tuple-element.174.refs_0_, bf16[24,1152]{1,0:T(8,128)(2,1)} %copy-done.27, bf16[24,1152]{1,0:T(8,128)(2,1)} %copy-done.28, ...), custom_call_target="tpu_custom_call", output_to_operand_aliasing={{0}: (8, {})} | custom-call | flops 3300000000 | bytes 1 | tf_op jit(solution)/shard_map/pallas_call | solution.py:97
  (141 shorter events, 50.6 us)
Async XLA Ops:
  4.3 10.4 %collective-permute-start.3 = (bf16[24,2432]{1,0:T(8,128)(2,1)}, bf16[24,2432]{1,0:T(8,128)(2,1)S(1)}, u32[]{:S(2)}, u32[]{:S(2)}) collective-permute-start(bf16[24,2432]{1,0:T(8,128)(2,1)} %get-tuple-element.104), channel_id=1, source_target_pairs={{0,1},{1,0},{2,3},{3,2},{4,5},{5,4},{6,7},{7,6},{8,9},{9,8},{10,11... | collective-permute-start | bytes 350216 | tf_op jit(solution)/shard_map/ppermute | solution.py:27
  7.4 21.1 %collective-permute-start.4 = (bf16[24,2432]{1,0:T(8,128)(2,1)}, bf16[24,2432]{1,0:T(8,128)(2,1)S(1)}, u32[]{:S(2)}, u32[]{:S(2)}) collective-permute-start(bf16[24,2432]{1,0:T(8,128)(2,1)} %get-tuple-element.105), channel_id=1, source_target_pairs={{0,2},{1,3},{2,0},{3,1},{4,6},{5,7},{6,4},{7,5},{8,10},{9,11},{10,... | collective-permute-start | bytes 350216 | tf_op jit(solution)/shard_map/ppermute | solution.py:27
  10.0 18.5 %collective-permute-start.5 = (bf16[24,2432]{1,0:T(8,128)(2,1)}, bf16[24,2432]{1,0:T(8,128)(2,1)S(1)}, u32[]{:S(2)}, u32[]{:S(2)}) collective-permute-start(bf16[24,2432]{1,0:T(8,128)(2,1)} %get-tuple-element.106), channel_id=1, source_target_pairs={{0,3},{1,2},{2,1},{3,0},{4,7},{5,6},{6,5},{7,4},{8,11},{9,10},{10,... | collective-permute-start | bytes 350216 | tf_op jit(solution)/shard_map/ppermute | solution.py:27
  10.3 28.3 %collective-permute-start.1 = (bf16[272,768]{1,0:T(8,128)(2,1)S(1)}, bf16[272,768]{1,0:T(8,128)(2,1)S(1)}, u32[]{:S(2)}, u32[]{:S(2)}) collective-permute-start(bf16[272,768]{1,0:T(8,128)(2,1)S(1)} %pad_maximum_fusion.refs_0_), channel_id=1, source_target_pairs={{0,2},{1,3},{2,0},{3,1},{4,6},{5,7},{6,4},{7,5},{8,10},{9,11},{10,... | collective-permute-start | bytes 1253384 | tf_op jit(solution)/shard_map/ppermute | solution.py:27
  12.3 26.4 %collective-permute-start = (bf16[272,768]{1,0:T(8,128)(2,1)S(1)}, bf16[272,768]{1,0:T(8,128)(2,1)S(1)}, u32[]{:S(2)}, u32[]{:S(2)}) collective-permute-start(bf16[272,768]{1,0:T(8,128)(2,1)S(1)} %pad_maximum_fusion.refs_0_), channel_id=1, source_target_pairs={{0,1},{1,0},{2,3},{3,2},{4,5},{5,4},{6,7},{7,6},{8,9},{9,8},{10,11... | collective-permute-start | bytes 1253384 | tf_op jit(solution)/shard_map/ppermute | solution.py:27
  38.7 12.8 %collective-permute-start.6 = (bf16[128,1280]{1,0:T(8,128)(2,1)}, bf16[128,1280]{1,0:T(8,128)(2,1)}, u32[]{:S(2)}, u32[]{:S(2)}) collective-permute-start(bf16[128,1280]{1,0:T(8,128)(2,1)} %get-tuple-element.109.refs_4_.refs_0_), channel_id=1, source_target_pairs={{0,4},{4,0},{8,12},{12,8},{16,20},{20,16},{24,28},{28,24},{1,5},{5... | collective-permute-start | bytes 983048 | tf_op jit(solution)/shard_map/ppermute | solution.py:27
  40.1 11.8 %collective-permute-start.12 = (bf16[128,1280]{1,0:T(8,128)(2,1)S(1)}, bf16[128,1280]{1,0:T(8,128)(2,1)}, u32[]{:S(2)}, u32[]{:S(2)}) collective-permute-start(bf16[128,1280]{1,0:T(8,128)(2,1)S(1)} %collective-permute-done.11.refs_10_.refs_6_), channel_id=1, source_target_pairs={{0,4},{4,0},{8,12},{12,8},{16,20},{20,16},{24,28},{28,24},{1,5},{5... | collective-permute-start | bytes 983048 | tf_op jit(solution)/shard_map/ppermute | solution.py:27
  43.7 11.6 %collective-permute-start.8 = (bf16[128,1280]{1,0:T(8,128)(2,1)S(1)}, bf16[128,1280]{1,0:T(8,128)(2,1)S(1)}, u32[]{:S(2)}, u32[]{:S(2)}) collective-permute-start(bf16[128,1280]{1,0:T(8,128)(2,1)S(1)} %collective-permute-done.7.refs_6_.refs_2_), channel_id=1, source_target_pairs={{0,4},{4,0},{8,12},{12,8},{16,20},{20,16},{24,28},{28,24},{1,5},{5... | collective-permute-start | bytes 983048 | tf_op jit(solution)/shard_map/ppermute | solution.py:27
  49.0 16.2 %collective-permute-start.18 = (bf16[192,1152]{1,0:T(8,128)(2,1)}, bf16[192,1152]{1,0:T(8,128)(2,1)S(1)}, u32[]{:S(2)}, u32[]{:S(2)}) collective-permute-start(bf16[192,1152]{1,0:T(8,128)(2,1)} %get-tuple-element.114.refs_0_.refs_4_.refs_8_), channel_id=1, source_target_pairs={{0,24},{4,28},{8,16},{12,20},{16,8},{20,12},{24,0},{28,4},{1,25},{... | collective-permute-start | bytes 1327112 | tf_op jit(solution)/shard_map/ppermute | solution.py:27
  51.4 18.1 %collective-permute-start.16 = (bf16[192,1152]{1,0:T(8,128)(2,1)}, bf16[192,1152]{1,0:T(8,128)(2,1)S(1)}, u32[]{:S(2)}, u32[]{:S(2)}) collective-permute-start(bf16[192,1152]{1,0:T(8,128)(2,1)} %get-tuple-element.114.refs_0_.refs_4_.refs_8_), channel_id=1, source_target_pairs={{0,16},{4,20},{8,24},{12,28},{16,0},{20,4},{24,8},{28,12},{1,17},{... | collective-permute-start | bytes 1327112 | tf_op jit(solution)/shard_map/ppermute | solution.py:27
  51.9 17.7 %collective-permute-start.14 = (bf16[192,1152]{1,0:T(8,128)(2,1)}, bf16[192,1152]{1,0:T(8,128)(2,1)S(1)}, u32[]{:S(2)}, u32[]{:S(2)}) collective-permute-start(bf16[192,1152]{1,0:T(8,128)(2,1)} %get-tuple-element.114.refs_0_.refs_4_.refs_8_), channel_id=1, source_target_pairs={{0,8},{4,12},{8,0},{12,4},{16,24},{20,28},{24,16},{28,20},{1,9},{5... | collective-permute-start | bytes 1327112 | tf_op jit(solution)/shard_map/ppermute | solution.py:27
  52.5 20.0 %collective-permute-start.21 = (bf16[256,768]{1,0:T(8,128)(2,1)S(1)}, bf16[256,768]{1,0:T(8,128)(2,1)}, u32[]{:S(2)}, u32[]{:S(2)}) collective-permute-start(bf16[256,768]{1,0:T(8,128)(2,1)S(1)} %copy-done.17), channel_id=1, source_target_pairs={{0,2},{1,3},{2,0},{3,1},{4,6},{5,7},{6,4},{7,5},{8,10},{9,11},{10,... | collective-permute-start | bytes 1179656 | tf_op jit(solution)/shard_map/ppermute | solution.py:27
  56.0 17.5 %collective-permute-start.20 = (bf16[256,768]{1,0:T(8,128)(2,1)S(1)}, bf16[256,768]{1,0:T(8,128)(2,1)}, u32[]{:S(2)}, u32[]{:S(2)}) collective-permute-start(bf16[256,768]{1,0:T(8,128)(2,1)S(1)} %copy-done.17), channel_id=1, source_target_pairs={{0,1},{1,0},{2,3},{3,2},{4,5},{5,4},{6,7},{7,6},{8,9},{9,8},{10,11... | collective-permute-start | bytes 1179656 | tf_op jit(solution)/shard_map/ppermute | solution.py:27
  73.5 14.3 %collective-permute-start.22 = (bf16[256,768]{1,0:T(8,128)(2,1)}, bf16[256,768]{1,0:T(8,128)(2,1)S(1)}, u32[]{:S(2)}, u32[]{:S(2)}) collective-permute-start(bf16[256,768]{1,0:T(8,128)(2,1)} %collective-permute-done.21.refs_2_), channel_id=1, source_target_pairs={{0,1},{1,0},{2,3},{3,2},{4,5},{5,4},{6,7},{7,6},{8,9},{9,8},{10,11... | collective-permute-start | bytes 1179656 | tf_op jit(solution)/shard_map/ppermute | solution.py:27
  74.2 13.5 %collective-permute-start.23 = (bf16[80,1024]{1,0:T(8,128)(2,1)}, bf16[80,1024]{1,0:T(8,128)(2,1)S(1)}, u32[]{:S(2)}, u32[]{:S(2)}) collective-permute-start(bf16[80,1024]{1,0:T(8,128)(2,1)} %get-tuple-element.123), channel_id=1, source_target_pairs={{0,2},{1,3},{2,0},{3,1},{4,6},{5,7},{6,4},{7,5},{8,10},{9,11},{10,... | collective-permute-start | bytes 491528 | tf_op jit(solution)/shard_map/ppermute | solution.py:27
  133.7 24.0 %collective-permute-start.30 = (bf16[80,1024]{1,0:T(8,128)(2,1)}, bf16[80,1024]{1,0:T(8,128)(2,1)}, u32[]{:S(2)}, u32[]{:S(2)}) collective-permute-start(bf16[80,1024]{1,0:T(8,128)(2,1)} %get-tuple-element.135.refs_0_), channel_id=1, source_target_pairs={{0,3},{1,2},{2,1},{3,0},{4,7},{5,6},{6,5},{7,4},{8,11},{9,10},{10,... | collective-permute-start | bytes 491528 | tf_op jit(solution)/shard_map/ppermute | solution.py:27
  135.1 25.1 %collective-permute-start.29 = (bf16[80,1024]{1,0:T(8,128)(2,1)}, bf16[80,1024]{1,0:T(8,128)(2,1)}, u32[]{:S(2)}, u32[]{:S(2)}) collective-permute-start(bf16[80,1024]{1,0:T(8,128)(2,1)} %get-tuple-element.135.refs_0_), channel_id=1, source_target_pairs={{0,2},{1,3},{2,0},{3,1},{4,6},{5,7},{6,4},{7,5},{8,10},{9,11},{10,... | collective-permute-start | bytes 491528 | tf_op jit(solution)/shard_map/ppermute | solution.py:27
  135.3 24.9 %collective-permute-start.28 = (bf16[80,1024]{1,0:T(8,128)(2,1)}, bf16[80,1024]{1,0:T(8,128)(2,1)}, u32[]{:S(2)}, u32[]{:S(2)}) collective-permute-start(bf16[80,1024]{1,0:T(8,128)(2,1)} %get-tuple-element.135.refs_0_), channel_id=1, source_target_pairs={{0,1},{1,0},{2,3},{3,2},{4,5},{5,4},{6,7},{7,6},{8,9},{9,8},{10,11... | collective-permute-start | bytes 491528 | tf_op jit(solution)/shard_map/ppermute | solution.py:27
  151.8 50.0 %all-to-all-start = ((bf16[8,192,1152]{2,1,0:T(8,128)(2,1)}), bf16[8,192,1152]{2,1,0:T(8,128)(2,1)S(1)}, u32[]{:S(2)}, u32[]{:S(2)}) async-start(bf16[8,192,1152]{2,1,0:T(8,128)(2,1)} %get-tuple-element.167), calls=%async_computation | async-start | bytes 7077888 | tf_op jit(solution)/shard_map/all_to_all | solution.py:1194
  155.7 28.0 %collective-permute-start.25 = (bf16[256,768]{1,0:T(8,128)(2,1)}, bf16[256,768]{1,0:T(8,128)(2,1)}, u32[]{:S(2)}, u32[]{:S(2)}) collective-permute-start(bf16[256,768]{1,0:T(8,128)(2,1)} %get-tuple-element.132), channel_id=1, source_target_pairs={{0,1},{1,0},{2,3},{3,2},{4,5},{5,4},{6,7},{7,6},{8,9},{9,8},{10,11... | collective-permute-start | bytes 1179656 | tf_op jit(solution)/shard_map/ppermute | solution.py:27
  155.8 30.2 %collective-permute-start.26 = (bf16[256,768]{1,0:T(8,128)(2,1)}, bf16[256,768]{1,0:T(8,128)(2,1)}, u32[]{:S(2)}, u32[]{:S(2)}) collective-permute-start(bf16[256,768]{1,0:T(8,128)(2,1)} %get-tuple-element.133), channel_id=1, source_target_pairs={{0,2},{1,3},{2,0},{3,1},{4,6},{5,7},{6,4},{7,5},{8,10},{9,11},{10,... | collective-permute-start | bytes 1179656 | tf_op jit(solution)/shard_map/ppermute | solution.py:27
  157.7 28.3 %collective-permute-start.27 = (bf16[256,768]{1,0:T(8,128)(2,1)}, bf16[256,768]{1,0:T(8,128)(2,1)}, u32[]{:S(2)}, u32[]{:S(2)}) collective-permute-start(bf16[256,768]{1,0:T(8,128)(2,1)} %get-tuple-element.134), channel_id=1, source_target_pairs={{0,3},{1,2},{2,1},{3,0},{4,7},{5,6},{6,5},{7,4},{8,11},{9,10},{10,... | collective-permute-start | bytes 1179656 | tf_op jit(solution)/shard_map/ppermute | solution.py:27
  178.6 14.9 %collective-permute-start.32 = (bf16[256,768]{1,0:T(8,128)(2,1)}, bf16[256,768]{1,0:T(8,128)(2,1)}, u32[]{:S(2)}, u32[]{:S(2)}) collective-permute-start(bf16[256,768]{1,0:T(8,128)(2,1)} %get-tuple-element.162), channel_id=1, source_target_pairs={{0,1},{1,0},{2,3},{3,2},{4,5},{5,4},{6,7},{7,6},{8,9},{9,8},{10,11... | collective-permute-start | bytes 1179656 | tf_op jit(solution)/shard_map/ppermute | solution.py:27
  178.7 39.8 %collective-permute-start.34 = (bf16[256,768]{1,0:T(8,128)(2,1)}, bf16[256,768]{1,0:T(8,128)(2,1)}, u32[]{:S(2)}, u32[]{:S(2)}) collective-permute-start(bf16[256,768]{1,0:T(8,128)(2,1)} %get-tuple-element.163), channel_id=1, source_target_pairs={{0,1},{1,0},{2,3},{3,2},{4,5},{5,4},{6,7},{7,6},{8,9},{9,8},{10,11... | collective-permute-start | bytes 1179656 | tf_op jit(solution)/shard_map/ppermute | solution.py:27
  186.0 24.5 %collective-permute-start.35 = (bf16[144,1152]{1,0:T(8,128)(2,1)}, bf16[144,1152]{1,0:T(8,128)(2,1)}, u32[]{:S(2)}, u32[]{:S(2)}) collective-permute-start(bf16[144,1152]{1,0:T(8,128)(2,1)} %get-tuple-element.164), channel_id=1, source_target_pairs={{0,8},{4,12},{8,0},{12,4},{16,24},{20,28},{24,16},{28,20},{1,9},{5... | collective-permute-start | bytes 995336 | tf_op jit(solution)/shard_map/ppermute | solution.py:27
  187.6 22.9 %collective-permute-start.36 = (bf16[144,1152]{1,0:T(8,128)(2,1)}, bf16[144,1152]{1,0:T(8,128)(2,1)}, u32[]{:S(2)}, u32[]{:S(2)}) collective-permute-start(bf16[144,1152]{1,0:T(8,128)(2,1)} %get-tuple-element.165), channel_id=1, source_target_pairs={{0,16},{4,20},{8,24},{12,28},{16,0},{20,4},{24,8},{28,12},{1,17},{... | collective-permute-start | bytes 995336 | tf_op jit(solution)/shard_map/ppermute | solution.py:27
  189.0 22.8 %collective-permute-start.37 = (bf16[144,1152]{1,0:T(8,128)(2,1)}, bf16[144,1152]{1,0:T(8,128)(2,1)}, u32[]{:S(2)}, u32[]{:S(2)}) collective-permute-start(bf16[144,1152]{1,0:T(8,128)(2,1)} %get-tuple-element.166), channel_id=1, source_target_pairs={{0,24},{4,28},{8,16},{12,20},{16,8},{20,12},{24,0},{28,4},{1,25},{... | collective-permute-start | bytes 995336 | tf_op jit(solution)/shard_map/ppermute | solution.py:27
  195.4 26.9 %collective-permute-start.33 = (bf16[256,768]{1,0:T(8,128)(2,1)}, bf16[256,768]{1,0:T(8,128)(2,1)}, u32[]{:S(2)}, u32[]{:S(2)}) collective-permute-start(bf16[256,768]{1,0:T(8,128)(2,1)} %add_convert_fusion), channel_id=1, source_target_pairs={{0,2},{1,3},{2,0},{3,1},{4,6},{5,7},{6,4},{7,5},{8,10},{9,11},{10,... | collective-permute-start | bytes 1179656 | tf_op jit(solution)/shard_map/ppermute | solution.py:27
  206.8 18.1 %all-to-all-start.1 = ((bf16[4,24,1152]{2,1,0:T(8,128)(2,1)}), bf16[4,24,1152]{2,1,0:T(8,128)(2,1)S(1)}, u32[]{:S(2)}, u32[]{:S(2)}) async-start(bf16[4,24,1152]{2,1,0:T(8,128)(2,1)} %bitcast.21), calls=%async_computation.1 | async-start | bytes 442368 | tf_op jit(solution)/shard_map/all_to_all | solution.py:1257
  214.1 15.1 %collective-permute-start.38 = (bf16[24,1152]{1,0:T(8,128)(2,1)}, bf16[24,1152]{1,0:T(8,128)(2,1)S(1)}, u32[]{:S(2)}, u32[]{:S(2)}) collective-permute-start(bf16[24,1152]{1,0:T(8,128)(2,1)} %get-tuple-element.178), channel_id=1, source_target_pairs={{0,1},{1,0},{2,3},{3,2},{4,5},{5,4},{6,7},{7,6},{8,9},{9,8},{10,11... | collective-permute-start | bytes 165896 | tf_op jit(solution)/shard_map/ppermute | solution.py:27
  214.8 14.5 %collective-permute-start.39 = (bf16[24,1152]{1,0:T(8,128)(2,1)}, bf16[24,1152]{1,0:T(8,128)(2,1)S(1)}, u32[]{:S(2)}, u32[]{:S(2)}) collective-permute-start(bf16[24,1152]{1,0:T(8,128)(2,1)} %get-tuple-element.179), channel_id=1, source_target_pairs={{0,2},{1,3},{2,0},{3,1},{4,6},{5,7},{6,4},{7,5},{8,10},{9,11},{10,... | collective-permute-start | bytes 165896 | tf_op jit(solution)/shard_map/ppermute | solution.py:27
  217.1 12.1 %collective-permute-start.40 = (bf16[24,1152]{1,0:T(8,128)(2,1)}, bf16[24,1152]{1,0:T(8,128)(2,1)S(1)}, u32[]{:S(2)}, u32[]{:S(2)}) collective-permute-start(bf16[24,1152]{1,0:T(8,128)(2,1)} %get-tuple-element.180), channel_id=1, source_target_pairs={{0,3},{1,2},{2,1},{3,0},{4,7},{5,6},{6,5},{7,4},{8,11},{9,10},{10,... | collective-permute-start | bytes 165896 | tf_op jit(solution)/shard_map/ppermute | solution.py:27
  (42 other events, 328.5 us)

commit v4 on v3

--- a/solution.py
+++ b/solution.py
@@ -87,7 +87,7 @@
     return lax.dot_general(a, b, (((ca,), (cb,)), ((), ())), preferred_element_type=f32)
 
 
-def call(kernel, outs, ins, scratch=(), us=1.0, aliases=None):
+def call(kernel, outs, ins, scratch=(), us=1.0):
     spaces = {"v": pltpu.VMEM, "s": pltpu.SMEM, "a": pl.ANY}
     held = [(array.shape, array.dtype) for array, space in ins if space == "v"]
     held += [(shape, dtype) for shape, dtype, space in outs if space == "v"]
@@ -100,7 +100,6 @@
         in_specs=[pl.BlockSpec(memory_space=spaces[space]) for _, space in ins],
         out_specs=[pl.BlockSpec(memory_space=spaces[space]) for _, _, space in outs],
         scratch_shapes=list(scratch),
-        input_output_aliases=aliases or {},
         compiler_params=pltpu.CompilerParams(vmem_limit_bytes=need),
         cost_estimate=pl.CostEstimate(flops=int(us * 1.1e9), bytes_accessed=1, transcendentals=0),
     )(*[array for array, _ in ins])
@@ -356,64 +355,28 @@
         finish(copies)
 
 
-def cot_kernel(nar, wid, meta, kinds, *refs):
-    cots, pieces = refs[:nar], refs[nar : nar + wid]
-    act_h, slope_h, cot_h, w_out_h, dssm_h, dgate_h = refs[nar + wid : nar + wid + 6]
-    act_r, slope_r, cot_r, w_out, dssm_o, dgate_o = refs[nar + wid + 6 : nar + wid + 12]
-    cot_sem, w_sem, in_sem, out_sem, w_out_sem = refs[nar + wid + 12 :]
-    total, d = cot_r.shape
-    size = total // nar
-    weights = place_w_out(pieces, w_out, w_sem, meta[1])
-    cot_copies = place_pieces(cots, cot_r, cot_sem, meta[0], size)
-    firsts = [(meta[0] ^ s) * size for s in range(nar)]
-    arriving = [move_rows([(act_h, act_r), (slope_h, slope_r)], in_sem, s, firsts[s], size) for s in range(nar)]
-    leaving = [
-        move_rows([(dssm_o, dssm_h), (dgate_o, dgate_h), (cot_r, cot_h)], out_sem, s, firsts[s], size)
-        for s in range(nar)
-    ]
-    w_out_leaving = pltpu.make_async_copy(w_out, w_out_h, w_out_sem)
-    begin(weights)
-    for s in range(nar):
-        begin([cot_copies[s]] + arriving[s])
-    finish(weights)
-    w_out_leaving.start()
-
-    def one_run(r, carry):
-        rows = pl.ds(pl.multiple_of(r * RUN, RUN), RUN)
-        d_gated = dot(cot_r[rows, :], w_out[:, pl.ds(pl.multiple_of(kinds[r] * d, LANES), d)], 1, 1)
-        dssm_o[rows, :] = d_gated * act_r[rows, :]
-        dgate_o[rows, :] = d_gated * slope_r[rows, :]
-        return carry
-
-    for s in range(nar):
-        finish([cot_copies[s]] + arriving[s])
-        first = (meta[0] ^ s) * (size // RUN)
-        each(first, size // RUN, one_run)
-        begin(leaving[s])
-    for copies in leaving:
-        finish(copies)
-    w_out_leaving.wait()
-
-
 def softplus(v):
     return jnp.maximum(v, 0.0) + jnp.log1p(jnp.exp(-jnp.abs(v)))
 
 
-def scan_kernel(rank, meta, kinds, *refs):
-    px_r, w_dt, table, mixed_h, dssm_h = refs[:5]
-    ssm_h, gmix_h, dpre_h, dpx_o, dlow_o, glog_o, gskip_o = refs[5:12]
-    mixed_r, dssm_r, ssm_o, gmix_o, dpre_o, in_sem, ssm_sem, out_sem = refs[12:20]
-    pxs, pre_s, step_s, states, bc, qs, gs, fs, dtk, dtu, r1s, r2s, cblk, bblk, adjs = refs[20:]
+def scan_kernel(nar, wid, rank, meta, kinds, *refs):
+    cots, pieces, refs = refs[:nar], refs[nar : nar + wid], refs[nar + wid :]
+    px_r, w_dt, table, mixed_h, act_h = refs[:5]
+    parts_h, refs = refs[5 : 5 + nar], refs[5 + nar :]
+    gated_h, dgs_h, cot_h, gmix_h, dpre_h, dpx_o, dlow_o, glog_o, gskip_o = refs[:9]
+    mixed_r, act_r, cot_r, w_out, dssm_r, ssm_o, gated_o, dgs_o, branch, gmix_o, dpre_o = refs[9:20]
+    in_sem, cot_sem, w_sem, mid_sem, part_sem, out_sem = refs[20:26]
+    pxs, pre_s, step_s, states, bc, qs, gs, fs, dtk, dtu, r1s, r2s, cblk, bblk, adjs = refs[26:]
     split = meta[2]
     total, es = mixed_r.shape
     ns = states.shape[1]
     groups = es // LANES
     runs = total // RUN
-    arriving = [
-        pltpu.make_async_copy(mixed_h, mixed_r, in_sem.at[0]),
-        pltpu.make_async_copy(dssm_h, dssm_r, in_sem.at[1]),
-    ]
-    begin(arriving)
+    d, size = cot_r.shape[1], total // nar
+    mixed_in = pltpu.make_async_copy(mixed_h, mixed_r, in_sem.at[0])
+    arriving = place_w_out(pieces, w_out, w_sem, meta[1]) + place_pieces(cots, cot_r, cot_sem, meta[0], size)
+    arriving.append(pltpu.make_async_copy(act_h, act_r, in_sem.at[1]))
+    begin([mixed_in] + arriving)
     lane = [slice(g * LANES, (g + 1) * LANES) for g in range(groups)]
     rates = -jnp.exp(table[T_LOG : T_LOG + ns, :])
     r1s[...] = rates
@@ -452,7 +415,7 @@
             return pl.ds(0, RUN * ns)
         return pl.ds(pl.multiple_of(r * (RUN * ns), RUN * ns), RUN * ns)
 
-    arriving[0].wait()
+    mixed_in.wait()
     for r in range(runs):
         rows, lanes_at = slice(r * RUN, (r + 1) * RUN), slice(r * RUN, (r + 1) * RUN)
         low = px_r[:rank, lanes_at]
@@ -506,13 +469,29 @@
             at = pl.ds(pl.multiple_of(r * RUN + q * 16, 16), 16)
             block = states[pl.ds(r * RUN + q * 16 + 1, 16)].reshape(16 * ns, es)
             ssm_o[at, :] = dot(cblk[at, :], block, 1, 0) + skip * mixed_r[at, :].astype(f32)
-        begin(move_rows([(ssm_o, ssm_h)], ssm_sem, r, r * RUN, RUN))
         return hs
 
     zero = jnp.zeros((ns, LANES), f32)
     lax.fori_loop(0, runs, forward, (zero,) * groups)
     gskip_o[...] = jnp.zeros_like(gskip_o)
-    arriving[1].wait()
+    finish(arriving)
+    leaving = []
+    for r in range(runs):
+        rows = slice(r * RUN, (r + 1) * RUN)
+        wide_at = pl.ds(pl.multiple_of(kinds[r] * d, LANES), d)
+        ssm, act = ssm_o[rows, :], act_r[rows, :]
+        d_gated = dot(cot_r[rows, :], w_out[:, wide_at], 1, 1)
+        dssm_r[rows, :] = d_gated * act
+        dgs_o[rows, :] = d_gated * ssm
+        gated = (ssm * act).astype(bf16)
+        gated_o[rows, :] = gated
+        branch[rows, :] = dot(gated, w_out[:, wide_at], 1, 0).astype(bf16)
+    for k, (source, target) in enumerate(((gated_o, gated_h), (dgs_o, dgs_h), (cot_r, cot_h))):
+        leaving.append(pltpu.make_async_copy(source, target, mid_sem.at[k]))
+    for s, part in enumerate(parts_h):
+        first = pl.multiple_of((meta[0] ^ s) * size, RUN)
+        leaving.append(pltpu.make_async_copy(branch.at[pl.ds(first, size), :], part, part_sem.at[s]))
+    begin(leaving)
     gather_k = lax.broadcasted_iota(jnp.int32, (2 * LANES, LANES), 0) // LANES
     gather_l = lax.broadcasted_iota(jnp.int32, (2 * LANES, LANES), 1) // ns
     gather = (gather_k == gather_l).astype(bf16)
@@ -602,20 +581,25 @@
         glog_o[:, lane[g]] = done[2][g] * rates[:, lane[g]]
 
     def settle(r, carry):
-        finish(move_rows([(ssm_o, ssm_h)], ssm_sem, r, r * RUN, RUN))
         finish(move_rows([(gmix_o, gmix_h), (dpre_o, dpre_h)], out_sem, r, r * RUN, RUN))
         return carry
 
     lax.fori_loop(0, runs, settle, 0)
-
-
-def scan_call(rank, xw, ns, meta, kinds, px, w_dt_l, table, mixed, dssm):
-    total, es = mixed.shape
+    finish(leaving)
+
+
+def scan_call(rank, xw, ns, meta, kinds, cots, pieces, px, w_dt_l, table, mixed, act):
+    (total, es), (own, d) = mixed.shape, cots[0].shape
+    nar, wid = len(cots), len(pieces)
+    out_cols = MODS * d
     bc_runs = total // RUN if total * ns * 2 * LANES * 4 <= 20 * 1024 * 1024 else 1
     return call(
-        functools.partial(scan_kernel, rank),
-        [
+        functools.partial(scan_kernel, nar, wid, rank),
+        [((own, d), bf16, "a")] * nar
+        + [
+            ((total, es), bf16, "a"),
             ((total, es), f32, "a"),
+            ((total, d), bf16, "a"),
             ((total, es), f32, "a"),
             ((total, es), bf16, "a"),
             ((xw, total), bf16, "v"),
@@ -624,15 +608,26 @@
             ((1, es), f32, "v"),
         ],
         [(meta, "s"), (kinds, "s")]
-        + [(px, "v"), (w_dt_l, "v"), (table, "v"), (mixed, "a"), (dssm, "a")],
+        + [(p, "a") for p in cots]
+        + [(p, "a") for p in pieces]
+        + [(px, "v"), (w_dt_l, "v"), (table, "v"), (mixed, "a"), (act, "a")],
         [
             pltpu.VMEM((total, es), bf16),
             pltpu.VMEM((total, es), f32),
-            pltpu.VMEM((total, es), f32),
+            pltpu.VMEM((total, d), bf16),
+            pltpu.VMEM((es, out_cols), bf16),
+            pltpu.VMEM((total, es), f32),
+            pltpu.VMEM((total, es), f32),
+            pltpu.VMEM((total, es), bf16),
+            pltpu.VMEM((total, es), f32),
+            pltpu.VMEM((total, d), bf16),
             pltpu.VMEM((total, es), f32),
             pltpu.VMEM((total, es), bf16),
             pltpu.SemaphoreType.DMA((2,)),
-            pltpu.SemaphoreType.DMA((1, total // RUN)),
+            pltpu.SemaphoreType.DMA((nar,)),
+            pltpu.SemaphoreType.DMA((out_cols // pieces[0].shape[1], wid)),
+            pltpu.SemaphoreType.DMA((3,)),
+            pltpu.SemaphoreType.DMA((nar,)),
             pltpu.SemaphoreType.DMA((2, total // RUN)),
             pltpu.VMEM((xw, total), f32),
             pltpu.VMEM((total, es), f32),
@@ -660,10 +655,10 @@
 
 def grads_kernel(wid, ep, rank, meta, kinds, *refs):
     hbm, (dlow_r, glog_r, gskip_r) = refs[:6], refs[6:9]
-    dgate_h, blocks_h, table_o = refs[9:12]
-    rows_in, (dgate_o, blocks_o, acc_out, acc_in, in_sem, out_sem, block_sem) = refs[12:18], refs[18:]
-    ssm_r, gated_r, dgate_r, cot_r, normed_r, dpre_r = rows_in
-    total, es = ssm_r.shape
+    dgate_h, gate_h, w_out_h, table_o = refs[9:13]
+    rows_in, (dgate_o, gate_o, w_out_o, acc_out, acc_in, in_sem, out_sem, block_sem) = refs[13:19], refs[19:]
+    gated_r, dgs_r, slope_r, cot_r, normed_r, dpre_r = rows_in
+    total, es = gated_r.shape
     d = cot_r.shape[1]
     size = total // CHUNKS
     arriving = [move_rows(list(zip(hbm, rows_in)), in_sem, c, c * size, size) for c in range(CHUNKS)]
@@ -681,7 +676,7 @@
         wide_at = pl.ds(pl.multiple_of(kind * d, LANES), d)
         es_at = pl.ds(pl.multiple_of(kind * es, LANES), es)
         acc_out[:, wide_at] += dot(gated_r[rows, :], cot_r[rows, :], 0, 0)
-        dgate = (dgate_r[rows, :] * ssm_r[rows, :]).astype(bf16)
+        dgate = (dgs_r[rows, :] * slope_r[rows, :]).astype(bf16)
         dgate_o[rows, :] = dgate
         acc_in[:, es_at] += dot(normed_r[rows, :], dgate, 0, 0)
         dpre = dpre_r[rows, :]
@@ -694,57 +689,19 @@
         finish(arriving[c])
         each(c * size // RUN, size // RUN, one_run)
         begin(leaving[c])
-    in_rows, width = acc_in.shape[0] // wid, acc_in.shape[1]
-    block_copies = [
-        pltpu.make_async_copy(blocks_o.at[v], blocks_h.at[v], block_sem.at[v]) for v in range(wid)
-    ]
-    for v in range(wid):
-        blocks_o[v, :in_rows, :] = acc_in[v * in_rows : (v + 1) * in_rows, :].astype(bf16)
-        block = acc_out[v * ep : (v + 1) * ep, :].astype(bf16)
-        for k in range(block.shape[1] // width):
-            first = in_rows + k * ep
-            blocks_o[v, first : first + ep, :] = block[:, k * width : (k + 1) * width]
-        block_copies[v].start()
+    in_rows = acc_in.shape[0] // wid
+    block_copies = []
+    for k, (source, target) in enumerate(((gate_o, gate_h), (w_out_o, w_out_h))):
+        for v in range(wid):
+            if k == 0:
+                gate_o[v] = acc_in[v * in_rows : (v + 1) * in_rows, :].astype(bf16)
+            else:
+                w_out_o[v] = acc_out[v * ep : (v + 1) * ep, :].astype(bf16)
+            block_copies.append(pltpu.make_async_copy(source.at[v], target.at[v], block_sem.at[k, v]))
+            block_copies[-1].start()
     table_o[base + T_SKIP : base + T_SKIP + 1, :] = gskip_r[...]
     table_o[base + T_LOG : base + T_LOG + glog_r.shape[0], :] = glog_r[...]
     for copies in leaving + [block_copies]:
-        finish(copies)
-
-
-def branch_kernel(nar, meta, kinds, ssm_h, act_h, w_out_h, *refs):
-    outs, gated_h = refs[:nar], refs[nar]
-    ssm_r, act_r, w_out, gated_o, branch, w_sem, in_sem, out_sem, part_sem = refs[nar + 1 :]
-    total, d = branch.shape
-    size = total // nar
-    weights = pltpu.make_async_copy(w_out_h, w_out, w_sem)
-    firsts = [(meta[0] ^ s) * size for s in range(nar)]
-    arriving = [move_rows([(ssm_h, ssm_r), (act_h, act_r)], in_sem, s, firsts[s], size) for s in range(nar)]
-    leaving = [move_rows([(gated_o, gated_h)], out_sem, s, firsts[s], size) for s in range(nar)]
-    part_copies = [
-        pltpu.make_async_copy(
-            branch.at[pl.ds(pl.multiple_of(firsts[s], RUN), size), :], outs[s], part_sem.at[s]
-        )
-        for s in range(nar)
-    ]
-    weights.start()
-    for s in reversed(range(nar)):
-        begin(arriving[s])
-    weights.wait()
-
-    def one_run(r, carry):
-        rows = pl.ds(pl.multiple_of(r * RUN, RUN), RUN)
-        wide_at = pl.ds(pl.multiple_of(kinds[r] * d, LANES), d)
-        gated = (ssm_r[rows, :] * act_r[rows, :]).astype(bf16)
-        gated_o[rows, :] = gated
-        branch[rows, :] = dot(gated, w_out[:, wide_at], 1, 0).astype(bf16)
-        return carry
-
-    for s in reversed(range(nar)):
-        finish(arriving[s])
-        first = (meta[0] ^ s) * (size // RUN)
-        each(first, size // RUN, one_run)
-        begin(leaving[s] + [part_copies[s]])
-    for copies in leaving + [part_copies]:
         finish(copies)
 
 
@@ -874,24 +831,27 @@
     finish(part_copies)
 
 
-def total_a_kernel(er, ep, blocks, in_o, out_o):
-    d = out_o.shape[2]
-    in_rows = in_o.shape[0]
-    summed = sum(blocks[v].astype(f32) for v in range(blocks.shape[0]))
-    in_o[...] = summed[:in_rows].astype(bf16)
-    wide = jnp.concatenate([summed[at : at + ep] for at in range(in_rows, summed.shape[0], ep)], axis=1)
+def total_gate_kernel(blocks, out):
+    out[...] = sum(blocks[v].astype(f32) for v in range(blocks.shape[0])).astype(bf16)
+
+
+def total_out_kernel(er, blocks, out):
+    d = out.shape[2]
+    summed = sum(blocks[v, :er, :].astype(f32) for v in range(blocks.shape[0]))
     for m in range(MODS):
-        out_o[m] = wide[:er, m * d : (m + 1) * d]
+        out[m] = summed[:, m * d : (m + 1) * d]
 
 
 def total_b_kernel(nar, chips, er, rank, taps, ns, meta, *refs):
-    pieces, outs = refs[:chips], refs[chips : chips + nar]
-    x_o, dt_o, bias_o, conv_o, conv_b_o, log_o, skip_o, rows_s = refs[chips + nar :]
-    dr = outs[0].shape[0]
+    pieces, gate_r, outs = refs[:chips], refs[chips], refs[chips + 1 : chips + 1 + nar]
+    x_o, dt_o, bias_o, conv_o, conv_b_o, log_o, skip_o, rows_s = refs[chips + 1 + nar :]
+    dr, width = outs[0].shape[0], gate_r.shape[1]
     in_rows = nar * dr
     summed = sum(piece[...].astype(f32) for piece in pieces)
+    gate = gate_r[...].astype(f32)
     for k in range(nar):
-        rows_s[k] = summed[k * dr : (k + 1) * dr].astype(bf16)
+        rows_s[k, :, :width] = summed[k * dr : (k + 1) * dr].astype(bf16)
+        rows_s[k, :, width:] = gate[k * dr : (k + 1) * dr].astype(bf16)
     for s in range(nar):
         outs[s][...] = rows_s[meta[0] ^ s]
     rest = summed[in_rows:]
@@ -929,44 +889,27 @@
     return jnp.concatenate([part[:, v * ep : v * ep + er] for v in range(wid) for part in parts], axis=1)
 
 
-def gate_rows_kernel(wid, er, ep, rows_r, w_h, grad_h, sums_o, w_r, grad_s, w_sem, out_sem):
-    nar, dr, _ = rows_r.shape
-    es, inner = wid * ep, wid * nar * er
-    loading = pltpu.make_async_copy(w_h.at[:, :, pl.ds(inner, inner)], w_r, w_sem)
-    loading.start()
-    sums = 0.0
-    for m in range(MODS):
-        row = in_order([rows_r[k, :, m * es : (m + 1) * es].astype(f32) for k in range(nar)], er, ep, wid)
-        grad_s[m] = row
-        if m == 0:
-            loading.wait()
-        sums = sums + jnp.sum(row * w_r[m].astype(f32), axis=1, keepdims=True)
-    storing = pltpu.make_async_copy(grad_s, grad_h.at[:, :, pl.ds(inner, inner)], out_sem)
-    storing.start()
-    sums_o[...] = jnp.broadcast_to(sums, (dr, LANES))
-    storing.wait()
-
-
-def front_rows_kernel(nar, wid, er, ep, meta, *refs):
-    pieces, (w_h, gain_r, sums_r, _, grad_h, gain_o, rows_s, w_r, grad_s, w_sem, out_sem) = refs[:nar], refs[nar:]
+def w_in_kernel(nar, wid, er, ep, meta, *refs):
+    pieces, (w_h, gain_r, grad_h, gain_o, rows_s, w_r, grad_s, w_sem, out_sem) = refs[:nar], refs[nar:]
     dr = pieces[0].shape[0]
     es, inner = wid * ep, wid * nar * er
-    loading = pltpu.make_async_copy(w_h.at[:, :, pl.ds(0, inner)], w_r, w_sem)
+    loading = pltpu.make_async_copy(w_h, w_r, w_sem)
     loading.start()
     for s in range(nar):
         rows_s[meta[0] ^ s] = pieces[s][...].astype(f32)
-    sums = sums_r[...]
-    storing = []
+    sums, storing = 0.0, []
     for m in range(MODS):
-        row = in_order([rows_s[k, :, m * es : (m + 1) * es] for k in range(nar)], er, ep, wid)
-        grad_s[m] = row
-        storing.append(
-            pltpu.make_async_copy(grad_s.at[m], grad_h.at[m, :, pl.ds(0, inner)], out_sem.at[m])
-        )
+        for half in range(2):
+            first = (half * MODS + m) * es
+            row = in_order([rows_s[k, :, first : first + es] for k in range(nar)], er, ep, wid)
+            at = slice(half * inner, (half + 1) * inner)
+            grad_s[m, :, at] = row
+            if m + half == 0:
+                loading.wait()
+            sums = sums + jnp.sum(row * w_r[m, :, at].astype(f32), axis=1, keepdims=True)
+        storing.append(pltpu.make_async_copy(grad_s.at[m], grad_h.at[m], out_sem.at[m]))
         storing[m].start()
-        if m == 0:
-            loading.wait()
-        sums = sums + jnp.sum(row * w_r[m].astype(f32), axis=1, keepdims=True)
+    sums = jnp.broadcast_to(sums, (dr, LANES))
     sums = jnp.concatenate([sums, jnp.zeros((LANES - dr, LANES), f32)], axis=0).T[0:1, :dr]
     gain_o[...] = sums / gain_r[...].astype(f32)
     finish(storing)
@@ -1105,77 +1048,39 @@
         us=0.1,
     )
     px_total = add_narrow(px, act, cot_pieces[-1])
-    cot, w_out_l, dssm, dgate_f = call(
-        functools.partial(cot_kernel, nar, wid),
-        [((total, d), bf16, "a"), ((es, out_cols), bf16, "a")] + [((total, es), f32, "a")] * 2,
-        [(meta, "s"), (kinds, "s")]
-        + [(p, "a") for p in cot_pieces]
-        + [(p, "a") for p in gate_pieces]
-        + [(act, "a"), (slope, "a")],
-        [
-            pltpu.VMEM((total, es), f32),
-            pltpu.VMEM((total, es), f32),
-            pltpu.VMEM((total, d), bf16),
-            pltpu.VMEM((es, out_cols), bf16),
-            pltpu.VMEM((total, es), f32),
-            pltpu.VMEM((total, es), f32),
-            pltpu.SemaphoreType.DMA((nar,)),
-            pltpu.SemaphoreType.DMA((out_cols // width, wid)),
-            pltpu.SemaphoreType.DMA((2, nar)),
-            pltpu.SemaphoreType.DMA((3, nar)),
-            pltpu.SemaphoreType.DMA(()),
-        ],
-        us=7.0,
+    res = scan_call(
+        rank, xw, ns, meta, kinds, cot_pieces, gate_pieces, px_total, w_dt_l, table, mixed, act
     )
-    ssm, gmix, dpre, dpx, dlow, glog, gskip = scan_call(
-        rank, xw, ns, meta, kinds, px_total, w_dt_l, table, mixed, dssm
-    )
+    branch_parts, (gated, dgs, cot, gmix, dpre, dpx, dlow, glog, gskip) = res[:nar], res[nar:]
     dpx_pieces = gather_narrow(dpx)
-    res = call(
-        functools.partial(branch_kernel, nar),
-        [((own, d), bf16, "a")] * nar + [((total, es), bf16, "a")],
-        [(meta, "s"), (kinds, "s"), (ssm, "a"), (act, "a"), (w_out_l, "a")],
-        [
-            pltpu.VMEM((total, es), f32),
-            pltpu.VMEM((total, es), f32),
-            pltpu.VMEM((es, out_cols), bf16),
-            pltpu.VMEM((total, es), bf16),
-            pltpu.VMEM((total, d), bf16),
-            pltpu.SemaphoreType.DMA(()),
-            pltpu.SemaphoreType.DMA((2, nar)),
-            pltpu.SemaphoreType.DMA((1, nar)),
-            pltpu.SemaphoreType.DMA((nar,)),
-        ],
-        us=5.0,
-    )
-    branch_parts, gated = res[:nar], res[nar]
     branch_pieces = scatter_narrow(branch_parts)
     in_rows = d // wid
-    rows_a = in_rows + ep * (out_cols // width)
-    dgate, blocks_a, table_g = call(
+    dgate, gate_blocks, w_out_blocks, table_g = call(
         functools.partial(grads_kernel, wid, ep, rank),
         [
             ((total, es), bf16, "a"),
-            ((wid, rows_a, width), bf16, "a"),
+            ((wid, in_rows, width), bf16, "a"),
+            ((wid, ep, out_cols), bf16, "a"),
             ((MODS * rank + table_rows, es), f32, "v"),
         ],
         [(meta, "s"), (kinds, "s")]
-        + [(a, "a") for a in (ssm, gated, dgate_f, cot, normed, dpre)]
+        + [(a, "a") for a in (gated, dgs, slope, cot, normed, dpre)]
         + [(a, "v") for a in (dlow, glog, gskip)],
         [
-            pltpu.VMEM((total, es), f32),
             pltpu.VMEM((total, es), bf16),
+            pltpu.VMEM((total, es), f32),
             pltpu.VMEM((total, es), f32),
             pltpu.VMEM((total, d), bf16),
             pltpu.VMEM((total, d), bf16),
             pltpu.VMEM((total, es), bf16),
             pltpu.VMEM((total, es), bf16),
-            pltpu.VMEM((wid, rows_a, width), bf16),
+            pltpu.VMEM((wid, in_rows, width), bf16),
+            pltpu.VMEM((wid, ep, out_cols), bf16),
             pltpu.VMEM((es, out_cols), f32),
             pltpu.VMEM((d, width), f32),
             pltpu.SemaphoreType.DMA((6, CHUNKS)),
             pltpu.SemaphoreType.DMA((1, CHUNKS)),
-            pltpu.SemaphoreType.DMA((wid,)),
+            pltpu.SemaphoreType.DMA((2, wid)),
         ],
         us=9.0,
     )
@@ -1191,7 +1096,7 @@
         )
         return [parts[0]] + [swap(parts[s], "wide", 2 * s) for s in range(1, chips)]
 
-    blocks_a = lax.all_to_all(blocks_a, "wide", 0, 0)
+    gate_blocks = lax.all_to_all(gate_blocks, "wide", 0, 0)
     rows_b = in_rows + ep
     dfront, same_b, peer_b = call(
         functools.partial(conv_kernel, nar, wid, taps, ep),
@@ -1240,7 +1145,7 @@
         us=30.0,
     )
     pieces_b = over_wide(same_b, peer_b, dn_parts[0])
-    dn_pieces, _ = sum_narrow(dn_parts, pieces_b[0])
+    dn_pieces, dn_kept = sum_narrow(dn_parts, pieces_b[0])
 
     mixed_out = call(
         mixed_kernel,
@@ -1248,16 +1153,15 @@
         [(tokens, "v")] + [(p, "v") for p in after(tuple(branch_pieces), pieces_b[0])],
         us=2.0,
     )[0]
-    gate_sum, grad_w_out = call(
-        functools.partial(total_a_kernel, er, ep),
-        [((in_rows, width), bf16, "v"), ((MODS, er, d), f32, "v")],
-        [(after(blocks_a, mixed_out), "v")],
-        us=3.0,
-    )
-    gate_back = lax.all_to_all(gate_sum.reshape(nar, dr, width), "narrow", 0, 0)
+    gate_sum = call(
+        total_gate_kernel,
+        [((in_rows, width), bf16, "v")],
+        [(after(gate_blocks, mixed_out, dn_kept), "v")],
+        us=2.0,
+    )[0]
     res = call(
         functools.partial(total_b_kernel, nar, chips, er, rank, taps, ns),
-        [((dr, width), bf16, "v")] * nar
+        [((dr, 2 * width), bf16, "v")] * nar
         + [
             ((MODS, er, xw), f32, "v"),
             ((MODS, rank, er), f32, "v"),
@@ -1267,8 +1171,8 @@
             ((ns, er), f32, "v"),
             ((1, er), f32, "v"),
         ],
-        [(meta, "s")] + [(p, "v") for p in after(tuple(pieces_b), gate_sum)],
-        [pltpu.VMEM((nar, dr, width), bf16)],
+        [(meta, "s")] + [(p, "v") for p in pieces_b] + [(gate_sum, "v")],
+        [pltpu.VMEM((nar, dr, 2 * width), bf16)],
         us=3.0,
     )
     back_parts = res[:nar]
@@ -1278,31 +1182,29 @@
         tokens_kernel,
         [((own, d), bf16, "v")],
         [(tokens, "v"), (cotangent, "v"), (gain_full, "v")]
-        + [(p, "v") for p in after(tuple(dn_pieces), back_parts[0])],
+        + [(p, "v") for p in dn_pieces],
+        us=0.1,
+    )[0]
+    w_out_blocks = lax.all_to_all(after(w_out_blocks, gate_sum), "wide", 0, 0)
+    grad_w_in, grad_gain = call(
+        functools.partial(w_in_kernel, nar, wid, er, ep),
+        [((MODS, dr, 2 * inner), f32, "a"), ((1, dr), f32, "v")],
+        [(meta, "s")] + [(p, "v") for p in back_pieces] + [(after(w_in_m, grad_tokens), "a"), (gain_row, "v")],
+        [
+            pltpu.VMEM((nar, dr, 2 * width), f32),
+            pltpu.VMEM((MODS, dr, 2 * inner), bf16),
+            pltpu.VMEM((MODS, dr, 2 * inner), f32),
+            pltpu.SemaphoreType.DMA(()),
+            pltpu.SemaphoreType.DMA((MODS,)),
+        ],
+        us=13.0,
+    )
+    grad_w_out = call(
+        functools.partial(total_out_kernel, er),
+        [((MODS, er, d), f32, "v")],
+        [(after(w_out_blocks, grad_gain), "v")],
         us=3.0,
     )[0]
-    half_scratch = [
-        pltpu.VMEM((MODS, dr, inner), bf16),
-        pltpu.VMEM((MODS, dr, inner), f32),
-        pltpu.SemaphoreType.DMA(()),
-    ]
-    grad_w_in, gate_sums = call(
-        functools.partial(gate_rows_kernel, wid, er, ep),
-        [((MODS, dr, 2 * inner), f32, "a"), ((dr, LANES), f32, "v")],
-        [(after(gate_back, grad_tokens), "v"), (w_in_m, "a")],
-        half_scratch + [pltpu.SemaphoreType.DMA(())],
-        us=3.0,
-    )
-    grad_w_in, grad_gain = call(
-        functools.partial(front_rows_kernel, nar, wid, er, ep),
-        [((MODS, dr, 2 * inner), f32, "a"), ((1, dr), f32, "v")],
-        [(meta, "s")]
-        + [(p, "v") for p in back_pieces]
-        + [(w_in_m, "a"), (gain_row, "v"), (gate_sums, "v"), (grad_w_in, "a")],
-        [pltpu.VMEM((nar, dr, width), f32)] + half_scratch + [pltpu.SemaphoreType.DMA((MODS,))],
-        us=3.0,
-        aliases={nar + 4: 0},
-    )
     grad_w_in, grad_w_out = grad_w_in.transpose(1, 0, 2), grad_w_out.transpose(1, 0, 2)
     grad_w_x, grad_w_dt = grad_w_x.transpose(1, 0, 2), grad_w_dt.transpose(1, 0, 2)
     grad_log = grad_log.T

time: 234 us -> 227 us (0.970)
  Pallas kernels: 114 us -> 105 us
    pallas_call x17 -> x15, Pallas kernels: 114 us -> 105 us  [call(): pl.pallas_call(kernel, out_shape=[jax.ShapeDtypeStruct(shape, dtype) for...]
    unnamed x62 -> x78, local copies, waits for them, and re-layouts: 5.53 us -> 7.22 us
  transfers between devices with their start and end apart: 43 -> 43, of which waited for: 15 -> 13; matrix products, arithmetic and copies ran while one was open for 1% -> 0% of each run, Pallas kernels for 31% -> 27%
where the time goes in v4:
time: 227 us
  Pallas kernels  105 us (46%)
  starting transfers between devices  57.2 us (25%)
  waiting for transfers between devices  53.3 us (23%)
  local copies, waits for them, and re-layouts  7.34 us (3%)
    pallas_call x15, Pallas kernels, call(): pl.pallas_call(kernel, out_shape=[jax.ShapeDtypeStruct(shape, dtype) for...  105 us
    ppermute x41, waiting for transfers between devices, swap(): return lax.ppermute(block, axis, [(i, i ^ flip) for i in range(count)])  51.8 us
    ppermute x41, starting transfers between devices, swap(): return lax.ppermute(block, axis, [(i, i ^ flip) for i in range(count)])  49.8 us
    unnamed x78, local copies, waits for them, and re-layouts  7.22 us
  transfers between devices with their start and end apart: 43, of which 13 were waited for; matrix products, arithmetic and copies ran while one was open for 0% of the time, Pallas kernels for 27%

profile of v4, /device:TPU:0, one launch (start us, length us, event | category | flops | bytes accessed | tf_op | source)
XLA Modules:
  0.0 226.6 jit_solution(11888173987818129437)
XLA Ops:
  1.9 2.5 %shard_map.229 = (bf16[24,2432]{1,0:T(8,128)(2,1)}, bf16[24,2432]{1,0:T(8,128)(2,1)}, bf16[24,2432]{1,0:T(8,128)(2,1)}, bf16[24,2432]{1,0:T(8,128)(2,1)}, bf16[3...) custom-call(s32[3]{0:T(128)} %pad_add_fusion.meta, bf16[3,24,3072]{2,1,0:T(8,128)(2,1)} %bitcast.20, bf16[1,24]{1,0:T(2,128)(2,1)} %bitcast.28, ...), custom_call_target="tpu_custom_call" | custom-call | flops 3300000000 | bytes 1 | tf_op jit(solution)/shard_map/pallas_call | solution.py:97
  4.3 3.1 %collective-permute-start.3 = (bf16[24,2432]{1,0:T(8,128)(2,1)}, bf16[24,2432]{1,0:T(8,128)(2,1)S(1)}, u32[]{:S(2)}, u32[]{:S(2)}) collective-permute-start(bf16[24,2432]{1,0:T(8,128)(2,1)} %get-tuple-element.93), channel_id=1, source_target_pairs={{0,1},{1,0},{2,3},{3,2},{4,5},{5,4},{6,7},{7,6},{8,9},{9,8},{10,11... | collective-permute-start | bytes 350216 | tf_op jit(solution)/shard_map/ppermute | solution.py:27
  7.4 2.6 %collective-permute-start.4 = (bf16[24,2432]{1,0:T(8,128)(2,1)}, bf16[24,2432]{1,0:T(8,128)(2,1)S(1)}, u32[]{:S(2)}, u32[]{:S(2)}) collective-permute-start(bf16[24,2432]{1,0:T(8,128)(2,1)} %get-tuple-element.94), channel_id=1, source_target_pairs={{0,2},{1,3},{2,0},{3,1},{4,6},{5,7},{6,4},{7,5},{8,10},{9,11},{10,... | collective-permute-start | bytes 350216 | tf_op jit(solution)/shard_map/ppermute | solution.py:27
  12.3 2.5 %collective-permute-start = (bf16[272,768]{1,0:T(8,128)(2,1)S(1)}, bf16[272,768]{1,0:T(8,128)(2,1)S(1)}, u32[]{:S(2)}, u32[]{:S(2)}) collective-permute-start(bf16[272,768]{1,0:T(8,128)(2,1)S(1)} %pad_maximum_fusion.refs_0_), channel_id=1, source_target_pairs={{0,1},{1,0},{2,3},{3,2},{4,5},{5,4},{6,7},{7,6},{8,9},{9,8},{10,11... | collective-permute-start | bytes 1253384 | tf_op jit(solution)/shard_map/ppermute | solution.py:27
  14.8 13.7 %collective-permute-done.4.refs_2_ = bf16[24,2432]{1,0:T(8,128)(2,1)S(1)} collective-permute-done((bf16[24,2432]{1,0:T(8,128)(2,1)}, bf16[24,2432]{1,0:T(8,128)(2,1)S(1)}, u32[]{:S(2)}, u32[]{:S(2)}) %collective-permute-start.4) | collective-permute-done | bytes 116768 | tf_op jit(solution)/shard_map/ppermute | solution.py:27
  29.2 2.7 %shard_map.230 = (bf16[128,1280]{1,0:T(8,128)(2,1)}, bf16[192,1152]{1,0:T(8,128)(2,1)}) custom-call(s32[3]{0:T(128)} %pad_add_fusion.meta, bf16[24,2432]{1,0:T(8,128)(2,1)} %get-tuple-element.92.refs_0_, bf16[24,2432]{1,0:T(8,128)(2,1)} %copy-done.32, bf16[24,2432]{1,0:T(8,128)(2,1)} %copy-done.33, bf16[24,2432]{1,0:T(8,128)(2,1)} %copy-done.34, ...), custom_call_target="tpu_custom_call" | custom-call | flops 2200000000 | bytes 1 | tf_op jit(solution)/shard_map/pallas_call | solution.py:97
  35.4 3.3 %collective-permute-done.1.refs_2_ = bf16[272,768]{1,0:T(8,128)(2,1)S(1)} collective-permute-done((bf16[272,768]{1,0:T(8,128)(2,1)S(1)}, bf16[272,768]{1,0:T(8,128)(2,1)S(1)}, u32[]{:S(2)}, u32[]{:S(2)}) %collective-permute-start.1) | collective-permute-done | bytes 417824 | tf_op jit(solution)/shard_map/ppermute | solution.py:27
  38.7 3.9 %collective-permute-done.9.refs_8_.refs_4_ = bf16[128,1280]{1,0:T(8,128)(2,1)S(1)} collective-permute-done((bf16[128,1280]{1,0:T(8,128)(2,1)}, bf16[128,1280]{1,0:T(8,128)(2,1)S(1)}, u32[]{:S(2)}, u32[]{:S(2)}) %collective-permute-start.9) | collective-permute-done | bytes 327712 | tf_op jit(solution)/shard_map/ppermute | solution.py:27
  44.2 4.8 %collective-permute-done.2.refs_3_ = bf16[272,768]{1,0:T(8,128)(2,1)S(1)} collective-permute-done((bf16[272,768]{1,0:T(8,128)(2,1)S(1)}, bf16[272,768]{1,0:T(8,128)(2,1)S(1)}, u32[]{:S(2)}, u32[]{:S(2)}) %collective-permute-start.2) | collective-permute-done | bytes 417824 | tf_op jit(solution)/shard_map/ppermute | solution.py:27
  49.0 2.4 %collective-permute-start.21 = (bf16[192,1152]{1,0:T(8,128)(2,1)}, bf16[192,1152]{1,0:T(8,128)(2,1)S(1)}, u32[]{:S(2)}, u32[]{:S(2)}) collective-permute-start(bf16[192,1152]{1,0:T(8,128)(2,1)} %get-tuple-element.105.refs_0_.refs_4_.refs_8_), channel_id=1, source_target_pairs={{0,24},{4,28},{8,16},{12,20},{16,8},{20,12},{24,0},{28,4},{1,25},{... | collective-permute-start | bytes 1327112 | tf_op jit(solution)/shard_map/ppermute | solution.py:27
  52.5 2.7 %collective-permute-start.14 = (bf16[256,768]{1,0:T(8,128)(2,1)S(1)}, bf16[256,768]{1,0:T(8,128)(2,1)}, u32[]{:S(2)}, u32[]{:S(2)}) collective-permute-start(bf16[256,768]{1,0:T(8,128)(2,1)S(1)} %copy-done.12), channel_id=1, source_target_pairs={{0,2},{1,3},{2,0},{3,1},{4,6},{5,7},{6,4},{7,5},{8,10},{9,11},{10,... | collective-permute-start | bytes 1179656 | tf_op jit(solution)/shard_map/ppermute | solution.py:27
  56.4 8.8 %shard_map.231 = (bf16[1024,768]{1,0:T(8,128)(2,1)}, f32[1024,384]{1,0:T(8,128)}, f32[1024,384]{1,0:T(8,128)}, bf16[1024,384]{1,0:T(8,128)(2,1)}, bf16[80,1024]{...) custom-call(s32[3]{0:T(128)} %pad_add_fusion.meta, ...), custom_call_target="tpu_custom_call" | custom-call | flops 9900000256 | bytes 1 | tf_op jit(solution)/shard_map/pallas_call | solution.py:97
  65.4 4.2 %collective-permute-done.19.refs_4_.refs_8_.refs_12_ = bf16[192,1152]{1,0:T(8,128)(2,1)S(1)} collective-permute-done((bf16[192,1152]{1,0:T(8,128)(2,1)}, bf16[192,1152]{1,0:T(8,128)(2,1)S(1)}, u32[]{:S(2)}, u32[]{:S(2)}) %collective-permute-start.19) | collective-permute-done | bytes 442400 | tf_op jit(solution)/shard_map/ppermute | solution.py:27
  70.0 2.7 %collective-permute-done.14.refs_2_ = bf16[256,768]{1,0:T(8,128)(2,1)} collective-permute-done((bf16[256,768]{1,0:T(8,128)(2,1)S(1)}, bf16[256,768]{1,0:T(8,128)(2,1)}, u32[]{:S(2)}, u32[]{:S(2)}) %collective-permute-start.14) | collective-permute-done | bytes 393248 | tf_op jit(solution)/shard_map/ppermute | solution.py:27
  76.6 5.4 %shard_map.232 = (f32[1024,384]{1,0:T(8,128)}, f32[1024,384]{1,0:T(8,128)}) custom-call(s32[3]{0:T(128)} %pad_add_fusion.meta, s32[8]{0:T(128)} %get-tuple-element.99.kinds, bf16[192,1152]{1,0:T(8,128)(2,1)} %get-tuple-element.105.refs_0_.refs_4_.refs_8_, bf16[192,1152]{1,0:T(8,128)(2,1)} %copy-done.7, bf16[192,1152]{1,0:T(8,128)(2,1)} %copy-done.6, ...), custom_call_target="tpu_custom_call" | custom-call | flops 110000000 | bytes 1 | tf_op jit(solution)/shard_map/pallas_call | solution.py:97
  82.0 6.1 %collective-permute-done.15.refs_3_ = bf16[256,768]{1,0:T(8,128)(2,1)} collective-permute-done((bf16[256,768]{1,0:T(8,128)(2,1)}, bf16[256,768]{1,0:T(8,128)(2,1)}, u32[]{:S(2)}, u32[]{:S(2)}) %collective-permute-start.15) | collective-permute-done | bytes 393248 | tf_op jit(solution)/shard_map/ppermute | solution.py:27
  88.1 2.5 %collective-permute-start.24 = (bf16[80,1024]{1,0:T(8,128)(2,1)S(1)}, bf16[80,1024]{1,0:T(8,128)(2,1)S(1)}, u32[]{:S(2)}, u32[]{:S(2)}) collective-permute-start(bf16[80,1024]{1,0:T(8,128)(2,1)S(1)} %add_convert_fusion.2), channel_id=1, source_target_pairs={{0,1},{1,0},{2,3},{3,2},{4,5},{5,4},{6,7},{7,6},{8,9},{9,8},{10,11... | collective-permute-start | bytes 491528 | tf_op jit(solution)/shard_map/ppermute | solution.py:27
  90.7 4.0 %collective-permute-done.24 = bf16[80,1024]{1,0:T(8,128)(2,1)S(1)} collective-permute-done((bf16[80,1024]{1,0:T(8,128)(2,1)S(1)}, bf16[80,1024]{1,0:T(8,128)(2,1)S(1)}, u32[]{:S(2)}, u32[]{:S(2)}) %collective-permute-start.24) | collective-permute-done | bytes 163872 | tf_op jit(solution)/shard_map/ppermute | solution.py:27
  95.4 39.2 %shard_map.233 = (bf16[256,768]{1,0:T(8,128)(2,1)}, bf16[256,768]{1,0:T(8,128)(2,1)}, bf16[256,768]{1,0:T(8,128)(2,1)}, bf16[256,768]{1,0:T(8,128)(2,1)}, bf16[1...) custom-call(s32[3]{0:T(128)} %pad_add_fusion.meta, ...), custom_call_target="tpu_custom_call" | custom-call | flops 44000002048 | bytes 1 | tf_op jit(solution)/shard_map/pallas_call | solution.py:97
  141.4 8.9 %shard_map.234 = (bf16[1024,384]{1,0:T(8,128)(2,1)}, bf16[8,96,1152]{2,1,0:T(8,128)(2,1)}, bf16[8,48,2304]{2,1,0:T(8,128)(2,1)}, f32[176,384]{1,0:T(8,128)}) custom-call(s32[3]{0:T(128)} %pad_add_fusion.meta, s32[8]{0:T(128)} %get-tuple-element.99.kinds, bf16[1024,384]{1,0:T(8,128)(2,1)} %get-tuple-element.122.refs_0_, ...), custom_call_target="tpu_custom_call" | custom-call | flops 9900000256 | bytes 1 | tf_op jit(solution)/shard_map/pallas_call | solution.py:97
  150.3 3.8 %all-to-all-start = ((bf16[8,96,1152]{2,1,0:T(8,128)(2,1)}), bf16[8,96,1152]{2,1,0:T(8,128)(2,1)S(1)}, u32[]{:S(2)}, u32[]{:S(2)}) async-start(bf16[8,96,1152]{2,1,0:T(8,128)(2,1)} %get-tuple-element.153), calls=%async_computation | async-start | bytes 3538944 | tf_op jit(solution)/shard_map/all_to_all | solution.py:1099
  157.0 10.6 %shard_map.235 = (bf16[1024,384]{1,0:T(8,128)(2,1)}, bf16[4,144,1152]{2,1,0:T(8,128)(2,1)}, bf16[4,144,1152]{2,1,0:T(8,128)(2,1)}) custom-call(s32[3]{0:T(128)} %pad_add_fusion.meta, s32[8]{0:T(128)} %get-tuple-element.99.kinds, bf16[80,1024]{1,0:T(8,128)(2,1)} %get-tuple-element.120.refs_0_, bf16[80,1024]{1,0:T(8,128)(2,1)} %copy-done.29, ...), custom_call_target="tpu_custom_call" | custom-call | flops 13200000000 | bytes 1 | tf_op jit(solution)/shard_map/pallas_call | solution.py:97
  167.7 7.7 %shard_map.236 = (bf16[256,768]{1,0:T(8,128)(2,1)}, bf16[256,768]{1,0:T(8,128)(2,1)}, bf16[256,768]{1,0:T(8,128)(2,1)}, bf16[256,768]{1,0:T(8,128)(2,1)}) custom-call(s32[3]{0:T(128)} %pad_add_fusion.meta, s32[8]{0:T(128)} %get-tuple-element.99.kinds, bf16[128,1280]{1,0:T(8,128)(2,1)} %get-tuple-element.98.refs_4_.refs_0_, bf16[128,1280]{1,0:T(8,128)(2,1)} %copy-done.25, ...), custom_call_target="tpu_custom_call" | custom-call | flops 32999999488 | bytes 1 | tf_op jit(solution)/shard_map/pallas_call | solution.py:97
  177.5 2.9 %shard_map.237 = (bf16[144,1152]{1,0:T(8,128)(2,1)}, bf16[144,1152]{1,0:T(8,128)(2,1)}, bf16[144,1152]{1,0:T(8,128)(2,1)}, bf16[144,1152]{1,0:T(8,128)(2,1)}) custom-call(s32[3]{0:T(128)} %pad_add_fusion.meta, bf16[4,144,1152]{2,1,0:T(8,128)(2,1)} %get-tuple-element.138.same, bf16[4,144,1152]{2,1,0:T(8,128)(2,1)} %collective-permute-done.31.peer), custom_call_target="tpu_custom_call" | custom-call | flops 3300000000 | bytes 1 | tf_op jit(solution)/shard_map/pallas_call | solution.py:97
  184.0 3.6 %collective-permute-done.32 = bf16[256,768]{1,0:T(8,128)(2,1)S(1)} collective-permute-done((bf16[256,768]{1,0:T(8,128)(2,1)}, bf16[256,768]{1,0:T(8,128)(2,1)S(1)}, u32[]{:S(2)}, u32[]{:S(2)}) %collective-permute-start.32) | collective-permute-done | bytes 393248 | tf_op jit(solution)/shard_map/ppermute | solution.py:27
  190.2 2.5 %shard_map.238 = bf16[256,768]{1,0:T(8,128)(2,1)} custom-call(bf16[256,768]{1,0:T(8,128)(2,1)} %x_r.3, bf16[256,768]{1,0:T(8,128)(2,1)} %get-tuple-element.141.refs_0_, bf16[256,768]{1,0:T(8,128)(2,1)} %copy-done.20, bf16[256,768]{1,0:T(8,128)(2,1)} %copy-done.21, bf16[256,768]{1,0:T(8,128)(2,1)} %collective-permute-done.27.refs_3_), custom_call_target="tpu_custom_call" | custom-call | flops 2200000000 | bytes 1 | tf_op jit(solution)/shard_map/pallas_call | solution.py:97
  196.2 3.6 %all-to-all-start.1 = ((bf16[8,48,2304]{2,1,0:T(8,128)(2,1)}), bf16[8,48,2304]{2,1,0:T(8,128)(2,1)S(1)}, u32[]{:S(2)}, u32[]{:S(2)}) async-start(bf16[8,48,2304]{2,1,0:T(8,128)(2,1)} %get-tuple-element.170), calls=%async_computation.1 | async-start | bytes 3538944 | tf_op jit(solution)/shard_map/all_to_all | solution.py:1188
  202.2 4.8 %collective-permute-start.38 = (bf16[24,2304]{1,0:T(8,128)(2,1)}, bf16[24,2304]{1,0:T(8,128)(2,1)S(1)}, u32[]{:S(2)}, u32[]{:S(2)}) collective-permute-start(bf16[24,2304]{1,0:T(8,128)(2,1)} %get-tuple-element.156), channel_id=1, source_target_pairs={{0,1},{1,0},{2,3},{3,2},{4,5},{5,4},{6,7},{7,6},{8,9},{9,8},{10,11... | collective-permute-start | bytes 331784 | tf_op jit(solution)/shard_map/ppermute | solution.py:27
  210.3 2.7 %shard_map.239 = bf16[256,768]{1,0:T(8,128)(2,1)} custom-call(bf16[256,768]{1,0:T(8,128)(2,1)} %x_r.3, bf16[256,768]{1,0:T(8,128)(2,1)} %cot_r.1, f32[1,768]{1,0:T(1,128)} %get-tuple-element.145.gain_r, bf16[256,768]{1,0:T(8,128)(2,1)} %get-tuple-element.137.refs_0_, bf16[256,768]{1,0:T(8,128)(2,1)} %copy-done.14, bf16[256,768]{1,0:T(8,128)(2,1)} %copy-done.13), custom_call_target="tpu_custom_call" | custom-call | flops 110000000 | bytes 1 | tf_op jit(solution)/shard_map/pallas_call | solution.py:97
  213.0 3.4 %collective-permute-done.39.refs_2_ = bf16[24,2304]{1,0:T(8,128)(2,1)S(1)} collective-permute-done((bf16[24,2304]{1,0:T(8,128)(2,1)}, bf16[24,2304]{1,0:T(8,128)(2,1)S(1)}, u32[]{:S(2)}, u32[]{:S(2)}) %collective-permute-start.39) | collective-permute-done | bytes 110624 | tf_op jit(solution)/shard_map/ppermute | solution.py:27
  217.0 4.3 %shard_map.242 = (f32[3,24,3072]{2,1,0:T(8,128)}, f32[1,24]{1,0:T(1,128)}) custom-call(s32[3]{0:T(128)} %pad_add_fusion.meta, bf16[24,2304]{1,0:T(8,128)(2,1)} %get-tuple-element.155.refs_0_, bf16[24,2304]{1,0:T(8,128)(2,1)} %copy-done.35, bf16[24,2304]{1,0:T(8,128)(2,1)} %copy-done.36, bf16[24,2304]{1,0:T(8,128)(2,1)} %copy-done.37, ...), custom_call_target="tpu_custom_call" | custom-call | flops 14300000256 | bytes 1 | tf_op jit(solution)/shard_map/pallas_call | solution.py:97
  224.1 2.5 %shard_map.243 = f32[3,48,768]{2,1,0:T(8,128)} custom-call(bf16[8,48,2304]{2,1,0:T(8,128)(2,1)} %copy-done.1), custom_call_target="tpu_custom_call" | custom-call | flops 3300000000 | bytes 1 | tf_op jit(solution)/shard_map/pallas_call | solution.py:97
  (155 shorter events, 46.6 us)
Async XLA Ops:
  4.3 10.4 %collective-permute-start.3 = (bf16[24,2432]{1,0:T(8,128)(2,1)}, bf16[24,2432]{1,0:T(8,128)(2,1)S(1)}, u32[]{:S(2)}, u32[]{:S(2)}) collective-permute-start(bf16[24,2432]{1,0:T(8,128)(2,1)} %get-tuple-element.93), channel_id=1, source_target_pairs={{0,1},{1,0},{2,3},{3,2},{4,5},{5,4},{6,7},{7,6},{8,9},{9,8},{10,11... | collective-permute-start | bytes 350216 | tf_op jit(solution)/shard_map/ppermute | solution.py:27
  7.4 21.1 %collective-permute-start.4 = (bf16[24,2432]{1,0:T(8,128)(2,1)}, bf16[24,2432]{1,0:T(8,128)(2,1)S(1)}, u32[]{:S(2)}, u32[]{:S(2)}) collective-permute-start(bf16[24,2432]{1,0:T(8,128)(2,1)} %get-tuple-element.94), channel_id=1, source_target_pairs={{0,2},{1,3},{2,0},{3,1},{4,6},{5,7},{6,4},{7,5},{8,10},{9,11},{10,... | collective-permute-start | bytes 350216 | tf_op jit(solution)/shard_map/ppermute | solution.py:27
  10.0 18.5 %collective-permute-start.5 = (bf16[24,2432]{1,0:T(8,128)(2,1)}, bf16[24,2432]{1,0:T(8,128)(2,1)S(1)}, u32[]{:S(2)}, u32[]{:S(2)}) collective-permute-start(bf16[24,2432]{1,0:T(8,128)(2,1)} %get-tuple-element.95), channel_id=1, source_target_pairs={{0,3},{1,2},{2,1},{3,0},{4,7},{5,6},{6,5},{7,4},{8,11},{9,10},{10,... | collective-permute-start | bytes 350216 | tf_op jit(solution)/shard_map/ppermute | solution.py:27
  10.3 28.3 %collective-permute-start.1 = (bf16[272,768]{1,0:T(8,128)(2,1)S(1)}, bf16[272,768]{1,0:T(8,128)(2,1)S(1)}, u32[]{:S(2)}, u32[]{:S(2)}) collective-permute-start(bf16[272,768]{1,0:T(8,128)(2,1)S(1)} %pad_maximum_fusion.refs_0_), channel_id=1, source_target_pairs={{0,2},{1,3},{2,0},{3,1},{4,6},{5,7},{6,4},{7,5},{8,10},{9,11},{10,... | collective-permute-start | bytes 1253384 | tf_op jit(solution)/shard_map/ppermute | solution.py:27
  12.3 26.4 %collective-permute-start = (bf16[272,768]{1,0:T(8,128)(2,1)S(1)}, bf16[272,768]{1,0:T(8,128)(2,1)S(1)}, u32[]{:S(2)}, u32[]{:S(2)}) collective-permute-start(bf16[272,768]{1,0:T(8,128)(2,1)S(1)} %pad_maximum_fusion.refs_0_), channel_id=1, source_target_pairs={{0,1},{1,0},{2,3},{3,2},{4,5},{5,4},{6,7},{7,6},{8,9},{9,8},{10,11... | collective-permute-start | bytes 1253384 | tf_op jit(solution)/shard_map/ppermute | solution.py:27
  31.9 10.8 %collective-permute-start.9 = (bf16[128,1280]{1,0:T(8,128)(2,1)}, bf16[128,1280]{1,0:T(8,128)(2,1)S(1)}, u32[]{:S(2)}, u32[]{:S(2)}) collective-permute-start(bf16[128,1280]{1,0:T(8,128)(2,1)} %get-tuple-element.98.refs_4_.refs_0_), channel_id=1, source_target_pairs={{0,16},{4,20},{8,24},{12,28},{16,0},{20,4},{24,8},{28,12},{1,17},{... | collective-permute-start | bytes 983048 | tf_op jit(solution)/shard_map/ppermute | solution.py:27
  38.6 10.4 %collective-permute-start.2 = (bf16[272,768]{1,0:T(8,128)(2,1)S(1)}, bf16[272,768]{1,0:T(8,128)(2,1)S(1)}, u32[]{:S(2)}, u32[]{:S(2)}) collective-permute-start(bf16[272,768]{1,0:T(8,128)(2,1)S(1)} %collective-permute-done.1.refs_2_), channel_id=1, source_target_pairs={{0,1},{1,0},{2,3},{3,2},{4,5},{5,4},{6,7},{7,6},{8,9},{9,8},{10,11... | collective-permute-start | bytes 1253384 | tf_op jit(solution)/shard_map/ppermute | solution.py:27
  38.6 12.8 %collective-permute-start.6 = (bf16[128,1280]{1,0:T(8,128)(2,1)}, bf16[128,1280]{1,0:T(8,128)(2,1)S(1)}, u32[]{:S(2)}, u32[]{:S(2)}) collective-permute-start(bf16[128,1280]{1,0:T(8,128)(2,1)} %get-tuple-element.98.refs_4_.refs_0_), channel_id=1, source_target_pairs={{0,4},{4,0},{8,12},{12,8},{16,20},{20,16},{24,28},{28,24},{1,5},{5... | collective-permute-start | bytes 983048 | tf_op jit(solution)/shard_map/ppermute | solution.py:27
  42.7 9.8 %collective-permute-start.12 = (bf16[128,1280]{1,0:T(8,128)(2,1)S(1)}, bf16[128,1280]{1,0:T(8,128)(2,1)S(1)}, u32[]{:S(2)}, u32[]{:S(2)}) collective-permute-start(bf16[128,1280]{1,0:T(8,128)(2,1)S(1)} %collective-permute-done.11.refs_10_.refs_6_), channel_id=1, source_target_pairs={{0,4},{4,0},{8,12},{12,8},{16,20},{20,16},{24,28},{28,24},{1,5},{5... | collective-permute-start | bytes 983048 | tf_op jit(solution)/shard_map/ppermute | solution.py:27
  44.2 11.0 %collective-permute-start.8 = (bf16[128,1280]{1,0:T(8,128)(2,1)S(1)}, bf16[128,1280]{1,0:T(8,128)(2,1)S(1)}, u32[]{:S(2)}, u32[]{:S(2)}) collective-permute-start(bf16[128,1280]{1,0:T(8,128)(2,1)S(1)} %collective-permute-done.7.refs_6_.refs_2_), channel_id=1, source_target_pairs={{0,4},{4,0},{8,12},{12,8},{16,20},{20,16},{24,28},{28,24},{1,5},{5... | collective-permute-start | bytes 983048 | tf_op jit(solution)/shard_map/ppermute | solution.py:27
  49.0 16.3 %collective-permute-start.21 = (bf16[192,1152]{1,0:T(8,128)(2,1)}, bf16[192,1152]{1,0:T(8,128)(2,1)S(1)}, u32[]{:S(2)}, u32[]{:S(2)}) collective-permute-start(bf16[192,1152]{1,0:T(8,128)(2,1)} %get-tuple-element.105.refs_0_.refs_4_.refs_8_), channel_id=1, source_target_pairs={{0,24},{4,28},{8,16},{12,20},{16,8},{20,12},{24,0},{28,4},{1,25},{... | collective-permute-start | bytes 1327112 | tf_op jit(solution)/shard_map/ppermute | solution.py:27
  51.4 18.1 %collective-permute-start.19 = (bf16[192,1152]{1,0:T(8,128)(2,1)}, bf16[192,1152]{1,0:T(8,128)(2,1)S(1)}, u32[]{:S(2)}, u32[]{:S(2)}) collective-permute-start(bf16[192,1152]{1,0:T(8,128)(2,1)} %get-tuple-element.105.refs_0_.refs_4_.refs_8_), channel_id=1, source_target_pairs={{0,16},{4,20},{8,24},{12,28},{16,0},{20,4},{24,8},{28,12},{1,17},{... | collective-permute-start | bytes 1327112 | tf_op jit(solution)/shard_map/ppermute | solution.py:27
  51.9 17.7 %collective-permute-start.17 = (bf16[192,1152]{1,0:T(8,128)(2,1)}, bf16[192,1152]{1,0:T(8,128)(2,1)S(1)}, u32[]{:S(2)}, u32[]{:S(2)}) collective-permute-start(bf16[192,1152]{1,0:T(8,128)(2,1)} %get-tuple-element.105.refs_0_.refs_4_.refs_8_), channel_id=1, source_target_pairs={{0,8},{4,12},{8,0},{12,4},{16,24},{20,28},{24,16},{28,20},{1,9},{5... | collective-permute-start | bytes 1327112 | tf_op jit(solution)/shard_map/ppermute | solution.py:27
  52.5 20.2 %collective-permute-start.14 = (bf16[256,768]{1,0:T(8,128)(2,1)S(1)}, bf16[256,768]{1,0:T(8,128)(2,1)}, u32[]{:S(2)}, u32[]{:S(2)}) collective-permute-start(bf16[256,768]{1,0:T(8,128)(2,1)S(1)} %copy-done.12), channel_id=1, source_target_pairs={{0,2},{1,3},{2,0},{3,1},{4,6},{5,7},{6,4},{7,5},{8,10},{9,11},{10,... | collective-permute-start | bytes 1179656 | tf_op jit(solution)/shard_map/ppermute | solution.py:27
  56.0 17.8 %collective-permute-start.13 = (bf16[256,768]{1,0:T(8,128)(2,1)S(1)}, bf16[256,768]{1,0:T(8,128)(2,1)}, u32[]{:S(2)}, u32[]{:S(2)}) collective-permute-start(bf16[256,768]{1,0:T(8,128)(2,1)S(1)} %copy-done.12), channel_id=1, source_target_pairs={{0,1},{1,0},{2,3},{3,2},{4,5},{5,4},{6,7},{7,6},{8,9},{9,8},{10,11... | collective-permute-start | bytes 1179656 | tf_op jit(solution)/shard_map/ppermute | solution.py:27
  73.7 14.3 %collective-permute-start.15 = (bf16[256,768]{1,0:T(8,128)(2,1)}, bf16[256,768]{1,0:T(8,128)(2,1)}, u32[]{:S(2)}, u32[]{:S(2)}) collective-permute-start(bf16[256,768]{1,0:T(8,128)(2,1)} %collective-permute-done.14.refs_2_), channel_id=1, source_target_pairs={{0,1},{1,0},{2,3},{3,2},{4,5},{5,4},{6,7},{7,6},{8,9},{9,8},{10,11... | collective-permute-start | bytes 1179656 | tf_op jit(solution)/shard_map/ppermute | solution.py:27
  74.4 13.7 %collective-permute-start.23 = (bf16[80,1024]{1,0:T(8,128)(2,1)}, bf16[80,1024]{1,0:T(8,128)(2,1)S(1)}, u32[]{:S(2)}, u32[]{:S(2)}) collective-permute-start(bf16[80,1024]{1,0:T(8,128)(2,1)} %get-tuple-element.112), channel_id=1, source_target_pairs={{0,2},{1,3},{2,0},{3,1},{4,6},{5,7},{6,4},{7,5},{8,10},{9,11},{10,... | collective-permute-start | bytes 491528 | tf_op jit(solution)/shard_map/ppermute | solution.py:27
  134.6 19.5 %collective-permute-start.28 = (bf16[80,1024]{1,0:T(8,128)(2,1)}, bf16[80,1024]{1,0:T(8,128)(2,1)S(1)}, u32[]{:S(2)}, u32[]{:S(2)}) collective-permute-start(bf16[80,1024]{1,0:T(8,128)(2,1)} %get-tuple-element.120.refs_0_), channel_id=1, source_target_pairs={{0,1},{1,0},{2,3},{3,2},{4,5},{5,4},{6,7},{7,6},{8,9},{9,8},{10,11... | collective-permute-start | bytes 491528 | tf_op jit(solution)/shard_map/ppermute | solution.py:27
  136.4 19.9 %collective-permute-start.29 = (bf16[80,1024]{1,0:T(8,128)(2,1)}, bf16[80,1024]{1,0:T(8,128)(2,1)S(1)}, u32[]{:S(2)}, u32[]{:S(2)}) collective-permute-start(bf16[80,1024]{1,0:T(8,128)(2,1)} %get-tuple-element.120.refs_0_), channel_id=1, source_target_pairs={{0,2},{1,3},{2,0},{3,1},{4,6},{5,7},{6,4},{7,5},{8,10},{9,11},{10,... | collective-permute-start | bytes 491528 | tf_op jit(solution)/shard_map/ppermute | solution.py:27
  137.0 19.3 %collective-permute-start.30 = (bf16[80,1024]{1,0:T(8,128)(2,1)}, bf16[80,1024]{1,0:T(8,128)(2,1)S(1)}, u32[]{:S(2)}, u32[]{:S(2)}) collective-permute-start(bf16[80,1024]{1,0:T(8,128)(2,1)} %get-tuple-element.120.refs_0_), channel_id=1, source_target_pairs={{0,3},{1,2},{2,1},{3,0},{4,7},{5,6},{6,5},{7,4},{8,11},{9,10},{10,... | collective-permute-start | bytes 491528 | tf_op jit(solution)/shard_map/ppermute | solution.py:27
  139.0 41.4 %collective-permute-start.25 = (bf16[256,768]{1,0:T(8,128)(2,1)}, bf16[256,768]{1,0:T(8,128)(2,1)S(1)}, u32[]{:S(2)}, u32[]{:S(2)}) collective-permute-start(bf16[256,768]{1,0:T(8,128)(2,1)} %get-tuple-element.117), channel_id=1, source_target_pairs={{0,1},{1,0},{2,3},{3,2},{4,5},{5,4},{6,7},{7,6},{8,9},{9,8},{10,11... | collective-permute-start | bytes 1179656 | tf_op jit(solution)/shard_map/ppermute | solution.py:27
  139.9 40.6 %collective-permute-start.26 = (bf16[256,768]{1,0:T(8,128)(2,1)}, bf16[256,768]{1,0:T(8,128)(2,1)S(1)}, u32[]{:S(2)}, u32[]{:S(2)}) collective-permute-start(bf16[256,768]{1,0:T(8,128)(2,1)} %get-tuple-element.118), channel_id=1, source_target_pairs={{0,2},{1,3},{2,0},{3,1},{4,6},{5,7},{6,4},{7,5},{8,10},{9,11},{10,... | collective-permute-start | bytes 1179656 | tf_op jit(solution)/shard_map/ppermute | solution.py:27
  150.3 42.3 %all-to-all-start = ((bf16[8,96,1152]{2,1,0:T(8,128)(2,1)}), bf16[8,96,1152]{2,1,0:T(8,128)(2,1)S(1)}, u32[]{:S(2)}, u32[]{:S(2)}) async-start(bf16[8,96,1152]{2,1,0:T(8,128)(2,1)} %get-tuple-element.153), calls=%async_computation | async-start | bytes 3538944 | tf_op jit(solution)/shard_map/all_to_all | solution.py:1099
  154.1 26.3 %collective-permute-start.27 = (bf16[256,768]{1,0:T(8,128)(2,1)}, bf16[256,768]{1,0:T(8,128)(2,1)}, u32[]{:S(2)}, u32[]{:S(2)}) collective-permute-start(bf16[256,768]{1,0:T(8,128)(2,1)} %get-tuple-element.119), channel_id=1, source_target_pairs={{0,3},{1,2},{2,1},{3,0},{4,7},{5,6},{6,5},{7,4},{8,11},{9,10},{10,... | collective-permute-start | bytes 1179656 | tf_op jit(solution)/shard_map/ppermute | solution.py:27
  175.4 12.2 %collective-permute-start.32 = (bf16[256,768]{1,0:T(8,128)(2,1)}, bf16[256,768]{1,0:T(8,128)(2,1)S(1)}, u32[]{:S(2)}, u32[]{:S(2)}) collective-permute-start(bf16[256,768]{1,0:T(8,128)(2,1)} %get-tuple-element.148), channel_id=1, source_target_pairs={{0,1},{1,0},{2,3},{3,2},{4,5},{5,4},{6,7},{7,6},{8,9},{9,8},{10,11... | collective-permute-start | bytes 1179656 | tf_op jit(solution)/shard_map/ppermute | solution.py:27
  175.5 33.9 %collective-permute-start.34 = (bf16[256,768]{1,0:T(8,128)(2,1)}, bf16[256,768]{1,0:T(8,128)(2,1)S(1)}, u32[]{:S(2)}, u32[]{:S(2)}) collective-permute-start(bf16[256,768]{1,0:T(8,128)(2,1)} %get-tuple-element.149), channel_id=1, source_target_pairs={{0,1},{1,0},{2,3},{3,2},{4,5},{5,4},{6,7},{7,6},{8,9},{9,8},{10,11... | collective-permute-start | bytes 1179656 | tf_op jit(solution)/shard_map/ppermute | solution.py:27
  180.5 19.4 %collective-permute-start.35 = (bf16[144,1152]{1,0:T(8,128)(2,1)}, bf16[144,1152]{1,0:T(8,128)(2,1)}, u32[]{:S(2)}, u32[]{:S(2)}) collective-permute-start(bf16[144,1152]{1,0:T(8,128)(2,1)} %get-tuple-element.150), channel_id=1, source_target_pairs={{0,8},{4,12},{8,0},{12,4},{16,24},{20,28},{24,16},{28,20},{1,9},{5... | collective-permute-start | bytes 995336 | tf_op jit(solution)/shard_map/ppermute | solution.py:27
  182.2 17.6 %collective-permute-start.36 = (bf16[144,1152]{1,0:T(8,128)(2,1)}, bf16[144,1152]{1,0:T(8,128)(2,1)}, u32[]{:S(2)}, u32[]{:S(2)}) collective-permute-start(bf16[144,1152]{1,0:T(8,128)(2,1)} %get-tuple-element.151), channel_id=1, source_target_pairs={{0,16},{4,20},{8,24},{12,28},{16,0},{20,4},{24,8},{28,12},{1,17},{... | collective-permute-start | bytes 995336 | tf_op jit(solution)/shard_map/ppermute | solution.py:27
  183.7 16.1 %collective-permute-start.37 = (bf16[144,1152]{1,0:T(8,128)(2,1)}, bf16[144,1152]{1,0:T(8,128)(2,1)}, u32[]{:S(2)}, u32[]{:S(2)}) collective-permute-start(bf16[144,1152]{1,0:T(8,128)(2,1)} %get-tuple-element.152), channel_id=1, source_target_pairs={{0,24},{4,28},{8,16},{12,20},{16,8},{20,12},{24,0},{28,4},{1,25},{... | collective-permute-start | bytes 995336 | tf_op jit(solution)/shard_map/ppermute | solution.py:27
  187.7 21.7 %collective-permute-start.33 = (bf16[256,768]{1,0:T(8,128)(2,1)S(1)}, bf16[256,768]{1,0:T(8,128)(2,1)S(1)}, u32[]{:S(2)}, u32[]{:S(2)}) collective-permute-start(bf16[256,768]{1,0:T(8,128)(2,1)S(1)} %add_convert_fusion), channel_id=1, source_target_pairs={{0,2},{1,3},{2,0},{3,1},{4,6},{5,7},{6,4},{7,5},{8,10},{9,11},{10,... | collective-permute-start | bytes 1179656 | tf_op jit(solution)/shard_map/ppermute | solution.py:27
  196.2 26.7 %all-to-all-start.1 = ((bf16[8,48,2304]{2,1,0:T(8,128)(2,1)}), bf16[8,48,2304]{2,1,0:T(8,128)(2,1)S(1)}, u32[]{:S(2)}, u32[]{:S(2)}) async-start(bf16[8,48,2304]{2,1,0:T(8,128)(2,1)} %get-tuple-element.170), calls=%async_computation.1 | async-start | bytes 3538944 | tf_op jit(solution)/shard_map/all_to_all | solution.py:1188
  202.2 10.8 %collective-permute-start.38 = (bf16[24,2304]{1,0:T(8,128)(2,1)}, bf16[24,2304]{1,0:T(8,128)(2,1)S(1)}, u32[]{:S(2)}, u32[]{:S(2)}) collective-permute-start(bf16[24,2304]{1,0:T(8,128)(2,1)} %get-tuple-element.156), channel_id=1, source_target_pairs={{0,1},{1,0},{2,3},{3,2},{4,5},{5,4},{6,7},{7,6},{8,9},{9,8},{10,11... | collective-permute-start | bytes 331784 | tf_op jit(solution)/shard_map/ppermute | solution.py:27
  (50 other events, 348.2 us)

commit v5 on v4

--- a/solution.py
+++ b/solution.py
@@ -87,13 +87,13 @@
     return lax.dot_general(a, b, (((ca,), (cb,)), ((), ())), preferred_element_type=f32)
 
 
-def call(kernel, outs, ins, scratch=(), us=1.0):
+def call(kernel, outs, ins, scratch=(), us=1.0, small=False):
     spaces = {"v": pltpu.VMEM, "s": pltpu.SMEM, "a": pl.ANY}
     held = [(array.shape, array.dtype) for array, space in ins if space == "v"]
     held += [(shape, dtype) for shape, dtype, space in outs if space == "v"]
     held += [(part.shape, part.dtype) for part in scratch if part.memory_space == pltpu.VMEM]
     need = sum(math.prod(shape) * jnp.dtype(dtype).itemsize for shape, dtype in held)
-    need = VMEM_LIMIT
+    need = min(need + need // 4 + VMEM_SPARE, VMEM_LIMIT) if small else VMEM_LIMIT
     return pl.pallas_call(
         kernel,
         out_shape=[jax.ShapeDtypeStruct(shape, dtype) for shape, dtype, _ in outs],
@@ -1151,13 +1151,13 @@
         mixed_kernel,
         [((own, d), bf16, "v")],
         [(tokens, "v")] + [(p, "v") for p in after(tuple(branch_pieces), pieces_b[0])],
-        us=2.0,
+        us=2.0, small=True,
     )[0]
     gate_sum = call(
         total_gate_kernel,
         [((in_rows, width), bf16, "v")],
         [(after(gate_blocks, mixed_out, dn_kept), "v")],
-        us=2.0,
+        us=2.0, small=True,
     )[0]
     res = call(
         functools.partial(total_b_kernel, nar, chips, er, rank, taps, ns),
@@ -1173,7 +1173,7 @@
         ],
         [(meta, "s")] + [(p, "v") for p in pieces_b] + [(gate_sum, "v")],
         [pltpu.VMEM((nar, dr, 2 * width), bf16)],
-        us=3.0,
+        us=3.0, small=True,
     )
     back_parts = res[:nar]
     grad_w_x, grad_w_dt, grad_dt_bias, grad_conv_w, grad_conv_b, grad_log, grad_skip = res[nar:]
@@ -1183,7 +1183,7 @@
         [((own, d), bf16, "v")],
         [(tokens, "v"), (cotangent, "v"), (gain_full, "v")]
         + [(p, "v") for p in dn_pieces],
-        us=0.1,
+        us=0.1, small=True,
     )[0]
     w_out_blocks = lax.all_to_all(after(w_out_blocks, gate_sum), "wide", 0, 0)
     grad_w_in, grad_gain = call(
@@ -1197,13 +1197,13 @@
             pltpu.SemaphoreType.DMA(()),
             pltpu.SemaphoreType.DMA((MODS,)),
         ],
-        us=13.0,
+        us=13.0, small=True,
     )
     grad_w_out = call(
         functools.partial(total_out_kernel, er),
         [((MODS, er, d), f32, "v")],
         [(after(w_out_blocks, grad_gain), "v")],
-        us=3.0,
+        us=3.0, small=True,
     )[0]
     grad_w_in, grad_w_out = grad_w_in.transpose(1, 0, 2), grad_w_out.transpose(1, 0, 2)
     grad_w_x, grad_w_dt = grad_w_x.transpose(1, 0, 2), grad_w_dt.transpose(1, 0, 2)

time: 227 us -> 223 us (0.982)
  Pallas kernels: 105 us -> 97.3 us
  waiting for transfers between devices: 53.3 us -> 56.8 us
    pallas_call x15, Pallas kernels: 105 us -> 97.3 us  [call(): pl.pallas_call(kernel, out_shape=[jax.ShapeDtypeStruct(shape, dtype) for...]
    ppermute x41, waiting for transfers between devices: 51.8 us -> 56.4 us  [swap(): return lax.ppermute(block, axis, [(i, i ^ flip) for i in range(count)])]
    unnamed x78 -> x76, local copies, waits for them, and re-layouts: 7.22 us -> 5.97 us
  transfers between devices with their start and end apart: 43 -> 43, of which waited for: 13 -> 15; matrix products, arithmetic and copies ran while one was open for 0% -> 1% of each run, Pallas kernels for 27% -> 25%
where the time goes in v5:
time: 223 us
  Pallas kernels  97.3 us (44%)
  starting transfers between devices  57.4 us (26%)
  waiting for transfers between devices  56.8 us (25%)
  local copies, waits for them, and re-layouts  6.09 us (3%)
  other arithmetic  3.45 us (2%)
    pallas_call x15, Pallas kernels, call(): pl.pallas_call(kernel, out_shape=[jax.ShapeDtypeStruct(shape, dtype) for...  97.3 us
    ppermute x41, waiting for transfers between devices, swap(): return lax.ppermute(block, axis, [(i, i ^ flip) for i in range(count)])  56.4 us
    ppermute x41, starting transfers between devices, swap(): return lax.ppermute(block, axis, [(i, i ^ flip) for i in range(count)])  49.8 us
    unnamed x76, local copies, waits for them, and re-layouts  5.97 us
  transfers between devices with their start and end apart: 43, of which 15 were waited for; matrix products, arithmetic and copies ran while one was open for 1% of the time, Pallas kernels for 25%

profile of v5, /device:TPU:0, one launch (start us, length us, event | category | flops | bytes accessed | tf_op | source)
XLA Modules:
  0.0 222.8 jit_solution(14033792773470746371)
XLA Ops:
  1.9 2.5 %shard_map.229 = (bf16[24,2432]{1,0:T(8,128)(2,1)}, bf16[24,2432]{1,0:T(8,128)(2,1)}, bf16[24,2432]{1,0:T(8,128)(2,1)}, bf16[24,2432]{1,0:T(8,128)(2,1)}, bf16[3...) custom-call(s32[3]{0:T(128)} %pad_add_fusion.meta, bf16[3,24,3072]{2,1,0:T(8,128)(2,1)} %bitcast.20, bf16[1,24]{1,0:T(2,128)(2,1)} %bitcast.22, ...), custom_call_target="tpu_custom_call" | custom-call | flops 3300000000 | bytes 1 | tf_op jit(solution)/shard_map/pallas_call | solution.py:97
  4.3 3.1 %collective-permute-start.3 = (bf16[24,2432]{1,0:T(8,128)(2,1)}, bf16[24,2432]{1,0:T(8,128)(2,1)S(1)}, u32[]{:S(2)}, u32[]{:S(2)}) collective-permute-start(bf16[24,2432]{1,0:T(8,128)(2,1)} %get-tuple-element.93), channel_id=1, source_target_pairs={{0,1},{1,0},{2,3},{3,2},{4,5},{5,4},{6,7},{7,6},{8,9},{9,8},{10,11... | collective-permute-start | bytes 350216 | tf_op jit(solution)/shard_map/ppermute | solution.py:27
  7.4 2.6 %collective-permute-start.4 = (bf16[24,2432]{1,0:T(8,128)(2,1)}, bf16[24,2432]{1,0:T(8,128)(2,1)S(1)}, u32[]{:S(2)}, u32[]{:S(2)}) collective-permute-start(bf16[24,2432]{1,0:T(8,128)(2,1)} %get-tuple-element.94), channel_id=1, source_target_pairs={{0,2},{1,3},{2,0},{3,1},{4,6},{5,7},{6,4},{7,5},{8,10},{9,11},{10,... | collective-permute-start | bytes 350216 | tf_op jit(solution)/shard_map/ppermute | solution.py:27
  12.3 2.5 %collective-permute-start = (bf16[272,768]{1,0:T(8,128)(2,1)S(1)}, bf16[272,768]{1,0:T(8,128)(2,1)S(1)}, u32[]{:S(2)}, u32[]{:S(2)}) collective-permute-start(bf16[272,768]{1,0:T(8,128)(2,1)S(1)} %pad_maximum_fusion.refs_0_), channel_id=1, source_target_pairs={{0,1},{1,0},{2,3},{3,2},{4,5},{5,4},{6,7},{7,6},{8,9},{9,8},{10,11... | collective-permute-start | bytes 1253384 | tf_op jit(solution)/shard_map/ppermute | solution.py:27
  14.8 13.7 %collective-permute-done.4.refs_2_ = bf16[24,2432]{1,0:T(8,128)(2,1)S(1)} collective-permute-done((bf16[24,2432]{1,0:T(8,128)(2,1)}, bf16[24,2432]{1,0:T(8,128)(2,1)S(1)}, u32[]{:S(2)}, u32[]{:S(2)}) %collective-permute-start.4) | collective-permute-done | bytes 116768 | tf_op jit(solution)/shard_map/ppermute | solution.py:27
  29.2 2.7 %shard_map.230 = (bf16[128,1280]{1,0:T(8,128)(2,1)}, bf16[192,1152]{1,0:T(8,128)(2,1)}) custom-call(s32[3]{0:T(128)} %pad_add_fusion.meta, bf16[24,2432]{1,0:T(8,128)(2,1)} %get-tuple-element.92.refs_0_, bf16[24,2432]{1,0:T(8,128)(2,1)} %copy-done.34, bf16[24,2432]{1,0:T(8,128)(2,1)} %copy-done.35, bf16[24,2432]{1,0:T(8,128)(2,1)} %copy-done.36, ...), custom_call_target="tpu_custom_call" | custom-call | flops 2200000000 | bytes 1 | tf_op jit(solution)/shard_map/pallas_call | solution.py:97
  35.4 3.3 %collective-permute-done.1.refs_2_ = bf16[272,768]{1,0:T(8,128)(2,1)S(1)} collective-permute-done((bf16[272,768]{1,0:T(8,128)(2,1)S(1)}, bf16[272,768]{1,0:T(8,128)(2,1)S(1)}, u32[]{:S(2)}, u32[]{:S(2)}) %collective-permute-start.1) | collective-permute-done | bytes 417824 | tf_op jit(solution)/shard_map/ppermute | solution.py:27
  38.7 3.9 %collective-permute-done.9.refs_8_.refs_4_ = bf16[128,1280]{1,0:T(8,128)(2,1)S(1)} collective-permute-done((bf16[128,1280]{1,0:T(8,128)(2,1)}, bf16[128,1280]{1,0:T(8,128)(2,1)S(1)}, u32[]{:S(2)}, u32[]{:S(2)}) %collective-permute-start.9) | collective-permute-done | bytes 327712 | tf_op jit(solution)/shard_map/ppermute | solution.py:27
  44.2 4.9 %collective-permute-done.2.refs_3_ = bf16[272,768]{1,0:T(8,128)(2,1)} collective-permute-done((bf16[272,768]{1,0:T(8,128)(2,1)S(1)}, bf16[272,768]{1,0:T(8,128)(2,1)}, u32[]{:S(2)}, u32[]{:S(2)}) %collective-permute-start.2) | collective-permute-done | bytes 417824 | tf_op jit(solution)/shard_map/ppermute | solution.py:27
  49.1 2.4 %collective-permute-start.21 = (bf16[192,1152]{1,0:T(8,128)(2,1)}, bf16[192,1152]{1,0:T(8,128)(2,1)S(1)}, u32[]{:S(2)}, u32[]{:S(2)}) collective-permute-start(bf16[192,1152]{1,0:T(8,128)(2,1)} %get-tuple-element.105.refs_0_.refs_4_.refs_8_), channel_id=1, source_target_pairs={{0,24},{4,28},{8,16},{12,20},{16,8},{20,12},{24,0},{28,4},{1,25},{... | collective-permute-start | bytes 1327112 | tf_op jit(solution)/shard_map/ppermute | solution.py:27
  52.7 2.6 %collective-permute-start.14 = (bf16[256,768]{1,0:T(8,128)(2,1)S(1)}, bf16[256,768]{1,0:T(8,128)(2,1)}, u32[]{:S(2)}, u32[]{:S(2)}) collective-permute-start(bf16[256,768]{1,0:T(8,128)(2,1)S(1)} %copy-done.1), channel_id=1, source_target_pairs={{0,2},{1,3},{2,0},{3,1},{4,6},{5,7},{6,4},{7,5},{8,10},{9,11},{10,... | collective-permute-start | bytes 1179656 | tf_op jit(solution)/shard_map/ppermute | solution.py:27
  56.6 8.7 %shard_map.231 = (bf16[1024,768]{1,0:T(8,128)(2,1)}, f32[1024,384]{1,0:T(8,128)}, f32[1024,384]{1,0:T(8,128)}, bf16[1024,384]{1,0:T(8,128)(2,1)}, bf16[80,1024]{...) custom-call(s32[3]{0:T(128)} %pad_add_fusion.meta, ...), custom_call_target="tpu_custom_call" | custom-call | flops 9900000256 | bytes 1 | tf_op jit(solution)/shard_map/pallas_call | solution.py:97
  65.4 4.2 %collective-permute-done.19.refs_4_.refs_8_.refs_12_ = bf16[192,1152]{1,0:T(8,128)(2,1)S(1)} collective-permute-done((bf16[192,1152]{1,0:T(8,128)(2,1)}, bf16[192,1152]{1,0:T(8,128)(2,1)S(1)}, u32[]{:S(2)}, u32[]{:S(2)}) %collective-permute-start.19) | collective-permute-done | bytes 442400 | tf_op jit(solution)/shard_map/ppermute | solution.py:27
  70.1 2.6 %collective-permute-done.14.refs_2_ = bf16[256,768]{1,0:T(8,128)(2,1)} collective-permute-done((bf16[256,768]{1,0:T(8,128)(2,1)S(1)}, bf16[256,768]{1,0:T(8,128)(2,1)}, u32[]{:S(2)}, u32[]{:S(2)}) %collective-permute-start.14) | collective-permute-done | bytes 393248 | tf_op jit(solution)/shard_map/ppermute | solution.py:27
  76.5 5.4 %shard_map.232 = (f32[1024,384]{1,0:T(8,128)}, f32[1024,384]{1,0:T(8,128)}) custom-call(s32[3]{0:T(128)} %pad_add_fusion.meta, s32[8]{0:T(128)} %get-tuple-element.99.kinds, bf16[192,1152]{1,0:T(8,128)(2,1)} %get-tuple-element.105.refs_0_.refs_4_.refs_8_, bf16[192,1152]{1,0:T(8,128)(2,1)} %copy-done.16, bf16[192,1152]{1,0:T(8,128)(2,1)} %copy-done.15, ...), custom_call_target="tpu_custom_call" | custom-call | flops 110000000 | bytes 1 | tf_op jit(solution)/shard_map/pallas_call | solution.py:97
  81.9 6.2 %collective-permute-done.15.refs_3_ = bf16[256,768]{1,0:T(8,128)(2,1)} collective-permute-done((bf16[256,768]{1,0:T(8,128)(2,1)}, bf16[256,768]{1,0:T(8,128)(2,1)}, u32[]{:S(2)}, u32[]{:S(2)}) %collective-permute-start.15) | collective-permute-done | bytes 393248 | tf_op jit(solution)/shard_map/ppermute | solution.py:27
  88.2 2.4 %collective-permute-start.24 = (bf16[80,1024]{1,0:T(8,128)(2,1)S(1)}, bf16[80,1024]{1,0:T(8,128)(2,1)S(1)}, u32[]{:S(2)}, u32[]{:S(2)}) collective-permute-start(bf16[80,1024]{1,0:T(8,128)(2,1)S(1)} %add_convert_fusion.2), channel_id=1, source_target_pairs={{0,1},{1,0},{2,3},{3,2},{4,5},{5,4},{6,7},{7,6},{8,9},{9,8},{10,11... | collective-permute-start | bytes 491528 | tf_op jit(solution)/shard_map/ppermute | solution.py:27
  90.6 4.0 %collective-permute-done.24 = bf16[80,1024]{1,0:T(8,128)(2,1)S(1)} collective-permute-done((bf16[80,1024]{1,0:T(8,128)(2,1)S(1)}, bf16[80,1024]{1,0:T(8,128)(2,1)S(1)}, u32[]{:S(2)}, u32[]{:S(2)}) %collective-permute-start.24) | collective-permute-done | bytes 163872 | tf_op jit(solution)/shard_map/ppermute | solution.py:27
  95.4 39.2 %shard_map.233 = (bf16[256,768]{1,0:T(8,128)(2,1)}, bf16[256,768]{1,0:T(8,128)(2,1)}, bf16[256,768]{1,0:T(8,128)(2,1)}, bf16[256,768]{1,0:T(8,128)(2,1)}, bf16[1...) custom-call(s32[3]{0:T(128)} %pad_add_fusion.meta, ...), custom_call_target="tpu_custom_call" | custom-call | flops 44000002048 | bytes 1 | tf_op jit(solution)/shard_map/pallas_call | solution.py:97
  141.3 8.9 %shard_map.234 = (bf16[1024,384]{1,0:T(8,128)(2,1)}, bf16[8,96,1152]{2,1,0:T(8,128)(2,1)}, bf16[8,48,2304]{2,1,0:T(8,128)(2,1)}, f32[176,384]{1,0:T(8,128)}) custom-call(s32[3]{0:T(128)} %pad_add_fusion.meta, s32[8]{0:T(128)} %get-tuple-element.99.kinds, bf16[1024,384]{1,0:T(8,128)(2,1)} %get-tuple-element.122.refs_0_, ...), custom_call_target="tpu_custom_call" | custom-call | flops 9900000256 | bytes 1 | tf_op jit(solution)/shard_map/pallas_call | solution.py:97
  150.2 3.8 %all-to-all-start = ((bf16[8,96,1152]{2,1,0:T(8,128)(2,1)}), bf16[8,96,1152]{2,1,0:T(8,128)(2,1)S(1)}, u32[]{:S(2)}, u32[]{:S(2)}) async-start(bf16[8,96,1152]{2,1,0:T(8,128)(2,1)} %get-tuple-element.153), calls=%async_computation | async-start | bytes 3538944 | tf_op jit(solution)/shard_map/all_to_all | solution.py:1099
  154.1 2.1 collective-permute-start.27
  156.9 10.6 %shard_map.235 = (bf16[1024,384]{1,0:T(8,128)(2,1)}, bf16[4,144,1152]{2,1,0:T(8,128)(2,1)}, bf16[4,144,1152]{2,1,0:T(8,128)(2,1)}) custom-call(s32[3]{0:T(128)} %pad_add_fusion.meta, s32[8]{0:T(128)} %get-tuple-element.99.kinds, bf16[80,1024]{1,0:T(8,128)(2,1)} %get-tuple-element.120.refs_0_, bf16[80,1024]{1,0:T(8,128)(2,1)} %copy-done.31, ...), custom_call_target="tpu_custom_call" | custom-call | flops 13200000000 | bytes 1 | tf_op jit(solution)/shard_map/pallas_call | solution.py:97
  167.6 7.7 %shard_map.236 = (bf16[256,768]{1,0:T(8,128)(2,1)}, bf16[256,768]{1,0:T(8,128)(2,1)}, bf16[256,768]{1,0:T(8,128)(2,1)}, bf16[256,768]{1,0:T(8,128)(2,1)}) custom-call(s32[3]{0:T(128)} %pad_add_fusion.meta, s32[8]{0:T(128)} %get-tuple-element.99.kinds, bf16[128,1280]{1,0:T(8,128)(2,1)} %get-tuple-element.98.refs_4_.refs_0_, bf16[128,1280]{1,0:T(8,128)(2,1)} %copy-done.27, ...), custom_call_target="tpu_custom_call" | custom-call | flops 32999999488 | bytes 1 | tf_op jit(solution)/shard_map/pallas_call | solution.py:97
  177.4 3.0 %shard_map.237 = (bf16[144,1152]{1,0:T(8,128)(2,1)}, bf16[144,1152]{1,0:T(8,128)(2,1)}, bf16[144,1152]{1,0:T(8,128)(2,1)}, bf16[144,1152]{1,0:T(8,128)(2,1)}) custom-call(s32[3]{0:T(128)} %pad_add_fusion.meta, bf16[4,144,1152]{2,1,0:T(8,128)(2,1)} %get-tuple-element.138.same, bf16[4,144,1152]{2,1,0:T(8,128)(2,1)} %collective-permute-done.31.peer), custom_call_target="tpu_custom_call" | custom-call | flops 3300000000 | bytes 1 | tf_op jit(solution)/shard_map/pallas_call | solution.py:97
  184.7 3.0 %collective-permute-done.32 = bf16[256,768]{1,0:T(8,128)(2,1)} collective-permute-done((bf16[256,768]{1,0:T(8,128)(2,1)}, bf16[256,768]{1,0:T(8,128)(2,1)}, u32[]{:S(2)}, u32[]{:S(2)}) %collective-permute-start.32) | collective-permute-done | bytes 393248 | tf_op jit(solution)/shard_map/ppermute | solution.py:27
  189.6 2.1 collective-permute-start.33
  195.0 3.7 %all-to-all-start.1 = ((bf16[8,48,2304]{2,1,0:T(8,128)(2,1)}), bf16[8,48,2304]{2,1,0:T(8,128)(2,1)S(1)}, u32[]{:S(2)}, u32[]{:S(2)}) async-start(bf16[8,48,2304]{2,1,0:T(8,128)(2,1)} %get-tuple-element.170), calls=%async_computation.1 | async-start | bytes 3538944 | tf_op jit(solution)/shard_map/all_to_all | solution.py:1188
  201.8 5.1 %collective-permute-start.38 = (bf16[24,2304]{1,0:T(8,128)(2,1)S(1)}, bf16[24,2304]{1,0:T(8,128)(2,1)S(1)}, u32[]{:S(2)}, u32[]{:S(2)}) collective-permute-start(bf16[24,2304]{1,0:T(8,128)(2,1)S(1)} %get-tuple-element.156), channel_id=1, source_target_pairs={{0,1},{1,0},{2,3},{3,2},{4,5},{5,4},{6,7},{7,6},{8,9},{9,8},{10,11... | collective-permute-start | bytes 331784 | tf_op jit(solution)/shard_map/ppermute | solution.py:27
  206.9 2.4 %collective-permute-start.40 = (bf16[24,2304]{1,0:T(8,128)(2,1)S(1)}, bf16[24,2304]{1,0:T(8,128)(2,1)S(1)}, u32[]{:S(2)}, u32[]{:S(2)}) collective-permute-start(bf16[24,2304]{1,0:T(8,128)(2,1)S(1)} %get-tuple-element.158), channel_id=1, source_target_pairs={{0,3},{1,2},{2,1},{3,0},{4,7},{5,6},{6,5},{7,4},{8,11},{9,10},{10,... | collective-permute-start | bytes 331784 | tf_op jit(solution)/shard_map/ppermute | solution.py:27
  209.4 6.6 %collective-permute-done.33.refs_1_ = bf16[256,768]{1,0:T(8,128)(2,1)S(1)} collective-permute-done((bf16[256,768]{1,0:T(8,128)(2,1)}, bf16[256,768]{1,0:T(8,128)(2,1)S(1)}, u32[]{:S(2)}, u32[]{:S(2)}) %collective-permute-start.33) | collective-permute-done | bytes 393248 | tf_op jit(solution)/shard_map/ppermute | solution.py:27
  218.2 3.3 %shard_map.242 = (f32[3,24,3072]{2,1,0:T(8,128)}, f32[1,24]{1,0:T(1,128)}) custom-call(s32[3]{0:T(128)S(1)} %copy-done.5, bf16[24,2304]{1,0:T(8,128)(2,1)S(1)} %get-tuple-element.155.refs_0_, bf16[24,2304]{1,0:T(8,128)(2,1)S(1)} %collective-permute-done.38.refs_1_, bf16[24,2304]{1,0:T(8,128)(2,1)S(1)} %collective-permute-done.39.refs_2_, ...), custom_call_target="tpu_custom_call" | custom-call | flops 14300000256 | bytes 1 | tf_op jit(solution)/shard_map/pallas_call | solution.py:97
  (153 shorter events, 41.6 us)
Async XLA Ops:
  7.4 21.1 %collective-permute-start.4 = (bf16[24,2432]{1,0:T(8,128)(2,1)}, bf16[24,2432]{1,0:T(8,128)(2,1)S(1)}, u32[]{:S(2)}, u32[]{:S(2)}) collective-permute-start(bf16[24,2432]{1,0:T(8,128)(2,1)} %get-tuple-element.94), channel_id=1, source_target_pairs={{0,2},{1,3},{2,0},{3,1},{4,6},{5,7},{6,4},{7,5},{8,10},{9,11},{10,... | collective-permute-start | bytes 350216 | tf_op jit(solution)/shard_map/ppermute | solution.py:27
  10.0 18.5 %collective-permute-start.5 = (bf16[24,2432]{1,0:T(8,128)(2,1)}, bf16[24,2432]{1,0:T(8,128)(2,1)S(1)}, u32[]{:S(2)}, u32[]{:S(2)}) collective-permute-start(bf16[24,2432]{1,0:T(8,128)(2,1)} %get-tuple-element.95), channel_id=1, source_target_pairs={{0,3},{1,2},{2,1},{3,0},{4,7},{5,6},{6,5},{7,4},{8,11},{9,10},{10,... | collective-permute-start | bytes 350216 | tf_op jit(solution)/shard_map/ppermute | solution.py:27
  10.3 28.3 %collective-permute-start.1 = (bf16[272,768]{1,0:T(8,128)(2,1)S(1)}, bf16[272,768]{1,0:T(8,128)(2,1)S(1)}, u32[]{:S(2)}, u32[]{:S(2)}) collective-permute-start(bf16[272,768]{1,0:T(8,128)(2,1)S(1)} %pad_maximum_fusion.refs_0_), channel_id=1, source_target_pairs={{0,2},{1,3},{2,0},{3,1},{4,6},{5,7},{6,4},{7,5},{8,10},{9,11},{10,... | collective-permute-start | bytes 1253384 | tf_op jit(solution)/shard_map/ppermute | solution.py:27
  12.3 26.4 %collective-permute-start = (bf16[272,768]{1,0:T(8,128)(2,1)S(1)}, bf16[272,768]{1,0:T(8,128)(2,1)S(1)}, u32[]{:S(2)}, u32[]{:S(2)}) collective-permute-start(bf16[272,768]{1,0:T(8,128)(2,1)S(1)} %pad_maximum_fusion.refs_0_), channel_id=1, source_target_pairs={{0,1},{1,0},{2,3},{3,2},{4,5},{5,4},{6,7},{7,6},{8,9},{9,8},{10,11... | collective-permute-start | bytes 1253384 | tf_op jit(solution)/shard_map/ppermute | solution.py:27
  31.9 10.8 %collective-permute-start.9 = (bf16[128,1280]{1,0:T(8,128)(2,1)}, bf16[128,1280]{1,0:T(8,128)(2,1)S(1)}, u32[]{:S(2)}, u32[]{:S(2)}) collective-permute-start(bf16[128,1280]{1,0:T(8,128)(2,1)} %get-tuple-element.98.refs_4_.refs_0_), channel_id=1, source_target_pairs={{0,16},{4,20},{8,24},{12,28},{16,0},{20,4},{24,8},{28,12},{1,17},{... | collective-permute-start | bytes 983048 | tf_op jit(solution)/shard_map/ppermute | solution.py:27
  38.6 10.5 %collective-permute-start.2 = (bf16[272,768]{1,0:T(8,128)(2,1)S(1)}, bf16[272,768]{1,0:T(8,128)(2,1)}, u32[]{:S(2)}, u32[]{:S(2)}) collective-permute-start(bf16[272,768]{1,0:T(8,128)(2,1)S(1)} %collective-permute-done.1.refs_2_), channel_id=1, source_target_pairs={{0,1},{1,0},{2,3},{3,2},{4,5},{5,4},{6,7},{7,6},{8,9},{9,8},{10,11... | collective-permute-start | bytes 1253384 | tf_op jit(solution)/shard_map/ppermute | solution.py:27
  38.6 12.9 %collective-permute-start.6 = (bf16[128,1280]{1,0:T(8,128)(2,1)}, bf16[128,1280]{1,0:T(8,128)(2,1)S(1)}, u32[]{:S(2)}, u32[]{:S(2)}) collective-permute-start(bf16[128,1280]{1,0:T(8,128)(2,1)} %get-tuple-element.98.refs_4_.refs_0_), channel_id=1, source_target_pairs={{0,4},{4,0},{8,12},{12,8},{16,20},{20,16},{24,28},{28,24},{1,5},{5... | collective-permute-start | bytes 983048 | tf_op jit(solution)/shard_map/ppermute | solution.py:27
  44.2 11.1 %collective-permute-start.8 = (bf16[128,1280]{1,0:T(8,128)(2,1)S(1)}, bf16[128,1280]{1,0:T(8,128)(2,1)S(1)}, u32[]{:S(2)}, u32[]{:S(2)}) collective-permute-start(bf16[128,1280]{1,0:T(8,128)(2,1)S(1)} %collective-permute-done.7.refs_6_.refs_2_), channel_id=1, source_target_pairs={{0,4},{4,0},{8,12},{12,8},{16,20},{20,16},{24,28},{28,24},{1,5},{5... | collective-permute-start | bytes 983048 | tf_op jit(solution)/shard_map/ppermute | solution.py:27
  49.1 16.2 %collective-permute-start.21 = (bf16[192,1152]{1,0:T(8,128)(2,1)}, bf16[192,1152]{1,0:T(8,128)(2,1)S(1)}, u32[]{:S(2)}, u32[]{:S(2)}) collective-permute-start(bf16[192,1152]{1,0:T(8,128)(2,1)} %get-tuple-element.105.refs_0_.refs_4_.refs_8_), channel_id=1, source_target_pairs={{0,24},{4,28},{8,16},{12,20},{16,8},{20,12},{24,0},{28,4},{1,25},{... | collective-permute-start | bytes 1327112 | tf_op jit(solution)/shard_map/ppermute | solution.py:27
  51.5 18.1 %collective-permute-start.19 = (bf16[192,1152]{1,0:T(8,128)(2,1)}, bf16[192,1152]{1,0:T(8,128)(2,1)S(1)}, u32[]{:S(2)}, u32[]{:S(2)}) collective-permute-start(bf16[192,1152]{1,0:T(8,128)(2,1)} %get-tuple-element.105.refs_0_.refs_4_.refs_8_), channel_id=1, source_target_pairs={{0,16},{4,20},{8,24},{12,28},{16,0},{20,4},{24,8},{28,12},{1,17},{... | collective-permute-start | bytes 1327112 | tf_op jit(solution)/shard_map/ppermute | solution.py:27
  52.1 17.7 %collective-permute-start.17 = (bf16[192,1152]{1,0:T(8,128)(2,1)}, bf16[192,1152]{1,0:T(8,128)(2,1)S(1)}, u32[]{:S(2)}, u32[]{:S(2)}) collective-permute-start(bf16[192,1152]{1,0:T(8,128)(2,1)} %get-tuple-element.105.refs_0_.refs_4_.refs_8_), channel_id=1, source_target_pairs={{0,8},{4,12},{8,0},{12,4},{16,24},{20,28},{24,16},{28,20},{1,9},{5... | collective-permute-start | bytes 1327112 | tf_op jit(solution)/shard_map/ppermute | solution.py:27
  52.7 20.1 %collective-permute-start.14 = (bf16[256,768]{1,0:T(8,128)(2,1)S(1)}, bf16[256,768]{1,0:T(8,128)(2,1)}, u32[]{:S(2)}, u32[]{:S(2)}) collective-permute-start(bf16[256,768]{1,0:T(8,128)(2,1)S(1)} %copy-done.1), channel_id=1, source_target_pairs={{0,2},{1,3},{2,0},{3,1},{4,6},{5,7},{6,4},{7,5},{8,10},{9,11},{10,... | collective-permute-start | bytes 1179656 | tf_op jit(solution)/shard_map/ppermute | solution.py:27
  56.0 17.8 %collective-permute-start.13 = (bf16[256,768]{1,0:T(8,128)(2,1)S(1)}, bf16[256,768]{1,0:T(8,128)(2,1)}, u32[]{:S(2)}, u32[]{:S(2)}) collective-permute-start(bf16[256,768]{1,0:T(8,128)(2,1)S(1)} %copy-done.1), channel_id=1, source_target_pairs={{0,1},{1,0},{2,3},{3,2},{4,5},{5,4},{6,7},{7,6},{8,9},{9,8},{10,11... | collective-permute-start | bytes 1179656 | tf_op jit(solution)/shard_map/ppermute | solution.py:27
  73.8 14.4 %collective-permute-start.15 = (bf16[256,768]{1,0:T(8,128)(2,1)}, bf16[256,768]{1,0:T(8,128)(2,1)}, u32[]{:S(2)}, u32[]{:S(2)}) collective-permute-start(bf16[256,768]{1,0:T(8,128)(2,1)} %collective-permute-done.14.refs_2_), channel_id=1, source_target_pairs={{0,1},{1,0},{2,3},{3,2},{4,5},{5,4},{6,7},{7,6},{8,9},{9,8},{10,11... | collective-permute-start | bytes 1179656 | tf_op jit(solution)/shard_map/ppermute | solution.py:27
  74.5 13.7 %collective-permute-start.23 = (bf16[80,1024]{1,0:T(8,128)(2,1)}, bf16[80,1024]{1,0:T(8,128)(2,1)S(1)}, u32[]{:S(2)}, u32[]{:S(2)}) collective-permute-start(bf16[80,1024]{1,0:T(8,128)(2,1)} %get-tuple-element.112), channel_id=1, source_target_pairs={{0,2},{1,3},{2,0},{3,1},{4,6},{5,7},{6,4},{7,5},{8,10},{9,11},{10,... | collective-permute-start | bytes 491528 | tf_op jit(solution)/shard_map/ppermute | solution.py:27
  134.6 19.5 %collective-permute-start.28 = (bf16[80,1024]{1,0:T(8,128)(2,1)}, bf16[80,1024]{1,0:T(8,128)(2,1)S(1)}, u32[]{:S(2)}, u32[]{:S(2)}) collective-permute-start(bf16[80,1024]{1,0:T(8,128)(2,1)} %get-tuple-element.120.refs_0_), channel_id=1, source_target_pairs={{0,1},{1,0},{2,3},{3,2},{4,5},{5,4},{6,7},{7,6},{8,9},{9,8},{10,11... | collective-permute-start | bytes 491528 | tf_op jit(solution)/shard_map/ppermute | solution.py:27
  136.4 19.8 %collective-permute-start.29 = (bf16[80,1024]{1,0:T(8,128)(2,1)}, bf16[80,1024]{1,0:T(8,128)(2,1)S(1)}, u32[]{:S(2)}, u32[]{:S(2)}) collective-permute-start(bf16[80,1024]{1,0:T(8,128)(2,1)} %get-tuple-element.120.refs_0_), channel_id=1, source_target_pairs={{0,2},{1,3},{2,0},{3,1},{4,6},{5,7},{6,4},{7,5},{8,10},{9,11},{10,... | collective-permute-start | bytes 491528 | tf_op jit(solution)/shard_map/ppermute | solution.py:27
  136.9 19.3 %collective-permute-start.30 = (bf16[80,1024]{1,0:T(8,128)(2,1)}, bf16[80,1024]{1,0:T(8,128)(2,1)S(1)}, u32[]{:S(2)}, u32[]{:S(2)}) collective-permute-start(bf16[80,1024]{1,0:T(8,128)(2,1)} %get-tuple-element.120.refs_0_), channel_id=1, source_target_pairs={{0,3},{1,2},{2,1},{3,0},{4,7},{5,6},{6,5},{7,4},{8,11},{9,10},{10,... | collective-permute-start | bytes 491528 | tf_op jit(solution)/shard_map/ppermute | solution.py:27
  139.0 41.4 %collective-permute-start.25 = (bf16[256,768]{1,0:T(8,128)(2,1)}, bf16[256,768]{1,0:T(8,128)(2,1)S(1)}, u32[]{:S(2)}, u32[]{:S(2)}) collective-permute-start(bf16[256,768]{1,0:T(8,128)(2,1)} %get-tuple-element.117), channel_id=1, source_target_pairs={{0,1},{1,0},{2,3},{3,2},{4,5},{5,4},{6,7},{7,6},{8,9},{9,8},{10,11... | collective-permute-start | bytes 1179656 | tf_op jit(solution)/shard_map/ppermute | solution.py:27
  139.9 40.6 %collective-permute-start.26 = (bf16[256,768]{1,0:T(8,128)(2,1)}, bf16[256,768]{1,0:T(8,128)(2,1)S(1)}, u32[]{:S(2)}, u32[]{:S(2)}) collective-permute-start(bf16[256,768]{1,0:T(8,128)(2,1)} %get-tuple-element.118), channel_id=1, source_target_pairs={{0,2},{1,3},{2,0},{3,1},{4,6},{5,7},{6,4},{7,5},{8,10},{9,11},{10,... | collective-permute-start | bytes 1179656 | tf_op jit(solution)/shard_map/ppermute | solution.py:27
  150.2 44.5 %all-to-all-start = ((bf16[8,96,1152]{2,1,0:T(8,128)(2,1)}), bf16[8,96,1152]{2,1,0:T(8,128)(2,1)S(1)}, u32[]{:S(2)}, u32[]{:S(2)}) async-start(bf16[8,96,1152]{2,1,0:T(8,128)(2,1)} %get-tuple-element.153), calls=%async_computation | async-start | bytes 3538944 | tf_op jit(solution)/shard_map/all_to_all | solution.py:1099
  154.1 27.1 %collective-permute-start.27 = (bf16[256,768]{1,0:T(8,128)(2,1)}, bf16[256,768]{1,0:T(8,128)(2,1)S(1)}, u32[]{:S(2)}, u32[]{:S(2)}) collective-permute-start(bf16[256,768]{1,0:T(8,128)(2,1)} %get-tuple-element.119), channel_id=1, source_target_pairs={{0,3},{1,2},{2,1},{3,0},{4,7},{5,6},{6,5},{7,4},{8,11},{9,10},{10,... | collective-permute-start | bytes 1179656 | tf_op jit(solution)/shard_map/ppermute | solution.py:27
  175.3 12.3 %collective-permute-start.32 = (bf16[256,768]{1,0:T(8,128)(2,1)}, bf16[256,768]{1,0:T(8,128)(2,1)}, u32[]{:S(2)}, u32[]{:S(2)}) collective-permute-start(bf16[256,768]{1,0:T(8,128)(2,1)} %get-tuple-element.148), channel_id=1, source_target_pairs={{0,1},{1,0},{2,3},{3,2},{4,5},{5,4},{6,7},{7,6},{8,9},{9,8},{10,11... | collective-permute-start | bytes 1179656 | tf_op jit(solution)/shard_map/ppermute | solution.py:27
  175.4 33.9 %collective-permute-start.34 = (bf16[256,768]{1,0:T(8,128)(2,1)}, bf16[256,768]{1,0:T(8,128)(2,1)S(1)}, u32[]{:S(2)}, u32[]{:S(2)}) collective-permute-start(bf16[256,768]{1,0:T(8,128)(2,1)} %get-tuple-element.149), channel_id=1, source_target_pairs={{0,1},{1,0},{2,3},{3,2},{4,5},{5,4},{6,7},{7,6},{8,9},{9,8},{10,11... | collective-permute-start | bytes 1179656 | tf_op jit(solution)/shard_map/ppermute | solution.py:27
  181.2 17.6 %collective-permute-start.35 = (bf16[144,1152]{1,0:T(8,128)(2,1)}, bf16[144,1152]{1,0:T(8,128)(2,1)}, u32[]{:S(2)}, u32[]{:S(2)}) collective-permute-start(bf16[144,1152]{1,0:T(8,128)(2,1)} %get-tuple-element.150), channel_id=1, source_target_pairs={{0,8},{4,12},{8,0},{12,4},{16,24},{20,28},{24,16},{28,20},{1,9},{5... | collective-permute-start | bytes 995336 | tf_op jit(solution)/shard_map/ppermute | solution.py:27
  182.9 16.8 %collective-permute-start.36 = (bf16[144,1152]{1,0:T(8,128)(2,1)}, bf16[144,1152]{1,0:T(8,128)(2,1)}, u32[]{:S(2)}, u32[]{:S(2)}) collective-permute-start(bf16[144,1152]{1,0:T(8,128)(2,1)} %get-tuple-element.151), channel_id=1, source_target_pairs={{0,16},{4,20},{8,24},{12,28},{16,0},{20,4},{24,8},{28,12},{1,17},{... | collective-permute-start | bytes 995336 | tf_op jit(solution)/shard_map/ppermute | solution.py:27
  184.4 15.3 %collective-permute-start.37 = (bf16[144,1152]{1,0:T(8,128)(2,1)}, bf16[144,1152]{1,0:T(8,128)(2,1)}, u32[]{:S(2)}, u32[]{:S(2)}) collective-permute-start(bf16[144,1152]{1,0:T(8,128)(2,1)} %get-tuple-element.152), channel_id=1, source_target_pairs={{0,24},{4,28},{8,16},{12,20},{16,8},{20,12},{24,0},{28,4},{1,25},{... | collective-permute-start | bytes 995336 | tf_op jit(solution)/shard_map/ppermute | solution.py:27
  189.6 26.4 %collective-permute-start.33 = (bf16[256,768]{1,0:T(8,128)(2,1)}, bf16[256,768]{1,0:T(8,128)(2,1)S(1)}, u32[]{:S(2)}, u32[]{:S(2)}) collective-permute-start(bf16[256,768]{1,0:T(8,128)(2,1)} %add_convert_fusion), channel_id=1, source_target_pairs={{0,2},{1,3},{2,0},{3,1},{4,6},{5,7},{6,4},{7,5},{8,10},{9,11},{10,... | collective-permute-start | bytes 1179656 | tf_op jit(solution)/shard_map/ppermute | solution.py:27
  195.0 26.8 %all-to-all-start.1 = ((bf16[8,48,2304]{2,1,0:T(8,128)(2,1)}), bf16[8,48,2304]{2,1,0:T(8,128)(2,1)S(1)}, u32[]{:S(2)}, u32[]{:S(2)}) async-start(bf16[8,48,2304]{2,1,0:T(8,128)(2,1)} %get-tuple-element.170), calls=%async_computation.1 | async-start | bytes 3538944 | tf_op jit(solution)/shard_map/all_to_all | solution.py:1188
  201.8 15.5 %collective-permute-start.38 = (bf16[24,2304]{1,0:T(8,128)(2,1)S(1)}, bf16[24,2304]{1,0:T(8,128)(2,1)S(1)}, u32[]{:S(2)}, u32[]{:S(2)}) collective-permute-start(bf16[24,2304]{1,0:T(8,128)(2,1)S(1)} %get-tuple-element.156), channel_id=1, source_target_pairs={{0,1},{1,0},{2,3},{3,2},{4,5},{5,4},{6,7},{7,6},{8,9},{9,8},{10,11... | collective-permute-start | bytes 331784 | tf_op jit(solution)/shard_map/ppermute | solution.py:27
  206.9 11.2 %collective-permute-start.39 = (bf16[24,2304]{1,0:T(8,128)(2,1)S(1)}, bf16[24,2304]{1,0:T(8,128)(2,1)S(1)}, u32[]{:S(2)}, u32[]{:S(2)}) collective-permute-start(bf16[24,2304]{1,0:T(8,128)(2,1)S(1)} %get-tuple-element.157), channel_id=1, source_target_pairs={{0,2},{1,3},{2,0},{3,1},{4,6},{5,7},{6,4},{7,5},{8,10},{9,11},{10,... | collective-permute-start | bytes 331784 | tf_op jit(solution)/shard_map/ppermute | solution.py:27
  206.9 11.2 %collective-permute-start.40 = (bf16[24,2304]{1,0:T(8,128)(2,1)S(1)}, bf16[24,2304]{1,0:T(8,128)(2,1)S(1)}, u32[]{:S(2)}, u32[]{:S(2)}) collective-permute-start(bf16[24,2304]{1,0:T(8,128)(2,1)S(1)} %get-tuple-element.158), channel_id=1, source_target_pairs={{0,3},{1,2},{2,1},{3,0},{4,7},{5,6},{6,5},{7,4},{8,11},{9,10},{10,... | collective-permute-start | bytes 331784 | tf_op jit(solution)/shard_map/ppermute | solution.py:27
  (49 other events, 405.2 us)

commit v6 on v5

--- a/solution.py
+++ b/solution.py
@@ -54,7 +54,8 @@
 
 
 def scatter_narrow(parts):
-    return [parts[0]] + [swap(parts[s], "narrow", s) for s in range(1, len(parts))]
+    arrived = [swap(parts[s], "narrow", s) for s in range(len(parts) - 1, 0, -1)]
+    return [parts[0]] + arrived[::-1]
 
 
 def sum_narrow(parts, *earlier):
@@ -160,7 +161,7 @@
 
 
 def split_kernel(
-    er, ep, wid, below, meta, w_r, gain_r, out_r, x_r, dt_r, bias_r, conv_r, conv_b_r, skip_r, log_r, *refs
+    er, ep, wid, below, w_r, gain_r, out_r, x_r, dt_r, bias_r, conv_r, conv_b_r, skip_r, log_r, *refs
 ):
     nar = len(refs) - 4
     outs, (small_o, out_o, rows_s, lanes) = refs[:nar], refs[nar:]
@@ -184,7 +185,7 @@
     for s in range(nar):
         rows_s[s, :, MODS * es : MODS * es + LANES] = gain
     for s in range(nar):
-        outs[s][...] = rows_s[meta[0] ^ s]
+        outs[s][...] = rows_s[lax.axis_index("narrow") ^ s]
     out_whole = jnp.concatenate([out_r[m].astype(f32) for m in range(MODS)], axis=1)
     if ep > er:
         out_whole = jnp.concatenate([out_whole, jnp.zeros((ep - er, out_whole.shape[1]), f32)], axis=0)
@@ -958,8 +959,7 @@
         functools.partial(split_kernel, er, ep, wid, below),
         [((dr, front_w + width), bf16, "v")] * nar
         + [((below, front_w), bf16, "v"), ((ep * (out_cols // width), width), bf16, "v")],
-        [(meta, "s")]
-        + [
+        [
             (a, "v")
             for a in (
                 w_in_m,

time: 223 us -> 222 us (level)
  no operation moved by 1% of the time
where the time goes in v6:
time: 222 us
  Pallas kernels  97.3 us (44%)
  starting transfers between devices  57.5 us (26%)
  waiting for transfers between devices  55.4 us (25%)
  local copies, waits for them, and re-layouts  6.09 us (3%)
  other arithmetic  3.45 us (2%)
    pallas_call x15, Pallas kernels, call(): pl.pallas_call(kernel, out_shape=[jax.ShapeDtypeStruct(shape, dtype) for...  97.3 us
    ppermute x41, waiting for transfers between devices, swap(): return lax.ppermute(block, axis, [(i, i ^ flip) for i in range(count)])  55.1 us
    ppermute x41, starting transfers between devices, swap(): return lax.ppermute(block, axis, [(i, i ^ flip) for i in range(count)])  50 us
    unnamed x76, local copies, waits for them, and re-layouts  5.97 us
  transfers between devices with their start and end apart: 43, of which 15 were waited for; matrix products, arithmetic and copies ran while one was open for 1% of the time, Pallas kernels for 25%

profile of v6, /device:TPU:0, one launch (start us, length us, event | category | flops | bytes accessed | tf_op | source)
XLA Modules:
  0.0 221.5 jit_solution(8384241415959200020)
XLA Ops:
  0.7 2.4 %shard_map.229 = (bf16[24,2432]{1,0:T(8,128)(2,1)}, bf16[24,2432]{1,0:T(8,128)(2,1)}, bf16[24,2432]{1,0:T(8,128)(2,1)}, bf16[24,2432]{1,0:T(8,128)(2,1)}, bf16[3...) custom-call(bf16[3,24,3072]{2,1,0:T(8,128)(2,1)} %bitcast.20, bf16[1,24]{1,0:T(2,128)(2,1)} %bitcast.22, ...), custom_call_target="tpu_custom_call" | custom-call | flops 3300000000 | bytes 1 | tf_op jit(solution)/shard_map/pallas_call | solution.py:98
  3.1 3.1 %collective-permute-start.3 = (bf16[24,2432]{1,0:T(8,128)(2,1)}, bf16[24,2432]{1,0:T(8,128)(2,1)S(1)}, u32[]{:S(2)}, u32[]{:S(2)}) collective-permute-start(bf16[24,2432]{1,0:T(8,128)(2,1)} %get-tuple-element.93), channel_id=1, source_target_pairs={{0,1},{1,0},{2,3},{3,2},{4,5},{5,4},{6,7},{7,6},{8,9},{9,8},{10,11... | collective-permute-start | bytes 350216 | tf_op jit(solution)/shard_map/ppermute | solution.py:27
  6.2 2.6 %collective-permute-start.4 = (bf16[24,2432]{1,0:T(8,128)(2,1)}, bf16[24,2432]{1,0:T(8,128)(2,1)S(1)}, u32[]{:S(2)}, u32[]{:S(2)}) collective-permute-start(bf16[24,2432]{1,0:T(8,128)(2,1)} %get-tuple-element.94), channel_id=1, source_target_pairs={{0,2},{1,3},{2,0},{3,1},{4,6},{5,7},{6,4},{7,5},{8,10},{9,11},{10,... | collective-permute-start | bytes 350216 | tf_op jit(solution)/shard_map/ppermute | solution.py:27
  11.0 2.5 %collective-permute-start = (bf16[272,768]{1,0:T(8,128)(2,1)S(1)}, bf16[272,768]{1,0:T(8,128)(2,1)S(1)}, u32[]{:S(2)}, u32[]{:S(2)}) collective-permute-start(bf16[272,768]{1,0:T(8,128)(2,1)S(1)} %pad_maximum_fusion.refs_0_), channel_id=1, source_target_pairs={{0,1},{1,0},{2,3},{3,2},{4,5},{5,4},{6,7},{7,6},{8,9},{9,8},{10,11... | collective-permute-start | bytes 1253384 | tf_op jit(solution)/shard_map/ppermute | solution.py:27
  14.8 12.5 %collective-permute-done.4.refs_2_ = bf16[24,2432]{1,0:T(8,128)(2,1)S(1)} collective-permute-done((bf16[24,2432]{1,0:T(8,128)(2,1)}, bf16[24,2432]{1,0:T(8,128)(2,1)S(1)}, u32[]{:S(2)}, u32[]{:S(2)}) %collective-permute-start.4) | collective-permute-done | bytes 116768 | tf_op jit(solution)/shard_map/ppermute | solution.py:27
  27.9 2.7 %shard_map.230 = (bf16[128,1280]{1,0:T(8,128)(2,1)}, bf16[192,1152]{1,0:T(8,128)(2,1)}) custom-call(s32[3]{0:T(128)} %pad_add_fusion.meta, bf16[24,2432]{1,0:T(8,128)(2,1)} %get-tuple-element.92.refs_0_, bf16[24,2432]{1,0:T(8,128)(2,1)} %copy-done.34, bf16[24,2432]{1,0:T(8,128)(2,1)} %copy-done.35, bf16[24,2432]{1,0:T(8,128)(2,1)} %copy-done.36, ...), custom_call_target="tpu_custom_call" | custom-call | flops 2200000000 | bytes 1 | tf_op jit(solution)/shard_map/pallas_call | solution.py:98
  34.1 3.3 %collective-permute-done.1.refs_2_ = bf16[272,768]{1,0:T(8,128)(2,1)S(1)} collective-permute-done((bf16[272,768]{1,0:T(8,128)(2,1)S(1)}, bf16[272,768]{1,0:T(8,128)(2,1)S(1)}, u32[]{:S(2)}, u32[]{:S(2)}) %collective-permute-start.1) | collective-permute-done | bytes 417824 | tf_op jit(solution)/shard_map/ppermute | solution.py:27
  37.5 3.9 %collective-permute-done.9.refs_8_.refs_4_ = bf16[128,1280]{1,0:T(8,128)(2,1)S(1)} collective-permute-done((bf16[128,1280]{1,0:T(8,128)(2,1)}, bf16[128,1280]{1,0:T(8,128)(2,1)S(1)}, u32[]{:S(2)}, u32[]{:S(2)}) %collective-permute-start.9) | collective-permute-done | bytes 327712 | tf_op jit(solution)/shard_map/ppermute | solution.py:27
  42.9 4.9 %collective-permute-done.2.refs_3_ = bf16[272,768]{1,0:T(8,128)(2,1)} collective-permute-done((bf16[272,768]{1,0:T(8,128)(2,1)S(1)}, bf16[272,768]{1,0:T(8,128)(2,1)}, u32[]{:S(2)}, u32[]{:S(2)}) %collective-permute-start.2) | collective-permute-done | bytes 417824 | tf_op jit(solution)/shard_map/ppermute | solution.py:27
  47.8 2.4 %collective-permute-start.21 = (bf16[192,1152]{1,0:T(8,128)(2,1)}, bf16[192,1152]{1,0:T(8,128)(2,1)S(1)}, u32[]{:S(2)}, u32[]{:S(2)}) collective-permute-start(bf16[192,1152]{1,0:T(8,128)(2,1)} %get-tuple-element.105.refs_0_.refs_4_.refs_8_), channel_id=1, source_target_pairs={{0,24},{4,28},{8,16},{12,20},{16,8},{20,12},{24,0},{28,4},{1,25},{... | collective-permute-start | bytes 1327112 | tf_op jit(solution)/shard_map/ppermute | solution.py:27
  51.4 2.6 %collective-permute-start.14 = (bf16[256,768]{1,0:T(8,128)(2,1)S(1)}, bf16[256,768]{1,0:T(8,128)(2,1)}, u32[]{:S(2)}, u32[]{:S(2)}) collective-permute-start(bf16[256,768]{1,0:T(8,128)(2,1)S(1)} %copy-done.1), channel_id=1, source_target_pairs={{0,2},{1,3},{2,0},{3,1},{4,6},{5,7},{6,4},{7,5},{8,10},{9,11},{10,... | collective-permute-start | bytes 1179656 | tf_op jit(solution)/shard_map/ppermute | solution.py:27
  55.3 8.7 %shard_map.231 = (bf16[1024,768]{1,0:T(8,128)(2,1)}, f32[1024,384]{1,0:T(8,128)}, f32[1024,384]{1,0:T(8,128)}, bf16[1024,384]{1,0:T(8,128)(2,1)}, bf16[80,1024]{...) custom-call(s32[3]{0:T(128)} %pad_add_fusion.meta, ...), custom_call_target="tpu_custom_call" | custom-call | flops 9900000256 | bytes 1 | tf_op jit(solution)/shard_map/pallas_call | solution.py:98
  64.2 4.2 %collective-permute-done.19.refs_4_.refs_8_.refs_12_ = bf16[192,1152]{1,0:T(8,128)(2,1)S(1)} collective-permute-done((bf16[192,1152]{1,0:T(8,128)(2,1)}, bf16[192,1152]{1,0:T(8,128)(2,1)S(1)}, u32[]{:S(2)}, u32[]{:S(2)}) %collective-permute-start.19) | collective-permute-done | bytes 442400 | tf_op jit(solution)/shard_map/ppermute | solution.py:27
  68.9 2.6 %collective-permute-done.14.refs_2_ = bf16[256,768]{1,0:T(8,128)(2,1)} collective-permute-done((bf16[256,768]{1,0:T(8,128)(2,1)S(1)}, bf16[256,768]{1,0:T(8,128)(2,1)}, u32[]{:S(2)}, u32[]{:S(2)}) %collective-permute-start.14) | collective-permute-done | bytes 393248 | tf_op jit(solution)/shard_map/ppermute | solution.py:27
  75.3 5.4 %shard_map.232 = (f32[1024,384]{1,0:T(8,128)}, f32[1024,384]{1,0:T(8,128)}) custom-call(s32[3]{0:T(128)} %pad_add_fusion.meta, s32[8]{0:T(128)} %get-tuple-element.99.kinds, bf16[192,1152]{1,0:T(8,128)(2,1)} %get-tuple-element.105.refs_0_.refs_4_.refs_8_, bf16[192,1152]{1,0:T(8,128)(2,1)} %copy-done.16, bf16[192,1152]{1,0:T(8,128)(2,1)} %copy-done.15, ...), custom_call_target="tpu_custom_call" | custom-call | flops 110000000 | bytes 1 | tf_op jit(solution)/shard_map/pallas_call | solution.py:98
  80.6 6.3 %collective-permute-done.15.refs_3_ = bf16[256,768]{1,0:T(8,128)(2,1)} collective-permute-done((bf16[256,768]{1,0:T(8,128)(2,1)}, bf16[256,768]{1,0:T(8,128)(2,1)}, u32[]{:S(2)}, u32[]{:S(2)}) %collective-permute-start.15) | collective-permute-done | bytes 393248 | tf_op jit(solution)/shard_map/ppermute | solution.py:27
  86.9 2.4 %collective-permute-start.24 = (bf16[80,1024]{1,0:T(8,128)(2,1)S(1)}, bf16[80,1024]{1,0:T(8,128)(2,1)S(1)}, u32[]{:S(2)}, u32[]{:S(2)}) collective-permute-start(bf16[80,1024]{1,0:T(8,128)(2,1)S(1)} %add_convert_fusion.2), channel_id=1, source_target_pairs={{0,1},{1,0},{2,3},{3,2},{4,5},{5,4},{6,7},{7,6},{8,9},{9,8},{10,11... | collective-permute-start | bytes 491528 | tf_op jit(solution)/shard_map/ppermute | solution.py:27
  89.4 4.0 %collective-permute-done.24 = bf16[80,1024]{1,0:T(8,128)(2,1)S(1)} collective-permute-done((bf16[80,1024]{1,0:T(8,128)(2,1)S(1)}, bf16[80,1024]{1,0:T(8,128)(2,1)S(1)}, u32[]{:S(2)}, u32[]{:S(2)}) %collective-permute-start.24) | collective-permute-done | bytes 163872 | tf_op jit(solution)/shard_map/ppermute | solution.py:27
  94.1 39.2 %shard_map.233 = (bf16[256,768]{1,0:T(8,128)(2,1)}, bf16[256,768]{1,0:T(8,128)(2,1)}, bf16[256,768]{1,0:T(8,128)(2,1)}, bf16[256,768]{1,0:T(8,128)(2,1)}, bf16[1...) custom-call(s32[3]{0:T(128)} %pad_add_fusion.meta, ...), custom_call_target="tpu_custom_call" | custom-call | flops 44000002048 | bytes 1 | tf_op jit(solution)/shard_map/pallas_call | solution.py:98
  140.1 8.9 %shard_map.234 = (bf16[1024,384]{1,0:T(8,128)(2,1)}, bf16[8,96,1152]{2,1,0:T(8,128)(2,1)}, bf16[8,48,2304]{2,1,0:T(8,128)(2,1)}, f32[176,384]{1,0:T(8,128)}) custom-call(s32[3]{0:T(128)} %pad_add_fusion.meta, s32[8]{0:T(128)} %get-tuple-element.99.kinds, bf16[1024,384]{1,0:T(8,128)(2,1)} %get-tuple-element.122.refs_0_, ...), custom_call_target="tpu_custom_call" | custom-call | flops 9900000256 | bytes 1 | tf_op jit(solution)/shard_map/pallas_call | solution.py:98
  148.9 3.8 %all-to-all-start = ((bf16[8,96,1152]{2,1,0:T(8,128)(2,1)}), bf16[8,96,1152]{2,1,0:T(8,128)(2,1)S(1)}, u32[]{:S(2)}, u32[]{:S(2)}) async-start(bf16[8,96,1152]{2,1,0:T(8,128)(2,1)} %get-tuple-element.153), calls=%async_computation | async-start | bytes 3538944 | tf_op jit(solution)/shard_map/all_to_all | solution.py:1099
  152.8 2.1 collective-permute-start.27
  155.7 10.6 %shard_map.235 = (bf16[1024,384]{1,0:T(8,128)(2,1)}, bf16[4,144,1152]{2,1,0:T(8,128)(2,1)}, bf16[4,144,1152]{2,1,0:T(8,128)(2,1)}) custom-call(s32[3]{0:T(128)} %pad_add_fusion.meta, s32[8]{0:T(128)} %get-tuple-element.99.kinds, bf16[80,1024]{1,0:T(8,128)(2,1)} %get-tuple-element.120.refs_0_, bf16[80,1024]{1,0:T(8,128)(2,1)} %copy-done.31, ...), custom_call_target="tpu_custom_call" | custom-call | flops 13200000000 | bytes 1 | tf_op jit(solution)/shard_map/pallas_call | solution.py:98
  166.3 7.7 %shard_map.236 = (bf16[256,768]{1,0:T(8,128)(2,1)}, bf16[256,768]{1,0:T(8,128)(2,1)}, bf16[256,768]{1,0:T(8,128)(2,1)}, bf16[256,768]{1,0:T(8,128)(2,1)}) custom-call(s32[3]{0:T(128)} %pad_add_fusion.meta, s32[8]{0:T(128)} %get-tuple-element.99.kinds, bf16[128,1280]{1,0:T(8,128)(2,1)} %get-tuple-element.98.refs_4_.refs_0_, bf16[128,1280]{1,0:T(8,128)(2,1)} %copy-done.27, ...), custom_call_target="tpu_custom_call" | custom-call | flops 32999999488 | bytes 1 | tf_op jit(solution)/shard_map/pallas_call | solution.py:98
  176.2 3.0 %shard_map.237 = (bf16[144,1152]{1,0:T(8,128)(2,1)}, bf16[144,1152]{1,0:T(8,128)(2,1)}, bf16[144,1152]{1,0:T(8,128)(2,1)}, bf16[144,1152]{1,0:T(8,128)(2,1)}) custom-call(s32[3]{0:T(128)} %pad_add_fusion.meta, bf16[4,144,1152]{2,1,0:T(8,128)(2,1)} %get-tuple-element.138.same, bf16[4,144,1152]{2,1,0:T(8,128)(2,1)} %collective-permute-done.31.peer), custom_call_target="tpu_custom_call" | custom-call | flops 3300000000 | bytes 1 | tf_op jit(solution)/shard_map/pallas_call | solution.py:98
  183.4 3.1 %collective-permute-done.32 = bf16[256,768]{1,0:T(8,128)(2,1)} collective-permute-done((bf16[256,768]{1,0:T(8,128)(2,1)}, bf16[256,768]{1,0:T(8,128)(2,1)}, u32[]{:S(2)}, u32[]{:S(2)}) %collective-permute-start.32) | collective-permute-done | bytes 393248 | tf_op jit(solution)/shard_map/ppermute | solution.py:27
  188.4 2.1 collective-permute-start.33
  193.7 3.7 %all-to-all-start.1 = ((bf16[8,48,2304]{2,1,0:T(8,128)(2,1)}), bf16[8,48,2304]{2,1,0:T(8,128)(2,1)S(1)}, u32[]{:S(2)}, u32[]{:S(2)}) async-start(bf16[8,48,2304]{2,1,0:T(8,128)(2,1)} %get-tuple-element.170), calls=%async_computation.1 | async-start | bytes 3538944 | tf_op jit(solution)/shard_map/all_to_all | solution.py:1188
  200.4 5.3 %collective-permute-start.38 = (bf16[24,2304]{1,0:T(8,128)(2,1)S(1)}, bf16[24,2304]{1,0:T(8,128)(2,1)S(1)}, u32[]{:S(2)}, u32[]{:S(2)}) collective-permute-start(bf16[24,2304]{1,0:T(8,128)(2,1)S(1)} %get-tuple-element.156), channel_id=1, source_target_pairs={{0,1},{1,0},{2,3},{3,2},{4,5},{5,4},{6,7},{7,6},{8,9},{9,8},{10,11... | collective-permute-start | bytes 331784 | tf_op jit(solution)/shard_map/ppermute | solution.py:27
  205.8 2.4 %collective-permute-start.40 = (bf16[24,2304]{1,0:T(8,128)(2,1)S(1)}, bf16[24,2304]{1,0:T(8,128)(2,1)S(1)}, u32[]{:S(2)}, u32[]{:S(2)}) collective-permute-start(bf16[24,2304]{1,0:T(8,128)(2,1)S(1)} %get-tuple-element.158), channel_id=1, source_target_pairs={{0,3},{1,2},{2,1},{3,0},{4,7},{5,6},{6,5},{7,4},{8,11},{9,10},{10,... | collective-permute-start | bytes 331784 | tf_op jit(solution)/shard_map/ppermute | solution.py:27
  208.2 6.6 %collective-permute-done.33.refs_1_ = bf16[256,768]{1,0:T(8,128)(2,1)S(1)} collective-permute-done((bf16[256,768]{1,0:T(8,128)(2,1)}, bf16[256,768]{1,0:T(8,128)(2,1)S(1)}, u32[]{:S(2)}, u32[]{:S(2)}) %collective-permute-start.33) | collective-permute-done | bytes 393248 | tf_op jit(solution)/shard_map/ppermute | solution.py:27
  216.9 3.3 %shard_map.242 = (f32[3,24,3072]{2,1,0:T(8,128)}, f32[1,24]{1,0:T(1,128)}) custom-call(s32[3]{0:T(128)S(1)} %copy-done.5, bf16[24,2304]{1,0:T(8,128)(2,1)S(1)} %get-tuple-element.155.refs_0_, bf16[24,2304]{1,0:T(8,128)(2,1)S(1)} %collective-permute-done.38.refs_1_, bf16[24,2304]{1,0:T(8,128)(2,1)S(1)} %collective-permute-done.39.refs_2_, ...), custom_call_target="tpu_custom_call" | custom-call | flops 14300000256 | bytes 1 | tf_op jit(solution)/shard_map/pallas_call | solution.py:98
  (153 shorter events, 41.5 us)
Async XLA Ops:
  3.1 11.6 %collective-permute-start.3 = (bf16[24,2432]{1,0:T(8,128)(2,1)}, bf16[24,2432]{1,0:T(8,128)(2,1)S(1)}, u32[]{:S(2)}, u32[]{:S(2)}) collective-permute-start(bf16[24,2432]{1,0:T(8,128)(2,1)} %get-tuple-element.93), channel_id=1, source_target_pairs={{0,1},{1,0},{2,3},{3,2},{4,5},{5,4},{6,7},{7,6},{8,9},{9,8},{10,11... | collective-permute-start | bytes 350216 | tf_op jit(solution)/shard_map/ppermute | solution.py:27
  6.2 21.1 %collective-permute-start.4 = (bf16[24,2432]{1,0:T(8,128)(2,1)}, bf16[24,2432]{1,0:T(8,128)(2,1)S(1)}, u32[]{:S(2)}, u32[]{:S(2)}) collective-permute-start(bf16[24,2432]{1,0:T(8,128)(2,1)} %get-tuple-element.94), channel_id=1, source_target_pairs={{0,2},{1,3},{2,0},{3,1},{4,6},{5,7},{6,4},{7,5},{8,10},{9,11},{10,... | collective-permute-start | bytes 350216 | tf_op jit(solution)/shard_map/ppermute | solution.py:27
  8.8 18.5 %collective-permute-start.5 = (bf16[24,2432]{1,0:T(8,128)(2,1)}, bf16[24,2432]{1,0:T(8,128)(2,1)S(1)}, u32[]{:S(2)}, u32[]{:S(2)}) collective-permute-start(bf16[24,2432]{1,0:T(8,128)(2,1)} %get-tuple-element.95), channel_id=1, source_target_pairs={{0,3},{1,2},{2,1},{3,0},{4,7},{5,6},{6,5},{7,4},{8,11},{9,10},{10,... | collective-permute-start | bytes 350216 | tf_op jit(solution)/shard_map/ppermute | solution.py:27
  9.1 28.3 %collective-permute-start.1 = (bf16[272,768]{1,0:T(8,128)(2,1)S(1)}, bf16[272,768]{1,0:T(8,128)(2,1)S(1)}, u32[]{:S(2)}, u32[]{:S(2)}) collective-permute-start(bf16[272,768]{1,0:T(8,128)(2,1)S(1)} %pad_maximum_fusion.refs_0_), channel_id=1, source_target_pairs={{0,2},{1,3},{2,0},{3,1},{4,6},{5,7},{6,4},{7,5},{8,10},{9,11},{10,... | collective-permute-start | bytes 1253384 | tf_op jit(solution)/shard_map/ppermute | solution.py:27
  11.0 26.4 %collective-permute-start = (bf16[272,768]{1,0:T(8,128)(2,1)S(1)}, bf16[272,768]{1,0:T(8,128)(2,1)S(1)}, u32[]{:S(2)}, u32[]{:S(2)}) collective-permute-start(bf16[272,768]{1,0:T(8,128)(2,1)S(1)} %pad_maximum_fusion.refs_0_), channel_id=1, source_target_pairs={{0,1},{1,0},{2,3},{3,2},{4,5},{5,4},{6,7},{7,6},{8,9},{9,8},{10,11... | collective-permute-start | bytes 1253384 | tf_op jit(solution)/shard_map/ppermute | solution.py:27
  30.6 10.8 %collective-permute-start.9 = (bf16[128,1280]{1,0:T(8,128)(2,1)}, bf16[128,1280]{1,0:T(8,128)(2,1)S(1)}, u32[]{:S(2)}, u32[]{:S(2)}) collective-permute-start(bf16[128,1280]{1,0:T(8,128)(2,1)} %get-tuple-element.98.refs_4_.refs_0_), channel_id=1, source_target_pairs={{0,16},{4,20},{8,24},{12,28},{16,0},{20,4},{24,8},{28,12},{1,17},{... | collective-permute-start | bytes 983048 | tf_op jit(solution)/shard_map/ppermute | solution.py:27
  37.4 12.9 %collective-permute-start.6 = (bf16[128,1280]{1,0:T(8,128)(2,1)}, bf16[128,1280]{1,0:T(8,128)(2,1)S(1)}, u32[]{:S(2)}, u32[]{:S(2)}) collective-permute-start(bf16[128,1280]{1,0:T(8,128)(2,1)} %get-tuple-element.98.refs_4_.refs_0_), channel_id=1, source_target_pairs={{0,4},{4,0},{8,12},{12,8},{16,20},{20,16},{24,28},{28,24},{1,5},{5... | collective-permute-start | bytes 983048 | tf_op jit(solution)/shard_map/ppermute | solution.py:27
  42.9 11.1 %collective-permute-start.8 = (bf16[128,1280]{1,0:T(8,128)(2,1)S(1)}, bf16[128,1280]{1,0:T(8,128)(2,1)S(1)}, u32[]{:S(2)}, u32[]{:S(2)}) collective-permute-start(bf16[128,1280]{1,0:T(8,128)(2,1)S(1)} %collective-permute-done.7.refs_6_.refs_2_), channel_id=1, source_target_pairs={{0,4},{4,0},{8,12},{12,8},{16,20},{20,16},{24,28},{28,24},{1,5},{5... | collective-permute-start | bytes 983048 | tf_op jit(solution)/shard_map/ppermute | solution.py:27
  47.8 16.2 %collective-permute-start.21 = (bf16[192,1152]{1,0:T(8,128)(2,1)}, bf16[192,1152]{1,0:T(8,128)(2,1)S(1)}, u32[]{:S(2)}, u32[]{:S(2)}) collective-permute-start(bf16[192,1152]{1,0:T(8,128)(2,1)} %get-tuple-element.105.refs_0_.refs_4_.refs_8_), channel_id=1, source_target_pairs={{0,24},{4,28},{8,16},{12,20},{16,8},{20,12},{24,0},{28,4},{1,25},{... | collective-permute-start | bytes 1327112 | tf_op jit(solution)/shard_map/ppermute | solution.py:27
  50.3 18.1 %collective-permute-start.19 = (bf16[192,1152]{1,0:T(8,128)(2,1)}, bf16[192,1152]{1,0:T(8,128)(2,1)S(1)}, u32[]{:S(2)}, u32[]{:S(2)}) collective-permute-start(bf16[192,1152]{1,0:T(8,128)(2,1)} %get-tuple-element.105.refs_0_.refs_4_.refs_8_), channel_id=1, source_target_pairs={{0,16},{4,20},{8,24},{12,28},{16,0},{20,4},{24,8},{28,12},{1,17},{... | collective-permute-start | bytes 1327112 | tf_op jit(solution)/shard_map/ppermute | solution.py:27
  50.8 17.7 %collective-permute-start.17 = (bf16[192,1152]{1,0:T(8,128)(2,1)}, bf16[192,1152]{1,0:T(8,128)(2,1)S(1)}, u32[]{:S(2)}, u32[]{:S(2)}) collective-permute-start(bf16[192,1152]{1,0:T(8,128)(2,1)} %get-tuple-element.105.refs_0_.refs_4_.refs_8_), channel_id=1, source_target_pairs={{0,8},{4,12},{8,0},{12,4},{16,24},{20,28},{24,16},{28,20},{1,9},{5... | collective-permute-start | bytes 1327112 | tf_op jit(solution)/shard_map/ppermute | solution.py:27
  51.4 20.1 %collective-permute-start.14 = (bf16[256,768]{1,0:T(8,128)(2,1)S(1)}, bf16[256,768]{1,0:T(8,128)(2,1)}, u32[]{:S(2)}, u32[]{:S(2)}) collective-permute-start(bf16[256,768]{1,0:T(8,128)(2,1)S(1)} %copy-done.1), channel_id=1, source_target_pairs={{0,2},{1,3},{2,0},{3,1},{4,6},{5,7},{6,4},{7,5},{8,10},{9,11},{10,... | collective-permute-start | bytes 1179656 | tf_op jit(solution)/shard_map/ppermute | solution.py:27
  54.8 17.8 %collective-permute-start.13 = (bf16[256,768]{1,0:T(8,128)(2,1)S(1)}, bf16[256,768]{1,0:T(8,128)(2,1)}, u32[]{:S(2)}, u32[]{:S(2)}) collective-permute-start(bf16[256,768]{1,0:T(8,128)(2,1)S(1)} %copy-done.1), channel_id=1, source_target_pairs={{0,1},{1,0},{2,3},{3,2},{4,5},{5,4},{6,7},{7,6},{8,9},{9,8},{10,11... | collective-permute-start | bytes 1179656 | tf_op jit(solution)/shard_map/ppermute | solution.py:27
  72.5 14.4 %collective-permute-start.15 = (bf16[256,768]{1,0:T(8,128)(2,1)}, bf16[256,768]{1,0:T(8,128)(2,1)}, u32[]{:S(2)}, u32[]{:S(2)}) collective-permute-start(bf16[256,768]{1,0:T(8,128)(2,1)} %collective-permute-done.14.refs_2_), channel_id=1, source_target_pairs={{0,1},{1,0},{2,3},{3,2},{4,5},{5,4},{6,7},{7,6},{8,9},{9,8},{10,11... | collective-permute-start | bytes 1179656 | tf_op jit(solution)/shard_map/ppermute | solution.py:27
  73.2 13.7 %collective-permute-start.23 = (bf16[80,1024]{1,0:T(8,128)(2,1)}, bf16[80,1024]{1,0:T(8,128)(2,1)S(1)}, u32[]{:S(2)}, u32[]{:S(2)}) collective-permute-start(bf16[80,1024]{1,0:T(8,128)(2,1)} %get-tuple-element.112), channel_id=1, source_target_pairs={{0,2},{1,3},{2,0},{3,1},{4,6},{5,7},{6,4},{7,5},{8,10},{9,11},{10,... | collective-permute-start | bytes 491528 | tf_op jit(solution)/shard_map/ppermute | solution.py:27
  133.3 19.5 %collective-permute-start.28 = (bf16[80,1024]{1,0:T(8,128)(2,1)}, bf16[80,1024]{1,0:T(8,128)(2,1)S(1)}, u32[]{:S(2)}, u32[]{:S(2)}) collective-permute-start(bf16[80,1024]{1,0:T(8,128)(2,1)} %get-tuple-element.120.refs_0_), channel_id=1, source_target_pairs={{0,1},{1,0},{2,3},{3,2},{4,5},{5,4},{6,7},{7,6},{8,9},{9,8},{10,11... | collective-permute-start | bytes 491528 | tf_op jit(solution)/shard_map/ppermute | solution.py:27
  135.1 19.8 %collective-permute-start.29 = (bf16[80,1024]{1,0:T(8,128)(2,1)}, bf16[80,1024]{1,0:T(8,128)(2,1)S(1)}, u32[]{:S(2)}, u32[]{:S(2)}) collective-permute-start(bf16[80,1024]{1,0:T(8,128)(2,1)} %get-tuple-element.120.refs_0_), channel_id=1, source_target_pairs={{0,2},{1,3},{2,0},{3,1},{4,6},{5,7},{6,4},{7,5},{8,10},{9,11},{10,... | collective-permute-start | bytes 491528 | tf_op jit(solution)/shard_map/ppermute | solution.py:27
  135.7 19.2 %collective-permute-start.30 = (bf16[80,1024]{1,0:T(8,128)(2,1)}, bf16[80,1024]{1,0:T(8,128)(2,1)S(1)}, u32[]{:S(2)}, u32[]{:S(2)}) collective-permute-start(bf16[80,1024]{1,0:T(8,128)(2,1)} %get-tuple-element.120.refs_0_), channel_id=1, source_target_pairs={{0,3},{1,2},{2,1},{3,0},{4,7},{5,6},{6,5},{7,4},{8,11},{9,10},{10,... | collective-permute-start | bytes 491528 | tf_op jit(solution)/shard_map/ppermute | solution.py:27
  137.8 41.4 %collective-permute-start.25 = (bf16[256,768]{1,0:T(8,128)(2,1)}, bf16[256,768]{1,0:T(8,128)(2,1)S(1)}, u32[]{:S(2)}, u32[]{:S(2)}) collective-permute-start(bf16[256,768]{1,0:T(8,128)(2,1)} %get-tuple-element.117), channel_id=1, source_target_pairs={{0,1},{1,0},{2,3},{3,2},{4,5},{5,4},{6,7},{7,6},{8,9},{9,8},{10,11... | collective-permute-start | bytes 1179656 | tf_op jit(solution)/shard_map/ppermute | solution.py:27
  138.6 40.5 %collective-permute-start.26 = (bf16[256,768]{1,0:T(8,128)(2,1)}, bf16[256,768]{1,0:T(8,128)(2,1)S(1)}, u32[]{:S(2)}, u32[]{:S(2)}) collective-permute-start(bf16[256,768]{1,0:T(8,128)(2,1)} %get-tuple-element.118), channel_id=1, source_target_pairs={{0,2},{1,3},{2,0},{3,1},{4,6},{5,7},{6,4},{7,5},{8,10},{9,11},{10,... | collective-permute-start | bytes 1179656 | tf_op jit(solution)/shard_map/ppermute | solution.py:27
  148.9 44.5 %all-to-all-start = ((bf16[8,96,1152]{2,1,0:T(8,128)(2,1)}), bf16[8,96,1152]{2,1,0:T(8,128)(2,1)S(1)}, u32[]{:S(2)}, u32[]{:S(2)}) async-start(bf16[8,96,1152]{2,1,0:T(8,128)(2,1)} %get-tuple-element.153), calls=%async_computation | async-start | bytes 3538944 | tf_op jit(solution)/shard_map/all_to_all | solution.py:1099
  152.8 27.1 %collective-permute-start.27 = (bf16[256,768]{1,0:T(8,128)(2,1)}, bf16[256,768]{1,0:T(8,128)(2,1)S(1)}, u32[]{:S(2)}, u32[]{:S(2)}) collective-permute-start(bf16[256,768]{1,0:T(8,128)(2,1)} %get-tuple-element.119), channel_id=1, source_target_pairs={{0,3},{1,2},{2,1},{3,0},{4,7},{5,6},{6,5},{7,4},{8,11},{9,10},{10,... | collective-permute-start | bytes 1179656 | tf_op jit(solution)/shard_map/ppermute | solution.py:27
  174.1 12.4 %collective-permute-start.32 = (bf16[256,768]{1,0:T(8,128)(2,1)}, bf16[256,768]{1,0:T(8,128)(2,1)}, u32[]{:S(2)}, u32[]{:S(2)}) collective-permute-start(bf16[256,768]{1,0:T(8,128)(2,1)} %get-tuple-element.148), channel_id=1, source_target_pairs={{0,1},{1,0},{2,3},{3,2},{4,5},{5,4},{6,7},{7,6},{8,9},{9,8},{10,11... | collective-permute-start | bytes 1179656 | tf_op jit(solution)/shard_map/ppermute | solution.py:27
  174.1 34.1 %collective-permute-start.34 = (bf16[256,768]{1,0:T(8,128)(2,1)}, bf16[256,768]{1,0:T(8,128)(2,1)S(1)}, u32[]{:S(2)}, u32[]{:S(2)}) collective-permute-start(bf16[256,768]{1,0:T(8,128)(2,1)} %get-tuple-element.149), channel_id=1, source_target_pairs={{0,1},{1,0},{2,3},{3,2},{4,5},{5,4},{6,7},{7,6},{8,9},{9,8},{10,11... | collective-permute-start | bytes 1179656 | tf_op jit(solution)/shard_map/ppermute | solution.py:27
  179.9 17.6 %collective-permute-start.35 = (bf16[144,1152]{1,0:T(8,128)(2,1)}, bf16[144,1152]{1,0:T(8,128)(2,1)}, u32[]{:S(2)}, u32[]{:S(2)}) collective-permute-start(bf16[144,1152]{1,0:T(8,128)(2,1)} %get-tuple-element.150), channel_id=1, source_target_pairs={{0,8},{4,12},{8,0},{12,4},{16,24},{20,28},{24,16},{28,20},{1,9},{5... | collective-permute-start | bytes 995336 | tf_op jit(solution)/shard_map/ppermute | solution.py:27
  181.6 16.7 %collective-permute-start.36 = (bf16[144,1152]{1,0:T(8,128)(2,1)}, bf16[144,1152]{1,0:T(8,128)(2,1)}, u32[]{:S(2)}, u32[]{:S(2)}) collective-permute-start(bf16[144,1152]{1,0:T(8,128)(2,1)} %get-tuple-element.151), channel_id=1, source_target_pairs={{0,16},{4,20},{8,24},{12,28},{16,0},{20,4},{24,8},{28,12},{1,17},{... | collective-permute-start | bytes 995336 | tf_op jit(solution)/shard_map/ppermute | solution.py:27
  183.1 15.3 %collective-permute-start.37 = (bf16[144,1152]{1,0:T(8,128)(2,1)}, bf16[144,1152]{1,0:T(8,128)(2,1)}, u32[]{:S(2)}, u32[]{:S(2)}) collective-permute-start(bf16[144,1152]{1,0:T(8,128)(2,1)} %get-tuple-element.152), channel_id=1, source_target_pairs={{0,24},{4,28},{8,16},{12,20},{16,8},{20,12},{24,0},{28,4},{1,25},{... | collective-permute-start | bytes 995336 | tf_op jit(solution)/shard_map/ppermute | solution.py:27
  188.4 26.4 %collective-permute-start.33 = (bf16[256,768]{1,0:T(8,128)(2,1)}, bf16[256,768]{1,0:T(8,128)(2,1)S(1)}, u32[]{:S(2)}, u32[]{:S(2)}) collective-permute-start(bf16[256,768]{1,0:T(8,128)(2,1)} %add_convert_fusion), channel_id=1, source_target_pairs={{0,2},{1,3},{2,0},{3,1},{4,6},{5,7},{6,4},{7,5},{8,10},{9,11},{10,... | collective-permute-start | bytes 1179656 | tf_op jit(solution)/shard_map/ppermute | solution.py:27
  193.7 26.8 %all-to-all-start.1 = ((bf16[8,48,2304]{2,1,0:T(8,128)(2,1)}), bf16[8,48,2304]{2,1,0:T(8,128)(2,1)S(1)}, u32[]{:S(2)}, u32[]{:S(2)}) async-start(bf16[8,48,2304]{2,1,0:T(8,128)(2,1)} %get-tuple-element.170), calls=%async_computation.1 | async-start | bytes 3538944 | tf_op jit(solution)/shard_map/all_to_all | solution.py:1188
  200.4 15.6 %collective-permute-start.38 = (bf16[24,2304]{1,0:T(8,128)(2,1)S(1)}, bf16[24,2304]{1,0:T(8,128)(2,1)S(1)}, u32[]{:S(2)}, u32[]{:S(2)}) collective-permute-start(bf16[24,2304]{1,0:T(8,128)(2,1)S(1)} %get-tuple-element.156), channel_id=1, source_target_pairs={{0,1},{1,0},{2,3},{3,2},{4,5},{5,4},{6,7},{7,6},{8,9},{9,8},{10,11... | collective-permute-start | bytes 331784 | tf_op jit(solution)/shard_map/ppermute | solution.py:27
  205.8 11.1 %collective-permute-start.39 = (bf16[24,2304]{1,0:T(8,128)(2,1)S(1)}, bf16[24,2304]{1,0:T(8,128)(2,1)S(1)}, u32[]{:S(2)}, u32[]{:S(2)}) collective-permute-start(bf16[24,2304]{1,0:T(8,128)(2,1)S(1)} %get-tuple-element.157), channel_id=1, source_target_pairs={{0,2},{1,3},{2,0},{3,1},{4,6},{5,7},{6,4},{7,5},{8,10},{9,11},{10,... | collective-permute-start | bytes 331784 | tf_op jit(solution)/shard_map/ppermute | solution.py:27
  205.8 11.1 %collective-permute-start.40 = (bf16[24,2304]{1,0:T(8,128)(2,1)S(1)}, bf16[24,2304]{1,0:T(8,128)(2,1)S(1)}, u32[]{:S(2)}, u32[]{:S(2)}) collective-permute-start(bf16[24,2304]{1,0:T(8,128)(2,1)S(1)} %get-tuple-element.158), channel_id=1, source_target_pairs={{0,3},{1,2},{2,1},{3,0},{4,7},{5,6},{6,5},{7,4},{8,11},{9,10},{10,... | collective-permute-start | bytes 331784 | tf_op jit(solution)/shard_map/ppermute | solution.py:27
  (49 other events, 403.9 us)

commit v7 on v6

--- a/solution.py
+++ b/solution.py
@@ -68,8 +68,18 @@
             arrived.append(got)
         else:
             rest = s ^ low_bit
-            parts[rest] = (after(parts[rest], *earlier).astype(f32) + got.astype(f32)).astype(bf16)
+            parts[rest] = call(
+                add_kernel,
+                [(got.shape, bf16, "v")],
+                [(after(parts[rest], *earlier), "v"), (got, "v")],
+                us=0.1,
+                small=True,
+            )[0]
     return arrived, parts[-2]
+
+
+def add_kernel(left, right, out):
+    out[...] = (left[...].astype(f32) + right[...].astype(f32)).astype(bf16)
 
 
 def near_wide(block):

time: 222 us -> 222 us (level)
  local copies, waits for them, and re-layouts: 6.09 us -> 8.76 us
    unnamed x76 -> x82, local copies, waits for them, and re-layouts: 5.97 us -> 8.64 us
    ppermute x41, waiting for transfers between devices: 55.1 us -> 52.7 us  [swap(): return lax.ppermute(block, axis, [(i, i ^ flip) for i in range(count)])]
    pallas_call x15 -> x16, Pallas kernels: 97.3 us -> 98.4 us  [call(): pl.pallas_call(kernel, out_shape=[jax.ShapeDtypeStruct(shape, dtype) for...]
  transfers between devices with their start and end apart: 43 -> 43, of which waited for: 15 -> 15; matrix products, arithmetic and copies ran while one was open for 1% -> 0% of each run, Pallas kernels for 25% -> 25%
where the time goes in v7:
time: 222 us
  Pallas kernels  98.4 us (44%)
  starting transfers between devices  57.5 us (26%)
  waiting for transfers between devices  53.6 us (24%)
  local copies, waits for them, and re-layouts  8.76 us (4%)
    pallas_call x16, Pallas kernels, call(): pl.pallas_call(kernel, out_shape=[jax.ShapeDtypeStruct(shape, dtype) for...  98.4 us
    ppermute x41, waiting for transfers between devices, swap(): return lax.ppermute(block, axis, [(i, i ^ flip) for i in range(count)])  52.7 us
    ppermute x41, starting transfers between devices, swap(): return lax.ppermute(block, axis, [(i, i ^ flip) for i in range(count)])  50 us
    unnamed x82, local copies, waits for them, and re-layouts  8.64 us
  transfers between devices with their start and end apart: 43, of which 15 were waited for; matrix products, arithmetic and copies ran while one was open for 0% of the time, Pallas kernels for 25%

profile of v7, /device:TPU:0, one launch (start us, length us, event | category | flops | bytes accessed | tf_op | source)
XLA Modules:
  0.0 221.6 jit_solution(16433629604553974047)
XLA Ops:
  0.7 2.4 %shard_map.229 = (bf16[24,2432]{1,0:T(8,128)(2,1)}, bf16[24,2432]{1,0:T(8,128)(2,1)}, bf16[24,2432]{1,0:T(8,128)(2,1)}, bf16[24,2432]{1,0:T(8,128)(2,1)}, bf16[3...) custom-call(bf16[3,24,3072]{2,1,0:T(8,128)(2,1)} %bitcast.20, bf16[1,24]{1,0:T(2,128)(2,1)} %bitcast.22, ...), custom_call_target="tpu_custom_call" | custom-call | flops 3300000000 | bytes 1 | tf_op jit(solution)/shard_map/pallas_call | solution.py:108
  3.1 3.1 %collective-permute-start.3 = (bf16[24,2432]{1,0:T(8,128)(2,1)}, bf16[24,2432]{1,0:T(8,128)(2,1)S(1)}, u32[]{:S(2)}, u32[]{:S(2)}) collective-permute-start(bf16[24,2432]{1,0:T(8,128)(2,1)} %get-tuple-element.93), channel_id=1, source_target_pairs={{0,1},{1,0},{2,3},{3,2},{4,5},{5,4},{6,7},{7,6},{8,9},{9,8},{10,11... | collective-permute-start | bytes 350216 | tf_op jit(solution)/shard_map/ppermute | solution.py:27
  6.2 2.6 %collective-permute-start.4 = (bf16[24,2432]{1,0:T(8,128)(2,1)}, bf16[24,2432]{1,0:T(8,128)(2,1)S(1)}, u32[]{:S(2)}, u32[]{:S(2)}) collective-permute-start(bf16[24,2432]{1,0:T(8,128)(2,1)} %get-tuple-element.94), channel_id=1, source_target_pairs={{0,2},{1,3},{2,0},{3,1},{4,6},{5,7},{6,4},{7,5},{8,10},{9,11},{10,... | collective-permute-start | bytes 350216 | tf_op jit(solution)/shard_map/ppermute | solution.py:27
  11.0 2.5 %collective-permute-start = (bf16[272,768]{1,0:T(8,128)(2,1)S(1)}, bf16[272,768]{1,0:T(8,128)(2,1)S(1)}, u32[]{:S(2)}, u32[]{:S(2)}) collective-permute-start(bf16[272,768]{1,0:T(8,128)(2,1)S(1)} %pad_maximum_fusion.refs_0_), channel_id=1, source_target_pairs={{0,1},{1,0},{2,3},{3,2},{4,5},{5,4},{6,7},{7,6},{8,9},{9,8},{10,11... | collective-permute-start | bytes 1253384 | tf_op jit(solution)/shard_map/ppermute | solution.py:27
  14.8 12.5 %collective-permute-done.4.refs_2_ = bf16[24,2432]{1,0:T(8,128)(2,1)S(1)} collective-permute-done((bf16[24,2432]{1,0:T(8,128)(2,1)}, bf16[24,2432]{1,0:T(8,128)(2,1)S(1)}, u32[]{:S(2)}, u32[]{:S(2)}) %collective-permute-start.4) | collective-permute-done | bytes 116768 | tf_op jit(solution)/shard_map/ppermute | solution.py:27
  27.9 2.7 %shard_map.230 = (bf16[128,1280]{1,0:T(8,128)(2,1)}, bf16[192,1152]{1,0:T(8,128)(2,1)}) custom-call(s32[3]{0:T(128)} %pad_add_fusion.meta, bf16[24,2432]{1,0:T(8,128)(2,1)} %get-tuple-element.92.refs_0_, bf16[24,2432]{1,0:T(8,128)(2,1)} %copy-done.37, bf16[24,2432]{1,0:T(8,128)(2,1)} %copy-done.38, bf16[24,2432]{1,0:T(8,128)(2,1)} %copy-done.39, ...), custom_call_target="tpu_custom_call" | custom-call | flops 2200000000 | bytes 1 | tf_op jit(solution)/shard_map/pallas_call | solution.py:108
  34.1 3.3 %collective-permute-done.1.refs_2_ = bf16[272,768]{1,0:T(8,128)(2,1)S(1)} collective-permute-done((bf16[272,768]{1,0:T(8,128)(2,1)S(1)}, bf16[272,768]{1,0:T(8,128)(2,1)S(1)}, u32[]{:S(2)}, u32[]{:S(2)}) %collective-permute-start.1) | collective-permute-done | bytes 417824 | tf_op jit(solution)/shard_map/ppermute | solution.py:27
  37.5 3.9 %collective-permute-done.9.refs_8_.refs_4_ = bf16[128,1280]{1,0:T(8,128)(2,1)S(1)} collective-permute-done((bf16[128,1280]{1,0:T(8,128)(2,1)}, bf16[128,1280]{1,0:T(8,128)(2,1)S(1)}, u32[]{:S(2)}, u32[]{:S(2)}) %collective-permute-start.9) | collective-permute-done | bytes 327712 | tf_op jit(solution)/shard_map/ppermute | solution.py:27
  42.9 4.9 %collective-permute-done.2.refs_3_ = bf16[272,768]{1,0:T(8,128)(2,1)} collective-permute-done((bf16[272,768]{1,0:T(8,128)(2,1)S(1)}, bf16[272,768]{1,0:T(8,128)(2,1)}, u32[]{:S(2)}, u32[]{:S(2)}) %collective-permute-start.2) | collective-permute-done | bytes 417824 | tf_op jit(solution)/shard_map/ppermute | solution.py:27
  47.8 2.4 %collective-permute-start.21 = (bf16[192,1152]{1,0:T(8,128)(2,1)}, bf16[192,1152]{1,0:T(8,128)(2,1)S(1)}, u32[]{:S(2)}, u32[]{:S(2)}) collective-permute-start(bf16[192,1152]{1,0:T(8,128)(2,1)} %get-tuple-element.105.refs_0_.refs_4_.refs_8_), channel_id=1, source_target_pairs={{0,24},{4,28},{8,16},{12,20},{16,8},{20,12},{24,0},{28,4},{1,25},{... | collective-permute-start | bytes 1327112 | tf_op jit(solution)/shard_map/ppermute | solution.py:27
  51.4 2.6 %collective-permute-start.14 = (bf16[256,768]{1,0:T(8,128)(2,1)S(1)}, bf16[256,768]{1,0:T(8,128)(2,1)}, u32[]{:S(2)}, u32[]{:S(2)}) collective-permute-start(bf16[256,768]{1,0:T(8,128)(2,1)S(1)} %copy-done.1), channel_id=1, source_target_pairs={{0,2},{1,3},{2,0},{3,1},{4,6},{5,7},{6,4},{7,5},{8,10},{9,11},{10,... | collective-permute-start | bytes 1179656 | tf_op jit(solution)/shard_map/ppermute | solution.py:27
  55.4 8.8 %shard_map.231 = (bf16[1024,768]{1,0:T(8,128)(2,1)}, f32[1024,384]{1,0:T(8,128)}, f32[1024,384]{1,0:T(8,128)}, bf16[1024,384]{1,0:T(8,128)(2,1)}, bf16[80,1024]{...) custom-call(s32[3]{0:T(128)} %pad_add_fusion.meta, ...), custom_call_target="tpu_custom_call" | custom-call | flops 9900000256 | bytes 1 | tf_op jit(solution)/shard_map/pallas_call | solution.py:108
  64.3 4.1 %collective-permute-done.19.refs_4_.refs_8_.refs_12_ = bf16[192,1152]{1,0:T(8,128)(2,1)S(1)} collective-permute-done((bf16[192,1152]{1,0:T(8,128)(2,1)}, bf16[192,1152]{1,0:T(8,128)(2,1)S(1)}, u32[]{:S(2)}, u32[]{:S(2)}) %collective-permute-start.19) | collective-permute-done | bytes 442400 | tf_op jit(solution)/shard_map/ppermute | solution.py:27
  68.9 2.6 %collective-permute-done.14.refs_2_ = bf16[256,768]{1,0:T(8,128)(2,1)} collective-permute-done((bf16[256,768]{1,0:T(8,128)(2,1)S(1)}, bf16[256,768]{1,0:T(8,128)(2,1)}, u32[]{:S(2)}, u32[]{:S(2)}) %collective-permute-start.14) | collective-permute-done | bytes 393248 | tf_op jit(solution)/shard_map/ppermute | solution.py:27
  75.3 5.4 %shard_map.232 = (f32[1024,384]{1,0:T(8,128)}, f32[1024,384]{1,0:T(8,128)}) custom-call(s32[3]{0:T(128)} %pad_add_fusion.meta, s32[8]{0:T(128)} %get-tuple-element.99.kinds, bf16[192,1152]{1,0:T(8,128)(2,1)} %get-tuple-element.105.refs_0_.refs_4_.refs_8_, bf16[192,1152]{1,0:T(8,128)(2,1)} %copy-done.19, bf16[192,1152]{1,0:T(8,128)(2,1)} %copy-done.18, ...), custom_call_target="tpu_custom_call" | custom-call | flops 110000000 | bytes 1 | tf_op jit(solution)/shard_map/pallas_call | solution.py:108
  80.6 6.3 %collective-permute-done.15.refs_3_ = bf16[256,768]{1,0:T(8,128)(2,1)} collective-permute-done((bf16[256,768]{1,0:T(8,128)(2,1)}, bf16[256,768]{1,0:T(8,128)(2,1)}, u32[]{:S(2)}, u32[]{:S(2)}) %collective-permute-start.15) | collective-permute-done | bytes 393248 | tf_op jit(solution)/shard_map/ppermute | solution.py:27
  87.0 2.4 %collective-permute-start.24 = (bf16[80,1024]{1,0:T(8,128)(2,1)S(1)}, bf16[80,1024]{1,0:T(8,128)(2,1)S(1)}, u32[]{:S(2)}, u32[]{:S(2)}) collective-permute-start(bf16[80,1024]{1,0:T(8,128)(2,1)S(1)} %add_convert_fusion.1), channel_id=1, source_target_pairs={{0,1},{1,0},{2,3},{3,2},{4,5},{5,4},{6,7},{7,6},{8,9},{9,8},{10,11... | collective-permute-start | bytes 491528 | tf_op jit(solution)/shard_map/ppermute | solution.py:27
  89.4 4.0 %collective-permute-done.24 = bf16[80,1024]{1,0:T(8,128)(2,1)S(1)} collective-permute-done((bf16[80,1024]{1,0:T(8,128)(2,1)S(1)}, bf16[80,1024]{1,0:T(8,128)(2,1)S(1)}, u32[]{:S(2)}, u32[]{:S(2)}) %collective-permute-start.24) | collective-permute-done | bytes 163872 | tf_op jit(solution)/shard_map/ppermute | solution.py:27
  94.1 39.2 %shard_map.233 = (bf16[256,768]{1,0:T(8,128)(2,1)}, bf16[256,768]{1,0:T(8,128)(2,1)}, bf16[256,768]{1,0:T(8,128)(2,1)}, bf16[256,768]{1,0:T(8,128)(2,1)}, bf16[1...) custom-call(s32[3]{0:T(128)} %pad_add_fusion.meta, ...), custom_call_target="tpu_custom_call" | custom-call | flops 44000002048 | bytes 1 | tf_op jit(solution)/shard_map/pallas_call | solution.py:108
  140.1 8.9 %shard_map.234 = (bf16[1024,384]{1,0:T(8,128)(2,1)}, bf16[8,96,1152]{2,1,0:T(8,128)(2,1)}, bf16[8,48,2304]{2,1,0:T(8,128)(2,1)}, f32[176,384]{1,0:T(8,128)}) custom-call(s32[3]{0:T(128)} %pad_add_fusion.meta, s32[8]{0:T(128)} %get-tuple-element.99.kinds, bf16[1024,384]{1,0:T(8,128)(2,1)} %get-tuple-element.122.refs_0_, ...), custom_call_target="tpu_custom_call" | custom-call | flops 9900000256 | bytes 1 | tf_op jit(solution)/shard_map/pallas_call | solution.py:108
  149.0 3.8 %all-to-all-start = ((bf16[8,96,1152]{2,1,0:T(8,128)(2,1)}), bf16[8,96,1152]{2,1,0:T(8,128)(2,1)S(1)}, u32[]{:S(2)}, u32[]{:S(2)}) async-start(bf16[8,96,1152]{2,1,0:T(8,128)(2,1)} %get-tuple-element.153), calls=%async_computation | async-start | bytes 3538944 | tf_op jit(solution)/shard_map/all_to_all | solution.py:1109
  152.8 2.1 collective-permute-start.27
  155.7 10.6 %shard_map.235 = (bf16[1024,384]{1,0:T(8,128)(2,1)}, bf16[4,144,1152]{2,1,0:T(8,128)(2,1)}, bf16[4,144,1152]{2,1,0:T(8,128)(2,1)}) custom-call(s32[3]{0:T(128)} %pad_add_fusion.meta, s32[8]{0:T(128)} %get-tuple-element.99.kinds, bf16[80,1024]{1,0:T(8,128)(2,1)} %get-tuple-element.120.refs_0_, bf16[80,1024]{1,0:T(8,128)(2,1)} %copy-done.34, ...), custom_call_target="tpu_custom_call" | custom-call | flops 13200000000 | bytes 1 | tf_op jit(solution)/shard_map/pallas_call | solution.py:108
  166.4 7.7 %shard_map.236 = (bf16[256,768]{1,0:T(8,128)(2,1)}, bf16[256,768]{1,0:T(8,128)(2,1)}, bf16[256,768]{1,0:T(8,128)(2,1)}, bf16[256,768]{1,0:T(8,128)(2,1)}) custom-call(s32[3]{0:T(128)} %pad_add_fusion.meta, s32[8]{0:T(128)} %get-tuple-element.99.kinds, bf16[128,1280]{1,0:T(8,128)(2,1)} %get-tuple-element.98.refs_4_.refs_0_, bf16[128,1280]{1,0:T(8,128)(2,1)} %copy-done.30, ...), custom_call_target="tpu_custom_call" | custom-call | flops 32999999488 | bytes 1 | tf_op jit(solution)/shard_map/pallas_call | solution.py:108
  176.2 2.9 %shard_map.237 = (bf16[144,1152]{1,0:T(8,128)(2,1)}, bf16[144,1152]{1,0:T(8,128)(2,1)}, bf16[144,1152]{1,0:T(8,128)(2,1)}, bf16[144,1152]{1,0:T(8,128)(2,1)}) custom-call(s32[3]{0:T(128)} %pad_add_fusion.meta, bf16[4,144,1152]{2,1,0:T(8,128)(2,1)} %get-tuple-element.138.same, bf16[4,144,1152]{2,1,0:T(8,128)(2,1)} %collective-permute-done.31.peer), custom_call_target="tpu_custom_call" | custom-call | flops 3300000000 | bytes 1 | tf_op jit(solution)/shard_map/pallas_call | solution.py:108
  183.3 3.0 %collective-permute-done.32.right = bf16[256,768]{1,0:T(8,128)(2,1)S(1)} collective-permute-done((bf16[256,768]{1,0:T(8,128)(2,1)}, bf16[256,768]{1,0:T(8,128)(2,1)S(1)}, u32[]{:S(2)}, u32[]{:S(2)}) %collective-permute-start.32) | collective-permute-done | bytes 393248 | tf_op jit(solution)/shard_map/ppermute | solution.py:27
  186.5 2.3 %collective-permute-start.33 = (bf16[256,768]{1,0:T(8,128)(2,1)S(1)}, bf16[256,768]{1,0:T(8,128)(2,1)S(1)}, u32[]{:S(2)}, u32[]{:S(2)}) collective-permute-start(bf16[256,768]{1,0:T(8,128)(2,1)S(1)} %shard_map.239), channel_id=1, source_target_pairs={{0,2},{1,3},{2,0},{3,1},{4,6},{5,7},{6,4},{7,5},{8,10},{9,11},{10,... | collective-permute-start | bytes 1179656 | tf_op jit(solution)/shard_map/ppermute | solution.py:27
  193.8 3.7 %all-to-all-start.1 = ((bf16[8,48,2304]{2,1,0:T(8,128)(2,1)}), bf16[8,48,2304]{2,1,0:T(8,128)(2,1)S(1)}, u32[]{:S(2)}, u32[]{:S(2)}) async-start(bf16[8,48,2304]{2,1,0:T(8,128)(2,1)} %get-tuple-element.170), calls=%async_computation.1 | async-start | bytes 3538944 | tf_op jit(solution)/shard_map/all_to_all | solution.py:1198
  202.3 5.2 %collective-permute-start.38 = (bf16[24,2304]{1,0:T(8,128)(2,1)S(1)}, bf16[24,2304]{1,0:T(8,128)(2,1)S(1)}, u32[]{:S(2)}, u32[]{:S(2)}) collective-permute-start(bf16[24,2304]{1,0:T(8,128)(2,1)S(1)} %get-tuple-element.156), channel_id=1, source_target_pairs={{0,1},{1,0},{2,3},{3,2},{4,5},{5,4},{6,7},{7,6},{8,9},{9,8},{10,11... | collective-permute-start | bytes 331784 | tf_op jit(solution)/shard_map/ppermute | solution.py:27
  207.5 2.4 %collective-permute-start.40 = (bf16[24,2304]{1,0:T(8,128)(2,1)S(1)}, bf16[24,2304]{1,0:T(8,128)(2,1)S(1)}, u32[]{:S(2)}, u32[]{:S(2)}) collective-permute-start(bf16[24,2304]{1,0:T(8,128)(2,1)S(1)} %get-tuple-element.158), channel_id=1, source_target_pairs={{0,3},{1,2},{2,1},{3,0},{4,7},{5,6},{6,5},{7,4},{8,11},{9,10},{10,... | collective-permute-start | bytes 331784 | tf_op jit(solution)/shard_map/ppermute | solution.py:27
  212.5 3.9 %collective-permute-done.39.refs_2_ = bf16[24,2304]{1,0:T(8,128)(2,1)S(1)} collective-permute-done((bf16[24,2304]{1,0:T(8,128)(2,1)S(1)}, bf16[24,2304]{1,0:T(8,128)(2,1)S(1)}, u32[]{:S(2)}, u32[]{:S(2)}) %collective-permute-start.39) | collective-permute-done | bytes 110624 | tf_op jit(solution)/shard_map/ppermute | solution.py:27
  216.4 3.3 %shard_map.243 = (f32[3,24,3072]{2,1,0:T(8,128)}, f32[1,24]{1,0:T(1,128)}) custom-call(s32[3]{0:T(128)S(1)} %copy-done.6, bf16[24,2304]{1,0:T(8,128)(2,1)S(1)} %get-tuple-element.155.refs_0_, bf16[24,2304]{1,0:T(8,128)(2,1)S(1)} %collective-permute-done.38.refs_1_, bf16[24,2304]{1,0:T(8,128)(2,1)S(1)} %collective-permute-done.39.refs_2_, ...), custom_call_target="tpu_custom_call" | custom-call | flops 14300000256 | bytes 1 | tf_op jit(solution)/shard_map/pallas_call | solution.py:108
  (159 shorter events, 44.2 us)
Async XLA Ops:
  3.1 11.6 %collective-permute-start.3 = (bf16[24,2432]{1,0:T(8,128)(2,1)}, bf16[24,2432]{1,0:T(8,128)(2,1)S(1)}, u32[]{:S(2)}, u32[]{:S(2)}) collective-permute-start(bf16[24,2432]{1,0:T(8,128)(2,1)} %get-tuple-element.93), channel_id=1, source_target_pairs={{0,1},{1,0},{2,3},{3,2},{4,5},{5,4},{6,7},{7,6},{8,9},{9,8},{10,11... | collective-permute-start | bytes 350216 | tf_op jit(solution)/shard_map/ppermute | solution.py:27
  6.2 21.1 %collective-permute-start.4 = (bf16[24,2432]{1,0:T(8,128)(2,1)}, bf16[24,2432]{1,0:T(8,128)(2,1)S(1)}, u32[]{:S(2)}, u32[]{:S(2)}) collective-permute-start(bf16[24,2432]{1,0:T(8,128)(2,1)} %get-tuple-element.94), channel_id=1, source_target_pairs={{0,2},{1,3},{2,0},{3,1},{4,6},{5,7},{6,4},{7,5},{8,10},{9,11},{10,... | collective-permute-start | bytes 350216 | tf_op jit(solution)/shard_map/ppermute | solution.py:27
  8.8 18.5 %collective-permute-start.5 = (bf16[24,2432]{1,0:T(8,128)(2,1)}, bf16[24,2432]{1,0:T(8,128)(2,1)S(1)}, u32[]{:S(2)}, u32[]{:S(2)}) collective-permute-start(bf16[24,2432]{1,0:T(8,128)(2,1)} %get-tuple-element.95), channel_id=1, source_target_pairs={{0,3},{1,2},{2,1},{3,0},{4,7},{5,6},{6,5},{7,4},{8,11},{9,10},{10,... | collective-permute-start | bytes 350216 | tf_op jit(solution)/shard_map/ppermute | solution.py:27
  9.1 28.3 %collective-permute-start.1 = (bf16[272,768]{1,0:T(8,128)(2,1)S(1)}, bf16[272,768]{1,0:T(8,128)(2,1)S(1)}, u32[]{:S(2)}, u32[]{:S(2)}) collective-permute-start(bf16[272,768]{1,0:T(8,128)(2,1)S(1)} %pad_maximum_fusion.refs_0_), channel_id=1, source_target_pairs={{0,2},{1,3},{2,0},{3,1},{4,6},{5,7},{6,4},{7,5},{8,10},{9,11},{10,... | collective-permute-start | bytes 1253384 | tf_op jit(solution)/shard_map/ppermute | solution.py:27
  11.0 26.4 %collective-permute-start = (bf16[272,768]{1,0:T(8,128)(2,1)S(1)}, bf16[272,768]{1,0:T(8,128)(2,1)S(1)}, u32[]{:S(2)}, u32[]{:S(2)}) collective-permute-start(bf16[272,768]{1,0:T(8,128)(2,1)S(1)} %pad_maximum_fusion.refs_0_), channel_id=1, source_target_pairs={{0,1},{1,0},{2,3},{3,2},{4,5},{5,4},{6,7},{7,6},{8,9},{9,8},{10,11... | collective-permute-start | bytes 1253384 | tf_op jit(solution)/shard_map/ppermute | solution.py:27
  30.6 10.8 %collective-permute-start.9 = (bf16[128,1280]{1,0:T(8,128)(2,1)}, bf16[128,1280]{1,0:T(8,128)(2,1)S(1)}, u32[]{:S(2)}, u32[]{:S(2)}) collective-permute-start(bf16[128,1280]{1,0:T(8,128)(2,1)} %get-tuple-element.98.refs_4_.refs_0_), channel_id=1, source_target_pairs={{0,16},{4,20},{8,24},{12,28},{16,0},{20,4},{24,8},{28,12},{1,17},{... | collective-permute-start | bytes 983048 | tf_op jit(solution)/shard_map/ppermute | solution.py:27
  37.4 10.5 %collective-permute-start.2 = (bf16[272,768]{1,0:T(8,128)(2,1)S(1)}, bf16[272,768]{1,0:T(8,128)(2,1)}, u32[]{:S(2)}, u32[]{:S(2)}) collective-permute-start(bf16[272,768]{1,0:T(8,128)(2,1)S(1)} %collective-permute-done.1.refs_2_), channel_id=1, source_target_pairs={{0,1},{1,0},{2,3},{3,2},{4,5},{5,4},{6,7},{7,6},{8,9},{9,8},{10,11... | collective-permute-start | bytes 1253384 | tf_op jit(solution)/shard_map/ppermute | solution.py:27
  37.4 12.9 %collective-permute-start.6 = (bf16[128,1280]{1,0:T(8,128)(2,1)}, bf16[128,1280]{1,0:T(8,128)(2,1)S(1)}, u32[]{:S(2)}, u32[]{:S(2)}) collective-permute-start(bf16[128,1280]{1,0:T(8,128)(2,1)} %get-tuple-element.98.refs_4_.refs_0_), channel_id=1, source_target_pairs={{0,4},{4,0},{8,12},{12,8},{16,20},{20,16},{24,28},{28,24},{1,5},{5... | collective-permute-start | bytes 983048 | tf_op jit(solution)/shard_map/ppermute | solution.py:27
  41.5 10.0 %collective-permute-start.12 = (bf16[128,1280]{1,0:T(8,128)(2,1)S(1)}, bf16[128,1280]{1,0:T(8,128)(2,1)S(1)}, u32[]{:S(2)}, u32[]{:S(2)}) collective-permute-start(bf16[128,1280]{1,0:T(8,128)(2,1)S(1)} %collective-permute-done.11.refs_10_.refs_6_), channel_id=1, source_target_pairs={{0,4},{4,0},{8,12},{12,8},{16,20},{20,16},{24,28},{28,24},{1,5},{5... | collective-permute-start | bytes 983048 | tf_op jit(solution)/shard_map/ppermute | solution.py:27
  42.9 11.1 %collective-permute-start.8 = (bf16[128,1280]{1,0:T(8,128)(2,1)S(1)}, bf16[128,1280]{1,0:T(8,128)(2,1)S(1)}, u32[]{:S(2)}, u32[]{:S(2)}) collective-permute-start(bf16[128,1280]{1,0:T(8,128)(2,1)S(1)} %collective-permute-done.7.refs_6_.refs_2_), channel_id=1, source_target_pairs={{0,4},{4,0},{8,12},{12,8},{16,20},{20,16},{24,28},{28,24},{1,5},{5... | collective-permute-start | bytes 983048 | tf_op jit(solution)/shard_map/ppermute | solution.py:27
  47.8 16.3 %collective-permute-start.21 = (bf16[192,1152]{1,0:T(8,128)(2,1)}, bf16[192,1152]{1,0:T(8,128)(2,1)S(1)}, u32[]{:S(2)}, u32[]{:S(2)}) collective-permute-start(bf16[192,1152]{1,0:T(8,128)(2,1)} %get-tuple-element.105.refs_0_.refs_4_.refs_8_), channel_id=1, source_target_pairs={{0,24},{4,28},{8,16},{12,20},{16,8},{20,12},{24,0},{28,4},{1,25},{... | collective-permute-start | bytes 1327112 | tf_op jit(solution)/shard_map/ppermute | solution.py:27
  50.3 18.1 %collective-permute-start.19 = (bf16[192,1152]{1,0:T(8,128)(2,1)}, bf16[192,1152]{1,0:T(8,128)(2,1)S(1)}, u32[]{:S(2)}, u32[]{:S(2)}) collective-permute-start(bf16[192,1152]{1,0:T(8,128)(2,1)} %get-tuple-element.105.refs_0_.refs_4_.refs_8_), channel_id=1, source_target_pairs={{0,16},{4,20},{8,24},{12,28},{16,0},{20,4},{24,8},{28,12},{1,17},{... | collective-permute-start | bytes 1327112 | tf_op jit(solution)/shard_map/ppermute | solution.py:27
  50.8 17.7 %collective-permute-start.17 = (bf16[192,1152]{1,0:T(8,128)(2,1)}, bf16[192,1152]{1,0:T(8,128)(2,1)S(1)}, u32[]{:S(2)}, u32[]{:S(2)}) collective-permute-start(bf16[192,1152]{1,0:T(8,128)(2,1)} %get-tuple-element.105.refs_0_.refs_4_.refs_8_), channel_id=1, source_target_pairs={{0,8},{4,12},{8,0},{12,4},{16,24},{20,28},{24,16},{28,20},{1,9},{5... | collective-permute-start | bytes 1327112 | tf_op jit(solution)/shard_map/ppermute | solution.py:27
  51.4 20.1 %collective-permute-start.14 = (bf16[256,768]{1,0:T(8,128)(2,1)S(1)}, bf16[256,768]{1,0:T(8,128)(2,1)}, u32[]{:S(2)}, u32[]{:S(2)}) collective-permute-start(bf16[256,768]{1,0:T(8,128)(2,1)S(1)} %copy-done.1), channel_id=1, source_target_pairs={{0,2},{1,3},{2,0},{3,1},{4,6},{5,7},{6,4},{7,5},{8,10},{9,11},{10,... | collective-permute-start | bytes 1179656 | tf_op jit(solution)/shard_map/ppermute | solution.py:27
  54.8 17.8 %collective-permute-start.13 = (bf16[256,768]{1,0:T(8,128)(2,1)S(1)}, bf16[256,768]{1,0:T(8,128)(2,1)}, u32[]{:S(2)}, u32[]{:S(2)}) collective-permute-start(bf16[256,768]{1,0:T(8,128)(2,1)S(1)} %copy-done.1), channel_id=1, source_target_pairs={{0,1},{1,0},{2,3},{3,2},{4,5},{5,4},{6,7},{7,6},{8,9},{9,8},{10,11... | collective-permute-start | bytes 1179656 | tf_op jit(solution)/shard_map/ppermute | solution.py:27
  72.6 14.3 %collective-permute-start.15 = (bf16[256,768]{1,0:T(8,128)(2,1)}, bf16[256,768]{1,0:T(8,128)(2,1)}, u32[]{:S(2)}, u32[]{:S(2)}) collective-permute-start(bf16[256,768]{1,0:T(8,128)(2,1)} %collective-permute-done.14.refs_2_), channel_id=1, source_target_pairs={{0,1},{1,0},{2,3},{3,2},{4,5},{5,4},{6,7},{7,6},{8,9},{9,8},{10,11... | collective-permute-start | bytes 1179656 | tf_op jit(solution)/shard_map/ppermute | solution.py:27
  73.2 13.7 %collective-permute-start.23 = (bf16[80,1024]{1,0:T(8,128)(2,1)}, bf16[80,1024]{1,0:T(8,128)(2,1)S(1)}, u32[]{:S(2)}, u32[]{:S(2)}) collective-permute-start(bf16[80,1024]{1,0:T(8,128)(2,1)} %get-tuple-element.112), channel_id=1, source_target_pairs={{0,2},{1,3},{2,0},{3,1},{4,6},{5,7},{6,4},{7,5},{8,10},{9,11},{10,... | collective-permute-start | bytes 491528 | tf_op jit(solution)/shard_map/ppermute | solution.py:27
  133.3 19.5 %collective-permute-start.28 = (bf16[80,1024]{1,0:T(8,128)(2,1)}, bf16[80,1024]{1,0:T(8,128)(2,1)S(1)}, u32[]{:S(2)}, u32[]{:S(2)}) collective-permute-start(bf16[80,1024]{1,0:T(8,128)(2,1)} %get-tuple-element.120.refs_0_), channel_id=1, source_target_pairs={{0,1},{1,0},{2,3},{3,2},{4,5},{5,4},{6,7},{7,6},{8,9},{9,8},{10,11... | collective-permute-start | bytes 491528 | tf_op jit(solution)/shard_map/ppermute | solution.py:27
  135.1 19.8 %collective-permute-start.29 = (bf16[80,1024]{1,0:T(8,128)(2,1)}, bf16[80,1024]{1,0:T(8,128)(2,1)S(1)}, u32[]{:S(2)}, u32[]{:S(2)}) collective-permute-start(bf16[80,1024]{1,0:T(8,128)(2,1)} %get-tuple-element.120.refs_0_), channel_id=1, source_target_pairs={{0,2},{1,3},{2,0},{3,1},{4,6},{5,7},{6,4},{7,5},{8,10},{9,11},{10,... | collective-permute-start | bytes 491528 | tf_op jit(solution)/shard_map/ppermute | solution.py:27
  135.7 19.3 %collective-permute-start.30 = (bf16[80,1024]{1,0:T(8,128)(2,1)}, bf16[80,1024]{1,0:T(8,128)(2,1)S(1)}, u32[]{:S(2)}, u32[]{:S(2)}) collective-permute-start(bf16[80,1024]{1,0:T(8,128)(2,1)} %get-tuple-element.120.refs_0_), channel_id=1, source_target_pairs={{0,3},{1,2},{2,1},{3,0},{4,7},{5,6},{6,5},{7,4},{8,11},{9,10},{10,... | collective-permute-start | bytes 491528 | tf_op jit(solution)/shard_map/ppermute | solution.py:27
  137.8 41.3 %collective-permute-start.25 = (bf16[256,768]{1,0:T(8,128)(2,1)}, bf16[256,768]{1,0:T(8,128)(2,1)S(1)}, u32[]{:S(2)}, u32[]{:S(2)}) collective-permute-start(bf16[256,768]{1,0:T(8,128)(2,1)} %get-tuple-element.117), channel_id=1, source_target_pairs={{0,1},{1,0},{2,3},{3,2},{4,5},{5,4},{6,7},{7,6},{8,9},{9,8},{10,11... | collective-permute-start | bytes 1179656 | tf_op jit(solution)/shard_map/ppermute | solution.py:27
  138.6 41.2 %collective-permute-start.26 = (bf16[256,768]{1,0:T(8,128)(2,1)}, bf16[256,768]{1,0:T(8,128)(2,1)}, u32[]{:S(2)}, u32[]{:S(2)}) collective-permute-start(bf16[256,768]{1,0:T(8,128)(2,1)} %get-tuple-element.118), channel_id=1, source_target_pairs={{0,2},{1,3},{2,0},{3,1},{4,6},{5,7},{6,4},{7,5},{8,10},{9,11},{10,... | collective-permute-start | bytes 1179656 | tf_op jit(solution)/shard_map/ppermute | solution.py:27
  149.0 43.9 %all-to-all-start = ((bf16[8,96,1152]{2,1,0:T(8,128)(2,1)}), bf16[8,96,1152]{2,1,0:T(8,128)(2,1)S(1)}, u32[]{:S(2)}, u32[]{:S(2)}) async-start(bf16[8,96,1152]{2,1,0:T(8,128)(2,1)} %get-tuple-element.153), calls=%async_computation | async-start | bytes 3538944 | tf_op jit(solution)/shard_map/all_to_all | solution.py:1109
  152.8 27.0 %collective-permute-start.27 = (bf16[256,768]{1,0:T(8,128)(2,1)}, bf16[256,768]{1,0:T(8,128)(2,1)}, u32[]{:S(2)}, u32[]{:S(2)}) collective-permute-start(bf16[256,768]{1,0:T(8,128)(2,1)} %get-tuple-element.119), channel_id=1, source_target_pairs={{0,3},{1,2},{2,1},{3,0},{4,7},{5,6},{6,5},{7,4},{8,11},{9,10},{10,... | collective-permute-start | bytes 1179656 | tf_op jit(solution)/shard_map/ppermute | solution.py:27
  174.1 12.3 %collective-permute-start.32 = (bf16[256,768]{1,0:T(8,128)(2,1)}, bf16[256,768]{1,0:T(8,128)(2,1)S(1)}, u32[]{:S(2)}, u32[]{:S(2)}) collective-permute-start(bf16[256,768]{1,0:T(8,128)(2,1)} %get-tuple-element.148), channel_id=1, source_target_pairs={{0,1},{1,0},{2,3},{3,2},{4,5},{5,4},{6,7},{7,6},{8,9},{9,8},{10,11... | collective-permute-start | bytes 1179656 | tf_op jit(solution)/shard_map/ppermute | solution.py:27
  174.2 35.7 %collective-permute-start.34 = (bf16[256,768]{1,0:T(8,128)(2,1)}, bf16[256,768]{1,0:T(8,128)(2,1)S(1)}, u32[]{:S(2)}, u32[]{:S(2)}) collective-permute-start(bf16[256,768]{1,0:T(8,128)(2,1)} %get-tuple-element.149), channel_id=1, source_target_pairs={{0,1},{1,0},{2,3},{3,2},{4,5},{5,4},{6,7},{7,6},{8,9},{9,8},{10,11... | collective-permute-start | bytes 1179656 | tf_op jit(solution)/shard_map/ppermute | solution.py:27
  179.8 17.8 %collective-permute-start.35 = (bf16[144,1152]{1,0:T(8,128)(2,1)}, bf16[144,1152]{1,0:T(8,128)(2,1)}, u32[]{:S(2)}, u32[]{:S(2)}) collective-permute-start(bf16[144,1152]{1,0:T(8,128)(2,1)} %get-tuple-element.150), channel_id=1, source_target_pairs={{0,8},{4,12},{8,0},{12,4},{16,24},{20,28},{24,16},{28,20},{1,9},{5... | collective-permute-start | bytes 995336 | tf_op jit(solution)/shard_map/ppermute | solution.py:27
  181.6 16.8 %collective-permute-start.36 = (bf16[144,1152]{1,0:T(8,128)(2,1)}, bf16[144,1152]{1,0:T(8,128)(2,1)}, u32[]{:S(2)}, u32[]{:S(2)}) collective-permute-start(bf16[144,1152]{1,0:T(8,128)(2,1)} %get-tuple-element.151), channel_id=1, source_target_pairs={{0,16},{4,20},{8,24},{12,28},{16,0},{20,4},{24,8},{28,12},{1,17},{... | collective-permute-start | bytes 995336 | tf_op jit(solution)/shard_map/ppermute | solution.py:27
  183.1 15.3 %collective-permute-start.37 = (bf16[144,1152]{1,0:T(8,128)(2,1)}, bf16[144,1152]{1,0:T(8,128)(2,1)}, u32[]{:S(2)}, u32[]{:S(2)}) collective-permute-start(bf16[144,1152]{1,0:T(8,128)(2,1)} %get-tuple-element.152), channel_id=1, source_target_pairs={{0,24},{4,28},{8,16},{12,20},{16,8},{20,12},{24,0},{28,4},{1,25},{... | collective-permute-start | bytes 995336 | tf_op jit(solution)/shard_map/ppermute | solution.py:27
  186.5 23.5 %collective-permute-start.33 = (bf16[256,768]{1,0:T(8,128)(2,1)S(1)}, bf16[256,768]{1,0:T(8,128)(2,1)S(1)}, u32[]{:S(2)}, u32[]{:S(2)}) collective-permute-start(bf16[256,768]{1,0:T(8,128)(2,1)S(1)} %shard_map.239), channel_id=1, source_target_pairs={{0,2},{1,3},{2,0},{3,1},{4,6},{5,7},{6,4},{7,5},{8,10},{9,11},{10,... | collective-permute-start | bytes 1179656 | tf_op jit(solution)/shard_map/ppermute | solution.py:27
  193.8 26.8 %all-to-all-start.1 = ((bf16[8,48,2304]{2,1,0:T(8,128)(2,1)}), bf16[8,48,2304]{2,1,0:T(8,128)(2,1)S(1)}, u32[]{:S(2)}, u32[]{:S(2)}) async-start(bf16[8,48,2304]{2,1,0:T(8,128)(2,1)} %get-tuple-element.170), calls=%async_computation.1 | async-start | bytes 3538944 | tf_op jit(solution)/shard_map/all_to_all | solution.py:1198
  202.3 10.2 %collective-permute-start.38 = (bf16[24,2304]{1,0:T(8,128)(2,1)S(1)}, bf16[24,2304]{1,0:T(8,128)(2,1)S(1)}, u32[]{:S(2)}, u32[]{:S(2)}) collective-permute-start(bf16[24,2304]{1,0:T(8,128)(2,1)S(1)} %get-tuple-element.156), channel_id=1, source_target_pairs={{0,1},{1,0},{2,3},{3,2},{4,5},{5,4},{6,7},{7,6},{8,9},{9,8},{10,11... | collective-permute-start | bytes 331784 | tf_op jit(solution)/shard_map/ppermute | solution.py:27
  (52 other events, 392.1 us)
